TPU v7x, 256 devices: a whole 4x4x8 slice. The times are simulated.
256 devices in a mesh: dp: 32 (over y, x, core), seq: 8 (over z).
Axes of the slice: x: 4, y: 4, z: 8, core: 2. Of those that a mesh axis runs over, the one named last changes fastest.
Arguments:
- query: bfloat16 [32768, 8192], P(('dp', 'seq')), may hold values from -40 to 40, as said below
- key_projection: bfloat16 [32768, 1024], P(('dp', 'seq')), may hold values from -40 to 40, as said below
- value: bfloat16 [32768, 1024], P(('dp', 'seq')), may hold values from -6 to 6
- d_out: bfloat16 [32768, 8192], P(('dp', 'seq')), may hold values from -6 to 6
- q_gain: float32 [128], replicated, may hold values from 0.1 to 1.9
- key_norm_gain: float32 [128], replicated, may hold values from 0.1 to 1.9
- seq_lengths: int32 [32, 3], P('dp'), may hold values from 1 to 512, 1024 in all within a row
- send_order: int32 [32, 8, 128], P('dp', 'seq'), may hold values from 0 to 127, each once within a row
- recv_order: int32 [32, 8, 128], P('dp', 'seq'), may hold values from 0 to 127, each once within a row
Outputs:
- attn_out: bfloat16 [32768, 8192], P(('dp', 'seq'))
- d_query: bfloat16 [32768, 8192], P(('dp', 'seq'))
- d_key: bfloat16 [32768, 1024], P(('dp', 'seq'))
- d_value: bfloat16 [32768, 1024], P(('dp', 'seq'))
Inputs may be any that keep to these rules, and one draw needn't show every extreme that they name: query is bounded in magnitude. key_projection is bounded in magnitude. `seq_lengths`: each group's 3 lengths sum to 1024, and the largest of each group is 512. `send_order`: each device's 128 entries are a permutation. `recv_order`: each device's 128 entries are a permutation.
All inputs are finite; a program needn't handle non-finite values.
Results may differ from a plain program's by a relative error of at most 0.0083.
Values may be sent and summed in bfloat16 or wider, within the bound.
No kernel may reach another device: no remote copies, remote signals or barrier semaphores. Data moves between devices by JAX's collectives and lax.ppermute only.
A program may use at most 128 MiB of HBM per device.

v0:
```python
import math

import jax
import jax.numpy as jnp
from jax import lax
from jax.sharding import PartitionSpec as P

QUERY_HEADS = 64
KEY_VALUE_HEADS = 8
HEAD_SIZE = 128


EPS = 1e-06


def for_sending(shard):
    return jax.tree.map(lambda a: a.astype(jnp.bfloat16) if a.dtype == jnp.float32 else a, shard)


def apply_norm(row_list, gain, heads):
    shaped = row_list.reshape(row_list.shape[0], heads, -1)
    factor = lax.rsqrt(jnp.mean(shaped * shaped, axis=-1, keepdims=True) + EPS)
    return (shaped * factor * gain).reshape(row_list.shape[0], -1)


def segment_of(position, lengths):
    ends = jnp.cumsum(lengths)
    return jnp.sum((position[:, None] >= ends[None, :]).astype(jnp.int32), axis=1)


def attend(
    query_head_split,
    key_head_split,
    value_head_split,
    heads_gradient,
    q_seg,
    q_pos,
    k_seg,
    k_pos,
    spans,
    block_rows,
):
    groups, query_group_ratio, q_len, width = query_head_split.shape
    k_len = key_head_split.shape[1]
    scale = width ** (-0.5)

    def per_group(items):
        q_all, k_one, v_one, d_all = items
        dk_total = jnp.zeros((k_len, width), jnp.float32)
        dv_total = jnp.zeros((k_len, width), jnp.float32)
        out_blocks = []
        dq_blocks = []
        for block_number, (start, length) in enumerate(spans):
            low_row = block_number * block_rows
            q_part = q_all[:, low_row : low_row + block_rows]
            d_part = d_all[:, low_row : low_row + block_rows]
            seg_part = q_seg[low_row : low_row + block_rows]
            pos_part = q_pos[low_row : low_row + block_rows]
            k_window = lax.dynamic_slice_in_dim(k_one, start, length, 0)
            v_window = lax.dynamic_slice_in_dim(v_one, start, length, 0)
            kseg_window = lax.dynamic_slice_in_dim(k_seg, start, length, 0)
            kpos_window = lax.dynamic_slice_in_dim(k_pos, start, length, 0)
            visible = (seg_part[:, None] == kseg_window[None, :]) & (
                kpos_window[None, :] <= pos_part[:, None]
            )
            scores = (
                jnp.einsum("hqd,kd->hqk", q_part, k_window, preferred_element_type=jnp.float32)
                * scale
            )
            expo = jnp.where(visible[None], jnp.exp(scores), 0.0)
            weights = expo / jnp.sum(expo, axis=-1, keepdims=True)
            weights_low = weights.astype(jnp.bfloat16)
            out = jnp.einsum(
                "hqk,kd->hqd", weights_low, v_window, preferred_element_type=jnp.float32
            ).astype(jnp.bfloat16)
            out_kept = lax.optimization_barrier(out)
            delta = jnp.sum(
                d_part.astype(jnp.float32) * out_kept.astype(jnp.float32), axis=-1, keepdims=True
            )
            d_weights = jnp.einsum(
                "hqd,kd->hqk", d_part, v_window, preferred_element_type=jnp.float32
            )
            d_scores = (weights * (d_weights - delta)).astype(jnp.bfloat16)
            d_q = (
                jnp.einsum("hqk,kd->hqd", d_scores, k_window, preferred_element_type=jnp.float32)
                * scale
            ).astype(jnp.bfloat16)
            dk_window = (
                jnp.einsum("hqk,hqd->kd", d_scores, q_part, preferred_element_type=jnp.float32)
                * scale
            )
            dv_window = jnp.einsum(
                "hqk,hqd->kd", weights_low, d_part, preferred_element_type=jnp.float32
            )
            dk_total = lax.dynamic_update_slice_in_dim(
                dk_total, lax.dynamic_slice_in_dim(dk_total, start, length, 0) + dk_window, start, 0
            )
            dv_total = lax.dynamic_update_slice_in_dim(
                dv_total, lax.dynamic_slice_in_dim(dv_total, start, length, 0) + dv_window, start, 0
            )
            out_blocks.append(out)
            dq_blocks.append(d_q)
        out_all = jnp.concatenate(out_blocks, axis=1)
        dq_all = jnp.concatenate(dq_blocks, axis=1)
        return (out_all, dq_all, dk_total, dv_total)

    return lax.map(per_group, (query_head_split, key_head_split, value_head_split, heads_gradient))


def heads_to_rows(values):
    groups, query_group_ratio, length, width = values.shape
    return values.transpose(2, 0, 1, 3).reshape(length, groups * query_group_ratio * width)


def per_device(
    query, key_projection, value, d_out, q_gain, key_norm_gain, seq_lengths, send_order, recv_order
):
    row_list = query.shape[0]
    query_group_ratio = QUERY_HEADS // KEY_VALUE_HEADS
    qn_float, q_pull = jax.vjp(
        lambda input_tensor: apply_norm(input_tensor, q_gain, QUERY_HEADS),
        query.astype(jnp.float32),
    )
    key_normed_single, key_fetcher = jax.vjp(
        lambda input_tensor: apply_norm(input_tensor, key_norm_gain, KEY_VALUE_HEADS),
        key_projection.astype(jnp.float32),
    )
    qn = qn_float.astype(jnp.bfloat16)
    kn = key_normed_single.astype(jnp.bfloat16)
    leaving = send_order[0, 0]
    arriving = recv_order[0, 0]
    lengths = seq_lengths[0]
    q_sent = qn[leaving]
    k_sent = kn[leaving]
    v_sent = value[leaving]
    d_sent = d_out[leaving]
    q_recv, k_recv, v_recv, d_recv = (
        lax.all_to_all(q_sent, "dp", split_axis=0, concat_axis=0, tiled=True),
        lax.all_to_all(k_sent, "dp", split_axis=0, concat_axis=0, tiled=True),
        lax.all_to_all(v_sent, "dp", split_axis=0, concat_axis=0, tiled=True),
        lax.all_to_all(d_sent, "dp", split_axis=0, concat_axis=0, tiled=True),
    )
    q_pack = q_recv[arriving]
    k_pack = k_recv[arriving]
    v_pack = v_recv[arriving]
    d_pack = d_recv[arriving]
    q_cols, k_cols, v_cols, d_cols = (
        lax.all_to_all(q_pack, "seq", split_axis=1, concat_axis=0, tiled=True),
        lax.all_to_all(k_pack, "seq", split_axis=1, concat_axis=0, tiled=True),
        lax.all_to_all(v_pack, "seq", split_axis=1, concat_axis=0, tiled=True),
        lax.all_to_all(d_pack, "seq", split_axis=1, concat_axis=0, tiled=True),
    )
    grand_total = q_cols.shape[0]
    local_groups = k_cols.shape[1] // HEAD_SIZE
    position = jnp.arange(grand_total, dtype=jnp.int32)
    segment = segment_of(position, lengths)
    block_rows = math.gcd(grand_total, max(128, grand_total // 8))
    window = min(grand_total, grand_total // 2 + block_rows)
    spans = [
        (
            max(0, (block_number + 1) * block_rows - window),
            min((block_number + 1) * block_rows, window),
        )
        for block_number in range(grand_total // block_rows)
    ]
    query_head_split = q_cols.reshape(
        grand_total, local_groups, query_group_ratio, HEAD_SIZE
    ).transpose(1, 2, 0, 3)
    heads_gradient = d_cols.reshape(
        grand_total, local_groups, query_group_ratio, HEAD_SIZE
    ).transpose(1, 2, 0, 3)
    key_head_split = k_cols.reshape(grand_total, local_groups, HEAD_SIZE).transpose(1, 0, 2)
    value_head_split = v_cols.reshape(grand_total, local_groups, HEAD_SIZE).transpose(1, 0, 2)
    out, d_q, dk_total, dv_total = attend(
        query_head_split,
        key_head_split,
        value_head_split,
        heads_gradient,
        segment,
        position,
        segment,
        position,
        spans,
        block_rows,
    )
    out_cols = heads_to_rows(out)
    dq_cols = heads_to_rows(d_q)
    dk_cols = (
        dk_total.astype(jnp.bfloat16)
        .transpose(1, 0, 2)
        .reshape(grand_total, local_groups * HEAD_SIZE)
    )
    dv_cols = (
        dv_total.astype(jnp.bfloat16)
        .transpose(1, 0, 2)
        .reshape(grand_total, local_groups * HEAD_SIZE)
    )
    out_rows, dq_rows, dk_rows, dv_rows = (
        lax.all_to_all(
            for_sending(out_cols), "seq", split_axis=0, concat_axis=1, tiled=True
        ).astype(out_cols.dtype),
        lax.all_to_all(for_sending(dq_cols), "seq", split_axis=0, concat_axis=1, tiled=True).astype(
            dq_cols.dtype
        ),
        lax.all_to_all(dk_cols, "seq", split_axis=0, concat_axis=1, tiled=True),
        lax.all_to_all(dv_cols, "seq", split_axis=0, concat_axis=1, tiled=True),
    )
    undo_recv = (
        jnp.zeros((row_list,), jnp.int32).at[arriving].set(jnp.arange(row_list, dtype=jnp.int32))
    )
    out_back = out_rows[undo_recv]
    dq_back = dq_rows[undo_recv]
    dk_back = dk_rows[undo_recv]
    dv_back = dv_rows[undo_recv]
    out_home, dq_home, dk_home, dv_home = (
        lax.all_to_all(for_sending(out_back), "dp", split_axis=0, concat_axis=0, tiled=True).astype(
            out_back.dtype
        ),
        lax.all_to_all(for_sending(dq_back), "dp", split_axis=0, concat_axis=0, tiled=True).astype(
            dq_back.dtype
        ),
        lax.all_to_all(dk_back, "dp", split_axis=0, concat_axis=0, tiled=True),
        lax.all_to_all(dv_back, "dp", split_axis=0, concat_axis=0, tiled=True),
    )
    undo_send = (
        jnp.zeros((row_list,), jnp.int32).at[leaving].set(jnp.arange(row_list, dtype=jnp.int32))
    )
    attn_out = out_home[undo_send]
    dqn = lax.optimization_barrier(dq_home[undo_send])
    dkn = lax.optimization_barrier(dk_home[undo_send])
    d_value = dv_home[undo_send]
    d_query = q_pull(dqn.astype(jnp.float32))[0].astype(jnp.bfloat16)
    d_key = key_fetcher(dkn.astype(jnp.float32))[0].astype(jnp.bfloat16)
    return (attn_out, d_query, d_key, d_value)


def solution(mesh):
    in_specs = (
        P(("dp", "seq"), None),
        P(("dp", "seq"), None),
        P(("dp", "seq"), None),
        P(("dp", "seq"), None),
        P(),
        P(),
        P("dp", None),
        P("dp", "seq", None),
        P("dp", "seq", None),
    )
    out_specs = (
        P(("dp", "seq"), None),
        P(("dp", "seq"), None),
        P(("dp", "seq"), None),
        P(("dp", "seq"), None),
    )
    return jax.shard_map(
        per_device, mesh=mesh, in_specs=in_specs, out_specs=out_specs, check_vma=False
    )
```

profile of v0, /device:TPU:1, one launch (start us, length us, event | category | flops | bytes accessed | tf_op | source)
XLA Modules:
  0.0 573.3 jit_solution(8171584031064099493)
XLA Ops:
  6.9 8.6 %all-to-all-start.2 = ((bf16[32,4,1024]{2,1,0:T(4,128)(2,1)}), bf16[32,4,1024]{2,1,0:T(4,128)(2,1)S(1)}, u32[]{:S(2)}, u32[]{:S(2)}) async-start(bf16[32,4,1024]{2,1,0:T(4,128)(2,1)} %all_to_all.174), calls=%async_computation.2 | async-start | bytes 524288 | tf_op jit(solution)/shard_map/all_to_all | solution.py:139
  17.5 2.7 copy.272
  21.9 2.5 all-to-all-done.2
  24.4 4.9 all-to-all-start.4
  31.3 6.9 %all-to-all-done.4 = bf16[32,4,1024]{2,1,0:T(4,128)(2,1)S(1)} async-done(((bf16[32,4,1024]{2,1,0:T(4,128)(2,1)}), bf16[32,4,1024]{2,1,0:T(4,128)(2,1)S(1)}, u32[]{:S(2)}, u32[]{:S(2)}) %all-to-all-start.4) | async-done | bytes 262176 | tf_op jit(solution)/shard_map/all_to_all | solution.py:140
  38.2 8.2 %all-to-all-start.3 = ((bf16[128,8,128]{2,0,1:T(8,128)(2,1)}), bf16[128,8,128]{2,0,1:T(8,128)(2,1)S(1)}, u32[]{:S(2)}, u32[]{:S(2)}) async-start(bf16[128,8,128]{2,0,1:T(8,128)(2,1)} %copy.203), calls=%async_computation.3 | async-start | bytes 524288 | tf_op jit(solution)/shard_map/all_to_all | solution.py:149
  46.4 3.3 multiply_reduce_fusion.1
  52.4 6.0 %all-to-all-done.3 = bf16[128,8,128]{2,0,1:T(8,128)(2,1)S(1)} async-done(((bf16[128,8,128]{2,0,1:T(8,128)(2,1)}), bf16[128,8,128]{2,0,1:T(8,128)(2,1)S(1)}, u32[]{:S(2)}, u32[]{:S(2)}) %all-to-all-start.3) | async-done | bytes 262176 | tf_op jit(solution)/shard_map/all_to_all | solution.py:149
  58.4 3.6 all-to-all-start.5
  65.2 4.1 fusion.2
  69.3 6.9 %gather_fusion = bf16[128,8192]{1,0:T(8,128)(2,1)} fusion(bf16[128,8192]{1,0:T(8,128)(2,1)} %fusion.2, s32[1024]{0:T(1024)S(1)} %pad_clamp_fusion.3), kind=kCustom, calls=%fused_computation | custom fusion | bytes 4194816 | tf_op jit(solution)/shard_map/gather | solution.py:133
  76.2 4.1 all_to_all.168
  80.3 5.2 all-to-all-start
  85.5 3.2 gather_fusion.8
  88.7 4.1 all_to_all.193
  92.8 20.7 %all-to-all-done = bf16[32,4,8192]{2,1,0:T(4,128)(2,1)} async-done(((bf16[32,4,8192]{2,1,0:T(4,128)(2,1)}), bf16[32,4,8192]{2,1,0:T(4,128)(2,1)}, u32[]{:S(2)}, u32[]{:S(2)}) %all-to-all-start) | async-done | bytes 2097184 | tf_op jit(solution)/shard_map/all_to_all | solution.py:138
  113.5 6.7 %all-to-all-start.8 = ((bf16[32,4,8192]{2,1,0:T(4,128)(2,1)}), bf16[32,4,8192]{2,1,0:T(4,128)(2,1)}, u32[]{:S(2)}, u32[]{:S(2)}) async-start(bf16[32,4,8192]{2,1,0:T(4,128)(2,1)} %all_to_all.193), calls=%async_computation.8 | async-start | bytes 4194304 | tf_op jit(solution)/shard_map/all_to_all | solution.py:141
  120.2 2.5 all_to_all.170
  122.8 3.2 gather_fusion.1
  126.0 3.1 copy.296
  129.1 19.1 %all-to-all-done.8 = bf16[32,4,8192]{2,1,0:T(4,128)(2,1)} async-done(((bf16[32,4,8192]{2,1,0:T(4,128)(2,1)}), bf16[32,4,8192]{2,1,0:T(4,128)(2,1)}, u32[]{:S(2)}, u32[]{:S(2)}) %all-to-all-start.8) | async-done | bytes 2097184 | tf_op jit(solution)/shard_map/all_to_all | solution.py:141
  148.2 6.9 %all-to-all-start.1 = ((bf16[128,8,1024]{2,0,1:T(8,128)(2,1)}), bf16[128,8,1024]{2,0,1:T(8,128)(2,1)}, u32[]{:S(2)}, u32[]{:S(2)}) async-start(bf16[128,8,1024]{2,0,1:T(8,128)(2,1)} %bitcast.335), calls=%async_computation.1 | async-start | bytes 4194304 | tf_op jit(solution)/shard_map/all_to_all | solution.py:148
  155.1 2.5 all_to_all.195
  157.7 3.2 gather_fusion.9
  160.8 3.3 copy.295
  164.1 42.8 %all-to-all-done.1 = bf16[128,8,1024]{2,0,1:T(8,128)(2,1)} async-done(((bf16[128,8,1024]{2,0,1:T(8,128)(2,1)}), bf16[128,8,1024]{2,0,1:T(8,128)(2,1)}, u32[]{:S(2)}, u32[]{:S(2)}) %all-to-all-start.1) | async-done | bytes 2097184 | tf_op jit(solution)/shard_map/all_to_all | solution.py:148
  206.9 4.5 all-to-all-start.9
  221.1 2.2 copy.274
  226.7 32.7 %all-to-all-done.9 = bf16[128,8,1024]{2,0,1:T(8,128)(2,1)} async-done(((bf16[128,8,1024]{2,0,1:T(8,128)(2,1)}), bf16[128,8,1024]{2,0,1:T(8,128)(2,1)}, u32[]{:S(2)}, u32[]{:S(2)}) %all-to-all-start.9) | async-done | bytes 2097184 | tf_op jit(solution)/shard_map/all_to_all | solution.py:151
  259.5 2.2 copy.277
  276.7 2.7 constant_dynamic-update-slice_fusion.6
  279.4 3.2 constant_dynamic-update-slice_fusion.5
  282.5 3.1 constant_dynamic-update-slice_fusion.4
  299.2 2.5 fusion.69
  301.8 2.5 fusion.64
  311.3 5.2 all-to-all-start.14
  316.6 2.5 multiply_convert_fusion.4
  337.5 6.6 %all-to-all-start.12 = ((bf16[8,128,128]{2,1,0:T(8,128)(2,1)}), bf16[8,128,128]{2,1,0:T(8,128)(2,1)S(1)}, u32[]{:S(2)}, u32[]{:S(2)}) async-start(bf16[8,128,128]{2,1,0:T(8,128)(2,1)} %bitcast.83), calls=%async_computation.12 | async-start | bytes 524288 | tf_op jit(solution)/shard_map/all_to_all | solution.py:205
  347.2 6.9 %all-to-all-done.12 = bf16[8,128,128]{2,1,0:T(8,128)(2,1)S(1)} async-done(((bf16[8,128,128]{2,1,0:T(8,128)(2,1)}), bf16[8,128,128]{2,1,0:T(8,128)(2,1)S(1)}, u32[]{:S(2)}, u32[]{:S(2)}) %all-to-all-start.12) | async-done | bytes 262176 | tf_op jit(solution)/shard_map/all_to_all | solution.py:205
  354.0 8.0 %all-to-all-start.15 = ((bf16[32,4,1024]{2,1,0:T(4,128)(2,1)}), bf16[32,4,1024]{2,1,0:T(4,128)(2,1)S(1)}, u32[]{:S(2)}, u32[]{:S(2)}) async-start(bf16[32,4,1024]{2,1,0:T(4,128)(2,1)} %all_to_all.217), calls=%async_computation.15 | async-start | bytes 524288 | tf_op jit(solution)/shard_map/all_to_all | solution.py:223
  365.1 5.9 %all-to-all-done.15 = bf16[32,4,1024]{2,1,0:T(4,128)(2,1)S(1)} async-done(((bf16[32,4,1024]{2,1,0:T(4,128)(2,1)}), bf16[32,4,1024]{2,1,0:T(4,128)(2,1)S(1)}, u32[]{:S(2)}, u32[]{:S(2)}) %all-to-all-start.15) | async-done | bytes 262176 | tf_op jit(solution)/shard_map/all_to_all | solution.py:223
  371.0 4.0 all-to-all-start.13
  376.3 2.2 copy.278
  380.1 3.8 all-to-all-done.13
  384.0 3.6 all-to-all-start.10
  387.6 4.3 copy.207
  391.8 4.2 all_to_all.186
  396.0 39.7 %all-to-all-done.10 = bf16[8,128,1024]{1,2,0:T(8,128)(2,1)S(1)} async-done(((bf16[8,128,1024]{1,2,0:T(8,128)(2,1)}), bf16[8,128,1024]{1,2,0:T(8,128)(2,1)S(1)}, u32[]{:S(2)}, u32[]{:S(2)}) %all-to-all-start.10) | async-done | bytes 2097184 | tf_op jit(solution)/shard_map/all_to_all | solution.py:202
  437.0 4.9 all-to-all-start.6
  442.0 2.9 copy.266
  444.9 3.2 gather_fusion.10
  448.1 4.1 all_to_all.203
  452.2 39.3 %all-to-all-done.6 = bf16[8,128,1024]{2,1,0:T(8,128)(2,1)} async-done(((bf16[8,128,1024]{2,1,0:T(8,128)(2,1)}), bf16[8,128,1024]{2,1,0:T(8,128)(2,1)}, u32[]{:S(2)}, u32[]{:S(2)}) %all-to-all-start.6) | async-done | bytes 2097184 | tf_op jit(solution)/shard_map/all_to_all | solution.py:199
  491.4 8.0 %all-to-all-start.11 = ((bf16[32,4,8192]{2,1,0:T(4,128)(2,1)}), bf16[32,4,8192]{2,1,0:T(4,128)(2,1)}, u32[]{:S(2)}, u32[]{:S(2)}) async-start(bf16[32,4,8192]{2,1,0:T(4,128)(2,1)} %all_to_all.203), calls=%async_computation.11 | async-start | bytes 4194304 | tf_op jit(solution)/shard_map/all_to_all | solution.py:219
  507.2 3.2 gather_fusion.6
  510.4 4.1 all_to_all.190
  514.5 12.9 %all-to-all-done.11 = bf16[32,4,8192]{2,1,0:T(4,128)(2,1)} async-done(((bf16[32,4,8192]{2,1,0:T(4,128)(2,1)}), bf16[32,4,8192]{2,1,0:T(4,128)(2,1)}, u32[]{:S(2)}, u32[]{:S(2)}) %all-to-all-start.11) | async-done | bytes 2097184 | tf_op jit(solution)/shard_map/all_to_all | solution.py:219
  527.3 6.7 %all-to-all-start.7 = ((bf16[32,4,8192]{2,1,0:T(4,128)(2,1)}), bf16[32,4,8192]{2,1,0:T(4,128)(2,1)}, u32[]{:S(2)}, u32[]{:S(2)}) async-start(bf16[32,4,8192]{2,1,0:T(4,128)(2,1)} %all_to_all.190), calls=%async_computation.7 | async-start | bytes 4194304 | tf_op jit(solution)/shard_map/all_to_all | solution.py:216
  534.0 2.9 all_to_all.205
  537.0 3.2 gather_fusion.11
  548.9 8.6 %fusion.3 = bf16[128,8192]{1,0:T(8,128)(2,1)} fusion(bf16[128,8192]{1,0:T(8,128)(2,1)S(1)} %copy-done.6, bf16[128,8192]{1,0:T(8,128)(2,1)S(1)} %copy-done.7, f32[16,8,64,128]{3,2,1,0:T(8,128)S(1)} %bitcast.344, f32[16,8,64,128]{3,2,1,0:T(8,128)S(1)} %bitcast.341, f32[8192]{0:T(1024)S(1)} %copy-done.46), kind=kLoop, calls=%fused_computation.27 | loop fusion | flops 8388608 | bytes 14712832 | tf_op jit(solution)/shard_map/convert_element_type | solution.py:232
  557.4 4.6 all-to-all-done.7
  562.0 4.0 all_to_all.192
  566.0 7.1 %gather_fusion.7 = bf16[128,8192]{1,0:T(8,128)(2,1)} fusion(bf16[128,8192]{1,0:T(8,128)(2,1)} %all_to_all.192, s32[1024]{0:T(1024)S(1)} %pad_clamp_fusion), kind=kCustom, calls=%fused_computation.7 | custom fusion | bytes 4194816 | tf_op jit(solution)/shard_map/gather | solution.py:228
  (366 shorter events, 110.4 us)
Async XLA Ops:
  0.6 84.9 %copy-start = (bf16[128,8192]{1,0:T(8,128)(2,1)S(1)}, bf16[128,8192]{1,0:T(8,128)(2,1)}, u32[]{:S(2)}) copy-start(bf16[128,8192]{1,0:T(8,128)(2,1)} %param.12) | copy-start | bytes 6291460
  0.6 4.4 copy-start.23
  0.7 3.2 copy-start.85
  1.5 2.6 copy-start.87
  6.9 17.5 %all-to-all-start.2 = ((bf16[32,4,1024]{2,1,0:T(4,128)(2,1)}), bf16[32,4,1024]{2,1,0:T(4,128)(2,1)S(1)}, u32[]{:S(2)}, u32[]{:S(2)}) async-start(bf16[32,4,1024]{2,1,0:T(4,128)(2,1)} %all_to_all.174), calls=%async_computation.2 | async-start | bytes 524288 | tf_op jit(solution)/shard_map/all_to_all | solution.py:139
  17.5 2.7 copy-start.8
  20.3 9.1 %copy-start.88 = (s32[1,1,128]{2,1,0:T(1,128)S(1)}, s32[1,1,128]{2,1,0:T(1,128)}, u32[]{:S(2)}) copy-start(s32[1,1,128]{2,1,0:T(1,128)} %param.17) | copy-start | bytes 1540
  24.4 13.8 %all-to-all-start.4 = ((bf16[32,4,1024]{2,1,0:T(4,128)(2,1)}), bf16[32,4,1024]{2,1,0:T(4,128)(2,1)S(1)}, u32[]{:S(2)}, u32[]{:S(2)}) async-start(bf16[32,4,1024]{2,1,0:T(4,128)(2,1)} %all_to_all.180), calls=%async_computation.4 | async-start | bytes 524288 | tf_op jit(solution)/shard_map/all_to_all | solution.py:140
  38.2 20.2 %all-to-all-start.3 = ((bf16[128,8,128]{2,0,1:T(8,128)(2,1)}), bf16[128,8,128]{2,0,1:T(8,128)(2,1)S(1)}, u32[]{:S(2)}, u32[]{:S(2)}) async-start(bf16[128,8,128]{2,0,1:T(8,128)(2,1)} %copy.203), calls=%async_computation.3 | async-start | bytes 524288 | tf_op jit(solution)/shard_map/all_to_all | solution.py:149
  46.4 3.4 copy-start.83
  50.4 12.8 %copy-start.45 = (f32[8192]{0:T(1024)}, f32[8192]{0:T(1024)S(1)}, u32[]{:S(2)}) copy-start(f32[8192]{0:T(1024)S(1)} %broadcast_bitcast_fusion) | copy-start | bytes 98308
  58.4 21.9 %all-to-all-start.5 = ((bf16[128,8,128]{2,0,1:T(8,128)(2,1)}), bf16[128,8,128]{2,0,1:T(8,128)(2,1)S(1)}, u32[]{:S(2)}, u32[]{:S(2)}) async-start(bf16[128,8,128]{2,0,1:T(8,128)(2,1)} %copy.205), calls=%async_computation.5 | async-start | bytes 524288 | tf_op jit(solution)/shard_map/all_to_all | solution.py:150
  62.0 3.2 copy-start.5
  80.3 33.1 %all-to-all-start = ((bf16[32,4,8192]{2,1,0:T(4,128)(2,1)}), bf16[32,4,8192]{2,1,0:T(4,128)(2,1)}, u32[]{:S(2)}, u32[]{:S(2)}) async-start(bf16[32,4,8192]{2,1,0:T(4,128)(2,1)} %all_to_all.168), calls=%async_computation | async-start | bytes 4194304 | tf_op jit(solution)/shard_map/all_to_all | solution.py:138
  113.5 34.7 %all-to-all-start.8 = ((bf16[32,4,8192]{2,1,0:T(4,128)(2,1)}), bf16[32,4,8192]{2,1,0:T(4,128)(2,1)}, u32[]{:S(2)}, u32[]{:S(2)}) async-start(bf16[32,4,8192]{2,1,0:T(4,128)(2,1)} %all_to_all.193), calls=%async_computation.8 | async-start | bytes 4194304 | tf_op jit(solution)/shard_map/all_to_all | solution.py:141
  148.2 58.6 %all-to-all-start.1 = ((bf16[128,8,1024]{2,0,1:T(8,128)(2,1)}), bf16[128,8,1024]{2,0,1:T(8,128)(2,1)}, u32[]{:S(2)}, u32[]{:S(2)}) async-start(bf16[128,8,1024]{2,0,1:T(8,128)(2,1)} %bitcast.335), calls=%async_computation.1 | async-start | bytes 4194304 | tf_op jit(solution)/shard_map/all_to_all | solution.py:148
  206.9 4.5 copy-start.89
  206.9 52.6 %all-to-all-start.9 = ((bf16[128,8,1024]{2,0,1:T(8,128)(2,1)}), bf16[128,8,1024]{2,0,1:T(8,128)(2,1)}, u32[]{:S(2)}, u32[]{:S(2)}) async-start(bf16[128,8,1024]{2,0,1:T(8,128)(2,1)} %bitcast.334), calls=%async_computation.9 | async-start | bytes 4194304 | tf_op jit(solution)/shard_map/all_to_all | solution.py:151
  216.6 8.7 %copy-start.40 = (bf16[2,128,128]{2,1,0:T(8,128)(2,1)}, bf16[2,128,128]{2,1,0:T(8,128)(2,1)S(1)}, u32[]{:S(2)}) copy-start(bf16[2,128,128]{2,1,0:T(8,128)(2,1)S(1)} %dynamic_slice.292) | copy-start | bytes 196612
  223.6 3.2 copy-start.11
  261.7 2.4 copy-start.12
  262.0 46.8 %copy-start.9 = (bf16[1024,1,8,128]{3,0,2,1:T(8,128)(2,1)}, bf16[1024,1,8,128]{3,0,2,1:T(8,128)(2,1)S(1)}, u32[]{:S(2)}) copy-start(bf16[1024,1,8,128]{3,0,2,1:T(8,128)(2,1)S(1)} %copy.297) | copy-start | bytes 6291460
  268.1 2.1 copy-start.34
  268.1 2.1 copy-start.66
  272.4 2.2 copy-start.30
  272.4 2.2 copy-start.62
  282.5 3.2 copy-start.59
  282.5 3.2 copy-start.70
  282.5 3.2 copy-start.99
  294.7 2.5 copy-start.51
  296.1 20.4 %copy-start.49 = (f32[128,128]{1,0:T(8,128)}, f32[128,128]{1,0:T(8,128)S(1)}, u32[]{:S(2)}) copy-start(f32[128,128]{1,0:T(8,128)S(1)} %fusion.75) | copy-start | bytes 196612
  299.2 2.5 copy-start.77
  301.8 2.5 copy-start.71
  301.8 2.5 copy-start.100
  309.7 6.9 %copy-start.61 = (bf16[4,128,128]{2,1,0:T(8,128)(2,1)S(1)}, bf16[4,128,128]{2,1,0:T(8,128)(2,1)}, u32[]{:S(2)}) copy-start(bf16[4,128,128]{2,1,0:T(8,128)(2,1)} %dynamic_slice.297) | copy-start | bytes 393220
  311.3 26.2 %all-to-all-start.14 = ((bf16[8,128,128]{2,1,0:T(8,128)(2,1)}), bf16[8,128,128]{2,1,0:T(8,128)(2,1)S(1)}, u32[]{:S(2)}, u32[]{:S(2)}) async-start(bf16[8,128,128]{2,1,0:T(8,128)(2,1)} %bitcast.95), calls=%async_computation.14 | async-start | bytes 524288 | tf_op jit(solution)/shard_map/all_to_all | solution.py:206
  316.6 2.6 copy-start.10
  316.6 2.6 copy-start.60
  316.6 3.1 copy-start.101
  322.5 5.4 copy-start.17
  331.4 3.5 copy-start.15
  331.4 3.5 copy-start.43
  332.0 4.2 copy-start.37
  335.0 9.2 %copy-start.18 = (bf16[8,128,640]{2,1,0:T(8,128)(2,1)S(1)}, bf16[8,128,640]{2,1,0:T(8,128)(2,1)}, u32[]{:S(2)}) copy-start(bf16[8,128,640]{2,1,0:T(8,128)(2,1)} %copy-done.17) | copy-start | bytes 3932164
  335.0 9.2 %copy-start.35 = (bf16[5,128,128]{2,1,0:T(8,128)(2,1)S(1)}, bf16[5,128,128]{2,1,0:T(8,128)(2,1)}, u32[]{:S(2)}) copy-start(bf16[5,128,128]{2,1,0:T(8,128)(2,1)} %get-tuple-element.47) | copy-start | bytes 491524
  336.2 9.3 %copy-start.82 = (s32[1024]{0:T(1024)S(1)}, s32[1024]{0:T(1024)}, u32[]{:S(2)}) copy-start(s32[1024]{0:T(1024)} %pad_clamp_fusion.1) | copy-start | bytes 12292
  337.5 16.5 %all-to-all-start.12 = ((bf16[8,128,128]{2,1,0:T(8,128)(2,1)}), bf16[8,128,128]{2,1,0:T(8,128)(2,1)S(1)}, u32[]{:S(2)}, u32[]{:S(2)}) async-start(bf16[8,128,128]{2,1,0:T(8,128)(2,1)} %bitcast.83), calls=%async_computation.12 | async-start | bytes 524288 | tf_op jit(solution)/shard_map/all_to_all | solution.py:205
  345.4 16.6 %copy-start.33 = (bf16[5,128,128]{2,1,0:T(8,128)(2,1)S(1)}, bf16[5,128,128]{2,1,0:T(8,128)(2,1)}, u32[]{:S(2)}) copy-start(bf16[5,128,128]{2,1,0:T(8,128)(2,1)} %get-tuple-element.46) | copy-start | bytes 491524
  354.0 17.0 %all-to-all-start.15 = ((bf16[32,4,1024]{2,1,0:T(4,128)(2,1)}), bf16[32,4,1024]{2,1,0:T(4,128)(2,1)S(1)}, u32[]{:S(2)}, u32[]{:S(2)}) async-start(bf16[32,4,1024]{2,1,0:T(4,128)(2,1)} %all_to_all.217), calls=%async_computation.15 | async-start | bytes 524288 | tf_op jit(solution)/shard_map/all_to_all | solution.py:223
  363.4 11.6 %copy-start.16 = (bf16[8,128,640]{2,1,0:T(8,128)(2,1)S(1)}, bf16[8,128,640]{2,1,0:T(8,128)(2,1)}, u32[]{:S(2)}) copy-start(bf16[8,128,640]{2,1,0:T(8,128)(2,1)} %copy-done.15) | copy-start | bytes 3932164
  363.4 11.6 %copy-start.31 = (bf16[5,128,128]{2,1,0:T(8,128)(2,1)S(1)}, bf16[5,128,128]{2,1,0:T(8,128)(2,1)}, u32[]{:S(2)}) copy-start(bf16[5,128,128]{2,1,0:T(8,128)(2,1)} %get-tuple-element.45) | copy-start | bytes 491524
  371.0 5.3 copy-start.28
  371.0 13.0 %all-to-all-start.13 = ((bf16[32,4,1024]{2,1,0:T(4,128)(2,1)}), bf16[32,4,1024]{2,1,0:T(4,128)(2,1)S(1)}, u32[]{:S(2)}, u32[]{:S(2)}) async-start(bf16[32,4,1024]{2,1,0:T(4,128)(2,1)} %all_to_all.210), calls=%async_computation.13 | async-start | bytes 524288 | tf_op jit(solution)/shard_map/all_to_all | solution.py:222
  384.0 51.7 %all-to-all-start.10 = ((bf16[8,128,1024]{1,2,0:T(8,128)(2,1)}), bf16[8,128,1024]{1,2,0:T(8,128)(2,1)S(1)}, u32[]{:S(2)}, u32[]{:S(2)}) async-start(bf16[8,128,1024]{1,2,0:T(8,128)(2,1)} %copy.221), calls=%async_computation.10 | async-start | bytes 4194304 | tf_op jit(solution)/shard_map/all_to_all | solution.py:202
  437.0 54.4 %all-to-all-start.6 = ((bf16[8,128,1024]{2,1,0:T(8,128)(2,1)}), bf16[8,128,1024]{2,1,0:T(8,128)(2,1)}, u32[]{:S(2)}, u32[]{:S(2)}) async-start(bf16[8,128,1024]{2,1,0:T(8,128)(2,1)} %all_to_all.186), calls=%async_computation.6 | async-start | bytes 4194304 | tf_op jit(solution)/shard_map/all_to_all | solution.py:199
  452.2 48.4 %copy-start.29 = (bf16[32,4,1024]{2,1,0:T(4,128)(2,1)S(1)}, bf16[32,4,1024]{2,1,0:T(4,128)(2,1)}, u32[]{:S(2)}) copy-start(bf16[32,4,1024]{2,1,0:T(4,128)(2,1)} %copy-done.28) | copy-start | bytes 786436
  491.4 35.9 %all-to-all-start.11 = ((bf16[32,4,8192]{2,1,0:T(4,128)(2,1)}), bf16[32,4,8192]{2,1,0:T(4,128)(2,1)}, u32[]{:S(2)}, u32[]{:S(2)}) async-start(bf16[32,4,8192]{2,1,0:T(4,128)(2,1)} %all_to_all.203), calls=%async_computation.11 | async-start | bytes 4194304 | tf_op jit(solution)/shard_map/all_to_all | solution.py:219
  527.3 34.7 %all-to-all-start.7 = ((bf16[32,4,8192]{2,1,0:T(4,128)(2,1)}), bf16[32,4,8192]{2,1,0:T(4,128)(2,1)}, u32[]{:S(2)}, u32[]{:S(2)}) async-start(bf16[32,4,8192]{2,1,0:T(4,128)(2,1)} %all_to_all.190), calls=%async_computation.7 | async-start | bytes 4194304 | tf_op jit(solution)/shard_map/all_to_all | solution.py:216
  542.9 2.2 copy-start.4
  545.1 2.4 copy-start.6
  545.1 2.4 copy-start.7
  546.4 2.5 copy-start.3
  546.4 2.5 copy-start.46
  566.0 7.1 %copy-start.1 = (bf16[128,8192]{1,0:T(8,128)(2,1)S(1)}, bf16[128,8192]{1,0:T(8,128)(2,1)}, u32[]{:S(2)}) copy-start(bf16[128,8192]{1,0:T(8,128)(2,1)} %param.12) | copy-start | bytes 6291460
  (54 other events, 76.1 us)
where the time goes:
time: 581 us; the launch traced here: 573 us
  waiting for transfers between devices  244 us (42%)
  local copies, waits for them, and re-layouts  135 us (23%)
  starting transfers between devices  95.6 us (16%)
  matrix products  63.3 us (11%)
  other arithmetic  32.9 us (6%)
    all_to_all x1, waiting for transfers between devices, per_device(): lax.all_to_all(q_pack, 'seq', split_axis=1, concat_axis=0, tiled=True)  42.8 us
    all_to_all x1, waiting for transfers between devices, per_device(): lax.all_to_all(for_sending(dq_cols), 'seq', split_axis=0, concat_axis=1,...  39.7 us
    all_to_all x1, waiting for transfers between devices, per_device(): lax.all_to_all(for_sending(out_cols), 'seq', split_axis=0, concat_axis=1,...  39.3 us
    all_to_all x1, waiting for transfers between devices, per_device(): lax.all_to_all(d_pack, 'seq', split_axis=1, concat_axis=0, tiled=True)  32.7 us
    unnamed x213, local copies, waits for them, and re-layouts  28.9 us
    all_to_all x1, waiting for transfers between devices, per_device(): lax.all_to_all(q_sent, 'dp', split_axis=0, concat_axis=0, tiled=True)  20.7 us
    all_to_all x1, waiting for transfers between devices, per_device(): lax.all_to_all(d_sent, 'dp', split_axis=0, concat_axis=0, tiled=True)  19.1 us
    dot_general x8, matrix products, per_group(): jnp.einsum('hqk,kd->hqd', weights_low, v_window, preferred_element_type=j...  16.2 us
  transfers between devices with their start and end apart: 16, of which 14 were waited for; matrix products, arithmetic and copies ran while one was open for 21% of the time, Pallas kernels for 0%

commit v1 on v0

v1 whole, which is shorter than its diff:
```python
import functools

import jax
import jax.numpy as jnp
from jax import lax
from jax.experimental import pallas as pl
from jax.experimental.pallas import tpu as pltpu
from jax.sharding import PartitionSpec as P

Q_HEADS = 64
KV_HEADS = 8
HEAD = 128
RATIO = Q_HEADS // KV_HEADS
EPS = 1e-06
ROWS = 128
GROUPS = 32
SHARE = ROWS // GROUPS
SPLIT = 4
CHUNK = SHARE * SPLIT
TALL = GROUPS * CHUNK
WIDE = 2 * HEAD
BACK = 4
WINDOW = (BACK + 1) * ROWS
SCALE = HEAD ** (-0.5)
LOG2E = 1.4426950408889634
FIRST = 6
VMEM_LIMIT = 40 * 1024 * 1024
F32 = jnp.float32
BF16 = jnp.bfloat16


def params():
    return pltpu.CompilerParams(vmem_limit_bytes=VMEM_LIMIT)


def cost(flops, moved, trans=0):
    return pl.CostEstimate(flops=int(flops), bytes_accessed=int(moved), transcendentals=int(trans))


def dot(a, b, dims):
    return lax.dot_general(a, b, (dims, ((), ())), preferred_element_type=F32)


MM = ((1,), (0,))
MT = ((1,), (1,))
TM = ((0,), (0,))


def iota(shape, dim):
    return lax.broadcasted_iota(jnp.int32, shape, dim)


def tall_row(index):
    row = (index // CHUNK) * SHARE + index % SHARE
    part = (index // SHARE) % SPLIT
    return row, part


def home_matrix(order_ref):
    spread_row, _ = tall_row(iota((ROWS, TALL), 1))
    spread = (spread_row == iota((ROWS, TALL), 0)).astype(BF16)
    order = jnp.broadcast_to(order_ref[...].astype(F32), (16, ROWS)).astype(BF16)
    source = dot(order, spread, MM)[:1]
    _, part = tall_row(iota((1, TALL), 1))
    code = source + (part * ROWS).astype(F32)
    return (iota((TALL, TALL), 0).astype(F32) == code).astype(BF16)


def pack_matrix(order_ref):
    row, part = tall_row(iota((TALL, SPLIT * ROWS), 0))
    order = order_ref[...]
    code = jnp.concatenate([order + p * ROWS for p in range(SPLIT)], axis=1)
    return (row + part * ROWS == code).astype(BF16)


def norm(x, gain):
    factor = lax.rsqrt(jnp.mean(x * x, axis=-1, keepdims=True) + EPS)
    return x * factor * gain


def norm_back(x, gain, dy):
    factor = lax.rsqrt(jnp.mean(x * x, axis=-1, keepdims=True) + EPS)
    g = dy * gain
    inner = jnp.mean(x * g, axis=-1, keepdims=True)
    return factor * g - x * (factor * factor * factor * inner)


def head_cols(h):
    return slice(h * HEAD, (h + 1) * HEAD)


def send_kv_kernel(order_ref, gain_ref, k_ref, v_ref, out_ref):
    gain = gain_ref[...]
    kn = [
        norm(k_ref[:, head_cols(h)].astype(F32), gain).astype(BF16) for h in range(KV_HEADS)
    ]
    half = KV_HEADS * HEAD // 2
    stack = jnp.concatenate(
        [
            jnp.concatenate(kn[: KV_HEADS // 2], axis=1),
            jnp.concatenate(kn[KV_HEADS // 2 :], axis=1),
            v_ref[:, :half],
            v_ref[:, half:],
        ],
        axis=0,
    )
    sent = dot(home_matrix(order_ref), stack, TM).astype(BF16)
    out_ref[...] = sent.reshape(GROUPS, CHUNK, half)


def send_kv(order, gain, key_projection, value):
    half = KV_HEADS * HEAD // 2
    return pl.pallas_call(
        send_kv_kernel,
        out_shape=jax.ShapeDtypeStruct((GROUPS, CHUNK, half), BF16),
        compiler_params=params(),
        cost_estimate=cost(2 * TALL * TALL * half, 3 << 19),
        name="send_kv",
    )(order, gain, key_projection, value)


def send_rows_kernel(order_ref, gain_ref, q_ref, d_ref, out_ref, home_ref):
    @pl.when(pl.program_id(0) == 0)
    def _():
        home_ref[...] = home_matrix(order_ref)

    gain = gain_ref[...]
    qn = [norm(q_ref[:, head_cols(h)].astype(F32), gain).astype(BF16) for h in range(RATIO)]
    stack = jnp.concatenate(
        [
            jnp.concatenate(
                [qn[2 * p], qn[2 * p + 1], d_ref[:, p * WIDE : (p + 1) * WIDE]], axis=1
            )
            for p in range(SPLIT)
        ],
        axis=0,
    )
    sent = dot(home_ref[...], stack, TM).astype(BF16)
    out_ref[...] = sent.reshape(GROUPS, CHUNK, 2 * WIDE)


def send_rows(order, gain, query, d_out, first, count):
    return pl.pallas_call(
        send_rows_kernel,
        grid=(count,),
        in_specs=[
            pl.BlockSpec((1, ROWS), lambda h: (0, 0)),
            pl.BlockSpec((1, HEAD), lambda h: (0, 0)),
            pl.BlockSpec((ROWS, RATIO * HEAD), lambda h: (0, h + first)),
            pl.BlockSpec((ROWS, RATIO * HEAD), lambda h: (0, h + first)),
        ],
        out_specs=pl.BlockSpec((GROUPS, CHUNK, 2 * WIDE), lambda h: (0, 0, h)),
        out_shape=jax.ShapeDtypeStruct((GROUPS, CHUNK, count * 2 * WIDE), BF16),
        scratch_shapes=[pltpu.VMEM((TALL, TALL), BF16)],
        compiler_params=params(),
        cost_estimate=cost(count * 2 * TALL * TALL * 2 * WIDE, count << 20),
        name="send_rows",
    )(order, gain, query, d_out)


def sort_kv_kernel(order_ref, in_ref, first_ref, last_ref):
    half = KV_HEADS * HEAD // 2
    rows = dot(pack_matrix(order_ref), in_ref[...].reshape(TALL, half), TM).astype(BF16)
    for h in range(KV_HEADS):
        ref, at = (first_ref, h) if h < FIRST else (last_ref, h - FIRST)
        part, cols = h // (KV_HEADS // 2), head_cols(h % (KV_HEADS // 2))
        k = rows[part * ROWS : (part + 1) * ROWS, cols]
        v = rows[(part + 2) * ROWS : (part + 3) * ROWS, cols]
        ref[:, at * WIDE : (at + 1) * WIDE] = jnp.concatenate([k, v], axis=1)


def sort_kv(order, received):
    return pl.pallas_call(
        sort_kv_kernel,
        out_shape=[
            jax.ShapeDtypeStruct((ROWS, count * WIDE), BF16)
            for count in (FIRST, KV_HEADS - FIRST)
        ],
        compiler_params=params(),
        cost_estimate=cost(2 * TALL**3, 1 << 20),
        name="sort_kv",
    )(order, received)


def attend_kernel(meta_ref, order_ref, qd_ref, *refs):
    kv_refs = refs[: BACK + 1]
    out_ref = refs[BACK + 1]
    part_refs = refs[BACK + 2 : 2 * BACK + 3]
    bias_ref = refs[2 * BACK + 3]

    @pl.when(pl.program_id(0) == 0)
    def _():
        row, _ = tall_row(iota((TALL, ROWS), 0))
        hit = row == order_ref[...]
        position = jnp.sum(
            jnp.where(hit, iota((TALL, ROWS), 1).astype(F32), 0.0), axis=1, keepdims=True
        )
        base = meta_ref[3] * ROWS
        position = position + base.astype(F32)
        end0 = meta_ref[0].astype(F32)
        end1 = (meta_ref[0] + meta_ref[1]).astype(F32)
        start = jnp.where(position < end0, 0.0, jnp.where(position < end1, end0, end1))
        key = (iota((TALL, WINDOW), 1) + (base - BACK * ROWS)).astype(F32)
        bias_ref[...] = jnp.where((key >= start) & (key <= position), 0.0, -1e30)

    kw = jnp.concatenate([r[:, :HEAD] for r in kv_refs], axis=0)
    vw = jnp.concatenate([r[:, HEAD:] for r in kv_refs], axis=0)
    dk = jnp.zeros((WINDOW, HEAD), F32)
    dv = jnp.zeros((WINDOW, HEAD), F32)
    step = TALL // 2
    for e in range(2):
        for low in range(0, TALL, step):
            g0, g1 = low // CHUNK, (low + step) // CHUNK
            q = qd_ref[g0:g1, :, e * HEAD : (e + 1) * HEAD].reshape(step, HEAD)
            d = qd_ref[g0:g1, :, WIDE + e * HEAD : WIDE + (e + 1) * HEAD].reshape(step, HEAD)
            scores = dot(q, kw, MT)
            expo = jnp.exp2(scores * (SCALE * LOG2E) + bias_ref[low : low + step, :])
            weights = expo * (1.0 / jnp.sum(expo, axis=-1, keepdims=True))
            low_weights = weights.astype(BF16)
            out = dot(low_weights, vw, MM).astype(BF16)
            delta = jnp.sum(d.astype(F32) * out.astype(F32), axis=-1, keepdims=True)
            d_weights = dot(d, vw, MT)
            d_scores = (weights * (d_weights - delta)).astype(BF16)
            dq = (dot(d_scores, kw, MM) * SCALE).astype(BF16)
            dk = dk + dot(d_scores, q, TM)
            dv = dv + dot(low_weights, d, TM)
            out_ref[g0:g1, :, e * HEAD : (e + 1) * HEAD] = out.reshape(g1 - g0, CHUNK, HEAD)
            out_ref[g0:g1, :, WIDE + e * HEAD : WIDE + (e + 1) * HEAD] = dq.reshape(
                g1 - g0, CHUNK, HEAD
            )
    dk = dk * SCALE
    for n, ref in enumerate(part_refs):
        ref[:, :HEAD] = dk[n * ROWS : (n + 1) * ROWS].astype(ref.dtype)
        ref[:, HEAD:] = dv[n * ROWS : (n + 1) * ROWS].astype(ref.dtype)


def attend(meta, order, received, blocks, count):
    kv_spec = pl.BlockSpec((ROWS, WIDE), lambda h: (0, h))
    elements = count * RATIO * ROWS * WINDOW
    return pl.pallas_call(
        attend_kernel,
        grid=(count,),
        in_specs=[
            pl.BlockSpec(memory_space=pltpu.SMEM),
            pl.BlockSpec((1, ROWS), lambda h: (0, 0)),
            pl.BlockSpec((GROUPS, CHUNK, 2 * WIDE), lambda h: (0, 0, h)),
        ]
        + [kv_spec] * (BACK + 1),
        out_specs=[pl.BlockSpec((GROUPS, CHUNK, 2 * WIDE), lambda h: (0, 0, h))]
        + [kv_spec] * (BACK + 1),
        out_shape=[jax.ShapeDtypeStruct((GROUPS, CHUNK, count * 2 * WIDE), BF16)]
        + [
            jax.ShapeDtypeStruct((ROWS, count * WIDE), BF16 if n == 0 else F32)
            for n in range(BACK + 1)
        ],
        scratch_shapes=[pltpu.VMEM((TALL, WINDOW), F32)],
        compiler_params=params(),
        cost_estimate=cost(12 * elements * HEAD, count * (3 << 20), elements),
        name="attend",
    )(meta, order, received, *blocks)


def return_kv_kernel(order_ref, *refs):
    first, last, sums, out_ref = refs[0], refs[1], refs[2:4], refs[4]
    total = [
        jnp.concatenate(
            [
                (r[...].astype(F32) + p[...]).astype(BF16)
                for r, p in zip((first, last), sums)
            ],
            axis=1,
        )
    ][0]
    quarter = KV_HEADS // 2
    rows = []
    for which in range(2):
        for part in range(2):
            rows.append(
                jnp.concatenate(
                    [
                        total[:, h * WIDE + which * HEAD : h * WIDE + (which + 1) * HEAD]
                        for h in range(part * quarter, (part + 1) * quarter)
                    ],
                    axis=1,
                )
            )
    stack = jnp.concatenate(rows, axis=0)
    out_ref[...] = (
        dot(pack_matrix(order_ref), stack, MM)
        .astype(BF16)
        .reshape(GROUPS, CHUNK, quarter * HEAD)
    )


def return_kv(order, first, last, own_first, own_last):
    half = KV_HEADS * HEAD // 2
    return pl.pallas_call(
        return_kv_kernel,
        out_shape=jax.ShapeDtypeStruct((GROUPS, CHUNK, half), BF16),
        compiler_params=params(),
        cost_estimate=cost(2 * TALL**3, 3 << 20),
        name="return_kv",
    )(order, first, last, own_first, own_last)


def finish_rows_kernel(order_ref, gain_ref, q_ref, in_ref, *refs):
    out_ref, dq_ref, home_ref = refs[-3:]

    @pl.when(pl.program_id(0) == 0)
    def _():
        home_ref[...] = home_matrix(order_ref)

    gain = gain_ref[...]
    rows = dot(home_ref[...], in_ref[...].reshape(TALL, 2 * WIDE), MM)
    for part in range(SPLIT):
        mine = rows[part * ROWS : (part + 1) * ROWS]
        cols = slice(part * WIDE, (part + 1) * WIDE)
        out_ref[:, cols] = mine[:, :WIDE].astype(BF16)
        for e in range(2):
            at = slice(part * WIDE + e * HEAD, part * WIDE + (e + 1) * HEAD)
            dy = mine[:, WIDE + e * HEAD : WIDE + (e + 1) * HEAD]
            dq_ref[:, at] = norm_back(q_ref[:, at].astype(F32), gain, dy).astype(BF16)


def finish_rows(order, gain, query, received, first, count, earlier=()):
    block = pl.BlockSpec((ROWS, RATIO * HEAD), lambda h: (0, h + first))
    whole = jax.ShapeDtypeStruct((ROWS, Q_HEADS * HEAD), BF16)
    return pl.pallas_call(
        finish_rows_kernel,
        grid=(count,),
        in_specs=[
            pl.BlockSpec((1, ROWS), lambda h: (0, 0)),
            pl.BlockSpec((1, HEAD), lambda h: (0, 0)),
            block,
            pl.BlockSpec((GROUPS, CHUNK, 2 * WIDE), lambda h: (0, 0, h)),
        ]
        + [pl.BlockSpec(memory_space=pl.ANY)] * len(earlier),
        out_specs=[block, block],
        out_shape=[whole, whole],
        scratch_shapes=[pltpu.VMEM((TALL, TALL), BF16)],
        input_output_aliases={4 + n: n for n in range(len(earlier))},
        compiler_params=params(),
        cost_estimate=cost(count * 2 * TALL * TALL * 2 * WIDE, count * (5 << 18)),
        name="finish_rows",
    )(order, gain, query, received, *earlier)


def finish_kv_kernel(order_ref, gain_ref, k_ref, in_ref, dk_ref, dv_ref):
    half = KV_HEADS * HEAD // 2
    gain = gain_ref[...]
    rows = dot(home_matrix(order_ref), in_ref[...].reshape(TALL, half), MM)
    for h in range(KV_HEADS):
        part, cols = h // (KV_HEADS // 2), head_cols(h % (KV_HEADS // 2))
        dy = rows[part * ROWS : (part + 1) * ROWS, cols]
        dk_ref[:, head_cols(h)] = norm_back(
            k_ref[:, head_cols(h)].astype(F32), gain, dy
        ).astype(BF16)
    dv_ref[:, :half] = rows[2 * ROWS : 3 * ROWS].astype(BF16)
    dv_ref[:, half:] = rows[3 * ROWS :].astype(BF16)


def finish_kv(order, gain, key_projection, received):
    half = KV_HEADS * HEAD // 2
    columns = received.shape[2] // half
    block = pl.BlockSpec((ROWS, KV_HEADS * HEAD), lambda i: (0, 0))
    whole = jax.ShapeDtypeStruct((ROWS, KV_HEADS * HEAD), BF16)
    return pl.pallas_call(
        finish_kv_kernel,
        grid=(1,),
        in_specs=[
            pl.BlockSpec((1, ROWS), lambda i: (0, 0)),
            pl.BlockSpec((1, HEAD), lambda i: (0, 0)),
            block,
            pl.BlockSpec((GROUPS, CHUNK, half), lambda i: (0, 0, columns - 1)),
        ],
        out_specs=[block, block],
        out_shape=[whole, whole],
        compiler_params=params(),
        cost_estimate=cost(2 * TALL**3, 3 << 19),
        name="finish_kv",
    )(order, gain, key_projection, received)


def exchange(array):
    return lax.all_to_all(array, "dp", split_axis=0, concat_axis=0, tiled=True)


def along(array, step):
    count = lax.axis_size("seq")
    return lax.ppermute(array, "seq", [(i, (i + step) % count) for i in range(count)])


def per_device(
    query, key_projection, value, d_out, q_gain, key_norm_gain, seq_lengths, send_order, recv_order
):
    leaving = send_order.reshape(1, ROWS)
    arriving = recv_order.reshape(1, ROWS)
    q_gain = q_gain.reshape(1, HEAD)
    k_gain = key_norm_gain.reshape(1, HEAD)
    place = lax.axis_index("seq").astype(jnp.int32)
    meta = jnp.concatenate([seq_lengths[0], place[None]])
    counts = (FIRST, KV_HEADS - FIRST)
    starts = (0, FIRST)

    kv_sent = send_kv(leaving, k_gain, key_projection, value)
    kv_received = exchange(kv_sent)
    sent = [
        send_rows(leaving, q_gain, query, d_out, first, count)
        for first, count in zip(starts, counts)
    ]
    kv_received, sent[0] = lax.optimization_barrier((kv_received, sent[0]))
    received_first = exchange(sent[0])
    received_first, sent[1] = lax.optimization_barrier((received_first, sent[1]))
    received = [received_first, exchange(sent[1])]

    chains = []
    for block in sort_kv(arriving, kv_received):
        chain = [block]
        for _ in range(BACK):
            chain.append(along(chain[-1], 1))
        chains.append(chain[::-1])

    results, totals, own = [], [], []
    for n in range(2):
        result, *parts = attend(meta, arriving, received[n], chains[n], counts[n])
        total = parts[0]
        for part in parts[1:-1]:
            total = (along(total, -1).astype(F32) + part).astype(BF16)
        totals.append(along(total, -1))
        own.append(parts[-1])
        results.append(result)

    back_first = exchange(results[0])
    kv_back = return_kv(arriving, totals[0], totals[1], own[0], own[1])
    kv_back, results[1], back_first = lax.optimization_barrier((kv_back, results[1], back_first))
    back_last = exchange(jnp.concatenate([results[1], kv_back], axis=2))

    outs = finish_rows(leaving, q_gain, query, back_first, starts[0], counts[0])
    attn_out, d_query = finish_rows(
        leaving, q_gain, query, back_last, starts[1], counts[1], earlier=outs
    )
    d_key, d_value = finish_kv(leaving, k_gain, key_projection, back_last)
    return attn_out, d_query, d_key, d_value


def solution(mesh):
    rows = P(("dp", "seq"), None)
    in_specs = (rows, rows, rows, rows, P(), P(), P("dp", None)) + (P("dp", "seq", None),) * 2
    return jax.shard_map(
        per_device, mesh=mesh, in_specs=in_specs, out_specs=(rows,) * 4, check_vma=False
    )
```

time: 581 us -> 223 us (0.38); the launches traced: 573 us -> 222 us
  waiting for transfers between devices: 244 us -> 89.7 us
  local copies, waits for them, and re-layouts: 135 us -> 17.8 us
  matrix products: 63.3 us -> 0 us
  Pallas kernels: 0 us -> 53.9 us
  starting transfers between devices: 95.6 us -> 54.6 us
  other arithmetic: 32.9 us -> 4.76 us
    all_to_all x16 -> x5, waiting for transfers between devices: 244 us -> 19.4 us  [exchange(): return lax.all_to_all(array, 'dp', split_axis=0, concat_axis=0, tiled=True)]
    ppermute x0 -> x16, waiting for transfers between devices: none -> 70.3 us  [along(): lax.ppermute(array, 'seq', [(i, (i + step) % count) for i in range(count)])]
    dot_general x47 -> x0, matrix products: 61.5 us -> none  [the longest x8 16.2 us: per_group(): jnp.einsum('hqk,kd->hqd', weights_low, v_window, preferred_element_type=j...]
    all_to_all x16 -> x5, starting transfers between devices: 95.6 us -> 41.6 us  [exchange(): return lax.all_to_all(array, 'dp', split_axis=0, concat_axis=0, tiled=True)]
    pallas_call x0 -> x10, Pallas kernels: none -> 53.9 us  [the longest x2 32.5 us: attend(): pl.pallas_call(attend_kernel, grid=(count,), in_specs=[pl.BlockSpec(memor...]
    all_to_all x26 -> x0, local copies, waits for them, and re-layouts: 50.6 us -> none  [the longest x2 8.06 us: per_device(): lax.all_to_all(for_sending(out_back), 'dp', split_axis=0, concat_axis=0,...]
    gather x18 -> x0, local copies, waits for them, and re-layouts: 41.1 us -> none  [the longest x1 7.09 us: per_device(): attn_out = out_home[undo_send]]
    convert_element_type x6, other arithmetic: 15.3 us -> 1.56 us  [per_device(): total = (along(total, -1).astype(F32) + part).astype(BF16)]
  transfers between devices with their start and end apart: 16 -> 21, of which waited for: 14 -> 12; matrix products, arithmetic and copies ran while one was open for 21% -> 1% of each run, Pallas kernels for 0% -> 21%
where the time goes in v1:
time: 223 us; the launch traced here: 222 us
  waiting for transfers between devices  89.7 us (40%)
  starting transfers between devices  54.6 us (24%)
  Pallas kernels  53.9 us (24%)
  local copies, waits for them, and re-layouts  17.8 us (8%)
  other arithmetic  4.76 us (2%)
    ppermute x16, waiting for transfers between devices, along(): lax.ppermute(array, 'seq', [(i, (i + step) % count) for i in range(count)])  70.3 us
    all_to_all x5, starting transfers between devices, exchange(): return lax.all_to_all(array, 'dp', split_axis=0, concat_axis=0, tiled=True)  41.6 us
    pallas_call x2, Pallas kernels, attend(): pl.pallas_call(attend_kernel, grid=(count,), in_specs=[pl.BlockSpec(memor...  32.5 us
    all_to_all x5, waiting for transfers between devices, exchange(): return lax.all_to_all(array, 'dp', split_axis=0, concat_axis=0, tiled=True)  19.4 us
    unnamed x58, local copies, waits for them, and re-layouts  17.8 us
    ppermute x16, starting transfers between devices, along(): lax.ppermute(array, 'seq', [(i, (i + step) % count) for i in range(count)])  12.9 us
    pallas_call x2, Pallas kernels, finish_rows(): pl.pallas_call(finish_rows_kernel, grid=(count,), in_specs=[pl.BlockSpec(...  9.81 us
    pallas_call x2, Pallas kernels, send_rows(): pl.pallas_call(send_rows_kernel, grid=(count,), in_specs=[pl.BlockSpec((1...  6.79 us
  transfers between devices with their start and end apart: 21, of which 12 were waited for; matrix products, arithmetic and copies ran while one was open for 1% of the time, Pallas kernels for 21%

profile of v1, /device:TPU:1, one launch (start us, length us, event | category | flops | bytes accessed | tf_op | source)
XLA Modules:
  0.0 221.7 jit_solution(16716712761415319277)
XLA Ops:
  0.6 0.0 copy-start.6
  0.7 1.1 copy-done.6
  1.7 0.9 copy-done.15
  2.7 0.7 copy-done.16
  3.4 0.7 copy-done.19
  4.0 1.5 send_kv.1
  5.5 8.6 %all-to-all-start = ((bf16[32,16,512]{2,1,0:T(8,128)(2,1)}), bf16[32,16,512]{2,1,0:T(8,128)(2,1)S(1)}, u32[]{:S(2)}, u32[]{:S(2)}) async-start(bf16[32,16,512]{2,1,0:T(8,128)(2,1)} %send_kv.1), calls=%async_computation | async-start | bytes 1048576 | tf_op jit(solution)/shard_map/all_to_all | solution.py:385
  14.1 0.0 copy-start.2
  14.1 1.6 copy-done.2
  15.7 4.4 %send_rows.2 = bf16[32,16,3072]{2,1,0:T(8,128)(2,1)S(1)} custom-call(s32[1,128]{1,0:T(1,128)S(1)} %bitcast.7, f32[1,128]{1,0:T(1,128)S(1)} %bitcast.12, bf16[128,8192]{1,0:T(8,128)(2,1)S(1)} %copy-done, bf16[128,8192]{1,0:T(8,128)(2,1)S(1)} %copy-done.2), custom_call_target="tpu_custom_call" | custom-call | flops 1610612736 | bytes 6291456 | tf_op jit(solution)/shard_map/send_rows/pallas_call | solution.py:143
  20.1 1.7 copy-done.1
  21.8 3.9 %all-to-all-done.in_ref = bf16[32,16,512]{2,1,0:T(8,128)(2,1)S(1)} async-done(((bf16[32,16,512]{2,1,0:T(8,128)(2,1)}), bf16[32,16,512]{2,1,0:T(8,128)(2,1)S(1)}, u32[]{:S(2)}, u32[]{:S(2)}) %all-to-all-start) | async-done | bytes 524320 | tf_op jit(solution)/shard_map/all_to_all | solution.py:385
  25.6 4.8 %all-to-all-start.1 = ((bf16[32,16,3072]{2,1,0:T(8,128)(2,1)}), bf16[32,16,3072]{2,1,0:T(8,128)(2,1)}, u32[]{:S(2)}, u32[]{:S(2)}) async-start(bf16[32,16,3072]{2,1,0:T(8,128)(2,1)} %copy-done.1), calls=%async_computation.1 | async-start | bytes 6291456 | tf_op jit(solution)/shard_map/all_to_all | solution.py:385
  30.5 0.5 sort_kv.1
  31.0 0.0 copy-start.26
  31.0 0.6 copy-done.26
  31.7 1.6 collective-permute-start
  33.3 13.2 %collective-permute-done.refs_3_ = bf16[128,1536]{1,0:T(8,128)(2,1)S(1)} collective-permute-done((bf16[128,1536]{1,0:T(8,128)(2,1)S(1)}, bf16[128,1536]{1,0:T(8,128)(2,1)S(1)}, u32[]{:S(2)}, u32[]{:S(2)}) %collective-permute-start) | collective-permute-done | bytes 393248 | tf_op jit(solution)/shard_map/ppermute | solution.py:390
  46.5 0.8 copy-done.22
  47.3 10.3 %collective-permute-done.1.refs_2_ = bf16[128,1536]{1,0:T(8,128)(2,1)S(1)} collective-permute-done((bf16[128,1536]{1,0:T(8,128)(2,1)S(1)}, bf16[128,1536]{1,0:T(8,128)(2,1)S(1)}, u32[]{:S(2)}, u32[]{:S(2)}) %collective-permute-start.1) | collective-permute-done | bytes 393248 | tf_op jit(solution)/shard_map/ppermute | solution.py:390
  57.6 0.7 copy-done.24
  58.3 9.6 %collective-permute-done.2.refs_1_ = bf16[128,1536]{1,0:T(8,128)(2,1)} collective-permute-done((bf16[128,1536]{1,0:T(8,128)(2,1)S(1)}, bf16[128,1536]{1,0:T(8,128)(2,1)}, u32[]{:S(2)}, u32[]{:S(2)}) %collective-permute-start.2) | collective-permute-done | bytes 393248 | tf_op jit(solution)/shard_map/ppermute | solution.py:390
  67.9 1.6 copy-done.3
  69.5 2.4 %send_rows.3 = bf16[32,16,1024]{2,1,0:T(8,128)(2,1)} custom-call(s32[1,128]{1,0:T(1,128)S(1)} %bitcast.8, f32[1,128]{1,0:T(1,128)S(1)} %bitcast.13, bf16[128,8192]{1,0:T(8,128)(2,1)S(1)} %copy-done, bf16[128,8192]{1,0:T(8,128)(2,1)S(1)} %copy-done.3), custom_call_target="tpu_custom_call" | custom-call | flops 536870912 | bytes 2097152 | tf_op jit(solution)/shard_map/send_rows/pallas_call | solution.py:143
  71.9 9.8 %all-to-all-start.2 = ((bf16[32,16,1024]{2,1,0:T(8,128)(2,1)}), bf16[32,16,1024]{2,1,0:T(8,128)(2,1)S(1)}, u32[]{:S(2)}, u32[]{:S(2)}) async-start(bf16[32,16,1024]{2,1,0:T(8,128)(2,1)} %send_rows.3), calls=%async_computation.2 | async-start | bytes 2097152 | tf_op jit(solution)/shard_map/all_to_all | solution.py:385
  81.7 0.7 pad_add_fusion.meta_ref
  82.5 1.0 copy-done.23
  83.5 1.0 copy-done.25
  84.5 24.2 %attend.2 = (bf16[32,16,3072]{2,1,0:T(8,128)(2,1)S(1)}, bf16[128,1536]{1,0:T(8,128)(2,1)}, f32[128,1536]{1,0:T(8,128)S(1)}, f32[128,1536]{1,0:T(8,128)S(1)}, f32...) custom-call(s32[4]{0:T(128)S(1)} %pad_add_fusion.meta_ref, s32[1,128]{1,0:T(1,128)S(1)} %bitcast.19, ...), custom_call_target="tpu_custom_call" | custom-call | flops 6039797760 | bytes 18874368 | tf_op jit(solution)/shard_map/attend/pallas_call | solution.py:240
  108.7 1.6 copy-done.4
  110.3 0.9 copy-done.8
  111.2 0.9 copy-done.10
  112.1 1.0 copy-done.12
  113.0 1.0 copy-done.14
  114.0 3.0 %collective-permute-start.4 = (bf16[128,1536]{1,0:T(8,128)(2,1)}, bf16[128,1536]{1,0:T(8,128)(2,1)}, u32[]{:S(2)}, u32[]{:S(2)}) collective-permute-start(bf16[128,1536]{1,0:T(8,128)(2,1)} %get-tuple-element.35), channel_id=1, source_target_pairs={{0,7},{1,0},{2,1},{3,2},{4,3},{5,4},{6,5},{7,6},{8,15},{9,8},{10,9... | collective-permute-start | bytes 1179656 | tf_op jit(solution)/shard_map/ppermute | solution.py:390
  117.0 5.8 %collective-permute-done.8.refs_3_ = bf16[128,512]{1,0:T(8,128)(2,1)S(1)} collective-permute-done((bf16[128,512]{1,0:T(8,128)(2,1)S(1)}, bf16[128,512]{1,0:T(8,128)(2,1)S(1)}, u32[]{:S(2)}, u32[]{:S(2)}) %collective-permute-start.8) | collective-permute-done | bytes 131104 | tf_op jit(solution)/shard_map/ppermute | solution.py:390
  122.8 8.5 %all-to-all-start.3 = ((bf16[32,16,3072]{2,1,0:T(8,128)(2,1)}), bf16[32,16,3072]{2,1,0:T(8,128)(2,1)}, u32[]{:S(2)}, u32[]{:S(2)}) async-start(bf16[32,16,3072]{2,1,0:T(8,128)(2,1)} %copy-done.4), calls=%async_computation.3 | async-start | bytes 6291456 | tf_op jit(solution)/shard_map/all_to_all | solution.py:385
  131.4 0.1 collective-permute-start.10
  131.5 1.3 add_convert_fusion.2
  132.8 3.0 %collective-permute-start.5 = (bf16[128,1536]{1,0:T(8,128)(2,1)S(1)}, bf16[128,1536]{1,0:T(8,128)(2,1)S(1)}, u32[]{:S(2)}, u32[]{:S(2)}) collective-permute-start(bf16[128,1536]{1,0:T(8,128)(2,1)S(1)} %add_convert_fusion.2), channel_id=1, source_target_pairs={{0,7},{1,0},{2,1},{3,2},{4,3},{5,4},{6,5},{7,6},{8,15},{9,8},{10,9... | collective-permute-start | bytes 1179656 | tf_op jit(solution)/shard_map/ppermute | solution.py:390
  135.8 2.3 %collective-permute-done.10.refs_1_ = bf16[128,512]{1,0:T(8,128)(2,1)S(1)} collective-permute-done((bf16[128,512]{1,0:T(8,128)(2,1)S(1)}, bf16[128,512]{1,0:T(8,128)(2,1)S(1)}, u32[]{:S(2)}, u32[]{:S(2)}) %collective-permute-start.10) | collective-permute-done | bytes 131104 | tf_op jit(solution)/shard_map/ppermute | solution.py:390
  138.1 5.6 %collective-permute-done.11.refs_0_ = bf16[128,512]{1,0:T(8,128)(2,1)S(1)} collective-permute-done((bf16[128,512]{1,0:T(8,128)(2,1)S(1)}, bf16[128,512]{1,0:T(8,128)(2,1)S(1)}, u32[]{:S(2)}, u32[]{:S(2)}) %collective-permute-start.11) | collective-permute-done | bytes 131104 | tf_op jit(solution)/shard_map/ppermute | solution.py:390
  143.8 8.3 %attend.3 = (bf16[32,16,1024]{2,1,0:T(8,128)(2,1)S(1)}, bf16[128,512]{1,0:T(8,128)(2,1)S(1)}, f32[128,512]{1,0:T(8,128)S(1)}, f32[128,512]{1,0:T(8,128)S(1)}, f3...) custom-call(s32[4]{0:T(128)S(1)} %pad_add_fusion.meta_ref, s32[1,128]{1,0:T(1,128)S(1)} %bitcast.20, ...), custom_call_target="tpu_custom_call" | custom-call | flops 2013265920 | bytes 6291456 | tf_op jit(solution)/shard_map/attend/pallas_call | solution.py:240
  152.0 0.0 copy-start.5
  152.0 0.0 copy-start.11
  152.0 0.1 collective-permute-start.12
  152.2 0.1 add_convert_fusion.1
  152.3 0.1 collective-permute-start.6
  152.4 4.0 %collective-permute-done.12 = bf16[128,512]{1,0:T(8,128)(2,1)S(1)} collective-permute-done((bf16[128,512]{1,0:T(8,128)(2,1)S(1)}, bf16[128,512]{1,0:T(8,128)(2,1)S(1)}, u32[]{:S(2)}, u32[]{:S(2)}) %collective-permute-start.12) | collective-permute-done | bytes 131104 | tf_op jit(solution)/shard_map/ppermute | solution.py:390
  156.4 1.3 collective-permute-start.13
  157.7 9.3 %collective-permute-done.13 = bf16[128,512]{1,0:T(8,128)(2,1)S(1)} collective-permute-done((bf16[128,512]{1,0:T(8,128)(2,1)S(1)}, bf16[128,512]{1,0:T(8,128)(2,1)S(1)}, u32[]{:S(2)}, u32[]{:S(2)}) %collective-permute-start.13) | collective-permute-done | bytes 131104 | tf_op jit(solution)/shard_map/ppermute | solution.py:390
  167.0 1.3 collective-permute-start.14
  168.3 0.1 add_convert_fusion
  168.4 0.1 collective-permute-start.7
  168.5 2.8 %collective-permute-done.14 = bf16[128,512]{1,0:T(8,128)(2,1)S(1)} collective-permute-done((bf16[128,512]{1,0:T(8,128)(2,1)S(1)}, bf16[128,512]{1,0:T(8,128)(2,1)S(1)}, u32[]{:S(2)}, u32[]{:S(2)}) %collective-permute-start.14) | collective-permute-done | bytes 131104 | tf_op jit(solution)/shard_map/ppermute | solution.py:390
  171.3 2.3 %collective-permute-start.15 = (bf16[128,512]{1,0:T(8,128)(2,1)S(1)}, bf16[128,512]{1,0:T(8,128)(2,1)S(1)}, u32[]{:S(2)}, u32[]{:S(2)}) collective-permute-start(bf16[128,512]{1,0:T(8,128)(2,1)S(1)} %add_convert_fusion.3), channel_id=1, source_target_pairs={{0,7},{1,0},{2,1},{3,2},{4,3},{5,4},{6,5},{7,6},{8,15},{9,8},{10,9... | collective-permute-start | bytes 393224 | tf_op jit(solution)/shard_map/ppermute | solution.py:390
  173.7 7.3 %collective-permute-done.15.refs_1_ = bf16[128,512]{1,0:T(8,128)(2,1)S(1)} collective-permute-done((bf16[128,512]{1,0:T(8,128)(2,1)S(1)}, bf16[128,512]{1,0:T(8,128)(2,1)S(1)}, u32[]{:S(2)}, u32[]{:S(2)}) %collective-permute-start.15) | collective-permute-done | bytes 131104 | tf_op jit(solution)/shard_map/ppermute | solution.py:390
  181.0 0.5 return_kv.1
  181.5 2.5 %pad_maximum_fusion = bf16[32,16,1536]{2,1,0:T(8,128)(2,1)} fusion(bf16[32,16,512]{2,1,0:T(8,128)(2,1)S(1)} %return_kv.1, bf16[32,16,1024]{2,1,0:T(8,128)(2,1)} %copy-done.5), kind=kLoop, calls=%fused_computation | loop fusion | flops 3145728 | bytes 3145728 | tf_op jit(solution)/shard_map/concatenate | solution.py:436
  184.0 9.9 %all-to-all-start.4 = ((bf16[32,16,1536]{2,1,0:T(8,128)(2,1)}), bf16[32,16,1536]{2,1,0:T(8,128)(2,1)}, u32[]{:S(2)}, u32[]{:S(2)}) async-start(bf16[32,16,1536]{2,1,0:T(8,128)(2,1)} %pad_maximum_fusion), calls=%async_computation.4 | async-start | bytes 3145728 | tf_op jit(solution)/shard_map/all_to_all | solution.py:385
  193.9 6.7 %finish_rows.2 = (bf16[128,8192]{1,0:T(8,128)(2,1)}, bf16[128,8192]{1,0:T(8,128)(2,1)}) custom-call(s32[1,128]{1,0:T(1,128)S(1)} %bitcast.9, f32[1,128]{1,0:T(1,128)S(1)} %bitcast.14, bf16[128,8192]{1,0:T(8,128)(2,1)S(1)} %copy-done, bf16[32,16,3072]{2,1,0:T(8,128)(2,1)} %all-to-all-done.3.in_ref), custom_call_target="tpu_custom_call" | custom-call | flops 1610612736 | bytes 7864320 | tf_op jit(solution)/shard_map/finish_rows/pallas_call | solution.py:328
  200.6 15.5 %all-to-all-done.4.in_ref = bf16[32,16,1536]{2,1,0:T(8,128)(2,1)} async-done(((bf16[32,16,1536]{2,1,0:T(8,128)(2,1)}), bf16[32,16,1536]{2,1,0:T(8,128)(2,1)}, u32[]{:S(2)}, u32[]{:S(2)}) %all-to-all-start.4) | async-done | bytes 1572896 | tf_op jit(solution)/shard_map/all_to_all | solution.py:385
  216.1 2.4 %finish_kv.1 = (bf16[128,1024]{1,0:T(8,128)(2,1)}, bf16[128,1024]{1,0:T(8,128)(2,1)}) custom-call(s32[1,128]{1,0:T(1,128)S(1)} %bitcast.10, f32[1,128]{1,0:T(1,128)S(1)} %bitcast.17, bf16[128,1024]{1,0:T(8,128)(2,1)S(1)} %copy-done.7, bf16[32,16,1536]{2,1,0:T(8,128)(2,1)} %all-to-all-done.4.in_ref), custom_call_target="tpu_custom_call" | custom-call | flops 268435456 | bytes 1572864 | tf_op jit(solution)/shard_map/finish_kv/pallas_call | solution.py:367
  218.5 3.1 %finish_rows.3 = (bf16[128,8192]{1,0:T(8,128)(2,1)}, bf16[128,8192]{1,0:T(8,128)(2,1)}) custom-call(s32[1,128]{1,0:T(1,128)S(1)} %bitcast.11, f32[1,128]{1,0:T(1,128)S(1)} %bitcast.15, bf16[128,8192]{1,0:T(8,128)(2,1)S(1)} %copy-done, bf16[32,16,1536]{2,1,0:T(8,128)(2,1)} %all-to-all-done.4.in_ref, ...), custom_call_target="tpu_custom_call", output_to_operand_aliasing={{0}: (4, {}), {1}: (5, {})} | custom-call | flops 536870912 | bytes 2621440 | tf_op jit(solution)/shard_map/finish_rows/pallas_call | solution.py:328
  (54 shorter events, 0.2 us)
Async XLA Ops:
  0.6 13.4 %copy-start = (bf16[128,8192]{1,0:T(8,128)(2,1)S(1)}, bf16[128,8192]{1,0:T(8,128)(2,1)}, u32[]{:S(2)}) copy-start(bf16[128,8192]{1,0:T(8,128)(2,1)} %q_ref.7) | copy-start | bytes 6291460
  0.6 1.1 copy-start.6
  1.7 0.9 copy-start.15
  2.7 0.7 copy-start.16
  3.3 0.7 copy-start.19
  4.0 10.1 %copy-start.17 = (s32[1,1,128]{2,1,0:T(1,128)S(1)}, s32[1,1,128]{2,1,0:T(1,128)}, u32[]{:S(2)}) copy-start(s32[1,1,128]{2,1,0:T(1,128)} %param.16) | copy-start | bytes 1540
  4.0 10.1 %copy-start.18 = (f32[128]{0:T(128)S(1)}, f32[128]{0:T(128)}, u32[]{:S(2)}) copy-start(f32[128]{0:T(128)} %param.13) | copy-start | bytes 1540
  5.5 20.1 %all-to-all-start = ((bf16[32,16,512]{2,1,0:T(8,128)(2,1)}), bf16[32,16,512]{2,1,0:T(8,128)(2,1)S(1)}, u32[]{:S(2)}, u32[]{:S(2)}) async-start(bf16[32,16,512]{2,1,0:T(8,128)(2,1)} %send_kv.1), calls=%async_computation | async-start | bytes 1048576 | tf_op jit(solution)/shard_map/all_to_all | solution.py:385
  14.1 1.6 copy-start.2
  20.1 1.7 copy-start.1
  21.8 8.7 %copy-start.21 = (s32[1,1,128]{2,1,0:T(1,128)S(1)}, s32[1,1,128]{2,1,0:T(1,128)}, u32[]{:S(2)}) copy-start(s32[1,1,128]{2,1,0:T(1,128)} %param.17) | copy-start | bytes 1540
  25.6 46.3 %all-to-all-start.1 = ((bf16[32,16,3072]{2,1,0:T(8,128)(2,1)}), bf16[32,16,3072]{2,1,0:T(8,128)(2,1)}, u32[]{:S(2)}, u32[]{:S(2)}) async-start(bf16[32,16,3072]{2,1,0:T(8,128)(2,1)} %copy-done.1), calls=%async_computation.1 | async-start | bytes 6291456 | tf_op jit(solution)/shard_map/all_to_all | solution.py:385
  31.0 0.7 copy-start.26
  31.7 14.8 %collective-permute-start = (bf16[128,1536]{1,0:T(8,128)(2,1)S(1)}, bf16[128,1536]{1,0:T(8,128)(2,1)S(1)}, u32[]{:S(2)}, u32[]{:S(2)}) collective-permute-start(bf16[128,1536]{1,0:T(8,128)(2,1)S(1)} %get-tuple-element.34.refs_4_), channel_id=1, source_target_pairs={{0,1},{1,2},{2,3},{3,4},{4,5},{5,6},{6,7},{7,0},{8,9},{9,10},{10,1... | collective-permute-start | bytes 1179656 | tf_op jit(solution)/shard_map/ppermute | solution.py:390
  46.5 11.1 %collective-permute-start.1 = (bf16[128,1536]{1,0:T(8,128)(2,1)S(1)}, bf16[128,1536]{1,0:T(8,128)(2,1)S(1)}, u32[]{:S(2)}, u32[]{:S(2)}) collective-permute-start(bf16[128,1536]{1,0:T(8,128)(2,1)S(1)} %collective-permute-done.refs_3_), channel_id=1, source_target_pairs={{0,1},{1,2},{2,3},{3,4},{4,5},{5,6},{6,7},{7,0},{8,9},{9,10},{10,1... | collective-permute-start | bytes 1179656 | tf_op jit(solution)/shard_map/ppermute | solution.py:390
  46.5 0.8 copy-start.22
  57.6 10.3 %collective-permute-start.2 = (bf16[128,1536]{1,0:T(8,128)(2,1)S(1)}, bf16[128,1536]{1,0:T(8,128)(2,1)}, u32[]{:S(2)}, u32[]{:S(2)}) collective-permute-start(bf16[128,1536]{1,0:T(8,128)(2,1)S(1)} %collective-permute-done.1.refs_2_), channel_id=1, source_target_pairs={{0,1},{1,2},{2,3},{3,4},{4,5},{5,6},{6,7},{7,0},{8,9},{9,10},{10,1... | collective-permute-start | bytes 1179656 | tf_op jit(solution)/shard_map/ppermute | solution.py:390
  57.6 0.7 copy-start.24
  67.9 14.6 %collective-permute-start.3 = (bf16[128,1536]{1,0:T(8,128)(2,1)}, bf16[128,1536]{1,0:T(8,128)(2,1)}, u32[]{:S(2)}, u32[]{:S(2)}) collective-permute-start(bf16[128,1536]{1,0:T(8,128)(2,1)} %collective-permute-done.2.refs_1_), channel_id=1, source_target_pairs={{0,1},{1,2},{2,3},{3,4},{4,5},{5,6},{6,7},{7,0},{8,9},{9,10},{10,1... | collective-permute-start | bytes 1179656 | tf_op jit(solution)/shard_map/ppermute | solution.py:390
  67.9 1.6 copy-start.3
  71.9 50.9 %all-to-all-start.2 = ((bf16[32,16,1024]{2,1,0:T(8,128)(2,1)}), bf16[32,16,1024]{2,1,0:T(8,128)(2,1)S(1)}, u32[]{:S(2)}, u32[]{:S(2)}) async-start(bf16[32,16,1024]{2,1,0:T(8,128)(2,1)} %send_rows.3), calls=%async_computation.2 | async-start | bytes 2097152 | tf_op jit(solution)/shard_map/all_to_all | solution.py:385
  82.5 1.0 copy-start.23
  83.5 1.0 copy-start.25
  84.4 32.5 %copy-start.27 = (bf16[128,512]{1,0:T(8,128)(2,1)S(1)}, bf16[128,512]{1,0:T(8,128)(2,1)}, u32[]{:S(2)}) copy-start(bf16[128,512]{1,0:T(8,128)(2,1)} %copy-done.26) | copy-start | bytes 393220
  108.7 1.6 copy-start.4
  110.3 0.9 copy-start.8
  111.2 0.9 copy-start.10
  112.1 1.0 copy-start.12
  113.0 1.0 copy-start.14
  114.0 17.4 %collective-permute-start.4 = (bf16[128,1536]{1,0:T(8,128)(2,1)}, bf16[128,1536]{1,0:T(8,128)(2,1)}, u32[]{:S(2)}, u32[]{:S(2)}) collective-permute-start(bf16[128,1536]{1,0:T(8,128)(2,1)} %get-tuple-element.35), channel_id=1, source_target_pairs={{0,7},{1,0},{2,1},{3,2},{4,3},{5,4},{6,5},{7,6},{8,15},{9,8},{10,9... | collective-permute-start | bytes 1179656 | tf_op jit(solution)/shard_map/ppermute | solution.py:390
  117.0 5.8 %collective-permute-start.8 = (bf16[128,512]{1,0:T(8,128)(2,1)S(1)}, bf16[128,512]{1,0:T(8,128)(2,1)S(1)}, u32[]{:S(2)}, u32[]{:S(2)}) collective-permute-start(bf16[128,512]{1,0:T(8,128)(2,1)S(1)} %copy-done.27), channel_id=1, source_target_pairs={{0,1},{1,2},{2,3},{3,4},{4,5},{5,6},{6,7},{7,0},{8,9},{9,10},{10,1... | collective-permute-start | bytes 393224 | tf_op jit(solution)/shard_map/ppermute | solution.py:390
  122.8 8.6 %collective-permute-start.9 = (bf16[128,512]{1,0:T(8,128)(2,1)S(1)}, bf16[128,512]{1,0:T(8,128)(2,1)S(1)}, u32[]{:S(2)}, u32[]{:S(2)}) collective-permute-start(bf16[128,512]{1,0:T(8,128)(2,1)S(1)} %collective-permute-done.8.refs_3_), channel_id=1, source_target_pairs={{0,1},{1,2},{2,3},{3,4},{4,5},{5,6},{6,7},{7,0},{8,9},{9,10},{10,1... | collective-permute-start | bytes 393224 | tf_op jit(solution)/shard_map/ppermute | solution.py:390
  122.8 21.0 %copy-start.28 = (bf16[128,512]{1,0:T(8,128)(2,1)S(1)}, bf16[128,512]{1,0:T(8,128)(2,1)}, u32[]{:S(2)}) copy-start(bf16[128,512]{1,0:T(8,128)(2,1)} %copy-done.26) | copy-start | bytes 393220
  122.8 58.7 %all-to-all-start.3 = ((bf16[32,16,3072]{2,1,0:T(8,128)(2,1)}), bf16[32,16,3072]{2,1,0:T(8,128)(2,1)}, u32[]{:S(2)}, u32[]{:S(2)}) async-start(bf16[32,16,3072]{2,1,0:T(8,128)(2,1)} %copy-done.4), calls=%async_computation.3 | async-start | bytes 6291456 | tf_op jit(solution)/shard_map/all_to_all | solution.py:385
  131.4 6.8 %collective-permute-start.10 = (bf16[128,512]{1,0:T(8,128)(2,1)S(1)}, bf16[128,512]{1,0:T(8,128)(2,1)S(1)}, u32[]{:S(2)}, u32[]{:S(2)}) collective-permute-start(bf16[128,512]{1,0:T(8,128)(2,1)S(1)} %collective-permute-done.9.refs_2_), channel_id=1, source_target_pairs={{0,1},{1,2},{2,3},{3,4},{4,5},{5,6},{6,7},{7,0},{8,9},{9,10},{10,1... | collective-permute-start | bytes 393224 | tf_op jit(solution)/shard_map/ppermute | solution.py:390
  132.8 19.4 %copy-start.13 = (f32[128,1536]{1,0:T(8,128)S(1)}, f32[128,1536]{1,0:T(8,128)}, u32[]{:S(2)}) copy-start(f32[128,1536]{1,0:T(8,128)} %copy-done.12) | copy-start | bytes 2359300
  132.8 19.4 %collective-permute-start.5 = (bf16[128,1536]{1,0:T(8,128)(2,1)S(1)}, bf16[128,1536]{1,0:T(8,128)(2,1)S(1)}, u32[]{:S(2)}, u32[]{:S(2)}) collective-permute-start(bf16[128,1536]{1,0:T(8,128)(2,1)S(1)} %add_convert_fusion.2), channel_id=1, source_target_pairs={{0,7},{1,0},{2,1},{3,2},{4,3},{5,4},{6,5},{7,6},{8,15},{9,8},{10,9... | collective-permute-start | bytes 1179656 | tf_op jit(solution)/shard_map/ppermute | solution.py:390
  138.1 5.6 %collective-permute-start.11 = (bf16[128,512]{1,0:T(8,128)(2,1)S(1)}, bf16[128,512]{1,0:T(8,128)(2,1)S(1)}, u32[]{:S(2)}, u32[]{:S(2)}) collective-permute-start(bf16[128,512]{1,0:T(8,128)(2,1)S(1)} %collective-permute-done.10.refs_1_), channel_id=1, source_target_pairs={{0,1},{1,2},{2,3},{3,4},{4,5},{5,6},{6,7},{7,0},{8,9},{9,10},{10,1... | collective-permute-start | bytes 393224 | tf_op jit(solution)/shard_map/ppermute | solution.py:390
  152.0 16.4 %copy-start.5 = (bf16[32,16,1024]{2,1,0:T(8,128)(2,1)}, bf16[32,16,1024]{2,1,0:T(8,128)(2,1)S(1)}, u32[]{:S(2)}) copy-start(bf16[32,16,1024]{2,1,0:T(8,128)(2,1)S(1)} %get-tuple-element.49) | copy-start | bytes 3145732
  152.0 16.3 %copy-start.11 = (f32[128,1536]{1,0:T(8,128)S(1)}, f32[128,1536]{1,0:T(8,128)}, u32[]{:S(2)}) copy-start(f32[128,1536]{1,0:T(8,128)} %copy-done.10) | copy-start | bytes 2359300
  152.0 4.3 %collective-permute-start.12 = (bf16[128,512]{1,0:T(8,128)(2,1)S(1)}, bf16[128,512]{1,0:T(8,128)(2,1)S(1)}, u32[]{:S(2)}, u32[]{:S(2)}) collective-permute-start(bf16[128,512]{1,0:T(8,128)(2,1)S(1)} %get-tuple-element.41), channel_id=1, source_target_pairs={{0,7},{1,0},{2,1},{3,2},{4,3},{5,4},{6,5},{7,6},{8,15},{9,8},{10,9... | collective-permute-start | bytes 393224 | tf_op jit(solution)/shard_map/ppermute | solution.py:390
  152.2 28.8 %copy-start.9 = (f32[128,1536]{1,0:T(8,128)S(1)}, f32[128,1536]{1,0:T(8,128)}, u32[]{:S(2)}) copy-start(f32[128,1536]{1,0:T(8,128)} %copy-done.8) | copy-start | bytes 2359300
  152.3 16.0 %collective-permute-start.6 = (bf16[128,1536]{1,0:T(8,128)(2,1)S(1)}, bf16[128,1536]{1,0:T(8,128)(2,1)S(1)}, u32[]{:S(2)}, u32[]{:S(2)}) collective-permute-start(bf16[128,1536]{1,0:T(8,128)(2,1)S(1)} %add_convert_fusion.1), channel_id=1, source_target_pairs={{0,7},{1,0},{2,1},{3,2},{4,3},{5,4},{6,5},{7,6},{8,15},{9,8},{10,9... | collective-permute-start | bytes 1179656 | tf_op jit(solution)/shard_map/ppermute | solution.py:390
  156.4 10.6 %collective-permute-start.13 = (bf16[128,512]{1,0:T(8,128)(2,1)S(1)}, bf16[128,512]{1,0:T(8,128)(2,1)S(1)}, u32[]{:S(2)}, u32[]{:S(2)}) collective-permute-start(bf16[128,512]{1,0:T(8,128)(2,1)S(1)} %add_convert_fusion.5), channel_id=1, source_target_pairs={{0,7},{1,0},{2,1},{3,2},{4,3},{5,4},{6,5},{7,6},{8,15},{9,8},{10,9... | collective-permute-start | bytes 393224 | tf_op jit(solution)/shard_map/ppermute | solution.py:390
  167.0 4.3 %collective-permute-start.14 = (bf16[128,512]{1,0:T(8,128)(2,1)S(1)}, bf16[128,512]{1,0:T(8,128)(2,1)S(1)}, u32[]{:S(2)}, u32[]{:S(2)}) collective-permute-start(bf16[128,512]{1,0:T(8,128)(2,1)S(1)} %add_convert_fusion.4), channel_id=1, source_target_pairs={{0,7},{1,0},{2,1},{3,2},{4,3},{5,4},{6,5},{7,6},{8,15},{9,8},{10,9... | collective-permute-start | bytes 393224 | tf_op jit(solution)/shard_map/ppermute | solution.py:390
  168.4 12.6 %collective-permute-start.7 = (bf16[128,1536]{1,0:T(8,128)(2,1)S(1)}, bf16[128,1536]{1,0:T(8,128)(2,1)S(1)}, u32[]{:S(2)}, u32[]{:S(2)}) collective-permute-start(bf16[128,1536]{1,0:T(8,128)(2,1)S(1)} %add_convert_fusion), channel_id=1, source_target_pairs={{0,7},{1,0},{2,1},{3,2},{4,3},{5,4},{6,5},{7,6},{8,15},{9,8},{10,9... | collective-permute-start | bytes 1179656 | tf_op jit(solution)/shard_map/ppermute | solution.py:390
  171.3 9.7 %collective-permute-start.15 = (bf16[128,512]{1,0:T(8,128)(2,1)S(1)}, bf16[128,512]{1,0:T(8,128)(2,1)S(1)}, u32[]{:S(2)}, u32[]{:S(2)}) collective-permute-start(bf16[128,512]{1,0:T(8,128)(2,1)S(1)} %add_convert_fusion.3), channel_id=1, source_target_pairs={{0,7},{1,0},{2,1},{3,2},{4,3},{5,4},{6,5},{7,6},{8,15},{9,8},{10,9... | collective-permute-start | bytes 393224 | tf_op jit(solution)/shard_map/ppermute | solution.py:390
  184.0 32.1 %all-to-all-start.4 = ((bf16[32,16,1536]{2,1,0:T(8,128)(2,1)}), bf16[32,16,1536]{2,1,0:T(8,128)(2,1)}, u32[]{:S(2)}, u32[]{:S(2)}) async-start(bf16[32,16,1536]{2,1,0:T(8,128)(2,1)} %pad_maximum_fusion), calls=%async_computation.4 | async-start | bytes 3145728 | tf_op jit(solution)/shard_map/all_to_all | solution.py:385
  193.9 22.2 %copy-start.7 = (bf16[128,1024]{1,0:T(8,128)(2,1)S(1)}, bf16[128,1024]{1,0:T(8,128)(2,1)}, u32[]{:S(2)}) copy-start(bf16[128,1024]{1,0:T(8,128)(2,1)} %k_ref.3) | copy-start | bytes 786436
  193.9 22.2 %copy-start.20 = (f32[128]{0:T(128)S(1)}, f32[128]{0:T(128)}, u32[]{:S(2)}) copy-start(f32[128]{0:T(128)} %param.14) | copy-start | bytes 1540

commit v2 on v1

v2 whole, which is shorter than its diff:
```python
import functools

import jax
import jax.numpy as jnp
from jax import lax
from jax.experimental import pallas as pl
from jax.experimental.pallas import tpu as pltpu
from jax.sharding import PartitionSpec as P

Q_HEADS = 64
KV_HEADS = 8
HEAD = 128
RATIO = Q_HEADS // KV_HEADS
EPS = 1e-06
ROWS = 128
GROUPS = 32
SHARE = ROWS // GROUPS
SPLIT = 4
CHUNK = SHARE * SPLIT
TALL = GROUPS * CHUNK
WIDE = 2 * HEAD
BACK = 4
WINDOW = (BACK + 1) * ROWS
SCALE = HEAD ** (-0.5)
LOG2E = 1.4426950408889634
FIRST = 6
VMEM_LIMIT = 52 * 1024 * 1024
VMEM_WHOLE = 62 * 1024 * 1024
F32 = jnp.float32
BF16 = jnp.bfloat16


def params(limit=VMEM_LIMIT):
    return pltpu.CompilerParams(vmem_limit_bytes=limit)


def cost(flops, moved, trans=0):
    return pl.CostEstimate(flops=int(flops), bytes_accessed=int(moved), transcendentals=int(trans))


def dot(a, b, dims):
    return lax.dot_general(a, b, (dims, ((), ())), preferred_element_type=F32)


MM = ((1,), (0,))
MT = ((1,), (1,))
TM = ((0,), (0,))


def iota(shape, dim):
    return lax.broadcasted_iota(jnp.int32, shape, dim)


def tall_row(index):
    row = (index // CHUNK) * SHARE + index % SHARE
    part = (index // SHARE) % SPLIT
    return row, part


def home_matrix(order_ref):
    spread_row, _ = tall_row(iota((ROWS, TALL), 1))
    spread = (spread_row == iota((ROWS, TALL), 0)).astype(BF16)
    order = jnp.broadcast_to(order_ref[...].astype(F32), (16, ROWS)).astype(BF16)
    source = dot(order, spread, MM)[:1]
    _, part = tall_row(iota((1, TALL), 1))
    code = source + (part * ROWS).astype(F32)
    return (iota((TALL, TALL), 0).astype(F32) == code).astype(BF16)


def pack_matrix(order_ref):
    row, part = tall_row(iota((TALL, SPLIT * ROWS), 0))
    order = order_ref[...]
    code = jnp.concatenate([order + p * ROWS for p in range(SPLIT)], axis=1)
    return (row + part * ROWS == code).astype(BF16)


def norm(x, gain):
    factor = lax.rsqrt(jnp.mean(x * x, axis=-1, keepdims=True) + EPS)
    return x * factor * gain


def norm_back(x, gain, dy):
    factor = lax.rsqrt(jnp.mean(x * x, axis=-1, keepdims=True) + EPS)
    g = dy * gain
    inner = jnp.mean(x * g, axis=-1, keepdims=True)
    return factor * g - x * (factor * factor * factor * inner)


def head_cols(h):
    return slice(h * HEAD, (h + 1) * HEAD)


def send_kv_kernel(order_ref, gain_ref, k_ref, v_ref, out_ref):
    gain = gain_ref[...]
    kn = [
        norm(k_ref[:, head_cols(h)].astype(F32), gain).astype(BF16) for h in range(KV_HEADS)
    ]
    half = KV_HEADS * HEAD // 2
    stack = jnp.concatenate(
        [
            jnp.concatenate(kn[: KV_HEADS // 2], axis=1),
            jnp.concatenate(kn[KV_HEADS // 2 :], axis=1),
            v_ref[:, :half],
            v_ref[:, half:],
        ],
        axis=0,
    )
    sent = dot(home_matrix(order_ref), stack, TM).astype(BF16)
    out_ref[...] = sent.reshape(GROUPS, CHUNK, half)


def send_kv(order, gain, key_projection, value):
    half = KV_HEADS * HEAD // 2
    return pl.pallas_call(
        send_kv_kernel,
        out_shape=jax.ShapeDtypeStruct((GROUPS, CHUNK, half), BF16),
        compiler_params=params(VMEM_WHOLE),
        cost_estimate=cost(2 * TALL * TALL * half, 3 << 19),
        name="send_kv",
    )(order, gain, key_projection, value)


def send_rows_kernel(order_ref, gain_ref, q_ref, d_ref, out_ref, home_ref):
    @pl.when(pl.program_id(0) == 0)
    def _():
        home_ref[...] = home_matrix(order_ref)

    gain = gain_ref[...]
    qn = [norm(q_ref[:, head_cols(h)].astype(F32), gain).astype(BF16) for h in range(RATIO)]
    stack = jnp.concatenate(
        [
            jnp.concatenate(
                [qn[2 * p], qn[2 * p + 1], d_ref[:, p * WIDE : (p + 1) * WIDE]], axis=1
            )
            for p in range(SPLIT)
        ],
        axis=0,
    )
    sent = dot(home_ref[...], stack, TM).astype(BF16)
    out_ref[...] = sent.reshape(GROUPS, CHUNK, 2 * WIDE)


def send_rows(order, gain, query, d_out, first, count):
    return pl.pallas_call(
        send_rows_kernel,
        grid=(count,),
        in_specs=[
            pl.BlockSpec((1, ROWS), lambda h: (0, 0)),
            pl.BlockSpec((1, HEAD), lambda h: (0, 0)),
            pl.BlockSpec((ROWS, RATIO * HEAD), lambda h: (0, h + first)),
            pl.BlockSpec((ROWS, RATIO * HEAD), lambda h: (0, h + first)),
        ],
        out_specs=pl.BlockSpec((GROUPS, CHUNK, 2 * WIDE), lambda h: (0, 0, h)),
        out_shape=jax.ShapeDtypeStruct((GROUPS, CHUNK, count * 2 * WIDE), BF16),
        scratch_shapes=[pltpu.VMEM((TALL, TALL), BF16)],
        compiler_params=params(VMEM_WHOLE),
        cost_estimate=cost(count * 2 * TALL * TALL * 2 * WIDE, count << 20),
        name="send_rows",
    )(order, gain, query, d_out)


def sort_kv_kernel(order_ref, in_ref, first_ref, last_ref):
    half = KV_HEADS * HEAD // 2
    rows = dot(pack_matrix(order_ref), in_ref[...].reshape(TALL, half), TM).astype(BF16)
    for h in range(KV_HEADS):
        ref, at = (first_ref, h) if h < FIRST else (last_ref, h - FIRST)
        part, cols = h // (KV_HEADS // 2), head_cols(h % (KV_HEADS // 2))
        k = rows[part * ROWS : (part + 1) * ROWS, cols]
        v = rows[(part + 2) * ROWS : (part + 3) * ROWS, cols]
        ref[:, at * WIDE : (at + 1) * WIDE] = jnp.concatenate([k, v], axis=1)


def sort_kv(order, received):
    return pl.pallas_call(
        sort_kv_kernel,
        out_shape=[
            jax.ShapeDtypeStruct((ROWS, count * WIDE), BF16)
            for count in (FIRST, KV_HEADS - FIRST)
        ],
        compiler_params=params(),
        cost_estimate=cost(2 * TALL**3, 1 << 20),
        name="sort_kv",
    )(order, received)


def attend_kernel(meta_ref, order_ref, qd_ref, *refs):
    kv_refs = refs[: BACK + 1]
    out_ref = refs[BACK + 1]
    part_refs = refs[BACK + 2 : 2 * BACK + 3]
    bias_ref = refs[2 * BACK + 3]

    @pl.when(pl.program_id(0) == 0)
    def _():
        places = jnp.broadcast_to(iota((1, ROWS), 1).astype(F32), (16, ROWS)).astype(BF16)
        arrived = (iota((ROWS, ROWS), 0) == order_ref[...]).astype(BF16)
        place = dot(places, arrived, MT).astype(BF16)
        row, _ = tall_row(iota((ROWS, TALL), 1))
        spread = (row == iota((ROWS, TALL), 0)).astype(BF16)
        base = meta_ref[3] * ROWS
        position = dot(place, spread, MM)[:1] + base.astype(F32)
        end0 = meta_ref[0].astype(F32)
        end1 = (meta_ref[0] + meta_ref[1]).astype(F32)
        start = jnp.where(position < end0, 0.0, jnp.where(position < end1, end0, end1))
        key = (iota((WINDOW, TALL), 0) + (base - BACK * ROWS)).astype(F32)
        bias_ref[...] = jnp.where((key >= start) & (key <= position), 0.0, -1e30)

    kw = jnp.concatenate([r[:, :HEAD] for r in kv_refs], axis=0)
    vw = jnp.concatenate([r[:, HEAD:] for r in kv_refs], axis=0)

    def both(low):
        return jnp.concatenate(
            [
                qd_ref[:, :, low + e * HEAD : low + (e + 1) * HEAD].reshape(TALL, HEAD)
                for e in range(2)
            ],
            axis=0,
        )

    q, d = both(0), both(WIDE)
    scores = dot(kw, q, MT)
    d_weights = dot(vw, d, MT)
    bias = bias_ref[...]
    expo = jnp.exp2(scores * (SCALE * LOG2E) + jnp.concatenate([bias, bias], axis=1))
    weights = expo * (1.0 / jnp.sum(expo, axis=0, keepdims=True))
    low_weights = weights.astype(BF16)
    out = dot(vw, low_weights, TM).astype(BF16)
    delta = jnp.sum(d.astype(F32).T * out.astype(F32), axis=0, keepdims=True)
    d_scores = (weights * (d_weights - delta)).astype(BF16)
    dq = (dot(kw, d_scores, TM) * SCALE).astype(BF16)
    dk = dot(d_scores, q, MM) * SCALE
    dv = dot(low_weights, d, MM)
    for low, value in ((0, out.T), (WIDE, dq.T)):
        for e in range(2):
            out_ref[:, :, low + e * HEAD : low + (e + 1) * HEAD] = value[
                e * TALL : (e + 1) * TALL
            ].reshape(GROUPS, CHUNK, HEAD)
    for n, ref in enumerate(part_refs):
        ref[:, :HEAD] = dk[n * ROWS : (n + 1) * ROWS].astype(ref.dtype)
        ref[:, HEAD:] = dv[n * ROWS : (n + 1) * ROWS].astype(ref.dtype)


def attend(meta, order, received, blocks, count, room=0):
    kv_spec = pl.BlockSpec((ROWS, WIDE), lambda h: (0, h))
    elements = count * RATIO * ROWS * WINDOW
    return pl.pallas_call(
        attend_kernel,
        grid=(count,),
        in_specs=[
            pl.BlockSpec(memory_space=pltpu.SMEM),
            pl.BlockSpec((1, ROWS), lambda h: (0, 0)),
            pl.BlockSpec((GROUPS, CHUNK, 2 * WIDE), lambda h: (0, 0, h)),
        ]
        + [kv_spec] * (BACK + 1),
        out_specs=[pl.BlockSpec((GROUPS, CHUNK, 2 * WIDE), lambda h: (0, 0, h))]
        + [kv_spec] * (BACK + 1),
        out_shape=[jax.ShapeDtypeStruct((GROUPS, CHUNK, (count + room) * 2 * WIDE), BF16)]
        + [
            jax.ShapeDtypeStruct((ROWS, count * WIDE), BF16 if n == 0 else F32)
            for n in range(BACK + 1)
        ],
        scratch_shapes=[pltpu.VMEM((WINDOW, TALL), F32)],
        compiler_params=params(),
        cost_estimate=cost(12 * elements * HEAD, count * (3 << 20), elements),
        name="attend",
    )(meta, order, received, *blocks)


def return_kv_kernel(order_ref, first_ref, last_ref, own_first_ref, own_last_ref, _, out_ref):
    half = KV_HEADS * HEAD // 2
    total = jnp.concatenate(
        [
            (got[...].astype(F32) + own[...]).astype(BF16)
            for got, own in ((first_ref, own_first_ref), (last_ref, own_last_ref))
        ],
        axis=1,
    )

    def columns(which, part):
        heads = range(part * KV_HEADS // 2, (part + 1) * KV_HEADS // 2)
        return jnp.concatenate([total[:, head_cols(2 * h + which)] for h in heads], axis=1)

    stack = jnp.concatenate(
        [columns(which, part) for which in range(2) for part in range(2)], axis=0
    )
    rows = dot(pack_matrix(order_ref), stack, MM).astype(BF16)
    out_ref[...] = rows.reshape(GROUPS, CHUNK, half)


def return_kv(order, first, last, own_first, own_last, result):
    half = KV_HEADS * HEAD // 2
    place = result.shape[2] // half - 1
    small = [pl.BlockSpec(a.shape, lambda i: (0, 0)) for a in (first, last, own_first, own_last)]
    return pl.pallas_call(
        return_kv_kernel,
        grid=(1,),
        in_specs=[pl.BlockSpec((1, ROWS), lambda i: (0, 0)), *small]
        + [pl.BlockSpec(memory_space=pl.ANY)],
        out_specs=pl.BlockSpec((GROUPS, CHUNK, half), lambda i: (0, 0, place)),
        out_shape=jax.ShapeDtypeStruct(result.shape, BF16),
        input_output_aliases={5: 0},
        compiler_params=params(),
        cost_estimate=cost(2 * TALL**3, 3 << 20),
        name="return_kv",
    )(order, first, last, own_first, own_last, result)


def finish_rows_step(rows, gain, q_ref, out_ref, dq_ref):
    for part in range(SPLIT):
        mine = rows[part * ROWS : (part + 1) * ROWS]
        out_ref[:, part * WIDE : (part + 1) * WIDE] = mine[:, :WIDE].astype(BF16)
        for e in range(2):
            at = head_cols(2 * part + e)
            dy = mine[:, WIDE + e * HEAD : WIDE + (e + 1) * HEAD]
            dq_ref[:, at] = norm_back(q_ref[:, at].astype(F32), gain, dy).astype(BF16)


def finish_kv_step(rows, gain, k_ref, dk_ref, dv_ref):
    half = KV_HEADS * HEAD // 2
    for h in range(KV_HEADS):
        part, cols = h // (KV_HEADS // 2), head_cols(h % (KV_HEADS // 2))
        dy = rows[part * ROWS : (part + 1) * ROWS, cols]
        dk_ref[:, head_cols(h)] = norm_back(
            k_ref[:, head_cols(h)].astype(F32), gain, dy
        ).astype(BF16)
    dv_ref[:, :half] = rows[2 * ROWS : 3 * ROWS].astype(BF16)
    dv_ref[:, half:] = rows[3 * ROWS :].astype(BF16)


def finish_kernel(with_kv, order_ref, gain_ref, q_ref, in_ref, *refs):
    home_ref = refs[-1]
    step = pl.program_id(0)

    @pl.when(step == 0)
    def _():
        home_ref[...] = home_matrix(order_ref)

    rows = dot(home_ref[...], in_ref[...].reshape(TALL, 2 * WIDE), MM)
    if with_kv:
        k_gain_ref, k_ref, _, _, out_ref, dq_ref, dk_ref, dv_ref = refs[:-1]
        last = pl.num_programs(0) - 1

        @pl.when(step < last)
        def _():
            finish_rows_step(rows, gain_ref[...], q_ref, out_ref, dq_ref)

        @pl.when(step == last)
        def _():
            finish_kv_step(rows, k_gain_ref[...], k_ref, dk_ref, dv_ref)
    else:
        out_ref, dq_ref = refs[:-1]
        finish_rows_step(rows, gain_ref[...], q_ref, out_ref, dq_ref)


def finish(order, gain, query, received, first, count, kv=(), earlier=()):
    block = pl.BlockSpec((ROWS, RATIO * HEAD), lambda h: (0, jnp.minimum(h, count - 1) + first))
    whole = jax.ShapeDtypeStruct((ROWS, Q_HEADS * HEAD), BF16)
    row = pl.BlockSpec((1, ROWS), lambda h: (0, 0))
    kv_block = pl.BlockSpec((ROWS, KV_HEADS * HEAD), lambda h: (0, 0))
    kv_whole = jax.ShapeDtypeStruct((ROWS, KV_HEADS * HEAD), BF16)
    in_specs = [row, row, block, pl.BlockSpec((GROUPS, CHUNK, 2 * WIDE), lambda h: (0, 0, h))]
    if kv:
        in_specs += [row, kv_block] + [pl.BlockSpec(memory_space=pl.ANY)] * 2
    return pl.pallas_call(
        functools.partial(finish_kernel, bool(kv)),
        grid=(count + 1 if kv else count,),
        in_specs=in_specs,
        out_specs=[block, block] + ([kv_block] * 2 if kv else []),
        out_shape=[whole, whole] + ([kv_whole] * 2 if kv else []),
        scratch_shapes=[pltpu.VMEM((TALL, TALL), BF16)],
        input_output_aliases={6: 0, 7: 1} if kv else {},
        compiler_params=params(),
        cost_estimate=cost(count * 2 * TALL * TALL * 2 * WIDE, count * (5 << 18)),
        name="finish",
    )(order, gain, query, received, *kv, *earlier)


def exchange(array):
    return lax.all_to_all(array, "dp", split_axis=0, concat_axis=0, tiled=True)


def along(array, step):
    count = lax.axis_size("seq")
    return lax.ppermute(array, "seq", [(i, (i + step) % count) for i in range(count)])


def after(array, other):
    return lax.optimization_barrier((array, other))[0]


def per_device(
    query, key_projection, value, d_out, q_gain, key_norm_gain, seq_lengths, send_order, recv_order
):
    leaving = send_order.reshape(1, ROWS)
    arriving = recv_order.reshape(1, ROWS)
    q_gain = q_gain.reshape(1, HEAD)
    k_gain = key_norm_gain.reshape(1, HEAD)
    place = lax.axis_index("seq").astype(jnp.int32)
    meta = jnp.concatenate([seq_lengths[0], place[None]])
    counts = (FIRST, KV_HEADS - FIRST)
    starts = (0, FIRST)

    kv_sent = send_kv(leaving, k_gain, key_projection, value)
    kv_received = exchange(kv_sent)
    sent = [
        send_rows(leaving, q_gain, query, d_out, first, count)
        for first, count in zip(starts, counts)
    ]
    kv_received, *sent = lax.optimization_barrier((kv_received, *sent))
    received_first = exchange(sent[0])
    received_first, last = lax.optimization_barrier((received_first, sent[1]))
    received = [received_first, exchange(last)]

    firsts, lasts = ([block] for block in sort_kv(arriving, kv_received))
    for _ in range(BACK):
        block = after(lasts[-1], firsts[-1])
        firsts.append(along(firsts[-1], 1))
        lasts.append(along(block, 1))
    firsts[-1] = after(firsts[-1], lasts[-1])
    chains = [firsts[::-1], lasts[::-1]]

    results, totals, own = [], [], []
    for n in range(2):
        result, *parts = attend(meta, arriving, received[n], chains[n], counts[n], room=n)
        total = parts[0]
        for part in parts[1:-1]:
            total = (along(total, -1).astype(F32) + part).astype(BF16)
        totals.append(along(total, -1))
        own.append(parts[-1])
        results.append(result)

    back_first = exchange(results[0])
    merged = return_kv(arriving, *totals, *own, results[1])
    back_last = exchange(after(merged, back_first))

    outs = finish(leaving, q_gain, query, back_first, starts[0], counts[0])
    return tuple(
        finish(
            leaving,
            q_gain,
            query,
            back_last,
            starts[1],
            counts[1],
            kv=(k_gain, key_projection),
            earlier=outs,
        )
    )


def solution(mesh):
    rows = P(("dp", "seq"), None)
    in_specs = (rows, rows, rows, rows, P(), P(), P("dp", None)) + (P("dp", "seq", None),) * 2
    return jax.shard_map(
        per_device, mesh=mesh, in_specs=in_specs, out_specs=(rows,) * 4, check_vma=False
    )
```

time: 223 us -> 198 us (0.89)
  local copies, waits for them, and re-layouts: 17.8 us -> 0.05 us
  starting transfers between devices: 54.6 us -> 63 us
  waiting for transfers between devices: 89.7 us -> 82.3 us
  other arithmetic: 4.76 us -> 0.36 us
  Pallas kernels: 53.9 us -> 50.9 us
    unnamed x58 -> x22, local copies, waits for them, and re-layouts: 17.8 us -> 0.05 us
    pallas_call x2, Pallas kernels: 32.5 us -> 24.3 us  [attend(): pl.pallas_call(attend_kernel, grid=(count,), in_specs=[pl.BlockSpec(memor...]
    ppermute x16, starting transfers between devices: 12.9 us -> 17.1 us  [along(): lax.ppermute(array, 'seq', [(i, (i + step) % count) for i in range(count)])]
    all_to_all x5, starting transfers between devices: 41.6 us -> 45.9 us  [exchange(): return lax.all_to_all(array, 'dp', split_axis=0, concat_axis=0, tiled=True)]
    ppermute x16, waiting for transfers between devices: 70.3 us -> 66.2 us  [along(): lax.ppermute(array, 'seq', [(i, (i + step) % count) for i in range(count)])]
    pallas_call x2, Pallas kernels: 6.79 us -> 10.6 us  [send_rows(): pl.pallas_call(send_rows_kernel, grid=(count,), in_specs=[pl.BlockSpec((1...]
    all_to_all x5, waiting for transfers between devices: 19.4 us -> 16.1 us  [exchange(): return lax.all_to_all(array, 'dp', split_axis=0, concat_axis=0, tiled=True)]
    concatenate x1 -> x0, other arithmetic: 2.48 us -> none  [per_device(): back_last = exchange(jnp.concatenate([results[1], kv_back], axis=2))]
  transfers between devices with their start and end apart: 21 -> 21, of which waited for: 12 -> 12; matrix products, arithmetic and copies ran while one was open for 1% -> 0% of each run, Pallas kernels for 21% -> 22%
where the time goes in v2:
time: 198 us
  waiting for transfers between devices  82.3 us (42%)
  starting transfers between devices  63 us (32%)
  Pallas kernels  50.9 us (26%)
    ppermute x16, waiting for transfers between devices, along(): lax.ppermute(array, 'seq', [(i, (i + step) % count) for i in range(count)])  66.2 us
    all_to_all x5, starting transfers between devices, exchange(): return lax.all_to_all(array, 'dp', split_axis=0, concat_axis=0, tiled=True)  45.9 us
    pallas_call x2, Pallas kernels, attend(): pl.pallas_call(attend_kernel, grid=(count,), in_specs=[pl.BlockSpec(memor...  24.3 us
    ppermute x16, starting transfers between devices, along(): lax.ppermute(array, 'seq', [(i, (i + step) % count) for i in range(count)])  17.1 us
    all_to_all x5, waiting for transfers between devices, exchange(): return lax.all_to_all(array, 'dp', split_axis=0, concat_axis=0, tiled=True)  16.1 us
    pallas_call x2, Pallas kernels, finish(): pl.pallas_call(functools.partial(finish_kernel, bool(kv)), grid=(count +...  11.7 us
    pallas_call x2, Pallas kernels, send_rows(): pl.pallas_call(send_rows_kernel, grid=(count,), in_specs=[pl.BlockSpec((1...  10.6 us
  transfers between devices with their start and end apart: 21, of which 12 were waited for; matrix products, arithmetic and copies ran while one was open for 0% of the time, Pallas kernels for 22%

profile of v2, /device:TPU:1, one launch (start us, length us, event | category | flops | bytes accessed | tf_op | source)
XLA Modules:
  0.0 197.5 jit_solution(11832578048334311038)
XLA Ops:
  0.6 2.5 %send_kv.1 = bf16[32,16,512]{2,1,0:T(8,128)(2,1)} custom-call(s32[1,128]{1,0:T(1,128)} %bitcast.6, f32[1,128]{1,0:T(1,128)} %bitcast.15, bf16[128,1024]{1,0:T(8,128)(2,1)} %refs_1_.1, bf16[128,1024]{1,0:T(8,128)(2,1)} %v_ref.1), custom_call_target="tpu_custom_call" | custom-call | flops 268435456 | bytes 1572864 | tf_op jit(solution)/shard_map/send_kv/pallas_call | solution.py:114
  3.1 8.6 %all-to-all-start = ((bf16[32,16,512]{2,1,0:T(8,128)(2,1)}), bf16[32,16,512]{2,1,0:T(8,128)(2,1)S(1)}, u32[]{:S(2)}, u32[]{:S(2)}) async-start(bf16[32,16,512]{2,1,0:T(8,128)(2,1)} %send_kv.1), calls=%async_computation | async-start | bytes 1048576 | tf_op jit(solution)/shard_map/all_to_all | solution.py:378
  11.7 3.4 %send_rows.3 = bf16[32,16,1024]{2,1,0:T(8,128)(2,1)} custom-call(s32[1,128]{1,0:T(1,128)} %bitcast.7, f32[1,128]{1,0:T(1,128)} %bitcast.11, bf16[128,8192]{1,0:T(8,128)(2,1)} %q_ref.7, bf16[128,8192]{1,0:T(8,128)(2,1)} %d_ref.3), custom_call_target="tpu_custom_call" | custom-call | flops 536870912 | bytes 2097152 | tf_op jit(solution)/shard_map/send_rows/pallas_call | solution.py:144
  15.1 7.3 %send_rows.2 = bf16[32,16,3072]{2,1,0:T(8,128)(2,1)} custom-call(s32[1,128]{1,0:T(1,128)} %bitcast.8, f32[1,128]{1,0:T(1,128)} %bitcast.12, bf16[128,8192]{1,0:T(8,128)(2,1)} %q_ref.7, bf16[128,8192]{1,0:T(8,128)(2,1)} %d_ref.3), custom_call_target="tpu_custom_call" | custom-call | flops 1610612736 | bytes 6291456 | tf_op jit(solution)/shard_map/send_rows/pallas_call | solution.py:144
  22.4 0.9 all-to-all-done.in_ref
  23.3 6.5 %all-to-all-start.1 = ((bf16[32,16,3072]{2,1,0:T(8,128)(2,1)}), bf16[32,16,3072]{2,1,0:T(8,128)(2,1)}, u32[]{:S(2)}, u32[]{:S(2)}) async-start(bf16[32,16,3072]{2,1,0:T(8,128)(2,1)} %send_rows.2), calls=%async_computation.1 | async-start | bytes 6291456 | tf_op jit(solution)/shard_map/all_to_all | solution.py:378
  29.8 0.0 copy-start.10
  29.9 0.0 copy-done.5
  29.9 0.5 sort_kv.1
  30.4 0.0 copy-start.6
  30.4 1.7 collective-permute-start
  32.1 13.3 %collective-permute-done.refs_3_ = bf16[128,1536]{1,0:T(8,128)(2,1)S(1)} collective-permute-done((bf16[128,1536]{1,0:T(8,128)(2,1)S(1)}, bf16[128,1536]{1,0:T(8,128)(2,1)S(1)}, u32[]{:S(2)}, u32[]{:S(2)}) %collective-permute-start) | collective-permute-done | bytes 393248 | tf_op jit(solution)/shard_map/ppermute | solution.py:383
  45.4 0.0 collective-permute-start.1
  45.4 11.3 %collective-permute-done.1.refs_2_ = bf16[128,1536]{1,0:T(8,128)(2,1)S(1)} collective-permute-done((bf16[128,1536]{1,0:T(8,128)(2,1)S(1)}, bf16[128,1536]{1,0:T(8,128)(2,1)S(1)}, u32[]{:S(2)}, u32[]{:S(2)}) %collective-permute-start.1) | collective-permute-done | bytes 393248 | tf_op jit(solution)/shard_map/ppermute | solution.py:383
  56.7 0.0 collective-permute-start.2
  56.7 0.0 collective-permute-start.4
  56.7 13.3 %collective-permute-done.4.refs_3_ = bf16[128,512]{1,0:T(8,128)(2,1)S(1)} collective-permute-done((bf16[128,512]{1,0:T(8,128)(2,1)S(1)}, bf16[128,512]{1,0:T(8,128)(2,1)S(1)}, u32[]{:S(2)}, u32[]{:S(2)}) %collective-permute-start.4) | collective-permute-done | bytes 131104 | tf_op jit(solution)/shard_map/ppermute | solution.py:383
  70.0 0.0 collective-permute-start.5
  70.0 0.0 collective-permute-done.2.refs_1_
  70.0 0.0 collective-permute-start.3
  70.0 5.0 %collective-permute-done.5.refs_2_ = bf16[128,512]{1,0:T(8,128)(2,1)S(1)} collective-permute-done((bf16[128,512]{1,0:T(8,128)(2,1)S(1)}, bf16[128,512]{1,0:T(8,128)(2,1)S(1)}, u32[]{:S(2)}, u32[]{:S(2)}) %collective-permute-start.5) | collective-permute-done | bytes 131104 | tf_op jit(solution)/shard_map/ppermute | solution.py:383
  75.0 0.0 collective-permute-start.6
  75.0 0.0 all-to-all-done.1.qd_ref
  75.0 11.8 %all-to-all-start.2 = ((bf16[32,16,1024]{2,1,0:T(8,128)(2,1)}), bf16[32,16,1024]{2,1,0:T(8,128)(2,1)}, u32[]{:S(2)}, u32[]{:S(2)}) async-start(bf16[32,16,1024]{2,1,0:T(8,128)(2,1)} %send_rows.3), calls=%async_computation.2 | async-start | bytes 2097152 | tf_op jit(solution)/shard_map/all_to_all | solution.py:378
  86.8 0.0 collective-permute-done.6.refs_1_
  86.8 0.3 collective-permute-start.7
  87.1 0.0 copy-done.10
  87.1 0.1 pad_add_fusion.meta_ref
  87.2 5.6 %collective-permute-done.7.refs_0_ = bf16[128,512]{1,0:T(8,128)(2,1)S(1)} collective-permute-done((bf16[128,512]{1,0:T(8,128)(2,1)S(1)}, bf16[128,512]{1,0:T(8,128)(2,1)S(1)}, u32[]{:S(2)}, u32[]{:S(2)}) %collective-permute-start.7) | collective-permute-done | bytes 131104 | tf_op jit(solution)/shard_map/ppermute | solution.py:383
  92.8 0.0 collective-permute-done.3.refs_0_
  92.8 0.0 copy-done.6
  92.8 17.1 %attend.2 = (bf16[32,16,3072]{2,1,0:T(8,128)(2,1)}, bf16[128,1536]{1,0:T(8,128)(2,1)S(1)}, f32[128,1536]{1,0:T(8,128)}, f32[128,1536]{1,0:T(8,128)}, f32[128,1536]{1,0:T(8,128)}, /*index=5*/f32[128,1536]{1,0:T(8,128)}) custom-call(s32[4]{0:T(128)S(1)} %pad_add_fusion.meta_ref, s32[1,128]{1,0:T(1,128)S(1)} %bitcast.18, ...), custom_call_target="tpu_custom_call" | custom-call | flops 6039797760 | bytes 18874368 | tf_op jit(solution)/shard_map/attend/pallas_call | solution.py:245
  109.9 2.1 %collective-permute-start.8 = (bf16[128,1536]{1,0:T(8,128)(2,1)S(1)}, bf16[128,1536]{1,0:T(8,128)(2,1)S(1)}, u32[]{:S(2)}, u32[]{:S(2)}) collective-permute-start(bf16[128,1536]{1,0:T(8,128)(2,1)S(1)} %get-tuple-element.42), channel_id=1, source_target_pairs={{0,7},{1,0},{2,1},{3,2},{4,3},{5,4},{6,5},{7,6},{8,15},{9,8},{10,9... | collective-permute-start | bytes 1179656 | tf_op jit(solution)/shard_map/ppermute | solution.py:383
  112.0 0.0 all-to-all-done.2.qd_ref
  112.0 8.5 %all-to-all-start.3 = ((bf16[32,16,3072]{2,1,0:T(8,128)(2,1)}), bf16[32,16,3072]{2,1,0:T(8,128)(2,1)}, u32[]{:S(2)}, u32[]{:S(2)}) async-start(bf16[32,16,3072]{2,1,0:T(8,128)(2,1)} %get-tuple-element.54), calls=%async_computation.3 | async-start | bytes 6291456 | tf_op jit(solution)/shard_map/all_to_all | solution.py:378
  120.5 0.0 collective-permute-done.8
  120.5 0.0 copy-done.9
  120.6 0.1 add_convert_fusion.2
  120.6 0.0 copy-start.8
  120.6 2.3 %collective-permute-start.9 = (bf16[128,1536]{1,0:T(8,128)(2,1)S(1)}, bf16[128,1536]{1,0:T(8,128)(2,1)S(1)}, u32[]{:S(2)}, u32[]{:S(2)}) collective-permute-start(bf16[128,1536]{1,0:T(8,128)(2,1)S(1)} %add_convert_fusion.2), channel_id=1, source_target_pairs={{0,7},{1,0},{2,1},{3,2},{4,3},{5,4},{6,5},{7,6},{8,15},{9,8},{10,9... | collective-permute-start | bytes 1179656 | tf_op jit(solution)/shard_map/ppermute | solution.py:383
  123.0 7.2 %attend.3 = (bf16[32,16,1536]{2,1,0:T(8,128)(2,1)}, bf16[128,512]{1,0:T(8,128)(2,1)S(1)}, f32[128,512]{1,0:T(8,128)S(1)}, f32[128,512]{1,0:T(8,128)S(1)}, f32[12...) custom-call(s32[4]{0:T(128)S(1)} %pad_add_fusion.meta_ref, s32[1,128]{1,0:T(1,128)S(1)} %bitcast.19, ...), custom_call_target="tpu_custom_call" | custom-call | flops 2013265920 | bytes 6291456 | tf_op jit(solution)/shard_map/attend/pallas_call | solution.py:245
  130.1 0.1 collective-permute-start.12
  130.2 0.4 collective-permute-done.9
  130.6 0.1 add_convert_fusion.1
  130.7 2.4 %collective-permute-start.10 = (bf16[128,1536]{1,0:T(8,128)(2,1)S(1)}, bf16[128,1536]{1,0:T(8,128)(2,1)S(1)}, u32[]{:S(2)}, u32[]{:S(2)}) collective-permute-start(bf16[128,1536]{1,0:T(8,128)(2,1)S(1)} %add_convert_fusion.1), channel_id=1, source_target_pairs={{0,7},{1,0},{2,1},{3,2},{4,3},{5,4},{6,5},{7,6},{8,15},{9,8},{10,9... | collective-permute-start | bytes 1179656 | tf_op jit(solution)/shard_map/ppermute | solution.py:383
  133.1 1.3 collective-permute-done.12
  134.4 2.6 %collective-permute-start.13 = (bf16[128,512]{1,0:T(8,128)(2,1)S(1)}, bf16[128,512]{1,0:T(8,128)(2,1)S(1)}, u32[]{:S(2)}, u32[]{:S(2)}) collective-permute-start(bf16[128,512]{1,0:T(8,128)(2,1)S(1)} %add_convert_fusion.5), channel_id=1, source_target_pairs={{0,7},{1,0},{2,1},{3,2},{4,3},{5,4},{6,5},{7,6},{8,15},{9,8},{10,9... | collective-permute-start | bytes 393224 | tf_op jit(solution)/shard_map/ppermute | solution.py:383
  137.0 7.2 %collective-permute-done.13 = bf16[128,512]{1,0:T(8,128)(2,1)S(1)} collective-permute-done((bf16[128,512]{1,0:T(8,128)(2,1)S(1)}, bf16[128,512]{1,0:T(8,128)(2,1)S(1)}, u32[]{:S(2)}, u32[]{:S(2)}) %collective-permute-start.13) | collective-permute-done | bytes 131104 | tf_op jit(solution)/shard_map/ppermute | solution.py:383
  144.2 2.0 %collective-permute-start.14 = (bf16[128,512]{1,0:T(8,128)(2,1)S(1)}, bf16[128,512]{1,0:T(8,128)(2,1)S(1)}, u32[]{:S(2)}, u32[]{:S(2)}) collective-permute-start(bf16[128,512]{1,0:T(8,128)(2,1)S(1)} %add_convert_fusion.4), channel_id=1, source_target_pairs={{0,7},{1,0},{2,1},{3,2},{4,3},{5,4},{6,5},{7,6},{8,15},{9,8},{10,9... | collective-permute-start | bytes 393224 | tf_op jit(solution)/shard_map/ppermute | solution.py:383
  146.3 0.0 collective-permute-done.10
  146.3 0.1 add_convert_fusion
  146.4 0.1 collective-permute-start.11
  146.5 2.1 %collective-permute-done.14 = bf16[128,512]{1,0:T(8,128)(2,1)S(1)} collective-permute-done((bf16[128,512]{1,0:T(8,128)(2,1)S(1)}, bf16[128,512]{1,0:T(8,128)(2,1)S(1)}, u32[]{:S(2)}, u32[]{:S(2)}) %collective-permute-start.14) | collective-permute-done | bytes 131104 | tf_op jit(solution)/shard_map/ppermute | solution.py:383
  148.6 3.5 %collective-permute-start.15 = (bf16[128,512]{1,0:T(8,128)(2,1)S(1)}, bf16[128,512]{1,0:T(8,128)(2,1)S(1)}, u32[]{:S(2)}, u32[]{:S(2)}) collective-permute-start(bf16[128,512]{1,0:T(8,128)(2,1)S(1)} %add_convert_fusion.3), channel_id=1, source_target_pairs={{0,7},{1,0},{2,1},{3,2},{4,3},{5,4},{6,5},{7,6},{8,15},{9,8},{10,9... | collective-permute-start | bytes 393224 | tf_op jit(solution)/shard_map/ppermute | solution.py:383
  152.0 6.8 %collective-permute-done.15.last_ref = bf16[128,512]{1,0:T(8,128)(2,1)S(1)} collective-permute-done((bf16[128,512]{1,0:T(8,128)(2,1)S(1)}, bf16[128,512]{1,0:T(8,128)(2,1)S(1)}, u32[]{:S(2)}, u32[]{:S(2)}) %collective-permute-start.15) | collective-permute-done | bytes 131104 | tf_op jit(solution)/shard_map/ppermute | solution.py:383
  158.8 0.0 collective-permute-done.11.first_ref
  158.8 1.3 return_kv.1
  160.2 0.0 all-to-all-done.3.in_ref
  160.2 10.4 %all-to-all-start.4 = ((bf16[32,16,1536]{2,1,0:T(8,128)(2,1)}), bf16[32,16,1536]{2,1,0:T(8,128)(2,1)S(1)}, u32[]{:S(2)}, u32[]{:S(2)}) async-start(bf16[32,16,1536]{2,1,0:T(8,128)(2,1)} %return_kv.1), calls=%async_computation.4 | async-start | bytes 3145728 | tf_op jit(solution)/shard_map/all_to_all | solution.py:378
  170.6 0.0 copy-start
  170.6 0.0 copy-start.4
  170.6 6.9 %finish.2 = (bf16[128,8192]{1,0:T(8,128)(2,1)}, bf16[128,8192]{1,0:T(8,128)(2,1)}) custom-call(s32[1,128]{1,0:T(1,128)S(1)} %bitcast.9, f32[1,128]{1,0:T(1,128)S(1)} %bitcast.13, bf16[128,8192]{1,0:T(8,128)(2,1)} %q_ref.7, bf16[32,16,3072]{2,1,0:T(8,128)(2,1)} %all-to-all-done.3.in_ref), custom_call_target="tpu_custom_call" | custom-call | flops 1610612736 | bytes 7864320 | tf_op jit(solution)/shard_map/finish/pallas_call | solution.py:363
  177.6 15.2 %all-to-all-done.4.in_ref = bf16[32,16,1536]{2,1,0:T(8,128)(2,1)S(1)} async-done(((bf16[32,16,1536]{2,1,0:T(8,128)(2,1)}), bf16[32,16,1536]{2,1,0:T(8,128)(2,1)S(1)}, u32[]{:S(2)}, u32[]{:S(2)}) %all-to-all-start.4) | async-done | bytes 1572896 | tf_op jit(solution)/shard_map/all_to_all | solution.py:378
  192.8 4.7 %finish.3 = (bf16[128,8192]{1,0:T(8,128)(2,1)}, bf16[128,8192]{1,0:T(8,128)(2,1)}, bf16[128,1024]{1,0:T(8,128)(2,1)}, bf16[128,1024]{1,0:T(8,128)(2,1)}) custom-call(s32[1,128]{1,0:T(1,128)S(1)} %bitcast.10, f32[1,128]{1,0:T(1,128)S(1)} %bitcast.14, bf16[128,8192]{1,0:T(8,128)(2,1)} %q_ref.7, ...), custom_call_target="tpu_custom_call", output_to_operand_aliasing={{0}: (6, {}), {1}: (7, {})} | custom-call | flops 536870912 | bytes 2621440 | tf_op jit(solution)/shard_map/finish/pallas_call | solution.py:363
  (16 shorter events, 0.1 us)
Async XLA Ops:
  3.1 20.1 %all-to-all-start = ((bf16[32,16,512]{2,1,0:T(8,128)(2,1)}), bf16[32,16,512]{2,1,0:T(8,128)(2,1)S(1)}, u32[]{:S(2)}, u32[]{:S(2)}) async-start(bf16[32,16,512]{2,1,0:T(8,128)(2,1)} %send_kv.1), calls=%async_computation | async-start | bytes 1048576 | tf_op jit(solution)/shard_map/all_to_all | solution.py:378
  22.4 7.5 %copy-start.5 = (s32[1,1,128]{2,1,0:T(1,128)S(1)}, s32[1,1,128]{2,1,0:T(1,128)}, u32[]{:S(2)}) copy-start(s32[1,1,128]{2,1,0:T(1,128)} %param.17) | copy-start | bytes 1540
  23.3 51.7 %all-to-all-start.1 = ((bf16[32,16,3072]{2,1,0:T(8,128)(2,1)}), bf16[32,16,3072]{2,1,0:T(8,128)(2,1)}, u32[]{:S(2)}, u32[]{:S(2)}) async-start(bf16[32,16,3072]{2,1,0:T(8,128)(2,1)} %send_rows.2), calls=%async_computation.1 | async-start | bytes 6291456 | tf_op jit(solution)/shard_map/all_to_all | solution.py:378
  29.8 57.3 %copy-start.10 = (s32[1,3]{1,0:T(1,128)S(1)}, s32[1,3]{1,0:T(1,128)}, u32[]{:S(2)}) copy-start(s32[1,3]{1,0:T(1,128)} %param.15) | copy-start | bytes 40
  30.4 62.4 %copy-start.6 = (bf16[128,1536]{1,0:T(8,128)(2,1)}, bf16[128,1536]{1,0:T(8,128)(2,1)S(1)}, u32[]{:S(2)}) copy-start(bf16[128,1536]{1,0:T(8,128)(2,1)S(1)} %get-tuple-element.35.refs_4_) | copy-start | bytes 1179652
  30.4 15.0 %collective-permute-start = (bf16[128,1536]{1,0:T(8,128)(2,1)S(1)}, bf16[128,1536]{1,0:T(8,128)(2,1)S(1)}, u32[]{:S(2)}, u32[]{:S(2)}) collective-permute-start(bf16[128,1536]{1,0:T(8,128)(2,1)S(1)} %get-tuple-element.35.refs_4_), channel_id=1, source_target_pairs={{0,1},{1,2},{2,3},{3,4},{4,5},{5,6},{6,7},{7,0},{8,9},{9,10},{10,1... | collective-permute-start | bytes 1179656 | tf_op jit(solution)/shard_map/ppermute | solution.py:383
  45.4 11.3 %collective-permute-start.1 = (bf16[128,1536]{1,0:T(8,128)(2,1)S(1)}, bf16[128,1536]{1,0:T(8,128)(2,1)S(1)}, u32[]{:S(2)}, u32[]{:S(2)}) collective-permute-start(bf16[128,1536]{1,0:T(8,128)(2,1)S(1)} %collective-permute-done.refs_3_), channel_id=1, source_target_pairs={{0,1},{1,2},{2,3},{3,4},{4,5},{5,6},{6,7},{7,0},{8,9},{9,10},{10,1... | collective-permute-start | bytes 1179656 | tf_op jit(solution)/shard_map/ppermute | solution.py:383
  56.7 13.3 %collective-permute-start.2 = (bf16[128,1536]{1,0:T(8,128)(2,1)S(1)}, bf16[128,1536]{1,0:T(8,128)(2,1)S(1)}, u32[]{:S(2)}, u32[]{:S(2)}) collective-permute-start(bf16[128,1536]{1,0:T(8,128)(2,1)S(1)} %collective-permute-done.1.refs_2_), channel_id=1, source_target_pairs={{0,1},{1,2},{2,3},{3,4},{4,5},{5,6},{6,7},{7,0},{8,9},{9,10},{10,1... | collective-permute-start | bytes 1179656 | tf_op jit(solution)/shard_map/ppermute | solution.py:383
  56.7 13.3 %collective-permute-start.4 = (bf16[128,512]{1,0:T(8,128)(2,1)S(1)}, bf16[128,512]{1,0:T(8,128)(2,1)S(1)}, u32[]{:S(2)}, u32[]{:S(2)}) collective-permute-start(bf16[128,512]{1,0:T(8,128)(2,1)S(1)} %get-tuple-element.37.refs_4_), channel_id=1, source_target_pairs={{0,1},{1,2},{2,3},{3,4},{4,5},{5,6},{6,7},{7,0},{8,9},{9,10},{10,1... | collective-permute-start | bytes 393224 | tf_op jit(solution)/shard_map/ppermute | solution.py:383
  70.0 5.0 %collective-permute-start.5 = (bf16[128,512]{1,0:T(8,128)(2,1)S(1)}, bf16[128,512]{1,0:T(8,128)(2,1)S(1)}, u32[]{:S(2)}, u32[]{:S(2)}) collective-permute-start(bf16[128,512]{1,0:T(8,128)(2,1)S(1)} %collective-permute-done.4.refs_3_), channel_id=1, source_target_pairs={{0,1},{1,2},{2,3},{3,4},{4,5},{5,6},{6,7},{7,0},{8,9},{9,10},{10,1... | collective-permute-start | bytes 393224 | tf_op jit(solution)/shard_map/ppermute | solution.py:383
  70.0 22.8 %collective-permute-start.3 = (bf16[128,1536]{1,0:T(8,128)(2,1)S(1)}, bf16[128,1536]{1,0:T(8,128)(2,1)S(1)}, u32[]{:S(2)}, u32[]{:S(2)}) collective-permute-start(bf16[128,1536]{1,0:T(8,128)(2,1)S(1)} %collective-permute-done.2.refs_1_), channel_id=1, source_target_pairs={{0,1},{1,2},{2,3},{3,4},{4,5},{5,6},{6,7},{7,0},{8,9},{9,10},{10,1... | collective-permute-start | bytes 1179656 | tf_op jit(solution)/shard_map/ppermute | solution.py:383
  75.0 11.8 %collective-permute-start.6 = (bf16[128,512]{1,0:T(8,128)(2,1)S(1)}, bf16[128,512]{1,0:T(8,128)(2,1)S(1)}, u32[]{:S(2)}, u32[]{:S(2)}) collective-permute-start(bf16[128,512]{1,0:T(8,128)(2,1)S(1)} %collective-permute-done.5.refs_2_), channel_id=1, source_target_pairs={{0,1},{1,2},{2,3},{3,4},{4,5},{5,6},{6,7},{7,0},{8,9},{9,10},{10,1... | collective-permute-start | bytes 393224 | tf_op jit(solution)/shard_map/ppermute | solution.py:383
  75.0 37.0 %all-to-all-start.2 = ((bf16[32,16,1024]{2,1,0:T(8,128)(2,1)}), bf16[32,16,1024]{2,1,0:T(8,128)(2,1)}, u32[]{:S(2)}, u32[]{:S(2)}) async-start(bf16[32,16,1024]{2,1,0:T(8,128)(2,1)} %send_rows.3), calls=%async_computation.2 | async-start | bytes 2097152 | tf_op jit(solution)/shard_map/all_to_all | solution.py:378
  86.8 6.0 %collective-permute-start.7 = (bf16[128,512]{1,0:T(8,128)(2,1)S(1)}, bf16[128,512]{1,0:T(8,128)(2,1)S(1)}, u32[]{:S(2)}, u32[]{:S(2)}) collective-permute-start(bf16[128,512]{1,0:T(8,128)(2,1)S(1)} %collective-permute-done.6.refs_1_), channel_id=1, source_target_pairs={{0,1},{1,2},{2,3},{3,4},{4,5},{5,6},{6,7},{7,0},{8,9},{9,10},{10,1... | collective-permute-start | bytes 393224 | tf_op jit(solution)/shard_map/ppermute | solution.py:383
  109.9 10.7 %collective-permute-start.8 = (bf16[128,1536]{1,0:T(8,128)(2,1)S(1)}, bf16[128,1536]{1,0:T(8,128)(2,1)S(1)}, u32[]{:S(2)}, u32[]{:S(2)}) collective-permute-start(bf16[128,1536]{1,0:T(8,128)(2,1)S(1)} %get-tuple-element.42), channel_id=1, source_target_pairs={{0,7},{1,0},{2,1},{3,2},{4,3},{5,4},{6,5},{7,6},{8,15},{9,8},{10,9... | collective-permute-start | bytes 1179656 | tf_op jit(solution)/shard_map/ppermute | solution.py:383
  112.0 8.5 %copy-start.9 = (f32[128,1536]{1,0:T(8,128)S(1)}, f32[128,1536]{1,0:T(8,128)}, u32[]{:S(2)}) copy-start(f32[128,1536]{1,0:T(8,128)} %get-tuple-element.43) | copy-start | bytes 2359300
  112.0 48.2 %all-to-all-start.3 = ((bf16[32,16,3072]{2,1,0:T(8,128)(2,1)}), bf16[32,16,3072]{2,1,0:T(8,128)(2,1)}, u32[]{:S(2)}, u32[]{:S(2)}) async-start(bf16[32,16,3072]{2,1,0:T(8,128)(2,1)} %get-tuple-element.54), calls=%async_computation.3 | async-start | bytes 6291456 | tf_op jit(solution)/shard_map/all_to_all | solution.py:378
  120.6 10.0 %copy-start.8 = (f32[128,1536]{1,0:T(8,128)S(1)}, f32[128,1536]{1,0:T(8,128)}, u32[]{:S(2)}) copy-start(f32[128,1536]{1,0:T(8,128)} %get-tuple-element.44) | copy-start | bytes 2359300
  120.6 10.0 %collective-permute-start.9 = (bf16[128,1536]{1,0:T(8,128)(2,1)S(1)}, bf16[128,1536]{1,0:T(8,128)(2,1)S(1)}, u32[]{:S(2)}, u32[]{:S(2)}) collective-permute-start(bf16[128,1536]{1,0:T(8,128)(2,1)S(1)} %add_convert_fusion.2), channel_id=1, source_target_pairs={{0,7},{1,0},{2,1},{3,2},{4,3},{5,4},{6,5},{7,6},{8,15},{9,8},{10,9... | collective-permute-start | bytes 1179656 | tf_op jit(solution)/shard_map/ppermute | solution.py:383
  130.1 16.2 %copy-start.7 = (f32[128,1536]{1,0:T(8,128)S(1)}, f32[128,1536]{1,0:T(8,128)}, u32[]{:S(2)}) copy-start(f32[128,1536]{1,0:T(8,128)} %get-tuple-element.45) | copy-start | bytes 2359300
  130.1 4.2 %collective-permute-start.12 = (bf16[128,512]{1,0:T(8,128)(2,1)S(1)}, bf16[128,512]{1,0:T(8,128)(2,1)S(1)}, u32[]{:S(2)}, u32[]{:S(2)}) collective-permute-start(bf16[128,512]{1,0:T(8,128)(2,1)S(1)} %get-tuple-element.47), channel_id=1, source_target_pairs={{0,7},{1,0},{2,1},{3,2},{4,3},{5,4},{6,5},{7,6},{8,15},{9,8},{10,9... | collective-permute-start | bytes 393224 | tf_op jit(solution)/shard_map/ppermute | solution.py:383
  130.6 28.2 %copy-start.1 = (f32[128,1536]{1,0:T(8,128)S(1)}, f32[128,1536]{1,0:T(8,128)}, u32[]{:S(2)}) copy-start(f32[128,1536]{1,0:T(8,128)} %get-tuple-element.51.own_first_ref) | copy-start | bytes 2359300
  130.7 15.6 %collective-permute-start.10 = (bf16[128,1536]{1,0:T(8,128)(2,1)S(1)}, bf16[128,1536]{1,0:T(8,128)(2,1)S(1)}, u32[]{:S(2)}, u32[]{:S(2)}) collective-permute-start(bf16[128,1536]{1,0:T(8,128)(2,1)S(1)} %add_convert_fusion.1), channel_id=1, source_target_pairs={{0,7},{1,0},{2,1},{3,2},{4,3},{5,4},{6,5},{7,6},{8,15},{9,8},{10,9... | collective-permute-start | bytes 1179656 | tf_op jit(solution)/shard_map/ppermute | solution.py:383
  134.4 9.8 %collective-permute-start.13 = (bf16[128,512]{1,0:T(8,128)(2,1)S(1)}, bf16[128,512]{1,0:T(8,128)(2,1)S(1)}, u32[]{:S(2)}, u32[]{:S(2)}) collective-permute-start(bf16[128,512]{1,0:T(8,128)(2,1)S(1)} %add_convert_fusion.5), channel_id=1, source_target_pairs={{0,7},{1,0},{2,1},{3,2},{4,3},{5,4},{6,5},{7,6},{8,15},{9,8},{10,9... | collective-permute-start | bytes 393224 | tf_op jit(solution)/shard_map/ppermute | solution.py:383
  144.2 4.3 %collective-permute-start.14 = (bf16[128,512]{1,0:T(8,128)(2,1)S(1)}, bf16[128,512]{1,0:T(8,128)(2,1)S(1)}, u32[]{:S(2)}, u32[]{:S(2)}) collective-permute-start(bf16[128,512]{1,0:T(8,128)(2,1)S(1)} %add_convert_fusion.4), channel_id=1, source_target_pairs={{0,7},{1,0},{2,1},{3,2},{4,3},{5,4},{6,5},{7,6},{8,15},{9,8},{10,9... | collective-permute-start | bytes 393224 | tf_op jit(solution)/shard_map/ppermute | solution.py:383
  146.4 12.5 %collective-permute-start.11 = (bf16[128,1536]{1,0:T(8,128)(2,1)S(1)}, bf16[128,1536]{1,0:T(8,128)(2,1)S(1)}, u32[]{:S(2)}, u32[]{:S(2)}) collective-permute-start(bf16[128,1536]{1,0:T(8,128)(2,1)S(1)} %add_convert_fusion), channel_id=1, source_target_pairs={{0,7},{1,0},{2,1},{3,2},{4,3},{5,4},{6,5},{7,6},{8,15},{9,8},{10,9... | collective-permute-start | bytes 1179656 | tf_op jit(solution)/shard_map/ppermute | solution.py:383
  148.6 10.3 %collective-permute-start.15 = (bf16[128,512]{1,0:T(8,128)(2,1)S(1)}, bf16[128,512]{1,0:T(8,128)(2,1)S(1)}, u32[]{:S(2)}, u32[]{:S(2)}) collective-permute-start(bf16[128,512]{1,0:T(8,128)(2,1)S(1)} %add_convert_fusion.3), channel_id=1, source_target_pairs={{0,7},{1,0},{2,1},{3,2},{4,3},{5,4},{6,5},{7,6},{8,15},{9,8},{10,9... | collective-permute-start | bytes 393224 | tf_op jit(solution)/shard_map/ppermute | solution.py:383
  160.2 10.4 %copy-start.2 = (s32[1,1,128]{2,1,0:T(1,128)S(1)}, s32[1,1,128]{2,1,0:T(1,128)}, u32[]{:S(2)}) copy-start(s32[1,1,128]{2,1,0:T(1,128)} %param.16) | copy-start | bytes 1540
  160.2 10.4 %copy-start.3 = (f32[128]{0:T(128)S(1)}, f32[128]{0:T(128)}, u32[]{:S(2)}) copy-start(f32[128]{0:T(128)} %param.13) | copy-start | bytes 1540
  160.2 32.6 %all-to-all-start.4 = ((bf16[32,16,1536]{2,1,0:T(8,128)(2,1)}), bf16[32,16,1536]{2,1,0:T(8,128)(2,1)S(1)}, u32[]{:S(2)}, u32[]{:S(2)}) async-start(bf16[32,16,1536]{2,1,0:T(8,128)(2,1)} %return_kv.1), calls=%async_computation.4 | async-start | bytes 3145728 | tf_op jit(solution)/shard_map/all_to_all | solution.py:378
  170.6 22.2 %copy-start = (bf16[128,1024]{1,0:T(8,128)(2,1)S(1)}, bf16[128,1024]{1,0:T(8,128)(2,1)}, u32[]{:S(2)}) copy-start(bf16[128,1024]{1,0:T(8,128)(2,1)} %refs_1_.1) | copy-start | bytes 786436
  170.6 22.2 %copy-start.4 = (f32[128]{0:T(128)S(1)}, f32[128]{0:T(128)}, u32[]{:S(2)}) copy-start(f32[128]{0:T(128)} %param.14) | copy-start | bytes 1540

commit v3 on v2

--- a/solution.py
+++ b/solution.py
@@ -24,6 +24,7 @@
 SCALE = HEAD ** (-0.5)
 LOG2E = 1.4426950408889634
 FIRST = 6
+BATCHES = (3, 3, 2)
 VMEM_LIMIT = 52 * 1024 * 1024
 VMEM_WHOLE = 62 * 1024 * 1024
 F32 = jnp.float32
@@ -159,11 +160,11 @@
     )(order, gain, query, d_out)
 
 
-def sort_kv_kernel(order_ref, in_ref, first_ref, last_ref):
+def sort_kv_kernel(order_ref, in_ref, *out_refs):
     half = KV_HEADS * HEAD // 2
     rows = dot(pack_matrix(order_ref), in_ref[...].reshape(TALL, half), TM).astype(BF16)
-    for h in range(KV_HEADS):
-        ref, at = (first_ref, h) if h < FIRST else (last_ref, h - FIRST)
+    places = [(ref, at) for ref, count in zip(out_refs, BATCHES) for at in range(count)]
+    for h, (ref, at) in enumerate(places):
         part, cols = h // (KV_HEADS // 2), head_cols(h % (KV_HEADS // 2))
         k = rows[part * ROWS : (part + 1) * ROWS, cols]
         v = rows[(part + 2) * ROWS : (part + 3) * ROWS, cols]
@@ -173,10 +174,7 @@
 def sort_kv(order, received):
     return pl.pallas_call(
         sort_kv_kernel,
-        out_shape=[
-            jax.ShapeDtypeStruct((ROWS, count * WIDE), BF16)
-            for count in (FIRST, KV_HEADS - FIRST)
-        ],
+        out_shape=[jax.ShapeDtypeStruct((ROWS, count * WIDE), BF16) for count in BATCHES],
         compiler_params=params(),
         cost_estimate=cost(2 * TALL**3, 1 << 20),
         name="sort_kv",
@@ -185,9 +183,7 @@
 
 def attend_kernel(meta_ref, order_ref, qd_ref, *refs):
     kv_refs = refs[: BACK + 1]
-    out_ref = refs[BACK + 1]
-    part_refs = refs[BACK + 2 : 2 * BACK + 3]
-    bias_ref = refs[2 * BACK + 3]
+    out_ref, *part_refs, bias_ref = refs[-(BACK + 3) :]
 
     @pl.when(pl.program_id(0) == 0)
     def _():
@@ -239,38 +235,43 @@
         ref[:, HEAD:] = dv[n * ROWS : (n + 1) * ROWS].astype(ref.dtype)
 
 
-def attend(meta, order, received, blocks, count, room=0):
+def attend(meta, order, received, blocks, first, count, result, weight):
     kv_spec = pl.BlockSpec((ROWS, WIDE), lambda h: (0, h))
+    rows_spec = pl.BlockSpec((GROUPS, CHUNK, 2 * WIDE), lambda h: (0, 0, h + first))
     elements = count * RATIO * ROWS * WINDOW
+    fresh = isinstance(result, int)
+    shape = (GROUPS, CHUNK, result * 2 * WIDE) if fresh else result.shape
     return pl.pallas_call(
         attend_kernel,
         grid=(count,),
         in_specs=[
             pl.BlockSpec(memory_space=pltpu.SMEM),
             pl.BlockSpec((1, ROWS), lambda h: (0, 0)),
-            pl.BlockSpec((GROUPS, CHUNK, 2 * WIDE), lambda h: (0, 0, h)),
+            rows_spec,
         ]
-        + [kv_spec] * (BACK + 1),
-        out_specs=[pl.BlockSpec((GROUPS, CHUNK, 2 * WIDE), lambda h: (0, 0, h))]
-        + [kv_spec] * (BACK + 1),
-        out_shape=[jax.ShapeDtypeStruct((GROUPS, CHUNK, (count + room) * 2 * WIDE), BF16)]
+        + [kv_spec] * (BACK + 1)
+        + ([] if fresh else [pl.BlockSpec(memory_space=pl.ANY)]),
+        out_specs=[rows_spec] + [kv_spec] * (BACK + 1),
+        out_shape=[jax.ShapeDtypeStruct(shape, BF16)]
         + [
             jax.ShapeDtypeStruct((ROWS, count * WIDE), BF16 if n == 0 else F32)
             for n in range(BACK + 1)
         ],
         scratch_shapes=[pltpu.VMEM((WINDOW, TALL), F32)],
+        input_output_aliases={} if fresh else {BACK + 4: 0},
         compiler_params=params(),
-        cost_estimate=cost(12 * elements * HEAD, count * (3 << 20), elements),
+        cost_estimate=cost(weight * elements * HEAD, count * (3 << 20), elements),
         name="attend",
-    )(meta, order, received, *blocks)
-
-
-def return_kv_kernel(order_ref, first_ref, last_ref, own_first_ref, own_last_ref, _, out_ref):
-    half = KV_HEADS * HEAD // 2
+    )(meta, order, received, *blocks, *(() if fresh else (result,)))
+
+
+def return_kv_kernel(order_ref, *refs):
+    half = KV_HEADS * HEAD // 2
+    count, out_ref = len(BATCHES), refs[-1]
     total = jnp.concatenate(
         [
             (got[...].astype(F32) + own[...]).astype(BF16)
-            for got, own in ((first_ref, own_first_ref), (last_ref, own_last_ref))
+            for got, own in zip(refs[:count], refs[count : 2 * count])
         ],
         axis=1,
     )
@@ -286,22 +287,21 @@
     out_ref[...] = rows.reshape(GROUPS, CHUNK, half)
 
 
-def return_kv(order, first, last, own_first, own_last, result):
+def return_kv(order, got, own, result):
     half = KV_HEADS * HEAD // 2
     place = result.shape[2] // half - 1
-    small = [pl.BlockSpec(a.shape, lambda i: (0, 0)) for a in (first, last, own_first, own_last)]
+    small = [pl.BlockSpec(a.shape, lambda i: (0, 0)) for a in (order, *got, *own)]
     return pl.pallas_call(
         return_kv_kernel,
         grid=(1,),
-        in_specs=[pl.BlockSpec((1, ROWS), lambda i: (0, 0)), *small]
-        + [pl.BlockSpec(memory_space=pl.ANY)],
+        in_specs=small + [pl.BlockSpec(memory_space=pl.ANY)],
         out_specs=pl.BlockSpec((GROUPS, CHUNK, half), lambda i: (0, 0, place)),
         out_shape=jax.ShapeDtypeStruct(result.shape, BF16),
-        input_output_aliases={5: 0},
+        input_output_aliases={len(small): 0},
         compiler_params=params(),
         cost_estimate=cost(2 * TALL**3, 3 << 20),
         name="return_kv",
-    )(order, first, last, own_first, own_last, result)
+    )(order, *got, *own, result)
 
 
 def finish_rows_step(rows, gain, q_ref, out_ref, dq_ref):
@@ -384,7 +384,7 @@
 
 
 def after(array, other):
-    return lax.optimization_barrier((array, other))[0]
+    return array if other is None else lax.optimization_barrier((array, other))[0]
 
 
 def per_device(
@@ -407,29 +407,36 @@
     ]
     kv_received, *sent = lax.optimization_barrier((kv_received, *sent))
     received_first = exchange(sent[0])
-    received_first, last = lax.optimization_barrier((received_first, sent[1]))
-    received = [received_first, exchange(last)]
-
-    firsts, lasts = ([block] for block in sort_kv(arriving, kv_received))
-    for _ in range(BACK):
-        block = after(lasts[-1], firsts[-1])
-        firsts.append(along(firsts[-1], 1))
-        lasts.append(along(block, 1))
-    firsts[-1] = after(firsts[-1], lasts[-1])
-    chains = [firsts[::-1], lasts[::-1]]
-
-    results, totals, own = [], [], []
-    for n in range(2):
-        result, *parts = attend(meta, arriving, received[n], chains[n], counts[n], room=n)
+
+    first, second, third = ([block] for block in sort_kv(arriving, kv_received))
+    for n in range(BACK):
+        first.append(along(after(first[-1], second[n - 1] if n > 1 else None), 1))
+        second.append(along(second[-1], 1))
+    received_last = exchange(after(after(sent[1], received_first), first[BACK]))
+    for n in range(BACK):
+        block = after(third[-1], (first[BACK], None, received_last, None)[n])
+        third.append(along(block, 1))
+    second[-1] = after(second[-1], third[1])
+
+    def back_along(parts):
         total = parts[0]
         for part in parts[1:-1]:
             total = (along(total, -1).astype(F32) + part).astype(BF16)
-        totals.append(along(total, -1))
-        own.append(parts[-1])
-        results.append(result)
-
-    back_first = exchange(results[0])
-    merged = return_kv(arriving, *totals, *own, results[1])
+        return along(total, -1), parts[-1]
+
+    def attend_batch(rows, blocks, first, count, result, weight):
+        result, *parts = attend(
+            meta, arriving, rows, blocks[::-1], first, count, result, weight
+        )
+        return result, *back_along(parts)
+
+    result, got0, own0 = attend_batch(received_first, first, 0, BATCHES[0], FIRST, 4)
+    result, got1, own1 = attend_batch(
+        received_first, second, BATCHES[0], BATCHES[1], result, 36
+    )
+    back_first = exchange(result)
+    result, got2, own2 = attend_batch(received_last, third, 0, BATCHES[2], BATCHES[2] + 1, 36)
+    merged = return_kv(arriving, (got0, got1, got2), (own0, own1, own2), result)
     back_last = exchange(after(merged, back_first))
 
     outs = finish(leaving, q_gain, query, back_first, starts[0], counts[0])

time: 198 us -> 197 us (level)
  waiting for transfers between devices: 82.3 us -> 76.4 us
  starting transfers between devices: 63 us -> 65.4 us
  Pallas kernels: 50.9 us -> 53.2 us
    ppermute x16 -> x24, waiting for transfers between devices: 66.2 us -> 56.2 us  [along(): lax.ppermute(array, 'seq', [(i, (i + step) % count) for i in range(count)])]
    ppermute x16 -> x24, starting transfers between devices: 17.1 us -> 24.7 us  [along(): lax.ppermute(array, 'seq', [(i, (i + step) % count) for i in range(count)])]
    all_to_all x5, starting transfers between devices: 45.9 us -> 40.7 us  [exchange(): return lax.all_to_all(array, 'dp', split_axis=0, concat_axis=0, tiled=True)]
    all_to_all x5, waiting for transfers between devices: 16.1 us -> 20.2 us  [exchange(): return lax.all_to_all(array, 'dp', split_axis=0, concat_axis=0, tiled=True)]
    pallas_call x2 -> x3, Pallas kernels: 24.3 us -> 26.6 us  [attend(): pl.pallas_call(attend_kernel, grid=(count,), in_specs=[pl.BlockSpec(memor...]
  transfers between devices with their start and end apart: 21 -> 29, of which waited for: 12 -> 19; matrix products, arithmetic and copies ran while one was open for 0% -> 0% of each run, Pallas kernels for 22% -> 23%
where the time goes in v3:
time: 197 us; the launch traced here: 196 us
  waiting for transfers between devices  76.4 us (39%)
  starting transfers between devices  65.4 us (33%)
  Pallas kernels  53.2 us (27%)
    ppermute x24, waiting for transfers between devices, along(): lax.ppermute(array, 'seq', [(i, (i + step) % count) for i in range(count)])  56.2 us
    all_to_all x5, starting transfers between devices, exchange(): return lax.all_to_all(array, 'dp', split_axis=0, concat_axis=0, tiled=True)  40.7 us
    pallas_call x3, Pallas kernels, attend(): pl.pallas_call(attend_kernel, grid=(count,), in_specs=[pl.BlockSpec(memor...  26.6 us
    ppermute x24, starting transfers between devices, along(): lax.ppermute(array, 'seq', [(i, (i + step) % count) for i in range(count)])  24.7 us
    all_to_all x5, waiting for transfers between devices, exchange(): return lax.all_to_all(array, 'dp', split_axis=0, concat_axis=0, tiled=True)  20.2 us
    pallas_call x2, Pallas kernels, finish(): pl.pallas_call(functools.partial(finish_kernel, bool(kv)), grid=(count +...  11.7 us
    pallas_call x2, Pallas kernels, send_rows(): pl.pallas_call(send_rows_kernel, grid=(count,), in_specs=[pl.BlockSpec((1...  10.6 us
  transfers between devices with their start and end apart: 29, of which 19 were waited for; matrix products, arithmetic and copies ran while one was open for 0% of the time, Pallas kernels for 23%

profile of v3, /device:TPU:1, one launch (start us, length us, event | category | flops | bytes accessed | tf_op | source)
XLA Modules:
  0.0 196.3 jit_solution(17488235694596941196)
XLA Ops:
  0.6 2.5 %send_kv.1 = bf16[32,16,512]{2,1,0:T(8,128)(2,1)} custom-call(s32[1,128]{1,0:T(1,128)} %bitcast.6, f32[1,128]{1,0:T(1,128)} %bitcast.15, bf16[128,1024]{1,0:T(8,128)(2,1)} %refs_1_.1, bf16[128,1024]{1,0:T(8,128)(2,1)} %v_ref.1), custom_call_target="tpu_custom_call" | custom-call | flops 268435456 | bytes 1572864 | tf_op jit(solution)/shard_map/send_kv/pallas_call | solution.py:115
  3.1 8.6 %all-to-all-start = ((bf16[32,16,512]{2,1,0:T(8,128)(2,1)}), bf16[32,16,512]{2,1,0:T(8,128)(2,1)S(1)}, u32[]{:S(2)}, u32[]{:S(2)}) async-start(bf16[32,16,512]{2,1,0:T(8,128)(2,1)} %send_kv.1), calls=%async_computation | async-start | bytes 1048576 | tf_op jit(solution)/shard_map/all_to_all | solution.py:378
  11.7 3.4 %send_rows.3 = bf16[32,16,1024]{2,1,0:T(8,128)(2,1)} custom-call(s32[1,128]{1,0:T(1,128)} %bitcast.7, f32[1,128]{1,0:T(1,128)} %bitcast.11, bf16[128,8192]{1,0:T(8,128)(2,1)} %q_ref.7, bf16[128,8192]{1,0:T(8,128)(2,1)} %d_ref.3), custom_call_target="tpu_custom_call" | custom-call | flops 536870912 | bytes 2097152 | tf_op jit(solution)/shard_map/send_rows/pallas_call | solution.py:145
  15.1 7.2 %send_rows.2 = bf16[32,16,3072]{2,1,0:T(8,128)(2,1)} custom-call(s32[1,128]{1,0:T(1,128)} %bitcast.8, f32[1,128]{1,0:T(1,128)} %bitcast.12, bf16[128,8192]{1,0:T(8,128)(2,1)} %q_ref.7, bf16[128,8192]{1,0:T(8,128)(2,1)} %d_ref.3), custom_call_target="tpu_custom_call" | custom-call | flops 1610612736 | bytes 6291456 | tf_op jit(solution)/shard_map/send_rows/pallas_call | solution.py:145
  22.3 1.0 all-to-all-done.in_ref
  23.3 6.5 %all-to-all-start.1 = ((bf16[32,16,3072]{2,1,0:T(8,128)(2,1)}), bf16[32,16,3072]{2,1,0:T(8,128)(2,1)}, u32[]{:S(2)}, u32[]{:S(2)}) async-start(bf16[32,16,3072]{2,1,0:T(8,128)(2,1)} %send_rows.2), calls=%async_computation.1 | async-start | bytes 6291456 | tf_op jit(solution)/shard_map/all_to_all | solution.py:378
  29.7 0.0 copy-start.9
  29.8 0.5 sort_kv.1
  30.3 1.7 collective-permute-start
  32.0 1.6 collective-permute-start.2
  33.6 7.5 %collective-permute-done.refs_3_ = bf16[128,768]{1,0:T(8,128)(2,1)S(1)} collective-permute-done((bf16[128,768]{1,0:T(8,128)(2,1)S(1)}, bf16[128,768]{1,0:T(8,128)(2,1)S(1)}, u32[]{:S(2)}, u32[]{:S(2)}) %collective-permute-start) | collective-permute-done | bytes 196640 | tf_op jit(solution)/shard_map/ppermute | solution.py:383
  41.1 0.0 collective-permute-start.1
  41.1 4.2 %collective-permute-done.2.refs_3_ = bf16[128,768]{1,0:T(8,128)(2,1)S(1)} collective-permute-done((bf16[128,768]{1,0:T(8,128)(2,1)S(1)}, bf16[128,768]{1,0:T(8,128)(2,1)S(1)}, u32[]{:S(2)}, u32[]{:S(2)}) %collective-permute-start.2) | collective-permute-done | bytes 196640 | tf_op jit(solution)/shard_map/ppermute | solution.py:383
  45.3 0.0 collective-permute-start.4
  45.3 3.6 %collective-permute-done.1.refs_2_ = bf16[128,768]{1,0:T(8,128)(2,1)S(1)} collective-permute-done((bf16[128,768]{1,0:T(8,128)(2,1)S(1)}, bf16[128,768]{1,0:T(8,128)(2,1)S(1)}, u32[]{:S(2)}, u32[]{:S(2)}) %collective-permute-start.1) | collective-permute-done | bytes 196640 | tf_op jit(solution)/shard_map/ppermute | solution.py:383
  48.9 0.0 collective-permute-start.3
  48.9 4.2 %collective-permute-done.4.refs_2_ = bf16[128,768]{1,0:T(8,128)(2,1)S(1)} collective-permute-done((bf16[128,768]{1,0:T(8,128)(2,1)S(1)}, bf16[128,768]{1,0:T(8,128)(2,1)S(1)}, u32[]{:S(2)}, u32[]{:S(2)}) %collective-permute-start.4) | collective-permute-done | bytes 196640 | tf_op jit(solution)/shard_map/ppermute | solution.py:383
  53.1 4.1 %collective-permute-done.3.refs_1_ = bf16[128,768]{1,0:T(8,128)(2,1)S(1)} collective-permute-done((bf16[128,768]{1,0:T(8,128)(2,1)S(1)}, bf16[128,768]{1,0:T(8,128)(2,1)S(1)}, u32[]{:S(2)}, u32[]{:S(2)}) %collective-permute-start.3) | collective-permute-done | bytes 196640 | tf_op jit(solution)/shard_map/ppermute | solution.py:383
  57.2 0.0 collective-permute-start.5
  57.2 3.7 %collective-permute-done.10.refs_1_ = bf16[128,768]{1,0:T(8,128)(2,1)S(1)} collective-permute-done((bf16[128,768]{1,0:T(8,128)(2,1)S(1)}, bf16[128,768]{1,0:T(8,128)(2,1)S(1)}, u32[]{:S(2)}, u32[]{:S(2)}) %collective-permute-start.10) | collective-permute-done | bytes 196640 | tf_op jit(solution)/shard_map/ppermute | solution.py:383
  60.9 0.0 collective-permute-start.11
  60.9 4.1 %collective-permute-done.5.refs_0_ = bf16[128,768]{1,0:T(8,128)(2,1)S(1)} collective-permute-done((bf16[128,768]{1,0:T(8,128)(2,1)S(1)}, bf16[128,768]{1,0:T(8,128)(2,1)S(1)}, u32[]{:S(2)}, u32[]{:S(2)}) %collective-permute-start.5) | collective-permute-done | bytes 196640 | tf_op jit(solution)/shard_map/ppermute | solution.py:383
  65.0 4.0 %all-to-all-done.1.qd_ref = bf16[32,16,3072]{2,1,0:T(8,128)(2,1)} async-done(((bf16[32,16,3072]{2,1,0:T(8,128)(2,1)}), bf16[32,16,3072]{2,1,0:T(8,128)(2,1)}, u32[]{:S(2)}, u32[]{:S(2)}) %all-to-all-start.1) | async-done | bytes 3145760 | tf_op jit(solution)/shard_map/all_to_all | solution.py:378
  69.0 7.1 %all-to-all-start.2 = ((bf16[32,16,1024]{2,1,0:T(8,128)(2,1)}), bf16[32,16,1024]{2,1,0:T(8,128)(2,1)}, u32[]{:S(2)}, u32[]{:S(2)}) async-start(bf16[32,16,1024]{2,1,0:T(8,128)(2,1)} %send_rows.3), calls=%async_computation.2 | async-start | bytes 2097152 | tf_op jit(solution)/shard_map/all_to_all | solution.py:378
  76.1 0.1 pad_add_fusion.meta_ref
  76.2 0.0 collective-permute-done.11.refs_0_
  76.2 0.0 collective-permute-done.12.refs_3_
  76.2 9.7 %attend.3 = (bf16[32,16,3072]{2,1,0:T(8,128)(2,1)}, bf16[128,768]{1,0:T(8,128)(2,1)S(1)}, f32[128,768]{1,0:T(8,128)S(1)}, f32[128,768]{1,0:T(8,128)S(1)}, f32[128,768]{1,0:T(8,128)}, /*index=5*/f32[128,768]{1,0:T(8,128)}) custom-call(s32[4]{0:T(128)S(1)} %pad_add_fusion.meta_ref, s32[1,128]{1,0:T(1,128)S(1)} %bitcast.18, ...), custom_call_target="tpu_custom_call" | custom-call | flops 1006632960 | bytes 9437184 | tf_op jit(solution)/shard_map/attend/pallas_call | solution.py:244
  85.9 5.6 %collective-permute-start.6 = (bf16[128,768]{1,0:T(8,128)(2,1)S(1)}, bf16[128,768]{1,0:T(8,128)(2,1)S(1)}, u32[]{:S(2)}, u32[]{:S(2)}) collective-permute-start(bf16[128,768]{1,0:T(8,128)(2,1)S(1)} %get-tuple-element.44), channel_id=1, source_target_pairs={{0,7},{1,0},{2,1},{3,2},{4,3},{5,4},{6,5},{7,6},{8,15},{9,8},{10,9... | collective-permute-start | bytes 589832 | tf_op jit(solution)/shard_map/ppermute | solution.py:383
  91.4 9.8 %attend.4 = (bf16[32,16,3072]{2,1,0:T(8,128)(2,1)}, bf16[128,768]{1,0:T(8,128)(2,1)S(1)}, f32[128,768]{1,0:T(8,128)S(1)}, f32[128,768]{1,0:T(8,128)S(1)}, f32[128,768]{1,0:T(8,128)}, /*index=5*/f32[128,768]{1,0:T(8,128)}) custom-call(s32[4]{0:T(128)S(1)} %pad_add_fusion.meta_ref, s32[1,128]{1,0:T(1,128)S(1)} %bitcast.19, ...), custom_call_target="tpu_custom_call", output_to_operand_aliasing={{0}: (8, {})} | custom-call | flops 9059696640 | bytes 9437184 | tf_op jit(solution)/shard_map/attend/pallas_call | solution.py:244
  101.2 7.8 %all-to-all-start.3 = ((bf16[32,16,3072]{2,1,0:T(8,128)(2,1)}), bf16[32,16,3072]{2,1,0:T(8,128)(2,1)}, u32[]{:S(2)}, u32[]{:S(2)}) async-start(bf16[32,16,3072]{2,1,0:T(8,128)(2,1)} %get-tuple-element.68), calls=%async_computation.3 | async-start | bytes 6291456 | tf_op jit(solution)/shard_map/all_to_all | solution.py:378
  109.0 0.1 collective-permute-start.17
  109.1 2.7 %collective-permute-start.13 = (bf16[128,768]{1,0:T(8,128)(2,1)S(1)}, bf16[128,768]{1,0:T(8,128)(2,1)S(1)}, u32[]{:S(2)}, u32[]{:S(2)}) collective-permute-start(bf16[128,768]{1,0:T(8,128)(2,1)S(1)} %get-tuple-element.52), channel_id=1, source_target_pairs={{0,7},{1,0},{2,1},{3,2},{4,3},{5,4},{6,5},{7,6},{8,15},{9,8},{10,9... | collective-permute-start | bytes 589832 | tf_op jit(solution)/shard_map/ppermute | solution.py:383
  111.8 0.1 collective-permute-start.7
  111.9 3.3 %collective-permute-done.17.refs_2_ = bf16[128,512]{1,0:T(8,128)(2,1)S(1)} collective-permute-done((bf16[128,512]{1,0:T(8,128)(2,1)S(1)}, bf16[128,512]{1,0:T(8,128)(2,1)S(1)}, u32[]{:S(2)}, u32[]{:S(2)}) %collective-permute-start.17) | collective-permute-done | bytes 131104 | tf_op jit(solution)/shard_map/ppermute | solution.py:383
  115.2 0.0 collective-permute-start.18
  115.2 0.3 collective-permute-done.13
  115.5 3.5 %collective-permute-start.14 = (bf16[128,768]{1,0:T(8,128)(2,1)S(1)}, bf16[128,768]{1,0:T(8,128)(2,1)S(1)}, u32[]{:S(2)}, u32[]{:S(2)}) collective-permute-start(bf16[128,768]{1,0:T(8,128)(2,1)S(1)} %add_convert_fusion.2), channel_id=1, source_target_pairs={{0,7},{1,0},{2,1},{3,2},{4,3},{5,4},{6,5},{7,6},{8,15},{9,8},{10,9... | collective-permute-start | bytes 589832 | tf_op jit(solution)/shard_map/ppermute | solution.py:383
  119.1 1.6 collective-permute-done.18.refs_1_
  120.7 0.0 copy-start.8
  120.7 3.0 %collective-permute-start.8 = (bf16[128,768]{1,0:T(8,128)(2,1)S(1)}, bf16[128,768]{1,0:T(8,128)(2,1)S(1)}, u32[]{:S(2)}, u32[]{:S(2)}) collective-permute-start(bf16[128,768]{1,0:T(8,128)(2,1)S(1)} %add_convert_fusion.4), channel_id=1, source_target_pairs={{0,7},{1,0},{2,1},{3,2},{4,3},{5,4},{6,5},{7,6},{8,15},{9,8},{10,9... | collective-permute-start | bytes 589832 | tf_op jit(solution)/shard_map/ppermute | solution.py:383
  123.7 2.4 %collective-permute-done.19.refs_0_ = bf16[128,512]{1,0:T(8,128)(2,1)S(1)} collective-permute-done((bf16[128,512]{1,0:T(8,128)(2,1)S(1)}, bf16[128,512]{1,0:T(8,128)(2,1)S(1)}, u32[]{:S(2)}, u32[]{:S(2)}) %collective-permute-start.19) | collective-permute-done | bytes 131104 | tf_op jit(solution)/shard_map/ppermute | solution.py:383
  126.1 7.2 %attend.5 = (bf16[32,16,1536]{2,1,0:T(8,128)(2,1)}, bf16[128,512]{1,0:T(8,128)(2,1)S(1)}, f32[128,512]{1,0:T(8,128)S(1)}, f32[128,512]{1,0:T(8,128)S(1)}, f32[12...) custom-call(s32[4]{0:T(128)S(1)} %pad_add_fusion.meta_ref, s32[1,128]{1,0:T(1,128)S(1)} %bitcast.20, ...), custom_call_target="tpu_custom_call" | custom-call | flops 6039797760 | bytes 6291456 | tf_op jit(solution)/shard_map/attend/pallas_call | solution.py:244
  133.3 0.1 collective-permute-start.20
  133.4 0.0 collective-permute-done.14
  133.4 0.1 collective-permute-start.15
  133.5 4.1 %collective-permute-done.20 = bf16[128,512]{1,0:T(8,128)(2,1)S(1)} collective-permute-done((bf16[128,512]{1,0:T(8,128)(2,1)S(1)}, bf16[128,512]{1,0:T(8,128)(2,1)S(1)}, u32[]{:S(2)}, u32[]{:S(2)}) %collective-permute-start.20) | collective-permute-done | bytes 131104 | tf_op jit(solution)/shard_map/ppermute | solution.py:383
  137.6 1.3 collective-permute-start.21
  138.9 0.0 collective-permute-done.8
  139.0 0.1 collective-permute-start.9
  139.1 4.3 %collective-permute-done.21 = bf16[128,512]{1,0:T(8,128)(2,1)S(1)} collective-permute-done((bf16[128,512]{1,0:T(8,128)(2,1)S(1)}, bf16[128,512]{1,0:T(8,128)(2,1)S(1)}, u32[]{:S(2)}, u32[]{:S(2)}) %collective-permute-start.21) | collective-permute-done | bytes 131104 | tf_op jit(solution)/shard_map/ppermute | solution.py:383
  143.4 2.4 %collective-permute-start.22 = (bf16[128,512]{1,0:T(8,128)(2,1)S(1)}, bf16[128,512]{1,0:T(8,128)(2,1)S(1)}, u32[]{:S(2)}, u32[]{:S(2)}) collective-permute-start(bf16[128,512]{1,0:T(8,128)(2,1)S(1)} %add_convert_fusion.7), channel_id=1, source_target_pairs={{0,7},{1,0},{2,1},{3,2},{4,3},{5,4},{6,5},{7,6},{8,15},{9,8},{10,9... | collective-permute-start | bytes 393224 | tf_op jit(solution)/shard_map/ppermute | solution.py:383
  145.9 0.1 collective-permute-start.16
  146.0 4.4 %collective-permute-done.22 = bf16[128,512]{1,0:T(8,128)(2,1)S(1)} collective-permute-done((bf16[128,512]{1,0:T(8,128)(2,1)S(1)}, bf16[128,512]{1,0:T(8,128)(2,1)S(1)}, u32[]{:S(2)}, u32[]{:S(2)}) %collective-permute-start.22) | collective-permute-done | bytes 131104 | tf_op jit(solution)/shard_map/ppermute | solution.py:383
  150.4 2.3 %collective-permute-start.23 = (bf16[128,512]{1,0:T(8,128)(2,1)S(1)}, bf16[128,512]{1,0:T(8,128)(2,1)S(1)}, u32[]{:S(2)}, u32[]{:S(2)}) collective-permute-start(bf16[128,512]{1,0:T(8,128)(2,1)S(1)} %add_convert_fusion.6), channel_id=1, source_target_pairs={{0,7},{1,0},{2,1},{3,2},{4,3},{5,4},{6,5},{7,6},{8,15},{9,8},{10,9... | collective-permute-start | bytes 393224 | tf_op jit(solution)/shard_map/ppermute | solution.py:383
  152.7 1.8 collective-permute-done.16.refs_1_
  154.5 2.8 %collective-permute-done.23.refs_2_ = bf16[128,512]{1,0:T(8,128)(2,1)S(1)} collective-permute-done((bf16[128,512]{1,0:T(8,128)(2,1)S(1)}, bf16[128,512]{1,0:T(8,128)(2,1)S(1)}, u32[]{:S(2)}, u32[]{:S(2)}) %collective-permute-start.23) | collective-permute-done | bytes 131104 | tf_op jit(solution)/shard_map/ppermute | solution.py:383
  157.3 1.3 return_kv.1
  158.6 10.7 %all-to-all-start.4 = ((bf16[32,16,1536]{2,1,0:T(8,128)(2,1)}), bf16[32,16,1536]{2,1,0:T(8,128)(2,1)S(1)}, u32[]{:S(2)}, u32[]{:S(2)}) async-start(bf16[32,16,1536]{2,1,0:T(8,128)(2,1)} %return_kv.1), calls=%async_computation.4 | async-start | bytes 3145728 | tf_op jit(solution)/shard_map/all_to_all | solution.py:378
  169.4 0.0 copy-start
  169.4 0.0 copy-start.5
  169.4 6.9 %finish.2 = (bf16[128,8192]{1,0:T(8,128)(2,1)}, bf16[128,8192]{1,0:T(8,128)(2,1)}) custom-call(s32[1,128]{1,0:T(1,128)S(1)} %bitcast.9, f32[1,128]{1,0:T(1,128)S(1)} %bitcast.13, bf16[128,8192]{1,0:T(8,128)(2,1)} %q_ref.7, bf16[32,16,3072]{2,1,0:T(8,128)(2,1)} %all-to-all-done.3.in_ref), custom_call_target="tpu_custom_call" | custom-call | flops 1610612736 | bytes 7864320 | tf_op jit(solution)/shard_map/finish/pallas_call | solution.py:363
  176.4 15.2 %all-to-all-done.4.in_ref = bf16[32,16,1536]{2,1,0:T(8,128)(2,1)S(1)} async-done(((bf16[32,16,1536]{2,1,0:T(8,128)(2,1)}), bf16[32,16,1536]{2,1,0:T(8,128)(2,1)S(1)}, u32[]{:S(2)}, u32[]{:S(2)}) %all-to-all-start.4) | async-done | bytes 1572896 | tf_op jit(solution)/shard_map/all_to_all | solution.py:378
  191.6 4.7 %finish.3 = (bf16[128,8192]{1,0:T(8,128)(2,1)}, bf16[128,8192]{1,0:T(8,128)(2,1)}, bf16[128,1024]{1,0:T(8,128)(2,1)}, bf16[128,1024]{1,0:T(8,128)(2,1)}) custom-call(s32[1,128]{1,0:T(1,128)S(1)} %bitcast.10, f32[1,128]{1,0:T(1,128)S(1)} %bitcast.14, bf16[128,8192]{1,0:T(8,128)(2,1)} %q_ref.7, ...), custom_call_target="tpu_custom_call", output_to_operand_aliasing={{0}: (6, {}), {1}: (7, {})} | custom-call | flops 536870912 | bytes 2621440 | tf_op jit(solution)/shard_map/finish/pallas_call | solution.py:363
  (34 shorter events, 0.4 us)
Async XLA Ops:
  3.1 20.1 %all-to-all-start = ((bf16[32,16,512]{2,1,0:T(8,128)(2,1)}), bf16[32,16,512]{2,1,0:T(8,128)(2,1)S(1)}, u32[]{:S(2)}, u32[]{:S(2)}) async-start(bf16[32,16,512]{2,1,0:T(8,128)(2,1)} %send_kv.1), calls=%async_computation | async-start | bytes 1048576 | tf_op jit(solution)/shard_map/all_to_all | solution.py:378
  22.3 7.5 %copy-start.6 = (s32[1,1,128]{2,1,0:T(1,128)S(1)}, s32[1,1,128]{2,1,0:T(1,128)}, u32[]{:S(2)}) copy-start(s32[1,1,128]{2,1,0:T(1,128)} %param.17) | copy-start | bytes 1540
  23.3 45.7 %all-to-all-start.1 = ((bf16[32,16,3072]{2,1,0:T(8,128)(2,1)}), bf16[32,16,3072]{2,1,0:T(8,128)(2,1)}, u32[]{:S(2)}, u32[]{:S(2)}) async-start(bf16[32,16,3072]{2,1,0:T(8,128)(2,1)} %send_rows.2), calls=%async_computation.1 | async-start | bytes 6291456 | tf_op jit(solution)/shard_map/all_to_all | solution.py:378
  29.7 46.3 %copy-start.9 = (s32[1,3]{1,0:T(1,128)S(1)}, s32[1,3]{1,0:T(1,128)}, u32[]{:S(2)}) copy-start(s32[1,3]{1,0:T(1,128)} %param.15) | copy-start | bytes 40
  30.3 10.8 %collective-permute-start = (bf16[128,768]{1,0:T(8,128)(2,1)S(1)}, bf16[128,768]{1,0:T(8,128)(2,1)S(1)}, u32[]{:S(2)}, u32[]{:S(2)}) collective-permute-start(bf16[128,768]{1,0:T(8,128)(2,1)S(1)} %get-tuple-element.40.refs_4_), channel_id=1, source_target_pairs={{0,1},{1,2},{2,3},{3,4},{4,5},{5,6},{6,7},{7,0},{8,9},{9,10},{10,1... | collective-permute-start | bytes 589832 | tf_op jit(solution)/shard_map/ppermute | solution.py:383
  32.0 13.3 %collective-permute-start.2 = (bf16[128,768]{1,0:T(8,128)(2,1)S(1)}, bf16[128,768]{1,0:T(8,128)(2,1)S(1)}, u32[]{:S(2)}, u32[]{:S(2)}) collective-permute-start(bf16[128,768]{1,0:T(8,128)(2,1)S(1)} %get-tuple-element.41.refs_4_), channel_id=1, source_target_pairs={{0,1},{1,2},{2,3},{3,4},{4,5},{5,6},{6,7},{7,0},{8,9},{9,10},{10,1... | collective-permute-start | bytes 589832 | tf_op jit(solution)/shard_map/ppermute | solution.py:383
  41.1 7.8 %collective-permute-start.1 = (bf16[128,768]{1,0:T(8,128)(2,1)S(1)}, bf16[128,768]{1,0:T(8,128)(2,1)S(1)}, u32[]{:S(2)}, u32[]{:S(2)}) collective-permute-start(bf16[128,768]{1,0:T(8,128)(2,1)S(1)} %collective-permute-done.refs_3_), channel_id=1, source_target_pairs={{0,1},{1,2},{2,3},{3,4},{4,5},{5,6},{6,7},{7,0},{8,9},{9,10},{10,1... | collective-permute-start | bytes 589832 | tf_op jit(solution)/shard_map/ppermute | solution.py:383
  45.3 7.8 %collective-permute-start.4 = (bf16[128,768]{1,0:T(8,128)(2,1)S(1)}, bf16[128,768]{1,0:T(8,128)(2,1)S(1)}, u32[]{:S(2)}, u32[]{:S(2)}) collective-permute-start(bf16[128,768]{1,0:T(8,128)(2,1)S(1)} %collective-permute-done.2.refs_3_), channel_id=1, source_target_pairs={{0,1},{1,2},{2,3},{3,4},{4,5},{5,6},{6,7},{7,0},{8,9},{9,10},{10,1... | collective-permute-start | bytes 589832 | tf_op jit(solution)/shard_map/ppermute | solution.py:383
  48.9 8.3 %collective-permute-start.3 = (bf16[128,768]{1,0:T(8,128)(2,1)S(1)}, bf16[128,768]{1,0:T(8,128)(2,1)S(1)}, u32[]{:S(2)}, u32[]{:S(2)}) collective-permute-start(bf16[128,768]{1,0:T(8,128)(2,1)S(1)} %collective-permute-done.1.refs_2_), channel_id=1, source_target_pairs={{0,1},{1,2},{2,3},{3,4},{4,5},{5,6},{6,7},{7,0},{8,9},{9,10},{10,1... | collective-permute-start | bytes 589832 | tf_op jit(solution)/shard_map/ppermute | solution.py:383
  53.1 7.8 %collective-permute-start.10 = (bf16[128,768]{1,0:T(8,128)(2,1)S(1)}, bf16[128,768]{1,0:T(8,128)(2,1)S(1)}, u32[]{:S(2)}, u32[]{:S(2)}) collective-permute-start(bf16[128,768]{1,0:T(8,128)(2,1)S(1)} %collective-permute-done.4.refs_2_), channel_id=1, source_target_pairs={{0,1},{1,2},{2,3},{3,4},{4,5},{5,6},{6,7},{7,0},{8,9},{9,10},{10,1... | collective-permute-start | bytes 589832 | tf_op jit(solution)/shard_map/ppermute | solution.py:383
  57.2 7.8 %collective-permute-start.5 = (bf16[128,768]{1,0:T(8,128)(2,1)S(1)}, bf16[128,768]{1,0:T(8,128)(2,1)S(1)}, u32[]{:S(2)}, u32[]{:S(2)}) collective-permute-start(bf16[128,768]{1,0:T(8,128)(2,1)S(1)} %collective-permute-done.3.refs_1_), channel_id=1, source_target_pairs={{0,1},{1,2},{2,3},{3,4},{4,5},{5,6},{6,7},{7,0},{8,9},{9,10},{10,1... | collective-permute-start | bytes 589832 | tf_op jit(solution)/shard_map/ppermute | solution.py:383
  60.9 15.2 %collective-permute-start.11 = (bf16[128,768]{1,0:T(8,128)(2,1)S(1)}, bf16[128,768]{1,0:T(8,128)(2,1)S(1)}, u32[]{:S(2)}, u32[]{:S(2)}) collective-permute-start(bf16[128,768]{1,0:T(8,128)(2,1)S(1)} %collective-permute-done.10.refs_1_), channel_id=1, source_target_pairs={{0,1},{1,2},{2,3},{3,4},{4,5},{5,6},{6,7},{7,0},{8,9},{9,10},{10,1... | collective-permute-start | bytes 589832 | tf_op jit(solution)/shard_map/ppermute | solution.py:383
  65.0 11.2 %collective-permute-start.12 = (bf16[128,512]{1,0:T(8,128)(2,1)S(1)}, bf16[128,512]{1,0:T(8,128)(2,1)S(1)}, u32[]{:S(2)}, u32[]{:S(2)}) collective-permute-start(bf16[128,512]{1,0:T(8,128)(2,1)S(1)} %get-tuple-element.49.refs_4_), channel_id=1, source_target_pairs={{0,1},{1,2},{2,3},{3,4},{4,5},{5,6},{6,7},{7,0},{8,9},{9,10},{10,1... | collective-permute-start | bytes 393224 | tf_op jit(solution)/shard_map/ppermute | solution.py:383
  69.0 32.2 %all-to-all-start.2 = ((bf16[32,16,1024]{2,1,0:T(8,128)(2,1)}), bf16[32,16,1024]{2,1,0:T(8,128)(2,1)}, u32[]{:S(2)}, u32[]{:S(2)}) async-start(bf16[32,16,1024]{2,1,0:T(8,128)(2,1)} %send_rows.3), calls=%async_computation.2 | async-start | bytes 2097152 | tf_op jit(solution)/shard_map/all_to_all | solution.py:378
  85.9 25.9 %collective-permute-start.6 = (bf16[128,768]{1,0:T(8,128)(2,1)S(1)}, bf16[128,768]{1,0:T(8,128)(2,1)S(1)}, u32[]{:S(2)}, u32[]{:S(2)}) collective-permute-start(bf16[128,768]{1,0:T(8,128)(2,1)S(1)} %get-tuple-element.44), channel_id=1, source_target_pairs={{0,7},{1,0},{2,1},{3,2},{4,3},{5,4},{6,5},{7,6},{8,15},{9,8},{10,9... | collective-permute-start | bytes 589832 | tf_op jit(solution)/shard_map/ppermute | solution.py:383
  101.2 57.4 %all-to-all-start.3 = ((bf16[32,16,3072]{2,1,0:T(8,128)(2,1)}), bf16[32,16,3072]{2,1,0:T(8,128)(2,1)}, u32[]{:S(2)}, u32[]{:S(2)}) async-start(bf16[32,16,3072]{2,1,0:T(8,128)(2,1)} %get-tuple-element.68), calls=%async_computation.3 | async-start | bytes 6291456 | tf_op jit(solution)/shard_map/all_to_all | solution.py:378
  109.0 6.2 %collective-permute-start.17 = (bf16[128,512]{1,0:T(8,128)(2,1)S(1)}, bf16[128,512]{1,0:T(8,128)(2,1)S(1)}, u32[]{:S(2)}, u32[]{:S(2)}) collective-permute-start(bf16[128,512]{1,0:T(8,128)(2,1)S(1)} %collective-permute-done.12.refs_3_), channel_id=1, source_target_pairs={{0,1},{1,2},{2,3},{3,4},{4,5},{5,6},{6,7},{7,0},{8,9},{9,10},{10,1... | collective-permute-start | bytes 393224 | tf_op jit(solution)/shard_map/ppermute | solution.py:383
  109.1 6.4 %collective-permute-start.13 = (bf16[128,768]{1,0:T(8,128)(2,1)S(1)}, bf16[128,768]{1,0:T(8,128)(2,1)S(1)}, u32[]{:S(2)}, u32[]{:S(2)}) collective-permute-start(bf16[128,768]{1,0:T(8,128)(2,1)S(1)} %get-tuple-element.52), channel_id=1, source_target_pairs={{0,7},{1,0},{2,1},{3,2},{4,3},{5,4},{6,5},{7,6},{8,15},{9,8},{10,9... | collective-permute-start | bytes 589832 | tf_op jit(solution)/shard_map/ppermute | solution.py:383
  111.8 8.8 %collective-permute-start.7 = (bf16[128,768]{1,0:T(8,128)(2,1)S(1)}, bf16[128,768]{1,0:T(8,128)(2,1)S(1)}, u32[]{:S(2)}, u32[]{:S(2)}) collective-permute-start(bf16[128,768]{1,0:T(8,128)(2,1)S(1)} %add_convert_fusion.5), channel_id=1, source_target_pairs={{0,7},{1,0},{2,1},{3,2},{4,3},{5,4},{6,5},{7,6},{8,15},{9,8},{10,9... | collective-permute-start | bytes 589832 | tf_op jit(solution)/shard_map/ppermute | solution.py:383
  115.2 5.4 %collective-permute-start.18 = (bf16[128,512]{1,0:T(8,128)(2,1)S(1)}, bf16[128,512]{1,0:T(8,128)(2,1)S(1)}, u32[]{:S(2)}, u32[]{:S(2)}) collective-permute-start(bf16[128,512]{1,0:T(8,128)(2,1)S(1)} %collective-permute-done.17.refs_2_), channel_id=1, source_target_pairs={{0,1},{1,2},{2,3},{3,4},{4,5},{5,6},{6,7},{7,0},{8,9},{9,10},{10,1... | collective-permute-start | bytes 393224 | tf_op jit(solution)/shard_map/ppermute | solution.py:383
  115.5 17.8 %collective-permute-start.14 = (bf16[128,768]{1,0:T(8,128)(2,1)S(1)}, bf16[128,768]{1,0:T(8,128)(2,1)S(1)}, u32[]{:S(2)}, u32[]{:S(2)}) collective-permute-start(bf16[128,768]{1,0:T(8,128)(2,1)S(1)} %add_convert_fusion.2), channel_id=1, source_target_pairs={{0,7},{1,0},{2,1},{3,2},{4,3},{5,4},{6,5},{7,6},{8,15},{9,8},{10,9... | collective-permute-start | bytes 589832 | tf_op jit(solution)/shard_map/ppermute | solution.py:383
  120.6 5.4 %collective-permute-start.19 = (bf16[128,512]{1,0:T(8,128)(2,1)S(1)}, bf16[128,512]{1,0:T(8,128)(2,1)S(1)}, u32[]{:S(2)}, u32[]{:S(2)}) collective-permute-start(bf16[128,512]{1,0:T(8,128)(2,1)S(1)} %collective-permute-done.18.refs_1_), channel_id=1, source_target_pairs={{0,1},{1,2},{2,3},{3,4},{4,5},{5,6},{6,7},{7,0},{8,9},{9,10},{10,1... | collective-permute-start | bytes 393224 | tf_op jit(solution)/shard_map/ppermute | solution.py:383
  120.7 18.2 %copy-start.8 = (f32[128,768]{1,0:T(8,128)S(1)}, f32[128,768]{1,0:T(8,128)}, u32[]{:S(2)}) copy-start(f32[128,768]{1,0:T(8,128)} %get-tuple-element.47) | copy-start | bytes 1179652
  120.7 18.2 %collective-permute-start.8 = (bf16[128,768]{1,0:T(8,128)(2,1)S(1)}, bf16[128,768]{1,0:T(8,128)(2,1)S(1)}, u32[]{:S(2)}, u32[]{:S(2)}) collective-permute-start(bf16[128,768]{1,0:T(8,128)(2,1)S(1)} %add_convert_fusion.4), channel_id=1, source_target_pairs={{0,7},{1,0},{2,1},{3,2},{4,3},{5,4},{6,5},{7,6},{8,15},{9,8},{10,9... | collective-permute-start | bytes 589832 | tf_op jit(solution)/shard_map/ppermute | solution.py:383
  133.3 12.6 %copy-start.7 = (f32[128,768]{1,0:T(8,128)S(1)}, f32[128,768]{1,0:T(8,128)}, u32[]{:S(2)}) copy-start(f32[128,768]{1,0:T(8,128)} %get-tuple-element.55) | copy-start | bytes 1179652
  133.3 24.0 %copy-start.1 = (f32[128,768]{1,0:T(8,128)S(1)}, f32[128,768]{1,0:T(8,128)}, u32[]{:S(2)}) copy-start(f32[128,768]{1,0:T(8,128)} %get-tuple-element.64.refs_3_) | copy-start | bytes 1179652
  133.3 24.0 %copy-start.2 = (f32[128,768]{1,0:T(8,128)S(1)}, f32[128,768]{1,0:T(8,128)}, u32[]{:S(2)}) copy-start(f32[128,768]{1,0:T(8,128)} %get-tuple-element.65.refs_4_) | copy-start | bytes 1179652
  133.3 4.3 %collective-permute-start.20 = (bf16[128,512]{1,0:T(8,128)(2,1)S(1)}, bf16[128,512]{1,0:T(8,128)(2,1)S(1)}, u32[]{:S(2)}, u32[]{:S(2)}) collective-permute-start(bf16[128,512]{1,0:T(8,128)(2,1)S(1)} %get-tuple-element.60), channel_id=1, source_target_pairs={{0,7},{1,0},{2,1},{3,2},{4,3},{5,4},{6,5},{7,6},{8,15},{9,8},{10,9... | collective-permute-start | bytes 393224 | tf_op jit(solution)/shard_map/ppermute | solution.py:383
  133.4 12.4 %collective-permute-start.15 = (bf16[128,768]{1,0:T(8,128)(2,1)S(1)}, bf16[128,768]{1,0:T(8,128)(2,1)S(1)}, u32[]{:S(2)}, u32[]{:S(2)}) collective-permute-start(bf16[128,768]{1,0:T(8,128)(2,1)S(1)} %add_convert_fusion.1), channel_id=1, source_target_pairs={{0,7},{1,0},{2,1},{3,2},{4,3},{5,4},{6,5},{7,6},{8,15},{9,8},{10,9... | collective-permute-start | bytes 589832 | tf_op jit(solution)/shard_map/ppermute | solution.py:383
  137.6 5.7 %collective-permute-start.21 = (bf16[128,512]{1,0:T(8,128)(2,1)S(1)}, bf16[128,512]{1,0:T(8,128)(2,1)S(1)}, u32[]{:S(2)}, u32[]{:S(2)}) collective-permute-start(bf16[128,512]{1,0:T(8,128)(2,1)S(1)} %add_convert_fusion.8), channel_id=1, source_target_pairs={{0,7},{1,0},{2,1},{3,2},{4,3},{5,4},{6,5},{7,6},{8,15},{9,8},{10,9... | collective-permute-start | bytes 393224 | tf_op jit(solution)/shard_map/ppermute | solution.py:383
  139.0 13.8 %collective-permute-start.9 = (bf16[128,768]{1,0:T(8,128)(2,1)S(1)}, bf16[128,768]{1,0:T(8,128)(2,1)S(1)}, u32[]{:S(2)}, u32[]{:S(2)}) collective-permute-start(bf16[128,768]{1,0:T(8,128)(2,1)S(1)} %add_convert_fusion.3), channel_id=1, source_target_pairs={{0,7},{1,0},{2,1},{3,2},{4,3},{5,4},{6,5},{7,6},{8,15},{9,8},{10,9... | collective-permute-start | bytes 589832 | tf_op jit(solution)/shard_map/ppermute | solution.py:383
  143.4 7.0 %collective-permute-start.22 = (bf16[128,512]{1,0:T(8,128)(2,1)S(1)}, bf16[128,512]{1,0:T(8,128)(2,1)S(1)}, u32[]{:S(2)}, u32[]{:S(2)}) collective-permute-start(bf16[128,512]{1,0:T(8,128)(2,1)S(1)} %add_convert_fusion.7), channel_id=1, source_target_pairs={{0,7},{1,0},{2,1},{3,2},{4,3},{5,4},{6,5},{7,6},{8,15},{9,8},{10,9... | collective-permute-start | bytes 393224 | tf_op jit(solution)/shard_map/ppermute | solution.py:383
  145.9 8.6 %collective-permute-start.16 = (bf16[128,768]{1,0:T(8,128)(2,1)S(1)}, bf16[128,768]{1,0:T(8,128)(2,1)S(1)}, u32[]{:S(2)}, u32[]{:S(2)}) collective-permute-start(bf16[128,768]{1,0:T(8,128)(2,1)S(1)} %add_convert_fusion), channel_id=1, source_target_pairs={{0,7},{1,0},{2,1},{3,2},{4,3},{5,4},{6,5},{7,6},{8,15},{9,8},{10,9... | collective-permute-start | bytes 589832 | tf_op jit(solution)/shard_map/ppermute | solution.py:383
  150.4 6.9 %collective-permute-start.23 = (bf16[128,512]{1,0:T(8,128)(2,1)S(1)}, bf16[128,512]{1,0:T(8,128)(2,1)S(1)}, u32[]{:S(2)}, u32[]{:S(2)}) collective-permute-start(bf16[128,512]{1,0:T(8,128)(2,1)S(1)} %add_convert_fusion.6), channel_id=1, source_target_pairs={{0,7},{1,0},{2,1},{3,2},{4,3},{5,4},{6,5},{7,6},{8,15},{9,8},{10,9... | collective-permute-start | bytes 393224 | tf_op jit(solution)/shard_map/ppermute | solution.py:383
  158.6 10.7 %copy-start.3 = (s32[1,1,128]{2,1,0:T(1,128)S(1)}, s32[1,1,128]{2,1,0:T(1,128)}, u32[]{:S(2)}) copy-start(s32[1,1,128]{2,1,0:T(1,128)} %param.16) | copy-start | bytes 1540
  158.6 10.7 %copy-start.4 = (f32[128]{0:T(128)S(1)}, f32[128]{0:T(128)}, u32[]{:S(2)}) copy-start(f32[128]{0:T(128)} %param.13) | copy-start | bytes 1540
  158.6 32.9 %all-to-all-start.4 = ((bf16[32,16,1536]{2,1,0:T(8,128)(2,1)}), bf16[32,16,1536]{2,1,0:T(8,128)(2,1)S(1)}, u32[]{:S(2)}, u32[]{:S(2)}) async-start(bf16[32,16,1536]{2,1,0:T(8,128)(2,1)} %return_kv.1), calls=%async_computation.4 | async-start | bytes 3145728 | tf_op jit(solution)/shard_map/all_to_all | solution.py:378
  169.4 22.2 %copy-start = (bf16[128,1024]{1,0:T(8,128)(2,1)S(1)}, bf16[128,1024]{1,0:T(8,128)(2,1)}, u32[]{:S(2)}) copy-start(bf16[128,1024]{1,0:T(8,128)(2,1)} %refs_1_.1) | copy-start | bytes 786436
  169.4 22.2 %copy-start.5 = (f32[128]{0:T(128)S(1)}, f32[128]{0:T(128)}, u32[]{:S(2)}) copy-start(f32[128]{0:T(128)} %param.14) | copy-start | bytes 1540

commit v4 on v3

--- a/solution.py
+++ b/solution.py
@@ -380,7 +380,8 @@
 
 def along(array, step):
     count = lax.axis_size("seq")
-    return lax.ppermute(array, "seq", [(i, (i + step) % count) for i in range(count)])
+    pairs = [(i, i + step) for i in range(count) if 0 <= i + step < count]
+    return lax.ppermute(array, "seq", pairs)
 
 
 def after(array, other):
@@ -413,16 +414,16 @@
         first.append(along(after(first[-1], second[n - 1] if n > 1 else None), 1))
         second.append(along(second[-1], 1))
     received_last = exchange(after(after(sent[1], received_first), first[BACK]))
-    for n in range(BACK):
-        block = after(third[-1], (first[BACK], None, received_last, None)[n])
-        third.append(along(block, 1))
-    second[-1] = after(second[-1], third[1])
+    third[0] = after(third[0], first[BACK])
+    for _ in range(BACK):
+        third.append(along(third[-1], 1))
+    second[-1] = after(second[-1], third[2])
 
     def back_along(parts):
-        total = parts[0]
+        totals = parts[:1]
         for part in parts[1:-1]:
-            total = (along(total, -1).astype(F32) + part).astype(BF16)
-        return along(total, -1), parts[-1]
+            totals.append((along(totals[-1], -1).astype(F32) + part).astype(BF16))
+        return totals + [along(totals[-1], -1)], parts[-1]
 
     def attend_batch(rows, blocks, first, count, result, weight):
         result, *parts = attend(
@@ -430,13 +431,14 @@
         )
         return result, *back_along(parts)
 
-    result, got0, own0 = attend_batch(received_first, first, 0, BATCHES[0], FIRST, 4)
-    result, got1, own1 = attend_batch(
-        received_first, second, BATCHES[0], BATCHES[1], result, 36
-    )
-    back_first = exchange(result)
-    result, got2, own2 = attend_batch(received_last, third, 0, BATCHES[2], BATCHES[2] + 1, 36)
-    merged = return_kv(arriving, (got0, got1, got2), (own0, own1, own2), result)
+    result, sums0, own0 = attend_batch(received_first, first, 0, BATCHES[0], FIRST, 1)
+    result, sums1, own1 = attend_batch(
+        received_first, second, BATCHES[0], BATCHES[1], result, 24
+    )
+    back_first = exchange(after(after(result, third[3]), sums0[1]))
+    third[-1] = after(third[-1], sums0[2])
+    result, sums2, own2 = attend_batch(received_last, third, 0, BATCHES[2], BATCHES[2] + 1, 36)
+    merged = return_kv(arriving, (sums0[-1], sums1[-1], sums2[-1]), (own0, own1, own2), result)
     back_last = exchange(after(merged, back_first))
 
     outs = finish(leaving, q_gain, query, back_first, starts[0], counts[0])

time: 197 us -> 222 us (1.13)
  the two profiles are of different devices: /device:TPU:1 before, /device:TPU:96 now
where the time goes in v4:
time: 222 us; the launch traced here: 221 us
  starting transfers between devices  108 us (49%)
  waiting for transfers between devices  57.4 us (26%)
  Pallas kernels  53.2 us (24%)
    ppermute x24, starting transfers between devices, along(): return lax.ppermute(array, 'seq', pairs)  72.5 us
    ppermute x24, waiting for transfers between devices, along(): return lax.ppermute(array, 'seq', pairs)  39.2 us
    all_to_all x5, starting transfers between devices, exchange(): return lax.all_to_all(array, 'dp', split_axis=0, concat_axis=0, tiled=True)  36 us
    pallas_call x3, Pallas kernels, attend(): pl.pallas_call(attend_kernel, grid=(count,), in_specs=[pl.BlockSpec(memor...  26.7 us
    all_to_all x5, waiting for transfers between devices, exchange(): return lax.all_to_all(array, 'dp', split_axis=0, concat_axis=0, tiled=True)  18.2 us
    pallas_call x2, Pallas kernels, finish(): pl.pallas_call(functools.partial(finish_kernel, bool(kv)), grid=(count +...  11.6 us
    pallas_call x2, Pallas kernels, send_rows(): pl.pallas_call(send_rows_kernel, grid=(count,), in_specs=[pl.BlockSpec((1...  10.5 us
  transfers between devices with their start and end apart: 29, of which 13 were waited for; matrix products, arithmetic and copies ran while one was open for 0% of the time, Pallas kernels for 21%

profile of v4, /device:TPU:96, one launch (start us, length us, event | category | flops | bytes accessed | tf_op | source)
XLA Modules:
  0.0 220.6 jit_solution(10692446048153874992)
XLA Ops:
  0.6 2.5 %send_kv.1 = bf16[32,16,512]{2,1,0:T(8,128)(2,1)} custom-call(s32[1,128]{1,0:T(1,128)} %bitcast.6, f32[1,128]{1,0:T(1,128)} %bitcast.15, bf16[128,1024]{1,0:T(8,128)(2,1)} %refs_1_.1, bf16[128,1024]{1,0:T(8,128)(2,1)} %v_ref.1), custom_call_target="tpu_custom_call" | custom-call | flops 268435456 | bytes 1572864 | tf_op jit(solution)/shard_map/send_kv/pallas_call | solution.py:115
  3.1 7.3 %all-to-all-start = ((bf16[32,16,512]{2,1,0:T(8,128)(2,1)}), bf16[32,16,512]{2,1,0:T(8,128)(2,1)S(1)}, u32[]{:S(2)}, u32[]{:S(2)}) async-start(bf16[32,16,512]{2,1,0:T(8,128)(2,1)} %send_kv.1), calls=%async_computation | async-start | bytes 1048576 | tf_op jit(solution)/shard_map/all_to_all | solution.py:378
  10.5 3.4 %send_rows.3 = bf16[32,16,1024]{2,1,0:T(8,128)(2,1)} custom-call(s32[1,128]{1,0:T(1,128)} %bitcast.7, f32[1,128]{1,0:T(1,128)} %bitcast.11, bf16[128,8192]{1,0:T(8,128)(2,1)} %q_ref.7, bf16[128,8192]{1,0:T(8,128)(2,1)} %d_ref.3), custom_call_target="tpu_custom_call" | custom-call | flops 536870912 | bytes 2097152 | tf_op jit(solution)/shard_map/send_rows/pallas_call | solution.py:145
  13.8 7.2 %send_rows.2 = bf16[32,16,3072]{2,1,0:T(8,128)(2,1)} custom-call(s32[1,128]{1,0:T(1,128)} %bitcast.8, f32[1,128]{1,0:T(1,128)} %bitcast.12, bf16[128,8192]{1,0:T(8,128)(2,1)} %q_ref.7, bf16[128,8192]{1,0:T(8,128)(2,1)} %d_ref.3), custom_call_target="tpu_custom_call" | custom-call | flops 1610612736 | bytes 6291456 | tf_op jit(solution)/shard_map/send_rows/pallas_call | solution.py:145
  21.0 1.2 all-to-all-done.in_ref
  22.2 6.3 %all-to-all-start.1 = ((bf16[32,16,3072]{2,1,0:T(8,128)(2,1)}), bf16[32,16,3072]{2,1,0:T(8,128)(2,1)}, u32[]{:S(2)}, u32[]{:S(2)}) async-start(bf16[32,16,3072]{2,1,0:T(8,128)(2,1)} %send_rows.2), calls=%async_computation.1 | async-start | bytes 6291456 | tf_op jit(solution)/shard_map/all_to_all | solution.py:378
  28.6 0.0 copy-start.9
  28.6 0.5 sort_kv.1
  29.1 5.0 %collective-permute-start = (bf16[128,768]{1,0:T(8,128)(2,1)S(1)}, bf16[128,768]{1,0:T(8,128)(2,1)S(1)}, u32[]{:S(2)}, u32[]{:S(2)}) collective-permute-start(bf16[128,768]{1,0:T(8,128)(2,1)S(1)} %get-tuple-element.42.refs_4_), channel_id=1, source_target_pairs={{0,1},{1,2},{2,3},{3,4},{4,5},{5,6},{6,7},{8,9},{9,10},{10,11},{11... | collective-permute-start | bytes 589832 | tf_op jit(solution)/shard_map/ppermute | solution.py:384
  34.1 2.9 %collective-permute-start.2 = (bf16[128,768]{1,0:T(8,128)(2,1)S(1)}, bf16[128,768]{1,0:T(8,128)(2,1)S(1)}, u32[]{:S(2)}, u32[]{:S(2)}) collective-permute-start(bf16[128,768]{1,0:T(8,128)(2,1)S(1)} %get-tuple-element.43.refs_4_), channel_id=1, source_target_pairs={{0,1},{1,2},{2,3},{3,4},{4,5},{5,6},{6,7},{8,9},{9,10},{10,11},{11... | collective-permute-start | bytes 589832 | tf_op jit(solution)/shard_map/ppermute | solution.py:384
  37.1 2.3 %collective-permute-done.refs_3_ = bf16[128,768]{1,0:T(8,128)(2,1)S(1)} collective-permute-done((bf16[128,768]{1,0:T(8,128)(2,1)S(1)}, bf16[128,768]{1,0:T(8,128)(2,1)S(1)}, u32[]{:S(2)}, u32[]{:S(2)}) %collective-permute-start) | collective-permute-done | bytes 196640 | tf_op jit(solution)/shard_map/ppermute | solution.py:384
  39.4 5.6 %collective-permute-start.1 = (bf16[128,768]{1,0:T(8,128)(2,1)S(1)}, bf16[128,768]{1,0:T(8,128)(2,1)S(1)}, u32[]{:S(2)}, u32[]{:S(2)}) collective-permute-start(bf16[128,768]{1,0:T(8,128)(2,1)S(1)} %collective-permute-done.refs_3_), channel_id=1, source_target_pairs={{0,1},{1,2},{2,3},{3,4},{4,5},{5,6},{6,7},{8,9},{9,10},{10,11},{11... | collective-permute-start | bytes 589832 | tf_op jit(solution)/shard_map/ppermute | solution.py:384
  45.0 0.0 collective-permute-done.2.refs_3_
  45.0 3.5 %collective-permute-start.4 = (bf16[128,768]{1,0:T(8,128)(2,1)S(1)}, bf16[128,768]{1,0:T(8,128)(2,1)S(1)}, u32[]{:S(2)}, u32[]{:S(2)}) collective-permute-start(bf16[128,768]{1,0:T(8,128)(2,1)S(1)} %collective-permute-done.2.refs_3_), channel_id=1, source_target_pairs={{0,1},{1,2},{2,3},{3,4},{4,5},{5,6},{6,7},{8,9},{9,10},{10,11},{11... | collective-permute-start | bytes 589832 | tf_op jit(solution)/shard_map/ppermute | solution.py:384
  48.5 0.0 collective-permute-done.1.refs_2_
  48.5 5.3 %collective-permute-start.3 = (bf16[128,768]{1,0:T(8,128)(2,1)S(1)}, bf16[128,768]{1,0:T(8,128)(2,1)S(1)}, u32[]{:S(2)}, u32[]{:S(2)}) collective-permute-start(bf16[128,768]{1,0:T(8,128)(2,1)S(1)} %collective-permute-done.1.refs_2_), channel_id=1, source_target_pairs={{0,1},{1,2},{2,3},{3,4},{4,5},{5,6},{6,7},{8,9},{9,10},{10,11},{11... | collective-permute-start | bytes 589832 | tf_op jit(solution)/shard_map/ppermute | solution.py:384
  53.8 3.2 %collective-permute-done.3.refs_1_ = bf16[128,768]{1,0:T(8,128)(2,1)S(1)} collective-permute-done((bf16[128,768]{1,0:T(8,128)(2,1)S(1)}, bf16[128,768]{1,0:T(8,128)(2,1)S(1)}, u32[]{:S(2)}, u32[]{:S(2)}) %collective-permute-start.3) | collective-permute-done | bytes 196640 | tf_op jit(solution)/shard_map/ppermute | solution.py:384
  56.9 5.6 %collective-permute-start.5 = (bf16[128,768]{1,0:T(8,128)(2,1)S(1)}, bf16[128,768]{1,0:T(8,128)(2,1)S(1)}, u32[]{:S(2)}, u32[]{:S(2)}) collective-permute-start(bf16[128,768]{1,0:T(8,128)(2,1)S(1)} %collective-permute-done.3.refs_1_), channel_id=1, source_target_pairs={{0,1},{1,2},{2,3},{3,4},{4,5},{5,6},{6,7},{8,9},{9,10},{10,11},{11... | collective-permute-start | bytes 589832 | tf_op jit(solution)/shard_map/ppermute | solution.py:384
  62.5 1.9 collective-permute-start.10
  64.4 2.2 %collective-permute-done.5.refs_0_ = bf16[128,768]{1,0:T(8,128)(2,1)S(1)} collective-permute-done((bf16[128,768]{1,0:T(8,128)(2,1)S(1)}, bf16[128,768]{1,0:T(8,128)(2,1)S(1)}, u32[]{:S(2)}, u32[]{:S(2)}) %collective-permute-start.5) | collective-permute-done | bytes 196640 | tf_op jit(solution)/shard_map/ppermute | solution.py:384
  66.7 5.6 %collective-permute-start.12 = (bf16[128,512]{1,0:T(8,128)(2,1)S(1)}, bf16[128,512]{1,0:T(8,128)(2,1)S(1)}, u32[]{:S(2)}, u32[]{:S(2)}) collective-permute-start(bf16[128,512]{1,0:T(8,128)(2,1)S(1)} %get-tuple-element.51.refs_4_), channel_id=1, source_target_pairs={{0,1},{1,2},{2,3},{3,4},{4,5},{5,6},{6,7},{8,9},{9,10},{10,11},{11... | collective-permute-start | bytes 393224 | tf_op jit(solution)/shard_map/ppermute | solution.py:384
  72.3 0.0 collective-permute-done.10.refs_1_
  72.3 2.4 %collective-permute-start.11 = (bf16[128,768]{1,0:T(8,128)(2,1)S(1)}, bf16[128,768]{1,0:T(8,128)(2,1)S(1)}, u32[]{:S(2)}, u32[]{:S(2)}) collective-permute-start(bf16[128,768]{1,0:T(8,128)(2,1)S(1)} %collective-permute-done.10.refs_1_), channel_id=1, source_target_pairs={{0,1},{1,2},{2,3},{3,4},{4,5},{5,6},{6,7},{8,9},{9,10},{10,11},{11... | collective-permute-start | bytes 589832 | tf_op jit(solution)/shard_map/ppermute | solution.py:384
  74.7 7.6 %all-to-all-start.2 = ((bf16[32,16,1024]{2,1,0:T(8,128)(2,1)}), bf16[32,16,1024]{2,1,0:T(8,128)(2,1)}, u32[]{:S(2)}, u32[]{:S(2)}) async-start(bf16[32,16,1024]{2,1,0:T(8,128)(2,1)} %send_rows.3), calls=%async_computation.2 | async-start | bytes 2097152 | tf_op jit(solution)/shard_map/all_to_all | solution.py:378
  82.4 0.0 collective-permute-done.12.refs_3_
  82.4 1.9 collective-permute-start.13
  84.3 0.1 pad_add_fusion.meta_ref
  84.4 0.0 collective-permute-done.11.refs_0_
  84.4 5.5 %collective-permute-done.13.refs_2_ = bf16[128,512]{1,0:T(8,128)(2,1)S(1)} collective-permute-done((bf16[128,512]{1,0:T(8,128)(2,1)S(1)}, bf16[128,512]{1,0:T(8,128)(2,1)S(1)}, u32[]{:S(2)}, u32[]{:S(2)}) %collective-permute-start.13) | collective-permute-done | bytes 131104 | tf_op jit(solution)/shard_map/ppermute | solution.py:384
  89.9 3.4 %collective-permute-start.18 = (bf16[128,512]{1,0:T(8,128)(2,1)S(1)}, bf16[128,512]{1,0:T(8,128)(2,1)S(1)}, u32[]{:S(2)}, u32[]{:S(2)}) collective-permute-start(bf16[128,512]{1,0:T(8,128)(2,1)S(1)} %collective-permute-done.13.refs_2_), channel_id=1, source_target_pairs={{0,1},{1,2},{2,3},{3,4},{4,5},{5,6},{6,7},{8,9},{9,10},{10,11},{11... | collective-permute-start | bytes 393224 | tf_op jit(solution)/shard_map/ppermute | solution.py:384
  93.3 9.7 %attend.3 = (bf16[32,16,3072]{2,1,0:T(8,128)(2,1)}, bf16[128,768]{1,0:T(8,128)(2,1)S(1)}, f32[128,768]{1,0:T(8,128)S(1)}, f32[128,768]{1,0:T(8,128)S(1)}, f32[128,768]{1,0:T(8,128)}, /*index=5*/f32[128,768]{1,0:T(8,128)}) custom-call(s32[4]{0:T(128)S(1)} %pad_add_fusion.meta_ref, s32[1,128]{1,0:T(1,128)S(1)} %bitcast.18, ...), custom_call_target="tpu_custom_call" | custom-call | flops 251658240 | bytes 9437184 | tf_op jit(solution)/shard_map/attend/pallas_call | solution.py:244
  103.0 2.4 %collective-permute-start.6 = (bf16[128,768]{1,0:T(8,128)(2,1)S(1)}, bf16[128,768]{1,0:T(8,128)(2,1)S(1)}, u32[]{:S(2)}, u32[]{:S(2)}) collective-permute-start(bf16[128,768]{1,0:T(8,128)(2,1)S(1)} %get-tuple-element.46), channel_id=1, source_target_pairs={{1,0},{2,1},{3,2},{4,3},{5,4},{6,5},{7,6},{9,8},{10,9},{11,10},{12... | collective-permute-start | bytes 589832 | tf_op jit(solution)/shard_map/ppermute | solution.py:384
  105.4 9.8 %attend.4 = (bf16[32,16,3072]{2,1,0:T(8,128)(2,1)}, bf16[128,768]{1,0:T(8,128)(2,1)S(1)}, f32[128,768]{1,0:T(8,128)S(1)}, f32[128,768]{1,0:T(8,128)S(1)}, f32[128,768]{1,0:T(8,128)}, /*index=5*/f32[128,768]{1,0:T(8,128)}) custom-call(s32[4]{0:T(128)S(1)} %pad_add_fusion.meta_ref, s32[1,128]{1,0:T(1,128)S(1)} %bitcast.19, ...), custom_call_target="tpu_custom_call", output_to_operand_aliasing={{0}: (8, {})} | custom-call | flops 6039797760 | bytes 9437184 | tf_op jit(solution)/shard_map/attend/pallas_call | solution.py:244
  115.3 7.4 %all-to-all-start.3 = ((bf16[32,16,3072]{2,1,0:T(8,128)(2,1)}), bf16[32,16,3072]{2,1,0:T(8,128)(2,1)}, u32[]{:S(2)}, u32[]{:S(2)}) async-start(bf16[32,16,3072]{2,1,0:T(8,128)(2,1)} %get-tuple-element.72), calls=%async_computation.3 | async-start | bytes 6291456 | tf_op jit(solution)/shard_map/all_to_all | solution.py:378
  122.6 3.3 %collective-permute-start.14 = (bf16[128,768]{1,0:T(8,128)(2,1)S(1)}, bf16[128,768]{1,0:T(8,128)(2,1)S(1)}, u32[]{:S(2)}, u32[]{:S(2)}) collective-permute-start(bf16[128,768]{1,0:T(8,128)(2,1)S(1)} %get-tuple-element.54), channel_id=1, source_target_pairs={{1,0},{2,1},{3,2},{4,3},{5,4},{6,5},{7,6},{9,8},{10,9},{11,10},{12... | collective-permute-start | bytes 589832 | tf_op jit(solution)/shard_map/ppermute | solution.py:384
  125.9 3.8 %collective-permute-start.19 = (bf16[128,512]{1,0:T(8,128)(2,1)S(1)}, bf16[128,512]{1,0:T(8,128)(2,1)S(1)}, u32[]{:S(2)}, u32[]{:S(2)}) collective-permute-start(bf16[128,512]{1,0:T(8,128)(2,1)S(1)} %collective-permute-done.18.refs_1_), channel_id=1, source_target_pairs={{0,1},{1,2},{2,3},{3,4},{4,5},{5,6},{6,7},{8,9},{9,10},{10,11},{11... | collective-permute-start | bytes 393224 | tf_op jit(solution)/shard_map/ppermute | solution.py:384
  129.7 2.0 collective-permute-start.7
  131.8 1.0 collective-permute-done.14
  132.8 2.0 collective-permute-start.15
  134.9 5.6 %collective-permute-done.7 = bf16[128,768]{1,0:T(8,128)(2,1)S(1)} collective-permute-done((bf16[128,768]{1,0:T(8,128)(2,1)S(1)}, bf16[128,768]{1,0:T(8,128)(2,1)S(1)}, u32[]{:S(2)}, u32[]{:S(2)}) %collective-permute-start.7) | collective-permute-done | bytes 196640 | tf_op jit(solution)/shard_map/ppermute | solution.py:384
  140.5 0.0 copy-start.8
  140.5 2.2 %collective-permute-start.8 = (bf16[128,768]{1,0:T(8,128)(2,1)S(1)}, bf16[128,768]{1,0:T(8,128)(2,1)S(1)}, u32[]{:S(2)}, u32[]{:S(2)}) collective-permute-start(bf16[128,768]{1,0:T(8,128)(2,1)S(1)} %add_convert_fusion.4), channel_id=1, source_target_pairs={{1,0},{2,1},{3,2},{4,3},{5,4},{6,5},{7,6},{9,8},{10,9},{11,10},{12... | collective-permute-start | bytes 589832 | tf_op jit(solution)/shard_map/ppermute | solution.py:384
  142.7 0.0 collective-permute-done.19.refs_0_
  142.8 7.2 %attend.5 = (bf16[32,16,1536]{2,1,0:T(8,128)(2,1)}, bf16[128,512]{1,0:T(8,128)(2,1)S(1)}, f32[128,512]{1,0:T(8,128)S(1)}, f32[128,512]{1,0:T(8,128)S(1)}, f32[12...) custom-call(s32[4]{0:T(128)S(1)} %pad_add_fusion.meta_ref, s32[1,128]{1,0:T(1,128)S(1)} %bitcast.20, ...), custom_call_target="tpu_custom_call" | custom-call | flops 6039797760 | bytes 6291456 | tf_op jit(solution)/shard_map/attend/pallas_call | solution.py:244
  150.0 2.1 collective-permute-start.20
  152.1 1.9 collective-permute-start.16
  154.0 4.9 %collective-permute-done.20 = bf16[128,512]{1,0:T(8,128)(2,1)S(1)} collective-permute-done((bf16[128,512]{1,0:T(8,128)(2,1)S(1)}, bf16[128,512]{1,0:T(8,128)(2,1)S(1)}, u32[]{:S(2)}, u32[]{:S(2)}) %collective-permute-start.20) | collective-permute-done | bytes 131104 | tf_op jit(solution)/shard_map/ppermute | solution.py:384
  159.0 1.9 collective-permute-start.21
  160.9 0.0 collective-permute-done.8
  161.0 1.9 collective-permute-start.9
  162.9 4.2 %collective-permute-done.21 = bf16[128,512]{1,0:T(8,128)(2,1)S(1)} collective-permute-done((bf16[128,512]{1,0:T(8,128)(2,1)S(1)}, bf16[128,512]{1,0:T(8,128)(2,1)S(1)}, u32[]{:S(2)}, u32[]{:S(2)}) %collective-permute-start.21) | collective-permute-done | bytes 131104 | tf_op jit(solution)/shard_map/ppermute | solution.py:384
  167.1 1.9 collective-permute-start.22
  169.1 1.9 collective-permute-start.17
  171.0 4.2 %collective-permute-done.22 = bf16[128,512]{1,0:T(8,128)(2,1)S(1)} collective-permute-done((bf16[128,512]{1,0:T(8,128)(2,1)S(1)}, bf16[128,512]{1,0:T(8,128)(2,1)S(1)}, u32[]{:S(2)}, u32[]{:S(2)}) %collective-permute-start.22) | collective-permute-done | bytes 131104 | tf_op jit(solution)/shard_map/ppermute | solution.py:384
  175.2 1.9 collective-permute-start.23
  177.2 1.6 collective-permute-done.17.refs_1_
  178.7 4.6 %collective-permute-done.23.refs_2_ = bf16[128,512]{1,0:T(8,128)(2,1)S(1)} collective-permute-done((bf16[128,512]{1,0:T(8,128)(2,1)S(1)}, bf16[128,512]{1,0:T(8,128)(2,1)S(1)}, u32[]{:S(2)}, u32[]{:S(2)}) %collective-permute-start.23) | collective-permute-done | bytes 131104 | tf_op jit(solution)/shard_map/ppermute | solution.py:384
  183.3 1.3 return_kv.1
  184.6 7.3 %all-to-all-start.4 = ((bf16[32,16,1536]{2,1,0:T(8,128)(2,1)}), bf16[32,16,1536]{2,1,0:T(8,128)(2,1)S(1)}, u32[]{:S(2)}, u32[]{:S(2)}) async-start(bf16[32,16,1536]{2,1,0:T(8,128)(2,1)} %return_kv.1), calls=%async_computation.4 | async-start | bytes 3145728 | tf_op jit(solution)/shard_map/all_to_all | solution.py:378
  192.0 0.0 copy-start
  192.0 0.0 copy-start.5
  192.0 6.9 %finish.2 = (bf16[128,8192]{1,0:T(8,128)(2,1)}, bf16[128,8192]{1,0:T(8,128)(2,1)}) custom-call(s32[1,128]{1,0:T(1,128)S(1)} %bitcast.9, f32[1,128]{1,0:T(1,128)S(1)} %bitcast.13, bf16[128,8192]{1,0:T(8,128)(2,1)} %q_ref.7, bf16[32,16,3072]{2,1,0:T(8,128)(2,1)} %all-to-all-done.3.in_ref), custom_call_target="tpu_custom_call" | custom-call | flops 1610612736 | bytes 7864320 | tf_op jit(solution)/shard_map/finish/pallas_call | solution.py:363
  198.9 16.9 %all-to-all-done.4.in_ref = bf16[32,16,1536]{2,1,0:T(8,128)(2,1)S(1)} async-done(((bf16[32,16,1536]{2,1,0:T(8,128)(2,1)}), bf16[32,16,1536]{2,1,0:T(8,128)(2,1)S(1)}, u32[]{:S(2)}, u32[]{:S(2)}) %all-to-all-start.4) | async-done | bytes 1572896 | tf_op jit(solution)/shard_map/all_to_all | solution.py:378
  215.9 4.7 %finish.3 = (bf16[128,8192]{1,0:T(8,128)(2,1)}, bf16[128,8192]{1,0:T(8,128)(2,1)}, bf16[128,1024]{1,0:T(8,128)(2,1)}, bf16[128,1024]{1,0:T(8,128)(2,1)}) custom-call(s32[1,128]{1,0:T(1,128)S(1)} %bitcast.10, f32[1,128]{1,0:T(1,128)S(1)} %bitcast.14, bf16[128,8192]{1,0:T(8,128)(2,1)} %q_ref.7, ...), custom_call_target="tpu_custom_call", output_to_operand_aliasing={{0}: (6, {}), {1}: (7, {})} | custom-call | flops 536870912 | bytes 2621440 | tf_op jit(solution)/shard_map/finish/pallas_call | solution.py:363
  (34 shorter events, 0.4 us)
Async XLA Ops:
  3.1 19.1 %all-to-all-start = ((bf16[32,16,512]{2,1,0:T(8,128)(2,1)}), bf16[32,16,512]{2,1,0:T(8,128)(2,1)S(1)}, u32[]{:S(2)}, u32[]{:S(2)}) async-start(bf16[32,16,512]{2,1,0:T(8,128)(2,1)} %send_kv.1), calls=%async_computation | async-start | bytes 1048576 | tf_op jit(solution)/shard_map/all_to_all | solution.py:378
  21.0 7.6 %copy-start.6 = (s32[1,1,128]{2,1,0:T(1,128)S(1)}, s32[1,1,128]{2,1,0:T(1,128)}, u32[]{:S(2)}) copy-start(s32[1,1,128]{2,1,0:T(1,128)} %param.17) | copy-start | bytes 1540
  22.2 52.5 %all-to-all-start.1 = ((bf16[32,16,3072]{2,1,0:T(8,128)(2,1)}), bf16[32,16,3072]{2,1,0:T(8,128)(2,1)}, u32[]{:S(2)}, u32[]{:S(2)}) async-start(bf16[32,16,3072]{2,1,0:T(8,128)(2,1)} %send_rows.2), calls=%async_computation.1 | async-start | bytes 6291456 | tf_op jit(solution)/shard_map/all_to_all | solution.py:378
  28.6 55.8 %copy-start.9 = (s32[1,3]{1,0:T(1,128)S(1)}, s32[1,3]{1,0:T(1,128)}, u32[]{:S(2)}) copy-start(s32[1,3]{1,0:T(1,128)} %param.15) | copy-start | bytes 40
  29.1 10.3 %collective-permute-start = (bf16[128,768]{1,0:T(8,128)(2,1)S(1)}, bf16[128,768]{1,0:T(8,128)(2,1)S(1)}, u32[]{:S(2)}, u32[]{:S(2)}) collective-permute-start(bf16[128,768]{1,0:T(8,128)(2,1)S(1)} %get-tuple-element.42.refs_4_), channel_id=1, source_target_pairs={{0,1},{1,2},{2,3},{3,4},{4,5},{5,6},{6,7},{8,9},{9,10},{10,11},{11... | collective-permute-start | bytes 589832 | tf_op jit(solution)/shard_map/ppermute | solution.py:384
  34.1 10.8 %collective-permute-start.2 = (bf16[128,768]{1,0:T(8,128)(2,1)S(1)}, bf16[128,768]{1,0:T(8,128)(2,1)S(1)}, u32[]{:S(2)}, u32[]{:S(2)}) collective-permute-start(bf16[128,768]{1,0:T(8,128)(2,1)S(1)} %get-tuple-element.43.refs_4_), channel_id=1, source_target_pairs={{0,1},{1,2},{2,3},{3,4},{4,5},{5,6},{6,7},{8,9},{9,10},{10,11},{11... | collective-permute-start | bytes 589832 | tf_op jit(solution)/shard_map/ppermute | solution.py:384
  39.4 9.1 %collective-permute-start.1 = (bf16[128,768]{1,0:T(8,128)(2,1)S(1)}, bf16[128,768]{1,0:T(8,128)(2,1)S(1)}, u32[]{:S(2)}, u32[]{:S(2)}) collective-permute-start(bf16[128,768]{1,0:T(8,128)(2,1)S(1)} %collective-permute-done.refs_3_), channel_id=1, source_target_pairs={{0,1},{1,2},{2,3},{3,4},{4,5},{5,6},{6,7},{8,9},{9,10},{10,11},{11... | collective-permute-start | bytes 589832 | tf_op jit(solution)/shard_map/ppermute | solution.py:384
  45.0 8.8 %collective-permute-start.4 = (bf16[128,768]{1,0:T(8,128)(2,1)S(1)}, bf16[128,768]{1,0:T(8,128)(2,1)S(1)}, u32[]{:S(2)}, u32[]{:S(2)}) collective-permute-start(bf16[128,768]{1,0:T(8,128)(2,1)S(1)} %collective-permute-done.2.refs_3_), channel_id=1, source_target_pairs={{0,1},{1,2},{2,3},{3,4},{4,5},{5,6},{6,7},{8,9},{9,10},{10,11},{11... | collective-permute-start | bytes 589832 | tf_op jit(solution)/shard_map/ppermute | solution.py:384
  48.5 8.4 %collective-permute-start.3 = (bf16[128,768]{1,0:T(8,128)(2,1)S(1)}, bf16[128,768]{1,0:T(8,128)(2,1)S(1)}, u32[]{:S(2)}, u32[]{:S(2)}) collective-permute-start(bf16[128,768]{1,0:T(8,128)(2,1)S(1)} %collective-permute-done.1.refs_2_), channel_id=1, source_target_pairs={{0,1},{1,2},{2,3},{3,4},{4,5},{5,6},{6,7},{8,9},{9,10},{10,11},{11... | collective-permute-start | bytes 589832 | tf_op jit(solution)/shard_map/ppermute | solution.py:384
  56.9 9.8 %collective-permute-start.5 = (bf16[128,768]{1,0:T(8,128)(2,1)S(1)}, bf16[128,768]{1,0:T(8,128)(2,1)S(1)}, u32[]{:S(2)}, u32[]{:S(2)}) collective-permute-start(bf16[128,768]{1,0:T(8,128)(2,1)S(1)} %collective-permute-done.3.refs_1_), channel_id=1, source_target_pairs={{0,1},{1,2},{2,3},{3,4},{4,5},{5,6},{6,7},{8,9},{9,10},{10,11},{11... | collective-permute-start | bytes 589832 | tf_op jit(solution)/shard_map/ppermute | solution.py:384
  62.5 9.8 %collective-permute-start.10 = (bf16[128,768]{1,0:T(8,128)(2,1)S(1)}, bf16[128,768]{1,0:T(8,128)(2,1)S(1)}, u32[]{:S(2)}, u32[]{:S(2)}) collective-permute-start(bf16[128,768]{1,0:T(8,128)(2,1)S(1)} %collective-permute-done.4.refs_2_), channel_id=1, source_target_pairs={{0,1},{1,2},{2,3},{3,4},{4,5},{5,6},{6,7},{8,9},{9,10},{10,11},{11... | collective-permute-start | bytes 589832 | tf_op jit(solution)/shard_map/ppermute | solution.py:384
  66.7 15.7 %collective-permute-start.12 = (bf16[128,512]{1,0:T(8,128)(2,1)S(1)}, bf16[128,512]{1,0:T(8,128)(2,1)S(1)}, u32[]{:S(2)}, u32[]{:S(2)}) collective-permute-start(bf16[128,512]{1,0:T(8,128)(2,1)S(1)} %get-tuple-element.51.refs_4_), channel_id=1, source_target_pairs={{0,1},{1,2},{2,3},{3,4},{4,5},{5,6},{6,7},{8,9},{9,10},{10,11},{11... | collective-permute-start | bytes 393224 | tf_op jit(solution)/shard_map/ppermute | solution.py:384
  72.3 12.1 %collective-permute-start.11 = (bf16[128,768]{1,0:T(8,128)(2,1)S(1)}, bf16[128,768]{1,0:T(8,128)(2,1)S(1)}, u32[]{:S(2)}, u32[]{:S(2)}) collective-permute-start(bf16[128,768]{1,0:T(8,128)(2,1)S(1)} %collective-permute-done.10.refs_1_), channel_id=1, source_target_pairs={{0,1},{1,2},{2,3},{3,4},{4,5},{5,6},{6,7},{8,9},{9,10},{10,11},{11... | collective-permute-start | bytes 589832 | tf_op jit(solution)/shard_map/ppermute | solution.py:384
  74.7 40.5 %all-to-all-start.2 = ((bf16[32,16,1024]{2,1,0:T(8,128)(2,1)}), bf16[32,16,1024]{2,1,0:T(8,128)(2,1)}, u32[]{:S(2)}, u32[]{:S(2)}) async-start(bf16[32,16,1024]{2,1,0:T(8,128)(2,1)} %send_rows.3), calls=%async_computation.2 | async-start | bytes 2097152 | tf_op jit(solution)/shard_map/all_to_all | solution.py:378
  82.4 7.5 %collective-permute-start.13 = (bf16[128,512]{1,0:T(8,128)(2,1)S(1)}, bf16[128,512]{1,0:T(8,128)(2,1)S(1)}, u32[]{:S(2)}, u32[]{:S(2)}) collective-permute-start(bf16[128,512]{1,0:T(8,128)(2,1)S(1)} %collective-permute-done.12.refs_3_), channel_id=1, source_target_pairs={{0,1},{1,2},{2,3},{3,4},{4,5},{5,6},{6,7},{8,9},{9,10},{10,11},{11... | collective-permute-start | bytes 393224 | tf_op jit(solution)/shard_map/ppermute | solution.py:384
  89.9 25.3 %collective-permute-start.18 = (bf16[128,512]{1,0:T(8,128)(2,1)S(1)}, bf16[128,512]{1,0:T(8,128)(2,1)S(1)}, u32[]{:S(2)}, u32[]{:S(2)}) collective-permute-start(bf16[128,512]{1,0:T(8,128)(2,1)S(1)} %collective-permute-done.13.refs_2_), channel_id=1, source_target_pairs={{0,1},{1,2},{2,3},{3,4},{4,5},{5,6},{6,7},{8,9},{9,10},{10,11},{11... | collective-permute-start | bytes 393224 | tf_op jit(solution)/shard_map/ppermute | solution.py:384
  103.0 12.2 %collective-permute-start.6 = (bf16[128,768]{1,0:T(8,128)(2,1)S(1)}, bf16[128,768]{1,0:T(8,128)(2,1)S(1)}, u32[]{:S(2)}, u32[]{:S(2)}) collective-permute-start(bf16[128,768]{1,0:T(8,128)(2,1)S(1)} %get-tuple-element.46), channel_id=1, source_target_pairs={{1,0},{2,1},{3,2},{4,3},{5,4},{6,5},{7,6},{9,8},{10,9},{11,10},{12... | collective-permute-start | bytes 589832 | tf_op jit(solution)/shard_map/ppermute | solution.py:384
  115.3 69.4 %all-to-all-start.3 = ((bf16[32,16,3072]{2,1,0:T(8,128)(2,1)}), bf16[32,16,3072]{2,1,0:T(8,128)(2,1)}, u32[]{:S(2)}, u32[]{:S(2)}) async-start(bf16[32,16,3072]{2,1,0:T(8,128)(2,1)} %get-tuple-element.72), calls=%async_computation.3 | async-start | bytes 6291456 | tf_op jit(solution)/shard_map/all_to_all | solution.py:378
  122.6 10.1 %collective-permute-start.14 = (bf16[128,768]{1,0:T(8,128)(2,1)S(1)}, bf16[128,768]{1,0:T(8,128)(2,1)S(1)}, u32[]{:S(2)}, u32[]{:S(2)}) collective-permute-start(bf16[128,768]{1,0:T(8,128)(2,1)S(1)} %get-tuple-element.54), channel_id=1, source_target_pairs={{1,0},{2,1},{3,2},{4,3},{5,4},{6,5},{7,6},{9,8},{10,9},{11,10},{12... | collective-permute-start | bytes 589832 | tf_op jit(solution)/shard_map/ppermute | solution.py:384
  125.9 16.9 %collective-permute-start.19 = (bf16[128,512]{1,0:T(8,128)(2,1)S(1)}, bf16[128,512]{1,0:T(8,128)(2,1)S(1)}, u32[]{:S(2)}, u32[]{:S(2)}) collective-permute-start(bf16[128,512]{1,0:T(8,128)(2,1)S(1)} %collective-permute-done.18.refs_1_), channel_id=1, source_target_pairs={{0,1},{1,2},{2,3},{3,4},{4,5},{5,6},{6,7},{8,9},{9,10},{10,11},{11... | collective-permute-start | bytes 393224 | tf_op jit(solution)/shard_map/ppermute | solution.py:384
  129.7 10.8 %collective-permute-start.7 = (bf16[128,768]{1,0:T(8,128)(2,1)S(1)}, bf16[128,768]{1,0:T(8,128)(2,1)S(1)}, u32[]{:S(2)}, u32[]{:S(2)}) collective-permute-start(bf16[128,768]{1,0:T(8,128)(2,1)S(1)} %add_convert_fusion.5), channel_id=1, source_target_pairs={{1,0},{2,1},{3,2},{4,3},{5,4},{6,5},{7,6},{9,8},{10,9},{11,10},{12... | collective-permute-start | bytes 589832 | tf_op jit(solution)/shard_map/ppermute | solution.py:384
  132.8 19.2 %collective-permute-start.15 = (bf16[128,768]{1,0:T(8,128)(2,1)S(1)}, bf16[128,768]{1,0:T(8,128)(2,1)S(1)}, u32[]{:S(2)}, u32[]{:S(2)}) collective-permute-start(bf16[128,768]{1,0:T(8,128)(2,1)S(1)} %add_convert_fusion.2), channel_id=1, source_target_pairs={{1,0},{2,1},{3,2},{4,3},{5,4},{6,5},{7,6},{9,8},{10,9},{11,10},{12... | collective-permute-start | bytes 589832 | tf_op jit(solution)/shard_map/ppermute | solution.py:384
  140.5 20.5 %copy-start.8 = (f32[128,768]{1,0:T(8,128)S(1)}, f32[128,768]{1,0:T(8,128)}, u32[]{:S(2)}) copy-start(f32[128,768]{1,0:T(8,128)} %get-tuple-element.49) | copy-start | bytes 1179652
  140.5 20.4 %collective-permute-start.8 = (bf16[128,768]{1,0:T(8,128)(2,1)S(1)}, bf16[128,768]{1,0:T(8,128)(2,1)S(1)}, u32[]{:S(2)}, u32[]{:S(2)}) collective-permute-start(bf16[128,768]{1,0:T(8,128)(2,1)S(1)} %add_convert_fusion.4), channel_id=1, source_target_pairs={{1,0},{2,1},{3,2},{4,3},{5,4},{6,5},{7,6},{9,8},{10,9},{11,10},{12... | collective-permute-start | bytes 589832 | tf_op jit(solution)/shard_map/ppermute | solution.py:384
  150.0 19.1 %copy-start.7 = (f32[128,768]{1,0:T(8,128)S(1)}, f32[128,768]{1,0:T(8,128)}, u32[]{:S(2)}) copy-start(f32[128,768]{1,0:T(8,128)} %get-tuple-element.57) | copy-start | bytes 1179652
  150.0 33.3 %copy-start.1 = (f32[128,768]{1,0:T(8,128)S(1)}, f32[128,768]{1,0:T(8,128)}, u32[]{:S(2)}) copy-start(f32[128,768]{1,0:T(8,128)} %get-tuple-element.66.refs_3_) | copy-start | bytes 1179652
  150.0 33.3 %copy-start.2 = (f32[128,768]{1,0:T(8,128)S(1)}, f32[128,768]{1,0:T(8,128)}, u32[]{:S(2)}) copy-start(f32[128,768]{1,0:T(8,128)} %get-tuple-element.67.refs_4_) | copy-start | bytes 1179652
  150.0 9.0 %collective-permute-start.20 = (bf16[128,512]{1,0:T(8,128)(2,1)S(1)}, bf16[128,512]{1,0:T(8,128)(2,1)S(1)}, u32[]{:S(2)}, u32[]{:S(2)}) collective-permute-start(bf16[128,512]{1,0:T(8,128)(2,1)S(1)} %get-tuple-element.62), channel_id=1, source_target_pairs={{1,0},{2,1},{3,2},{4,3},{5,4},{6,5},{7,6},{9,8},{10,9},{11,10},{12... | collective-permute-start | bytes 393224 | tf_op jit(solution)/shard_map/ppermute | solution.py:384
  152.1 16.9 %collective-permute-start.16 = (bf16[128,768]{1,0:T(8,128)(2,1)S(1)}, bf16[128,768]{1,0:T(8,128)(2,1)S(1)}, u32[]{:S(2)}, u32[]{:S(2)}) collective-permute-start(bf16[128,768]{1,0:T(8,128)(2,1)S(1)} %add_convert_fusion.1), channel_id=1, source_target_pairs={{1,0},{2,1},{3,2},{4,3},{5,4},{6,5},{7,6},{9,8},{10,9},{11,10},{12... | collective-permute-start | bytes 589832 | tf_op jit(solution)/shard_map/ppermute | solution.py:384
  159.0 8.1 %collective-permute-start.21 = (bf16[128,512]{1,0:T(8,128)(2,1)S(1)}, bf16[128,512]{1,0:T(8,128)(2,1)S(1)}, u32[]{:S(2)}, u32[]{:S(2)}) collective-permute-start(bf16[128,512]{1,0:T(8,128)(2,1)S(1)} %add_convert_fusion.8), channel_id=1, source_target_pairs={{1,0},{2,1},{3,2},{4,3},{5,4},{6,5},{7,6},{9,8},{10,9},{11,10},{12... | collective-permute-start | bytes 393224 | tf_op jit(solution)/shard_map/ppermute | solution.py:384
  161.0 16.1 %collective-permute-start.9 = (bf16[128,768]{1,0:T(8,128)(2,1)S(1)}, bf16[128,768]{1,0:T(8,128)(2,1)S(1)}, u32[]{:S(2)}, u32[]{:S(2)}) collective-permute-start(bf16[128,768]{1,0:T(8,128)(2,1)S(1)} %add_convert_fusion.3), channel_id=1, source_target_pairs={{1,0},{2,1},{3,2},{4,3},{5,4},{6,5},{7,6},{9,8},{10,9},{11,10},{12... | collective-permute-start | bytes 589832 | tf_op jit(solution)/shard_map/ppermute | solution.py:384
  167.1 8.1 %collective-permute-start.22 = (bf16[128,512]{1,0:T(8,128)(2,1)S(1)}, bf16[128,512]{1,0:T(8,128)(2,1)S(1)}, u32[]{:S(2)}, u32[]{:S(2)}) collective-permute-start(bf16[128,512]{1,0:T(8,128)(2,1)S(1)} %add_convert_fusion.7), channel_id=1, source_target_pairs={{1,0},{2,1},{3,2},{4,3},{5,4},{6,5},{7,6},{9,8},{10,9},{11,10},{12... | collective-permute-start | bytes 393224 | tf_op jit(solution)/shard_map/ppermute | solution.py:384
  169.1 9.6 %collective-permute-start.17 = (bf16[128,768]{1,0:T(8,128)(2,1)S(1)}, bf16[128,768]{1,0:T(8,128)(2,1)S(1)}, u32[]{:S(2)}, u32[]{:S(2)}) collective-permute-start(bf16[128,768]{1,0:T(8,128)(2,1)S(1)} %add_convert_fusion), channel_id=1, source_target_pairs={{1,0},{2,1},{3,2},{4,3},{5,4},{6,5},{7,6},{9,8},{10,9},{11,10},{12... | collective-permute-start | bytes 589832 | tf_op jit(solution)/shard_map/ppermute | solution.py:384
  175.2 8.1 %collective-permute-start.23 = (bf16[128,512]{1,0:T(8,128)(2,1)S(1)}, bf16[128,512]{1,0:T(8,128)(2,1)S(1)}, u32[]{:S(2)}, u32[]{:S(2)}) collective-permute-start(bf16[128,512]{1,0:T(8,128)(2,1)S(1)} %add_convert_fusion.6), channel_id=1, source_target_pairs={{1,0},{2,1},{3,2},{4,3},{5,4},{6,5},{7,6},{9,8},{10,9},{11,10},{12... | collective-permute-start | bytes 393224 | tf_op jit(solution)/shard_map/ppermute | solution.py:384
  184.6 7.3 %copy-start.3 = (s32[1,1,128]{2,1,0:T(1,128)S(1)}, s32[1,1,128]{2,1,0:T(1,128)}, u32[]{:S(2)}) copy-start(s32[1,1,128]{2,1,0:T(1,128)} %param.16) | copy-start | bytes 1540
  184.6 7.3 %copy-start.4 = (f32[128]{0:T(128)S(1)}, f32[128]{0:T(128)}, u32[]{:S(2)}) copy-start(f32[128]{0:T(128)} %param.13) | copy-start | bytes 1540
  184.6 31.3 %all-to-all-start.4 = ((bf16[32,16,1536]{2,1,0:T(8,128)(2,1)}), bf16[32,16,1536]{2,1,0:T(8,128)(2,1)S(1)}, u32[]{:S(2)}, u32[]{:S(2)}) async-start(bf16[32,16,1536]{2,1,0:T(8,128)(2,1)} %return_kv.1), calls=%async_computation.4 | async-start | bytes 3145728 | tf_op jit(solution)/shard_map/all_to_all | solution.py:378
  192.0 23.9 %copy-start = (bf16[128,1024]{1,0:T(8,128)(2,1)S(1)}, bf16[128,1024]{1,0:T(8,128)(2,1)}, u32[]{:S(2)}) copy-start(bf16[128,1024]{1,0:T(8,128)(2,1)} %refs_1_.1) | copy-start | bytes 786436
  192.0 23.9 %copy-start.5 = (f32[128]{0:T(128)S(1)}, f32[128]{0:T(128)}, u32[]{:S(2)}) copy-start(f32[128]{0:T(128)} %param.14) | copy-start | bytes 1540

commit v5 on v4

v5 whole, which is shorter than its diff:
```python
import functools

import jax
import jax.numpy as jnp
from jax import lax
from jax.experimental import pallas as pl
from jax.experimental.pallas import tpu as pltpu
from jax.sharding import PartitionSpec as P

Q_HEADS = 64
KV_HEADS = 8
HEAD = 128
RATIO = Q_HEADS // KV_HEADS
EPS = 1e-06
ROWS = 128
GROUPS = 32
SHARE = ROWS // GROUPS
SPLIT = 4
CHUNK = SHARE * SPLIT
TALL = GROUPS * CHUNK
WIDE = 2 * HEAD
BACK = 4
WINDOW = (BACK + 1) * ROWS
SCALE = HEAD ** (-0.5)
LOG2E = 1.4426950408889634
SMALL = 2
LARGE = KV_HEADS - SMALL
WEIGHTS = (36, 36)
VMEM_LIMIT = 52 * 1024 * 1024
VMEM_WHOLE = 62 * 1024 * 1024
F32 = jnp.float32
BF16 = jnp.bfloat16


def params(limit=VMEM_LIMIT):
    return pltpu.CompilerParams(vmem_limit_bytes=limit)


def cost(flops, moved, trans=0):
    return pl.CostEstimate(flops=int(flops), bytes_accessed=int(moved), transcendentals=int(trans))


def dot(a, b, dims):
    return lax.dot_general(a, b, (dims, ((), ())), preferred_element_type=F32)


MM = ((1,), (0,))
MT = ((1,), (1,))
TM = ((0,), (0,))


def iota(shape, dim):
    return lax.broadcasted_iota(jnp.int32, shape, dim)


def tall_row(index):
    row = (index // CHUNK) * SHARE + index % SHARE
    part = (index // SHARE) % SPLIT
    return row, part


def home_matrix(order_ref):
    spread_row, _ = tall_row(iota((ROWS, TALL), 1))
    spread = (spread_row == iota((ROWS, TALL), 0)).astype(BF16)
    order = jnp.broadcast_to(order_ref[...].astype(F32), (16, ROWS)).astype(BF16)
    source = dot(order, spread, MM)[:1]
    _, part = tall_row(iota((1, TALL), 1))
    code = source + (part * ROWS).astype(F32)
    return (iota((TALL, TALL), 0).astype(F32) == code).astype(BF16)


def pack_matrix(order_ref):
    row, part = tall_row(iota((TALL, SPLIT * ROWS), 0))
    order = order_ref[...]
    code = jnp.concatenate([order + p * ROWS for p in range(SPLIT)], axis=1)
    return (row + part * ROWS == code).astype(BF16)


def norm(x, gain):
    factor = lax.rsqrt(jnp.mean(x * x, axis=-1, keepdims=True) + EPS)
    return x * factor * gain


def norm_back(x, gain, dy):
    factor = lax.rsqrt(jnp.mean(x * x, axis=-1, keepdims=True) + EPS)
    g = dy * gain
    inner = jnp.mean(x * g, axis=-1, keepdims=True)
    return factor * g - x * (factor * factor * factor * inner)


def head_cols(h):
    return slice(h * HEAD, (h + 1) * HEAD)


def send_rows_step(home, gain, q_ref, d_ref):
    qn = [norm(q_ref[:, head_cols(h)].astype(F32), gain).astype(BF16) for h in range(RATIO)]
    stack = jnp.concatenate(
        [
            jnp.concatenate(
                [qn[2 * p], qn[2 * p + 1], d_ref[:, p * WIDE : (p + 1) * WIDE]], axis=1
            )
            for p in range(SPLIT)
        ],
        axis=0,
    )
    return dot(home, stack, TM).astype(BF16)


def send_kv_step(home, gain, k_ref, v_ref):
    kn = [
        norm(k_ref[:, head_cols(h)].astype(F32), gain).astype(BF16) for h in range(KV_HEADS)
    ]
    half = KV_HEADS * HEAD // 2
    stack = jnp.concatenate(
        [
            jnp.concatenate(kn[: KV_HEADS // 2], axis=1),
            jnp.concatenate(kn[KV_HEADS // 2 :], axis=1),
            v_ref[:, :half],
            v_ref[:, half:],
        ],
        axis=0,
    )
    return dot(home, stack, TM).astype(BF16)


def send_kernel(with_kv, order_ref, gain_ref, q_ref, d_ref, *refs):
    *kv_refs, out_ref, home_ref = refs
    step = pl.program_id(0)

    @pl.when(step == 0)
    def _():
        home_ref[...] = home_matrix(order_ref)

    def rows():
        sent = send_rows_step(home_ref[...], gain_ref[...], q_ref, d_ref)
        out_ref[...] = sent.reshape(out_ref.shape)

    if not with_kv:
        rows()
        return
    last = pl.num_programs(0) - 1
    pl.when(step < last)(rows)

    @pl.when(step == last)
    def _():
        gain, k_ref, v_ref = kv_refs
        sent = send_kv_step(home_ref[...], gain[...], k_ref, v_ref)
        out_ref[...] = sent.reshape(out_ref.shape)


def send(order, gain, query, d_out, first, count, kv=()):
    row = pl.BlockSpec((1, ROWS), lambda h: (0, 0))
    block = pl.BlockSpec((ROWS, RATIO * HEAD), lambda h: (0, jnp.minimum(h, count - 1) + first))
    kv_block = pl.BlockSpec((ROWS, KV_HEADS * HEAD), lambda h: (0, 0))
    parts = count + 1 if kv else count
    return pl.pallas_call(
        functools.partial(send_kernel, bool(kv)),
        grid=(parts,),
        in_specs=[row, row, block, block] + ([row, kv_block, kv_block] if kv else []),
        out_specs=pl.BlockSpec((GROUPS, CHUNK, 2 * WIDE), lambda h: (0, 0, h)),
        out_shape=jax.ShapeDtypeStruct((GROUPS, CHUNK, parts * 2 * WIDE), BF16),
        scratch_shapes=[pltpu.VMEM((TALL, TALL), BF16)],
        compiler_params=params(VMEM_WHOLE),
        cost_estimate=cost(parts * 2 * TALL * TALL * 2 * WIDE, parts << 20),
        name="send",
    )(order, gain, query, d_out, *kv)


def sort_kv_kernel(order_ref, in_ref, *out_refs):
    half = KV_HEADS * HEAD // 2
    rows = dot(pack_matrix(order_ref), in_ref[...].reshape(TALL, half), TM).astype(BF16)
    counts = (SMALL, LARGE)
    places = [(ref, at) for ref, count in zip(out_refs, counts) for at in range(count)]
    for h, (ref, at) in enumerate(places):
        part, cols = h // (KV_HEADS // 2), head_cols(h % (KV_HEADS // 2))
        k = rows[part * ROWS : (part + 1) * ROWS, cols]
        v = rows[(part + 2) * ROWS : (part + 3) * ROWS, cols]
        ref[:, at * WIDE : (at + 1) * WIDE] = jnp.concatenate([k, v], axis=1)


def sort_kv(order, received):
    return pl.pallas_call(
        sort_kv_kernel,
        grid=(1,),
        in_specs=[
            pl.BlockSpec((1, ROWS), lambda i: (0, 0)),
            pl.BlockSpec((GROUPS, CHUNK, 2 * WIDE), lambda i: (0, 0, SMALL)),
        ],
        out_specs=[
            pl.BlockSpec((ROWS, count * WIDE), lambda i: (0, 0)) for count in (SMALL, LARGE)
        ],
        out_shape=[
            jax.ShapeDtypeStruct((ROWS, count * WIDE), BF16) for count in (SMALL, LARGE)
        ],
        compiler_params=params(),
        cost_estimate=cost(2 * TALL**3, 1 << 20),
        name="sort_kv",
    )(order, received)


def attend_kernel(meta_ref, order_ref, qd_ref, *refs):
    kv_refs = refs[: BACK + 1]
    out_ref, *part_refs, bias_ref = refs[-(BACK + 3) :]

    @pl.when(pl.program_id(0) == 0)
    def _():
        places = jnp.broadcast_to(iota((1, ROWS), 1).astype(F32), (16, ROWS)).astype(BF16)
        arrived = (iota((ROWS, ROWS), 0) == order_ref[...]).astype(BF16)
        place = dot(places, arrived, MT).astype(BF16)
        row, _ = tall_row(iota((ROWS, TALL), 1))
        spread = (row == iota((ROWS, TALL), 0)).astype(BF16)
        base = meta_ref[3] * ROWS
        position = dot(place, spread, MM)[:1] + base.astype(F32)
        end0 = meta_ref[0].astype(F32)
        end1 = (meta_ref[0] + meta_ref[1]).astype(F32)
        start = jnp.where(position < end0, 0.0, jnp.where(position < end1, end0, end1))
        key = (iota((WINDOW, TALL), 0) + (base - BACK * ROWS)).astype(F32)
        bias_ref[...] = jnp.where((key >= start) & (key <= position), 0.0, -1e30)

    kw = jnp.concatenate([r[:, :HEAD] for r in kv_refs], axis=0)
    vw = jnp.concatenate([r[:, HEAD:] for r in kv_refs], axis=0)

    def both(low):
        return jnp.concatenate(
            [
                qd_ref[:, :, low + e * HEAD : low + (e + 1) * HEAD].reshape(TALL, HEAD)
                for e in range(2)
            ],
            axis=0,
        )

    q, d = both(0), both(WIDE)
    scores = dot(kw, q, MT)
    d_weights = dot(vw, d, MT)
    bias = bias_ref[...]
    expo = jnp.exp2(scores * (SCALE * LOG2E) + jnp.concatenate([bias, bias], axis=1))
    weights = expo * (1.0 / jnp.sum(expo, axis=0, keepdims=True))
    low_weights = weights.astype(BF16)
    out = dot(vw, low_weights, TM).astype(BF16)
    delta = jnp.sum(d.astype(F32).T * out.astype(F32), axis=0, keepdims=True)
    d_scores = (weights * (d_weights - delta)).astype(BF16)
    dq = (dot(kw, d_scores, TM) * SCALE).astype(BF16)
    dk = dot(d_scores, q, MM) * SCALE
    dv = dot(low_weights, d, MM)
    for low, value in ((0, out.T), (WIDE, dq.T)):
        for e in range(2):
            out_ref[:, :, low + e * HEAD : low + (e + 1) * HEAD] = value[
                e * TALL : (e + 1) * TALL
            ].reshape(GROUPS, CHUNK, HEAD)
    for n, ref in enumerate(part_refs):
        ref[:, :HEAD] = dk[n * ROWS : (n + 1) * ROWS].astype(ref.dtype)
        ref[:, HEAD:] = dv[n * ROWS : (n + 1) * ROWS].astype(ref.dtype)


def attend(meta, order, received, blocks, count, weight):
    kv_spec = pl.BlockSpec((ROWS, WIDE), lambda h: (0, h))
    rows_spec = pl.BlockSpec((GROUPS, CHUNK, 2 * WIDE), lambda h: (0, 0, h))
    elements = count * RATIO * ROWS * WINDOW
    return pl.pallas_call(
        attend_kernel,
        grid=(count,),
        in_specs=[
            pl.BlockSpec(memory_space=pltpu.SMEM),
            pl.BlockSpec((1, ROWS), lambda h: (0, 0)),
            rows_spec,
        ]
        + [kv_spec] * (BACK + 1),
        out_specs=[rows_spec] + [kv_spec] * (BACK + 1),
        out_shape=[jax.ShapeDtypeStruct((GROUPS, CHUNK, count * 2 * WIDE), BF16)]
        + [
            jax.ShapeDtypeStruct((ROWS, count * WIDE), BF16 if n == 0 else F32)
            for n in range(BACK + 1)
        ],
        scratch_shapes=[pltpu.VMEM((WINDOW, TALL), F32)],
        compiler_params=params(),
        cost_estimate=cost(weight * elements * HEAD, count * (3 << 20), elements),
        name="attend",
    )(meta, order, received, *blocks)


def return_kv_kernel(order_ref, *refs):
    half = KV_HEADS * HEAD // 2
    count, out_ref = len(refs) // 2, refs[-1]
    total = jnp.concatenate(
        [
            (got[...].astype(F32) + own[...]).astype(BF16)
            for got, own in zip(refs[:count], refs[count : 2 * count])
        ],
        axis=1,
    )

    def columns(which, part):
        heads = range(part * KV_HEADS // 2, (part + 1) * KV_HEADS // 2)
        return jnp.concatenate([total[:, head_cols(2 * h + which)] for h in heads], axis=1)

    stack = jnp.concatenate(
        [columns(which, part) for which in range(2) for part in range(2)], axis=0
    )
    rows = dot(pack_matrix(order_ref), stack, MM).astype(BF16)
    out_ref[...] = rows.reshape(GROUPS, CHUNK, half)


def return_kv(order, got, own):
    half = KV_HEADS * HEAD // 2
    return pl.pallas_call(
        return_kv_kernel,
        out_shape=jax.ShapeDtypeStruct((GROUPS, CHUNK, half), BF16),
        compiler_params=params(),
        cost_estimate=cost(2 * TALL**3, 3 << 20),
        name="return_kv",
    )(order, *got, *own)


def finish_rows_step(rows, gain, q_ref, out_ref, dq_ref):
    for part in range(SPLIT):
        mine = rows[part * ROWS : (part + 1) * ROWS]
        out_ref[:, part * WIDE : (part + 1) * WIDE] = mine[:, :WIDE].astype(BF16)
        for e in range(2):
            at = head_cols(2 * part + e)
            dy = mine[:, WIDE + e * HEAD : WIDE + (e + 1) * HEAD]
            dq_ref[:, at] = norm_back(q_ref[:, at].astype(F32), gain, dy).astype(BF16)


def finish_rows_kernel(order_ref, gain_ref, q_ref, in_ref, *refs):
    out_ref, dq_ref, home_ref = refs[-3:]

    @pl.when(pl.program_id(0) == 0)
    def _():
        home_ref[...] = home_matrix(order_ref)

    rows = dot(home_ref[...], in_ref[...].reshape(TALL, 2 * WIDE), MM)
    finish_rows_step(rows, gain_ref[...], q_ref, out_ref, dq_ref)


def finish_rows(order, gain, query, received, first, count, earlier=()):
    block = pl.BlockSpec((ROWS, RATIO * HEAD), lambda h: (0, h + first))
    whole = jax.ShapeDtypeStruct((ROWS, Q_HEADS * HEAD), BF16)
    row = pl.BlockSpec((1, ROWS), lambda h: (0, 0))
    return pl.pallas_call(
        finish_rows_kernel,
        grid=(count,),
        in_specs=[row, row, block]
        + [pl.BlockSpec((GROUPS, CHUNK, 2 * WIDE), lambda h: (0, 0, h))]
        + [pl.BlockSpec(memory_space=pl.ANY)] * len(earlier),
        out_specs=[block, block],
        out_shape=[whole, whole],
        scratch_shapes=[pltpu.VMEM((TALL, TALL), BF16)],
        input_output_aliases={4 + n: n for n in range(len(earlier))},
        compiler_params=params(),
        cost_estimate=cost(count * 2 * TALL * TALL * 2 * WIDE, count * (5 << 18)),
        name="finish_rows",
    )(order, gain, query, received, *earlier)


def finish_kv_kernel(order_ref, gain_ref, k_ref, in_ref, dk_ref, dv_ref):
    half = KV_HEADS * HEAD // 2
    gain = gain_ref[...]
    rows = dot(home_matrix(order_ref), in_ref[...].reshape(TALL, half), MM)
    for h in range(KV_HEADS):
        part, cols = h // (KV_HEADS // 2), head_cols(h % (KV_HEADS // 2))
        dy = rows[part * ROWS : (part + 1) * ROWS, cols]
        dk_ref[:, head_cols(h)] = norm_back(
            k_ref[:, head_cols(h)].astype(F32), gain, dy
        ).astype(BF16)
    dv_ref[:, :half] = rows[2 * ROWS : 3 * ROWS].astype(BF16)
    dv_ref[:, half:] = rows[3 * ROWS :].astype(BF16)


def finish_kv(order, gain, key_projection, received):
    whole = jax.ShapeDtypeStruct((ROWS, KV_HEADS * HEAD), BF16)
    return pl.pallas_call(
        finish_kv_kernel,
        out_shape=[whole, whole],
        compiler_params=params(),
        cost_estimate=cost(2 * TALL**3, 3 << 19),
        name="finish_kv",
    )(order, gain, key_projection, received)


def exchange(array):
    return lax.all_to_all(array, "dp", split_axis=0, concat_axis=0, tiled=True)


def along(array, step):
    count = lax.axis_size("seq")
    return lax.ppermute(array, "seq", [(i, (i + step) % count) for i in range(count)])


def after(array, other):
    return array if other is None else lax.optimization_barrier((array, other))[0]


def per_device(
    query, key_projection, value, d_out, q_gain, key_norm_gain, seq_lengths, send_order, recv_order
):
    leaving = send_order.reshape(1, ROWS)
    arriving = recv_order.reshape(1, ROWS)
    q_gain = q_gain.reshape(1, HEAD)
    k_gain = key_norm_gain.reshape(1, HEAD)
    place = lax.axis_index("seq").astype(jnp.int32)
    meta = jnp.concatenate([seq_lengths[0], place[None]])

    sent_small = send(
        leaving, q_gain, query, d_out, 0, SMALL, kv=(k_gain, key_projection, value)
    )
    sent_large = send(leaving, q_gain, query, d_out, SMALL, LARGE)
    small_rows = exchange(sent_small)
    large_rows = exchange(after(sent_large, small_rows))

    small, large = ([block] for block in sort_kv(arriving, small_rows))
    for _ in range(BACK):
        small.append(along(small[-1], 1))
        large.append(along(large[-1], 1))

    def back_along(parts):
        totals = parts[:1]
        for part in parts[1:-1]:
            totals.append((along(totals[-1], -1).astype(F32) + part).astype(BF16))
        return totals + [along(totals[-1], -1)], parts[-1]

    small_result, *parts = attend(meta, arriving, small_rows, small[::-1], SMALL, WEIGHTS[0])
    small_sums, small_own = back_along(parts)
    small_result = after(after(small_result, large_rows), large[BACK - 1])
    small_back = exchange(small_result)
    large[-1] = after(large[-1], small_sums[1])
    large_result, *parts = attend(meta, arriving, large_rows, large[::-1], LARGE, WEIGHTS[1])
    large_sums, large_own = back_along(parts)
    large_back = exchange(after(large_result, small_back))
    kv_back = return_kv(arriving, (small_sums[-1], large_sums[-1]), (small_own, large_own))
    kv_back = exchange(after(kv_back, large_back))

    outs = finish_rows(leaving, q_gain, query, small_back, 0, SMALL)
    outs = finish_rows(leaving, q_gain, query, large_back, SMALL, LARGE, earlier=outs)
    return *outs, *finish_kv(leaving, k_gain, key_projection, kv_back)


def solution(mesh):
    rows = P(("dp", "seq"), None)
    in_specs = (rows, rows, rows, rows, P(), P(), P("dp", None)) + (P("dp", "seq", None),) * 2
    return jax.shard_map(
        per_device, mesh=mesh, in_specs=in_specs, out_specs=(rows,) * 4, check_vma=False
    )
```

time: 222 us -> 214 us (0.964)
  the two profiles are of different devices: /device:TPU:96 before, /device:TPU:1 now
where the time goes in v5:
time: 214 us; the launch traced here: 213 us
  waiting for transfers between devices  95.7 us (45%)
  starting transfers between devices  61.9 us (29%)
  Pallas kernels  51.1 us (24%)
    ppermute x16, waiting for transfers between devices, along(): lax.ppermute(array, 'seq', [(i, (i + step) % count) for i in range(count)])  79.2 us
    all_to_all x5, starting transfers between devices, exchange(): return lax.all_to_all(array, 'dp', split_axis=0, concat_axis=0, tiled=True)  46.2 us
    pallas_call x2, Pallas kernels, attend(): pl.pallas_call(attend_kernel, grid=(count,), in_specs=[pl.BlockSpec(memor...  24.1 us
    all_to_all x5, waiting for transfers between devices, exchange(): return lax.all_to_all(array, 'dp', split_axis=0, concat_axis=0, tiled=True)  16.6 us
    ppermute x16, starting transfers between devices, along(): lax.ppermute(array, 'seq', [(i, (i + step) % count) for i in range(count)])  15.8 us
    pallas_call x2, Pallas kernels, send(): pl.pallas_call(functools.partial(send_kernel, bool(kv)), grid=(parts,), i...  11.6 us
    pallas_call x2, Pallas kernels, finish_rows(): pl.pallas_call(finish_rows_kernel, grid=(count,), in_specs=[row, row, blo...  9.95 us
  transfers between devices with their start and end apart: 21, of which 13 were waited for; matrix products, arithmetic and copies ran while one was open for 1% of the time, Pallas kernels for 18%

profile of v5, /device:TPU:1, one launch (start us, length us, event | category | flops | bytes accessed | tf_op | source)
XLA Modules:
  0.0 212.9 jit_solution(10125011107566285633)
XLA Ops:
  0.6 4.4 %send.3 = bf16[32,16,1536]{2,1,0:T(8,128)(2,1)} custom-call(s32[1,128]{1,0:T(1,128)} %bitcast.10, f32[1,128]{1,0:T(1,128)} %bitcast.6, bf16[128,8192]{1,0:T(8,128)(2,1)} %q_ref.7, bf16[128,8192]{1,0:T(8,128)(2,1)} %d_ref.3, f32[1,128]{1,0:T(1,128)} %bitcast.19, bf16[128,1024]{1,0:T(8,128)(2,1)} %k_ref.1, bf16[128,1024]{1,0:T(8,128)(2,1)} %refs_2_.1), custom_call_target="tpu_custom_call" | custom-call | flops 805306368 | bytes 3145728 | tf_op jit(solution)/shard_map/send/pallas_call | solution.py:156
  5.0 8.6 %all-to-all-start = ((bf16[32,16,1536]{2,1,0:T(8,128)(2,1)}), bf16[32,16,1536]{2,1,0:T(8,128)(2,1)S(1)}, u32[]{:S(2)}, u32[]{:S(2)}) async-start(bf16[32,16,1536]{2,1,0:T(8,128)(2,1)} %send.3), calls=%async_computation | async-start | bytes 3145728 | tf_op jit(solution)/shard_map/all_to_all | solution.py:381
  13.6 7.2 %send.2 = bf16[32,16,3072]{2,1,0:T(8,128)(2,1)} custom-call(s32[1,128]{1,0:T(1,128)} %bitcast.11, f32[1,128]{1,0:T(1,128)} %bitcast.7, bf16[128,8192]{1,0:T(8,128)(2,1)} %q_ref.7, bf16[128,8192]{1,0:T(8,128)(2,1)} %d_ref.3), custom_call_target="tpu_custom_call" | custom-call | flops 1610612736 | bytes 6291456 | tf_op jit(solution)/shard_map/send/pallas_call | solution.py:156
  20.8 15.0 %all-to-all-done.in_ref.qd_ref = bf16[32,16,1536]{2,1,0:T(8,128)(2,1)S(1)} async-done(((bf16[32,16,1536]{2,1,0:T(8,128)(2,1)}), bf16[32,16,1536]{2,1,0:T(8,128)(2,1)S(1)}, u32[]{:S(2)}, u32[]{:S(2)}) %all-to-all-start) | async-done | bytes 1572896 | tf_op jit(solution)/shard_map/all_to_all | solution.py:381
  35.8 1.1 copy-done.8
  36.9 6.4 %all-to-all-start.1 = ((bf16[32,16,3072]{2,1,0:T(8,128)(2,1)}), bf16[32,16,3072]{2,1,0:T(8,128)(2,1)}, u32[]{:S(2)}, u32[]{:S(2)}) async-start(bf16[32,16,3072]{2,1,0:T(8,128)(2,1)} %send.2), calls=%async_computation.1 | async-start | bytes 6291456 | tf_op jit(solution)/shard_map/all_to_all | solution.py:381
  43.3 0.0 copy-done.3
  43.3 1.6 sort_kv.1
  44.9 0.0 copy-start.5
  44.9 1.7 collective-permute-start
  46.6 13.2 %collective-permute-done.refs_3_ = bf16[128,1536]{1,0:T(8,128)(2,1)S(1)} collective-permute-done((bf16[128,1536]{1,0:T(8,128)(2,1)S(1)}, bf16[128,1536]{1,0:T(8,128)(2,1)S(1)}, u32[]{:S(2)}, u32[]{:S(2)}) %collective-permute-start) | collective-permute-done | bytes 393248 | tf_op jit(solution)/shard_map/ppermute | solution.py:386
  59.8 0.0 collective-permute-start.1
  59.8 0.0 collective-permute-start.4
  59.8 13.9 %collective-permute-done.4.refs_3_ = bf16[128,512]{1,0:T(8,128)(2,1)S(1)} collective-permute-done((bf16[128,512]{1,0:T(8,128)(2,1)S(1)}, bf16[128,512]{1,0:T(8,128)(2,1)S(1)}, u32[]{:S(2)}, u32[]{:S(2)}) %collective-permute-start.4) | collective-permute-done | bytes 131104 | tf_op jit(solution)/shard_map/ppermute | solution.py:386
  73.8 0.0 collective-permute-start.5
  73.8 0.0 collective-permute-done.1.refs_2_
  73.8 0.0 collective-permute-start.2
  73.8 5.4 %collective-permute-done.5.refs_2_ = bf16[128,512]{1,0:T(8,128)(2,1)S(1)} collective-permute-done((bf16[128,512]{1,0:T(8,128)(2,1)S(1)}, bf16[128,512]{1,0:T(8,128)(2,1)S(1)}, u32[]{:S(2)}, u32[]{:S(2)}) %collective-permute-start.5) | collective-permute-done | bytes 131104 | tf_op jit(solution)/shard_map/ppermute | solution.py:386
  79.2 0.0 collective-permute-start.6
  79.2 10.4 %collective-permute-done.6.refs_1_ = bf16[128,512]{1,0:T(8,128)(2,1)S(1)} collective-permute-done((bf16[128,512]{1,0:T(8,128)(2,1)S(1)}, bf16[128,512]{1,0:T(8,128)(2,1)S(1)}, u32[]{:S(2)}, u32[]{:S(2)}) %collective-permute-start.6) | collective-permute-done | bytes 131104 | tf_op jit(solution)/shard_map/ppermute | solution.py:386
  89.6 0.0 collective-permute-start.7
  89.6 0.1 pad_add_fusion.meta_ref
  89.7 0.0 collective-permute-done.2.refs_1_
  89.7 0.0 collective-permute-start.3
  89.7 4.9 %collective-permute-done.7.refs_0_ = bf16[128,512]{1,0:T(8,128)(2,1)S(1)} collective-permute-done((bf16[128,512]{1,0:T(8,128)(2,1)S(1)}, bf16[128,512]{1,0:T(8,128)(2,1)S(1)}, u32[]{:S(2)}, u32[]{:S(2)}) %collective-permute-start.7) | collective-permute-done | bytes 131104 | tf_op jit(solution)/shard_map/ppermute | solution.py:386
  94.6 7.1 %attend.2 = (bf16[32,16,1024]{2,1,0:T(8,128)(2,1)}, bf16[128,512]{1,0:T(8,128)(2,1)S(1)}, f32[128,512]{1,0:T(8,128)S(1)}, f32[128,512]{1,0:T(8,128)S(1)}, f32[12...) custom-call(s32[4]{0:T(128)S(1)} %pad_add_fusion.meta_ref, s32[1,128]{1,0:T(1,128)S(1)} %bitcast.16, ...), custom_call_target="tpu_custom_call" | custom-call | flops 6039797760 | bytes 6291456 | tf_op jit(solution)/shard_map/attend/pallas_call | solution.py:259
  101.7 0.0 collective-permute-start.8
  101.7 3.8 %collective-permute-done.8 = bf16[128,512]{1,0:T(8,128)(2,1)S(1)} collective-permute-done((bf16[128,512]{1,0:T(8,128)(2,1)S(1)}, bf16[128,512]{1,0:T(8,128)(2,1)S(1)}, u32[]{:S(2)}, u32[]{:S(2)}) %collective-permute-start.8) | collective-permute-done | bytes 131104 | tf_op jit(solution)/shard_map/ppermute | solution.py:386
  105.6 0.0 collective-permute-done.3.refs_0_
  105.6 0.0 copy-start.6
  105.6 0.7 copy-done.6
  106.3 0.0 all-to-all-done.1.qd_ref
  106.4 13.7 %all-to-all-start.2 = ((bf16[32,16,1024]{2,1,0:T(8,128)(2,1)}), bf16[32,16,1024]{2,1,0:T(8,128)(2,1)S(1)}, u32[]{:S(2)}, u32[]{:S(2)}) async-start(bf16[32,16,1024]{2,1,0:T(8,128)(2,1)} %get-tuple-element.39), calls=%async_computation.2 | async-start | bytes 2097152 | tf_op jit(solution)/shard_map/all_to_all | solution.py:381
  120.1 17.0 %attend.3 = (bf16[32,16,3072]{2,1,0:T(8,128)(2,1)}, bf16[128,1536]{1,0:T(8,128)(2,1)}, f32[128,1536]{1,0:T(8,128)}, f32[128,1536]{1,0:T(8,128)}, f32[128,1536]{1,0:T(8,128)}, /*index=5*/f32[128,1536]{1,0:T(8,128)}) custom-call(s32[4]{0:T(128)S(1)} %pad_add_fusion.meta_ref, s32[1,128]{1,0:T(1,128)S(1)} %bitcast.17, ...), custom_call_target="tpu_custom_call" | custom-call | flops 18119393280 | bytes 18874368 | tf_op jit(solution)/shard_map/attend/pallas_call | solution.py:259
  137.1 1.0 collective-permute-start.12
  138.1 0.0 all-to-all-done.2.in_ref
  138.1 7.8 %all-to-all-start.3 = ((bf16[32,16,3072]{2,1,0:T(8,128)(2,1)}), bf16[32,16,3072]{2,1,0:T(8,128)(2,1)}, u32[]{:S(2)}, u32[]{:S(2)}) async-start(bf16[32,16,3072]{2,1,0:T(8,128)(2,1)} %get-tuple-element.40), calls=%async_computation.3 | async-start | bytes 6291456 | tf_op jit(solution)/shard_map/all_to_all | solution.py:381
  145.9 2.0 collective-permute-done.12
  147.9 1.1 add_convert_fusion.2
  149.0 2.2 %collective-permute-start.13 = (bf16[128,1536]{1,0:T(8,128)(2,1)S(1)}, bf16[128,1536]{1,0:T(8,128)(2,1)S(1)}, u32[]{:S(2)}, u32[]{:S(2)}) collective-permute-start(bf16[128,1536]{1,0:T(8,128)(2,1)S(1)} %add_convert_fusion.2), channel_id=1, source_target_pairs={{0,7},{1,0},{2,1},{3,2},{4,3},{5,4},{6,5},{7,6},{8,15},{9,8},{10,9... | collective-permute-start | bytes 1179656 | tf_op jit(solution)/shard_map/ppermute | solution.py:386
  151.2 7.5 %collective-permute-done.13 = bf16[128,1536]{1,0:T(8,128)(2,1)S(1)} collective-permute-done((bf16[128,1536]{1,0:T(8,128)(2,1)S(1)}, bf16[128,1536]{1,0:T(8,128)(2,1)S(1)}, u32[]{:S(2)}, u32[]{:S(2)}) %collective-permute-start.13) | collective-permute-done | bytes 393248 | tf_op jit(solution)/shard_map/ppermute | solution.py:386
  158.8 0.1 add_convert_fusion.1
  158.8 3.4 %collective-permute-start.14 = (bf16[128,1536]{1,0:T(8,128)(2,1)S(1)}, bf16[128,1536]{1,0:T(8,128)(2,1)S(1)}, u32[]{:S(2)}, u32[]{:S(2)}) collective-permute-start(bf16[128,1536]{1,0:T(8,128)(2,1)S(1)} %add_convert_fusion.1), channel_id=1, source_target_pairs={{0,7},{1,0},{2,1},{3,2},{4,3},{5,4},{6,5},{7,6},{8,15},{9,8},{10,9... | collective-permute-start | bytes 1179656 | tf_op jit(solution)/shard_map/ppermute | solution.py:386
  162.3 0.1 collective-permute-start.9
  162.4 9.3 %collective-permute-done.9 = bf16[128,512]{1,0:T(8,128)(2,1)S(1)} collective-permute-done((bf16[128,512]{1,0:T(8,128)(2,1)S(1)}, bf16[128,512]{1,0:T(8,128)(2,1)S(1)}, u32[]{:S(2)}, u32[]{:S(2)}) %collective-permute-start.9) | collective-permute-done | bytes 131104 | tf_op jit(solution)/shard_map/ppermute | solution.py:386
  171.6 3.6 %collective-permute-start.10 = (bf16[128,512]{1,0:T(8,128)(2,1)S(1)}, bf16[128,512]{1,0:T(8,128)(2,1)S(1)}, u32[]{:S(2)}, u32[]{:S(2)}) collective-permute-start(bf16[128,512]{1,0:T(8,128)(2,1)S(1)} %add_convert_fusion.4), channel_id=1, source_target_pairs={{0,7},{1,0},{2,1},{3,2},{4,3},{5,4},{6,5},{7,6},{8,15},{9,8},{10,9... | collective-permute-start | bytes 393224 | tf_op jit(solution)/shard_map/ppermute | solution.py:386
  175.2 0.0 collective-permute-done.14
  175.2 0.0 copy-done.9
  175.2 0.1 add_convert_fusion
  175.3 0.0 copy-start.1
  175.3 0.0 copy-start.2
  175.3 0.1 collective-permute-start.15
  175.4 1.7 collective-permute-done.10
  177.2 3.6 %collective-permute-start.11 = (bf16[128,512]{1,0:T(8,128)(2,1)S(1)}, bf16[128,512]{1,0:T(8,128)(2,1)S(1)}, u32[]{:S(2)}, u32[]{:S(2)}) collective-permute-start(bf16[128,512]{1,0:T(8,128)(2,1)S(1)} %add_convert_fusion.3), channel_id=1, source_target_pairs={{0,7},{1,0},{2,1},{3,2},{4,3},{5,4},{6,5},{7,6},{8,15},{9,8},{10,9... | collective-permute-start | bytes 393224 | tf_op jit(solution)/shard_map/ppermute | solution.py:386
  180.8 7.0 %collective-permute-done.11.refs_0_ = bf16[128,512]{1,0:T(8,128)(2,1)S(1)} collective-permute-done((bf16[128,512]{1,0:T(8,128)(2,1)S(1)}, bf16[128,512]{1,0:T(8,128)(2,1)S(1)}, u32[]{:S(2)}, u32[]{:S(2)}) %collective-permute-start.11) | collective-permute-done | bytes 131104 | tf_op jit(solution)/shard_map/ppermute | solution.py:386
  187.8 0.0 collective-permute-done.15.refs_1_
  187.8 2.5 %return_kv.1 = bf16[32,16,512]{2,1,0:T(8,128)(2,1)} custom-call(s32[1,128]{1,0:T(1,128)S(1)} %bitcast.18, bf16[128,512]{1,0:T(8,128)(2,1)S(1)} %collective-permute-done.11.refs_0_, bf16[128,1536]{1,0:T(8,128)(2,1)S(1)} %collective-permute-done.15.refs_1_, f32[128,512]{1,0:T(8,128)S(1)} %get-tuple-element.51.refs_2_, f32[128,1536]{1,0:T(8,128)} %get-tuple-element.52.refs_3_), custom_call_target="tpu_custom_call" | custom-call | flops 268435456 | bytes 3145728 | tf_op jit(solution)/shard_map/return_kv/pallas_call | solution.py:305
  190.3 0.0 all-to-all-done.3.in_ref
  190.3 9.7 %all-to-all-start.4 = ((bf16[32,16,512]{2,1,0:T(8,128)(2,1)}), bf16[32,16,512]{2,1,0:T(8,128)(2,1)S(1)}, u32[]{:S(2)}, u32[]{:S(2)}) async-start(bf16[32,16,512]{2,1,0:T(8,128)(2,1)} %return_kv.1), calls=%async_computation.4 | async-start | bytes 1048576 | tf_op jit(solution)/shard_map/all_to_all | solution.py:381
  199.9 3.0 %finish_rows.2 = (bf16[128,8192]{1,0:T(8,128)(2,1)}, bf16[128,8192]{1,0:T(8,128)(2,1)}) custom-call(s32[1,128]{1,0:T(1,128)S(1)} %bitcast.12, f32[1,128]{1,0:T(1,128)S(1)} %bitcast.8, bf16[128,8192]{1,0:T(8,128)(2,1)} %q_ref.7, bf16[32,16,1024]{2,1,0:T(8,128)(2,1)S(1)} %all-to-all-done.2.in_ref), custom_call_target="tpu_custom_call" | custom-call | flops 536870912 | bytes 2621440 | tf_op jit(solution)/shard_map/finish_rows/pallas_call | solution.py:339
  203.0 6.9 %finish_rows.3 = (bf16[128,8192]{1,0:T(8,128)(2,1)}, bf16[128,8192]{1,0:T(8,128)(2,1)}) custom-call(s32[1,128]{1,0:T(1,128)S(1)} %bitcast.13, f32[1,128]{1,0:T(1,128)S(1)} %bitcast.9, bf16[128,8192]{1,0:T(8,128)(2,1)} %q_ref.7, bf16[32,16,3072]{2,1,0:T(8,128)(2,1)} %all-to-all-done.3.in_ref, ...), custom_call_target="tpu_custom_call", output_to_operand_aliasing={{0}: (4, {}), {1}: (5, {})} | custom-call | flops 1610612736 | bytes 7864320 | tf_op jit(solution)/shard_map/finish_rows/pallas_call | solution.py:339
  209.9 1.6 all-to-all-done.4.in_ref
  211.5 0.0 copy-done.4
  211.5 1.4 finish_kv.1
  (20 shorter events, 0.1 us)
Async XLA Ops:
  5.0 30.8 %all-to-all-start = ((bf16[32,16,1536]{2,1,0:T(8,128)(2,1)}), bf16[32,16,1536]{2,1,0:T(8,128)(2,1)S(1)}, u32[]{:S(2)}, u32[]{:S(2)}) async-start(bf16[32,16,1536]{2,1,0:T(8,128)(2,1)} %send.3), calls=%async_computation | async-start | bytes 3145728 | tf_op jit(solution)/shard_map/all_to_all | solution.py:381
  20.8 22.5 %copy-start.3 = (s32[1,1,128]{2,1,0:T(1,128)S(1)}, s32[1,1,128]{2,1,0:T(1,128)}, u32[]{:S(2)}) copy-start(s32[1,1,128]{2,1,0:T(1,128)} %param.17) | copy-start | bytes 1540
  20.8 68.8 %copy-start.12 = (s32[1,3]{1,0:T(1,128)S(1)}, s32[1,3]{1,0:T(1,128)}, u32[]{:S(2)}) copy-start(s32[1,3]{1,0:T(1,128)} %param.15) | copy-start | bytes 40
  35.8 1.1 copy-start.8
  36.9 69.4 %all-to-all-start.1 = ((bf16[32,16,3072]{2,1,0:T(8,128)(2,1)}), bf16[32,16,3072]{2,1,0:T(8,128)(2,1)}, u32[]{:S(2)}, u32[]{:S(2)}) async-start(bf16[32,16,3072]{2,1,0:T(8,128)(2,1)} %send.2), calls=%async_computation.1 | async-start | bytes 6291456 | tf_op jit(solution)/shard_map/all_to_all | solution.py:381
  44.9 56.8 %copy-start.5 = (bf16[128,1536]{1,0:T(8,128)(2,1)}, bf16[128,1536]{1,0:T(8,128)(2,1)S(1)}, u32[]{:S(2)}) copy-start(bf16[128,1536]{1,0:T(8,128)(2,1)S(1)} %get-tuple-element.31.refs_4_) | copy-start | bytes 1179652
  44.9 14.9 %collective-permute-start = (bf16[128,1536]{1,0:T(8,128)(2,1)S(1)}, bf16[128,1536]{1,0:T(8,128)(2,1)S(1)}, u32[]{:S(2)}, u32[]{:S(2)}) collective-permute-start(bf16[128,1536]{1,0:T(8,128)(2,1)S(1)} %get-tuple-element.31.refs_4_), channel_id=1, source_target_pairs={{0,1},{1,2},{2,3},{3,4},{4,5},{5,6},{6,7},{7,0},{8,9},{9,10},{10,1... | collective-permute-start | bytes 1179656 | tf_op jit(solution)/shard_map/ppermute | solution.py:386
  59.8 13.9 %collective-permute-start.1 = (bf16[128,1536]{1,0:T(8,128)(2,1)S(1)}, bf16[128,1536]{1,0:T(8,128)(2,1)S(1)}, u32[]{:S(2)}, u32[]{:S(2)}) collective-permute-start(bf16[128,1536]{1,0:T(8,128)(2,1)S(1)} %collective-permute-done.refs_3_), channel_id=1, source_target_pairs={{0,1},{1,2},{2,3},{3,4},{4,5},{5,6},{6,7},{7,0},{8,9},{9,10},{10,1... | collective-permute-start | bytes 1179656 | tf_op jit(solution)/shard_map/ppermute | solution.py:386
  59.8 13.9 %collective-permute-start.4 = (bf16[128,512]{1,0:T(8,128)(2,1)S(1)}, bf16[128,512]{1,0:T(8,128)(2,1)S(1)}, u32[]{:S(2)}, u32[]{:S(2)}) collective-permute-start(bf16[128,512]{1,0:T(8,128)(2,1)S(1)} %get-tuple-element.32.refs_4_), channel_id=1, source_target_pairs={{0,1},{1,2},{2,3},{3,4},{4,5},{5,6},{6,7},{7,0},{8,9},{9,10},{10,1... | collective-permute-start | bytes 393224 | tf_op jit(solution)/shard_map/ppermute | solution.py:386
  73.8 5.4 %collective-permute-start.5 = (bf16[128,512]{1,0:T(8,128)(2,1)S(1)}, bf16[128,512]{1,0:T(8,128)(2,1)S(1)}, u32[]{:S(2)}, u32[]{:S(2)}) collective-permute-start(bf16[128,512]{1,0:T(8,128)(2,1)S(1)} %collective-permute-done.4.refs_3_), channel_id=1, source_target_pairs={{0,1},{1,2},{2,3},{3,4},{4,5},{5,6},{6,7},{7,0},{8,9},{9,10},{10,1... | collective-permute-start | bytes 393224 | tf_op jit(solution)/shard_map/ppermute | solution.py:386
  73.8 15.9 %collective-permute-start.2 = (bf16[128,1536]{1,0:T(8,128)(2,1)S(1)}, bf16[128,1536]{1,0:T(8,128)(2,1)S(1)}, u32[]{:S(2)}, u32[]{:S(2)}) collective-permute-start(bf16[128,1536]{1,0:T(8,128)(2,1)S(1)} %collective-permute-done.1.refs_2_), channel_id=1, source_target_pairs={{0,1},{1,2},{2,3},{3,4},{4,5},{5,6},{6,7},{7,0},{8,9},{9,10},{10,1... | collective-permute-start | bytes 1179656 | tf_op jit(solution)/shard_map/ppermute | solution.py:386
  79.2 10.4 %collective-permute-start.6 = (bf16[128,512]{1,0:T(8,128)(2,1)S(1)}, bf16[128,512]{1,0:T(8,128)(2,1)S(1)}, u32[]{:S(2)}, u32[]{:S(2)}) collective-permute-start(bf16[128,512]{1,0:T(8,128)(2,1)S(1)} %collective-permute-done.5.refs_2_), channel_id=1, source_target_pairs={{0,1},{1,2},{2,3},{3,4},{4,5},{5,6},{6,7},{7,0},{8,9},{9,10},{10,1... | collective-permute-start | bytes 393224 | tf_op jit(solution)/shard_map/ppermute | solution.py:386
  89.6 5.0 %collective-permute-start.7 = (bf16[128,512]{1,0:T(8,128)(2,1)S(1)}, bf16[128,512]{1,0:T(8,128)(2,1)S(1)}, u32[]{:S(2)}, u32[]{:S(2)}) collective-permute-start(bf16[128,512]{1,0:T(8,128)(2,1)S(1)} %collective-permute-done.6.refs_1_), channel_id=1, source_target_pairs={{0,1},{1,2},{2,3},{3,4},{4,5},{5,6},{6,7},{7,0},{8,9},{9,10},{10,1... | collective-permute-start | bytes 393224 | tf_op jit(solution)/shard_map/ppermute | solution.py:386
  89.7 15.9 %collective-permute-start.3 = (bf16[128,1536]{1,0:T(8,128)(2,1)S(1)}, bf16[128,1536]{1,0:T(8,128)(2,1)S(1)}, u32[]{:S(2)}, u32[]{:S(2)}) collective-permute-start(bf16[128,1536]{1,0:T(8,128)(2,1)S(1)} %collective-permute-done.2.refs_1_), channel_id=1, source_target_pairs={{0,1},{1,2},{2,3},{3,4},{4,5},{5,6},{6,7},{7,0},{8,9},{9,10},{10,1... | collective-permute-start | bytes 1179656 | tf_op jit(solution)/shard_map/ppermute | solution.py:386
  101.7 3.8 %collective-permute-start.8 = (bf16[128,512]{1,0:T(8,128)(2,1)S(1)}, bf16[128,512]{1,0:T(8,128)(2,1)S(1)}, u32[]{:S(2)}, u32[]{:S(2)}) collective-permute-start(bf16[128,512]{1,0:T(8,128)(2,1)S(1)} %get-tuple-element.33), channel_id=1, source_target_pairs={{0,7},{1,0},{2,1},{3,2},{4,3},{5,4},{6,5},{7,6},{8,15},{9,8},{10,9... | collective-permute-start | bytes 393224 | tf_op jit(solution)/shard_map/ppermute | solution.py:386
  105.6 0.7 copy-start.6
  106.4 13.7 %copy-start.7 = (bf16[128,1536]{1,0:T(8,128)(2,1)S(1)}, bf16[128,1536]{1,0:T(8,128)(2,1)}, u32[]{:S(2)}) copy-start(bf16[128,1536]{1,0:T(8,128)(2,1)} %copy-done.6) | copy-start | bytes 1179652
  106.4 31.7 %all-to-all-start.2 = ((bf16[32,16,1024]{2,1,0:T(8,128)(2,1)}), bf16[32,16,1024]{2,1,0:T(8,128)(2,1)S(1)}, u32[]{:S(2)}, u32[]{:S(2)}) async-start(bf16[32,16,1024]{2,1,0:T(8,128)(2,1)} %get-tuple-element.39), calls=%async_computation.2 | async-start | bytes 2097152 | tf_op jit(solution)/shard_map/all_to_all | solution.py:381
  137.1 10.9 %collective-permute-start.12 = (bf16[128,1536]{1,0:T(8,128)(2,1)}, bf16[128,1536]{1,0:T(8,128)(2,1)}, u32[]{:S(2)}, u32[]{:S(2)}) collective-permute-start(bf16[128,1536]{1,0:T(8,128)(2,1)} %get-tuple-element.47), channel_id=1, source_target_pairs={{0,7},{1,0},{2,1},{3,2},{4,3},{5,4},{6,5},{7,6},{8,15},{9,8},{10,9... | collective-permute-start | bytes 1179656 | tf_op jit(solution)/shard_map/ppermute | solution.py:386
  138.1 9.9 %copy-start.11 = (f32[128,1536]{1,0:T(8,128)S(1)}, f32[128,1536]{1,0:T(8,128)}, u32[]{:S(2)}) copy-start(f32[128,1536]{1,0:T(8,128)} %get-tuple-element.48) | copy-start | bytes 2359300
  138.1 52.2 %all-to-all-start.3 = ((bf16[32,16,3072]{2,1,0:T(8,128)(2,1)}), bf16[32,16,3072]{2,1,0:T(8,128)(2,1)}, u32[]{:S(2)}, u32[]{:S(2)}) async-start(bf16[32,16,3072]{2,1,0:T(8,128)(2,1)} %get-tuple-element.40), calls=%async_computation.3 | async-start | bytes 6291456 | tf_op jit(solution)/shard_map/all_to_all | solution.py:381
  145.9 12.8 %copy-start.10 = (f32[128,1536]{1,0:T(8,128)S(1)}, f32[128,1536]{1,0:T(8,128)}, u32[]{:S(2)}) copy-start(f32[128,1536]{1,0:T(8,128)} %get-tuple-element.49) | copy-start | bytes 2359300
  145.9 29.3 %copy-start.9 = (f32[128,1536]{1,0:T(8,128)S(1)}, f32[128,1536]{1,0:T(8,128)}, u32[]{:S(2)}) copy-start(f32[128,1536]{1,0:T(8,128)} %get-tuple-element.50) | copy-start | bytes 2359300
  149.0 9.7 %collective-permute-start.13 = (bf16[128,1536]{1,0:T(8,128)(2,1)S(1)}, bf16[128,1536]{1,0:T(8,128)(2,1)S(1)}, u32[]{:S(2)}, u32[]{:S(2)}) collective-permute-start(bf16[128,1536]{1,0:T(8,128)(2,1)S(1)} %add_convert_fusion.2), channel_id=1, source_target_pairs={{0,7},{1,0},{2,1},{3,2},{4,3},{5,4},{6,5},{7,6},{8,15},{9,8},{10,9... | collective-permute-start | bytes 1179656 | tf_op jit(solution)/shard_map/ppermute | solution.py:386
  158.8 16.4 %collective-permute-start.14 = (bf16[128,1536]{1,0:T(8,128)(2,1)S(1)}, bf16[128,1536]{1,0:T(8,128)(2,1)S(1)}, u32[]{:S(2)}, u32[]{:S(2)}) collective-permute-start(bf16[128,1536]{1,0:T(8,128)(2,1)S(1)} %add_convert_fusion.1), channel_id=1, source_target_pairs={{0,7},{1,0},{2,1},{3,2},{4,3},{5,4},{6,5},{7,6},{8,15},{9,8},{10,9... | collective-permute-start | bytes 1179656 | tf_op jit(solution)/shard_map/ppermute | solution.py:386
  162.3 9.4 %collective-permute-start.9 = (bf16[128,512]{1,0:T(8,128)(2,1)S(1)}, bf16[128,512]{1,0:T(8,128)(2,1)S(1)}, u32[]{:S(2)}, u32[]{:S(2)}) collective-permute-start(bf16[128,512]{1,0:T(8,128)(2,1)S(1)} %add_convert_fusion.5), channel_id=1, source_target_pairs={{0,7},{1,0},{2,1},{3,2},{4,3},{5,4},{6,5},{7,6},{8,15},{9,8},{10,9... | collective-permute-start | bytes 393224 | tf_op jit(solution)/shard_map/ppermute | solution.py:386
  171.6 5.5 %collective-permute-start.10 = (bf16[128,512]{1,0:T(8,128)(2,1)S(1)}, bf16[128,512]{1,0:T(8,128)(2,1)S(1)}, u32[]{:S(2)}, u32[]{:S(2)}) collective-permute-start(bf16[128,512]{1,0:T(8,128)(2,1)S(1)} %add_convert_fusion.4), channel_id=1, source_target_pairs={{0,7},{1,0},{2,1},{3,2},{4,3},{5,4},{6,5},{7,6},{8,15},{9,8},{10,9... | collective-permute-start | bytes 393224 | tf_op jit(solution)/shard_map/ppermute | solution.py:386
  175.3 24.6 %copy-start.1 = (f32[128]{0:T(128)S(1)}, f32[128]{0:T(128)}, u32[]{:S(2)}) copy-start(f32[128]{0:T(128)} %param.13) | copy-start | bytes 1540
  175.3 24.6 %copy-start.2 = (s32[1,1,128]{2,1,0:T(1,128)S(1)}, s32[1,1,128]{2,1,0:T(1,128)}, u32[]{:S(2)}) copy-start(s32[1,1,128]{2,1,0:T(1,128)} %param.16) | copy-start | bytes 1540
  175.3 12.4 %collective-permute-start.15 = (bf16[128,1536]{1,0:T(8,128)(2,1)S(1)}, bf16[128,1536]{1,0:T(8,128)(2,1)S(1)}, u32[]{:S(2)}, u32[]{:S(2)}) collective-permute-start(bf16[128,1536]{1,0:T(8,128)(2,1)S(1)} %add_convert_fusion), channel_id=1, source_target_pairs={{0,7},{1,0},{2,1},{3,2},{4,3},{5,4},{6,5},{7,6},{8,15},{9,8},{10,9... | collective-permute-start | bytes 1179656 | tf_op jit(solution)/shard_map/ppermute | solution.py:386
  177.2 10.6 %collective-permute-start.11 = (bf16[128,512]{1,0:T(8,128)(2,1)S(1)}, bf16[128,512]{1,0:T(8,128)(2,1)S(1)}, u32[]{:S(2)}, u32[]{:S(2)}) collective-permute-start(bf16[128,512]{1,0:T(8,128)(2,1)S(1)} %add_convert_fusion.3), channel_id=1, source_target_pairs={{0,7},{1,0},{2,1},{3,2},{4,3},{5,4},{6,5},{7,6},{8,15},{9,8},{10,9... | collective-permute-start | bytes 393224 | tf_op jit(solution)/shard_map/ppermute | solution.py:386
  190.3 21.2 %all-to-all-start.4 = ((bf16[32,16,512]{2,1,0:T(8,128)(2,1)}), bf16[32,16,512]{2,1,0:T(8,128)(2,1)S(1)}, u32[]{:S(2)}, u32[]{:S(2)}) async-start(bf16[32,16,512]{2,1,0:T(8,128)(2,1)} %return_kv.1), calls=%async_computation.4 | async-start | bytes 1048576 | tf_op jit(solution)/shard_map/all_to_all | solution.py:381
  203.0 8.5 %copy-start = (bf16[128,1024]{1,0:T(8,128)(2,1)S(1)}, bf16[128,1024]{1,0:T(8,128)(2,1)}, u32[]{:S(2)}) copy-start(bf16[128,1024]{1,0:T(8,128)(2,1)} %k_ref.1) | copy-start | bytes 786436
  203.0 8.5 %copy-start.4 = (f32[128]{0:T(128)S(1)}, f32[128]{0:T(128)}, u32[]{:S(2)}) copy-start(f32[128]{0:T(128)} %param.14) | copy-start | bytes 1540

commit v6 on v4

--- a/solution.py
+++ b/solution.py
@@ -24,7 +24,8 @@
 SCALE = HEAD ** (-0.5)
 LOG2E = 1.4426950408889634
 FIRST = 6
-BATCHES = (3, 3, 2)
+LAST = KV_HEADS - FIRST
+WEIGHTS = (12, 36)
 VMEM_LIMIT = 52 * 1024 * 1024
 VMEM_WHOLE = 62 * 1024 * 1024
 F32 = jnp.float32
@@ -160,21 +161,18 @@
     )(order, gain, query, d_out)
 
 
-def sort_kv_kernel(order_ref, in_ref, *out_refs):
+def sort_kv_kernel(order_ref, in_ref, k_ref, v_ref):
     half = KV_HEADS * HEAD // 2
     rows = dot(pack_matrix(order_ref), in_ref[...].reshape(TALL, half), TM).astype(BF16)
-    places = [(ref, at) for ref, count in zip(out_refs, BATCHES) for at in range(count)]
-    for h, (ref, at) in enumerate(places):
-        part, cols = h // (KV_HEADS // 2), head_cols(h % (KV_HEADS // 2))
-        k = rows[part * ROWS : (part + 1) * ROWS, cols]
-        v = rows[(part + 2) * ROWS : (part + 3) * ROWS, cols]
-        ref[:, at * WIDE : (at + 1) * WIDE] = jnp.concatenate([k, v], axis=1)
+    for n, ref in enumerate((k_ref, v_ref)):
+        ref[:, :half] = rows[2 * n * ROWS : (2 * n + 1) * ROWS]
+        ref[:, half:] = rows[(2 * n + 1) * ROWS : (2 * n + 2) * ROWS]
 
 
 def sort_kv(order, received):
     return pl.pallas_call(
         sort_kv_kernel,
-        out_shape=[jax.ShapeDtypeStruct((ROWS, count * WIDE), BF16) for count in BATCHES],
+        out_shape=[jax.ShapeDtypeStruct((ROWS, KV_HEADS * HEAD), BF16)] * 2,
         compiler_params=params(),
         cost_estimate=cost(2 * TALL**3, 1 << 20),
         name="sort_kv",
@@ -182,7 +180,7 @@
 
 
 def attend_kernel(meta_ref, order_ref, qd_ref, *refs):
-    kv_refs = refs[: BACK + 1]
+    k_refs, v_refs = refs[: BACK + 1], refs[BACK + 1 : 2 * BACK + 2]
     out_ref, *part_refs, bias_ref = refs[-(BACK + 3) :]
 
     @pl.when(pl.program_id(0) == 0)
@@ -200,8 +198,8 @@
         key = (iota((WINDOW, TALL), 0) + (base - BACK * ROWS)).astype(F32)
         bias_ref[...] = jnp.where((key >= start) & (key <= position), 0.0, -1e30)
 
-    kw = jnp.concatenate([r[:, :HEAD] for r in kv_refs], axis=0)
-    vw = jnp.concatenate([r[:, HEAD:] for r in kv_refs], axis=0)
+    kw = jnp.concatenate([r[...] for r in k_refs], axis=0)
+    vw = jnp.concatenate([r[...] for r in v_refs], axis=0)
 
     def both(low):
         return jnp.concatenate(
@@ -235,12 +233,11 @@
         ref[:, HEAD:] = dv[n * ROWS : (n + 1) * ROWS].astype(ref.dtype)
 
 
-def attend(meta, order, received, blocks, first, count, result, weight):
-    kv_spec = pl.BlockSpec((ROWS, WIDE), lambda h: (0, h))
-    rows_spec = pl.BlockSpec((GROUPS, CHUNK, 2 * WIDE), lambda h: (0, 0, h + first))
+def attend(meta, order, received, keys, values, first, count, room, weight):
+    head_spec = pl.BlockSpec((ROWS, HEAD), lambda h: (0, h + first))
+    part_spec = pl.BlockSpec((ROWS, WIDE), lambda h: (0, h))
+    rows_spec = pl.BlockSpec((GROUPS, CHUNK, 2 * WIDE), lambda h: (0, 0, h))
     elements = count * RATIO * ROWS * WINDOW
-    fresh = isinstance(result, int)
-    shape = (GROUPS, CHUNK, result * 2 * WIDE) if fresh else result.shape
     return pl.pallas_call(
         attend_kernel,
         grid=(count,),
@@ -249,25 +246,23 @@
             pl.BlockSpec((1, ROWS), lambda h: (0, 0)),
             rows_spec,
         ]
-        + [kv_spec] * (BACK + 1)
-        + ([] if fresh else [pl.BlockSpec(memory_space=pl.ANY)]),
-        out_specs=[rows_spec] + [kv_spec] * (BACK + 1),
-        out_shape=[jax.ShapeDtypeStruct(shape, BF16)]
+        + [head_spec] * (2 * BACK + 2),
+        out_specs=[rows_spec] + [part_spec] * (BACK + 1),
+        out_shape=[jax.ShapeDtypeStruct((GROUPS, CHUNK, (count + room) * 2 * WIDE), BF16)]
         + [
             jax.ShapeDtypeStruct((ROWS, count * WIDE), BF16 if n == 0 else F32)
             for n in range(BACK + 1)
         ],
         scratch_shapes=[pltpu.VMEM((WINDOW, TALL), F32)],
-        input_output_aliases={} if fresh else {BACK + 4: 0},
         compiler_params=params(),
         cost_estimate=cost(weight * elements * HEAD, count * (3 << 20), elements),
         name="attend",
-    )(meta, order, received, *blocks, *(() if fresh else (result,)))
+    )(meta, order, received, *keys, *values)
 
 
 def return_kv_kernel(order_ref, *refs):
     half = KV_HEADS * HEAD // 2
-    count, out_ref = len(BATCHES), refs[-1]
+    count, out_ref = (len(refs) - 2) // 2, refs[-1]
     total = jnp.concatenate(
         [
             (got[...].astype(F32) + own[...]).astype(BF16)
@@ -380,8 +375,7 @@
 
 def along(array, step):
     count = lax.axis_size("seq")
-    pairs = [(i, i + step) for i in range(count) if 0 <= i + step < count]
-    return lax.ppermute(array, "seq", pairs)
+    return lax.ppermute(array, "seq", [(i, (i + step) % count) for i in range(count)])
 
 
 def after(array, other):
@@ -409,15 +403,11 @@
     kv_received, *sent = lax.optimization_barrier((kv_received, *sent))
     received_first = exchange(sent[0])
 
-    first, second, third = ([block] for block in sort_kv(arriving, kv_received))
+    keys, values = ([block] for block in sort_kv(arriving, kv_received))
     for n in range(BACK):
-        first.append(along(after(first[-1], second[n - 1] if n > 1 else None), 1))
-        second.append(along(second[-1], 1))
-    received_last = exchange(after(after(sent[1], received_first), first[BACK]))
-    third[0] = after(third[0], first[BACK])
-    for _ in range(BACK):
-        third.append(along(third[-1], 1))
-    second[-1] = after(second[-1], third[2])
+        keys.append(along(after(keys[-1], values[n - 1] if n > 1 else None), 1))
+        values.append(along(values[-1], 1))
+    received_last = exchange(after(after(sent[1], received_first), values[BACK - 1]))
 
     def back_along(parts):
         totals = parts[:1]
@@ -425,20 +415,17 @@
             totals.append((along(totals[-1], -1).astype(F32) + part).astype(BF16))
         return totals + [along(totals[-1], -1)], parts[-1]
 
-    def attend_batch(rows, blocks, first, count, result, weight):
-        result, *parts = attend(
-            meta, arriving, rows, blocks[::-1], first, count, result, weight
-        )
-        return result, *back_along(parts)
-
-    result, sums0, own0 = attend_batch(received_first, first, 0, BATCHES[0], FIRST, 1)
-    result, sums1, own1 = attend_batch(
-        received_first, second, BATCHES[0], BATCHES[1], result, 24
-    )
-    back_first = exchange(after(after(result, third[3]), sums0[1]))
-    third[-1] = after(third[-1], sums0[2])
-    result, sums2, own2 = attend_batch(received_last, third, 0, BATCHES[2], BATCHES[2] + 1, 36)
-    merged = return_kv(arriving, (sums0[-1], sums1[-1], sums2[-1]), (own0, own1, own2), result)
+    result, *parts = attend(
+        meta, arriving, received_first, keys[::-1], values[::-1], 0, FIRST, 0, WEIGHTS[0]
+    )
+    sums0, own0 = back_along(parts)
+    back_first = exchange(result)
+    keys[0] = after(keys[0], sums0[1])
+    result, *parts = attend(
+        meta, arriving, received_last, keys[::-1], values[::-1], FIRST, LAST, 1, WEIGHTS[1]
+    )
+    sums1, own1 = back_along(parts)
+    merged = return_kv(arriving, (sums0[-1], sums1[-1]), (own0, own1), result)
     back_last = exchange(after(merged, back_first))
 
     outs = finish(leaving, q_gain, query, back_first, starts[0], counts[0])

time: 222 us -> 188 us (0.85)
  the two profiles are of different devices: /device:TPU:96 before, /device:TPU:1 now
where the time goes in v6:
time: 188 us; the launch traced here: 186 us
  waiting for transfers between devices  73.8 us (39%)
  starting transfers between devices  59.1 us (31%)
  Pallas kernels  51.1 us (27%)
    ppermute x16, waiting for transfers between devices, along(): lax.ppermute(array, 'seq', [(i, (i + step) % count) for i in range(count)])  57.6 us
    all_to_all x5, starting transfers between devices, exchange(): return lax.all_to_all(array, 'dp', split_axis=0, concat_axis=0, tiled=True)  42 us
    pallas_call x2, Pallas kernels, attend(): pl.pallas_call(attend_kernel, grid=(count,), in_specs=[pl.BlockSpec(memor...  24.6 us
    ppermute x16, starting transfers between devices, along(): lax.ppermute(array, 'seq', [(i, (i + step) % count) for i in range(count)])  17.1 us
    all_to_all x5, waiting for transfers between devices, exchange(): return lax.all_to_all(array, 'dp', split_axis=0, concat_axis=0, tiled=True)  16.2 us
    pallas_call x2, Pallas kernels, finish(): pl.pallas_call(functools.partial(finish_kernel, bool(kv)), grid=(count +...  11.6 us
    pallas_call x2, Pallas kernels, send_rows(): pl.pallas_call(send_rows_kernel, grid=(count,), in_specs=[pl.BlockSpec((1...  10.6 us
  transfers between devices with their start and end apart: 21, of which 14 were waited for; matrix products, arithmetic and copies ran while one was open for 0% of the time, Pallas kernels for 24%

profile of v6, /device:TPU:1, one launch (start us, length us, event | category | flops | bytes accessed | tf_op | source)
XLA Modules:
  0.0 186.3 jit_solution(9293515829197467766)
XLA Ops:
  0.6 2.5 %send_kv.1 = bf16[32,16,512]{2,1,0:T(8,128)(2,1)} custom-call(s32[1,128]{1,0:T(1,128)} %bitcast.6, f32[1,128]{1,0:T(1,128)} %bitcast.15, bf16[128,1024]{1,0:T(8,128)(2,1)} %refs_1_.1, bf16[128,1024]{1,0:T(8,128)(2,1)} %v_ref.1), custom_call_target="tpu_custom_call" | custom-call | flops 268435456 | bytes 1572864 | tf_op jit(solution)/shard_map/send_kv/pallas_call | solution.py:116
  3.1 8.6 %all-to-all-start = ((bf16[32,16,512]{2,1,0:T(8,128)(2,1)}), bf16[32,16,512]{2,1,0:T(8,128)(2,1)S(1)}, u32[]{:S(2)}, u32[]{:S(2)}) async-start(bf16[32,16,512]{2,1,0:T(8,128)(2,1)} %send_kv.1), calls=%async_computation | async-start | bytes 1048576 | tf_op jit(solution)/shard_map/all_to_all | solution.py:373
  11.7 3.4 %send_rows.3 = bf16[32,16,1024]{2,1,0:T(8,128)(2,1)} custom-call(s32[1,128]{1,0:T(1,128)} %bitcast.7, f32[1,128]{1,0:T(1,128)} %bitcast.11, bf16[128,8192]{1,0:T(8,128)(2,1)} %q_ref.7, bf16[128,8192]{1,0:T(8,128)(2,1)} %d_ref.3), custom_call_target="tpu_custom_call" | custom-call | flops 536870912 | bytes 2097152 | tf_op jit(solution)/shard_map/send_rows/pallas_call | solution.py:146
  15.1 7.2 %send_rows.2 = bf16[32,16,3072]{2,1,0:T(8,128)(2,1)} custom-call(s32[1,128]{1,0:T(1,128)} %bitcast.8, f32[1,128]{1,0:T(1,128)} %bitcast.12, bf16[128,8192]{1,0:T(8,128)(2,1)} %q_ref.7, bf16[128,8192]{1,0:T(8,128)(2,1)} %d_ref.3), custom_call_target="tpu_custom_call" | custom-call | flops 1610612736 | bytes 6291456 | tf_op jit(solution)/shard_map/send_rows/pallas_call | solution.py:146
  22.3 1.0 all-to-all-done.in_ref
  23.3 6.5 %all-to-all-start.1 = ((bf16[32,16,3072]{2,1,0:T(8,128)(2,1)}), bf16[32,16,3072]{2,1,0:T(8,128)(2,1)}, u32[]{:S(2)}, u32[]{:S(2)}) async-start(bf16[32,16,3072]{2,1,0:T(8,128)(2,1)} %send_rows.2), calls=%async_computation.1 | async-start | bytes 6291456 | tf_op jit(solution)/shard_map/all_to_all | solution.py:373
  29.8 0.0 copy-start.17
  29.8 0.5 sort_kv.1
  30.3 1.7 collective-permute-start
  32.0 1.6 collective-permute-start.2
  33.7 8.9 %collective-permute-done.refs_3_ = bf16[128,1024]{1,0:T(8,128)(2,1)S(1)} collective-permute-done((bf16[128,1024]{1,0:T(8,128)(2,1)S(1)}, bf16[128,1024]{1,0:T(8,128)(2,1)S(1)}, u32[]{:S(2)}, u32[]{:S(2)}) %collective-permute-start) | collective-permute-done | bytes 262176 | tf_op jit(solution)/shard_map/ppermute | solution.py:378
  42.5 0.0 collective-permute-start.1
  42.5 5.6 %collective-permute-done.2.refs_8_ = bf16[128,1024]{1,0:T(8,128)(2,1)S(1)} collective-permute-done((bf16[128,1024]{1,0:T(8,128)(2,1)S(1)}, bf16[128,1024]{1,0:T(8,128)(2,1)S(1)}, u32[]{:S(2)}, u32[]{:S(2)}) %collective-permute-start.2) | collective-permute-done | bytes 262176 | tf_op jit(solution)/shard_map/ppermute | solution.py:378
  48.2 0.0 collective-permute-start.4
  48.2 5.6 %collective-permute-done.1.refs_2_ = bf16[128,1024]{1,0:T(8,128)(2,1)S(1)} collective-permute-done((bf16[128,1024]{1,0:T(8,128)(2,1)S(1)}, bf16[128,1024]{1,0:T(8,128)(2,1)S(1)}, u32[]{:S(2)}, u32[]{:S(2)}) %collective-permute-start.1) | collective-permute-done | bytes 262176 | tf_op jit(solution)/shard_map/ppermute | solution.py:378
  53.8 0.0 collective-permute-start.3
  53.8 5.6 %collective-permute-done.4.refs_7_ = bf16[128,1024]{1,0:T(8,128)(2,1)S(1)} collective-permute-done((bf16[128,1024]{1,0:T(8,128)(2,1)S(1)}, bf16[128,1024]{1,0:T(8,128)(2,1)S(1)}, u32[]{:S(2)}, u32[]{:S(2)}) %collective-permute-start.4) | collective-permute-done | bytes 262176 | tf_op jit(solution)/shard_map/ppermute | solution.py:378
  59.4 0.0 collective-permute-start.6
  59.4 5.6 %collective-permute-done.3.refs_1_ = bf16[128,1024]{1,0:T(8,128)(2,1)S(1)} collective-permute-done((bf16[128,1024]{1,0:T(8,128)(2,1)S(1)}, bf16[128,1024]{1,0:T(8,128)(2,1)S(1)}, u32[]{:S(2)}, u32[]{:S(2)}) %collective-permute-start.3) | collective-permute-done | bytes 262176 | tf_op jit(solution)/shard_map/ppermute | solution.py:378
  65.0 0.0 collective-permute-start.5
  65.0 0.0 copy-done.16
  65.0 5.6 %collective-permute-done.6.refs_6_ = bf16[128,1024]{1,0:T(8,128)(2,1)S(1)} collective-permute-done((bf16[128,1024]{1,0:T(8,128)(2,1)S(1)}, bf16[128,1024]{1,0:T(8,128)(2,1)S(1)}, u32[]{:S(2)}, u32[]{:S(2)}) %collective-permute-start.6) | collective-permute-done | bytes 262176 | tf_op jit(solution)/shard_map/ppermute | solution.py:378
  70.6 0.0 collective-permute-start.7
  70.6 0.0 all-to-all-done.1.qd_ref
  70.6 8.2 %all-to-all-start.2 = ((bf16[32,16,1024]{2,1,0:T(8,128)(2,1)}), bf16[32,16,1024]{2,1,0:T(8,128)(2,1)S(1)}, u32[]{:S(2)}, u32[]{:S(2)}) async-start(bf16[32,16,1024]{2,1,0:T(8,128)(2,1)} %send_rows.3), calls=%async_computation.2 | async-start | bytes 2097152 | tf_op jit(solution)/shard_map/all_to_all | solution.py:373
  78.8 0.0 copy-done.17
  78.9 0.1 pad_add_fusion.meta_ref
  78.9 0.0 collective-permute-done.5.refs_0_
  78.9 2.8 %collective-permute-done.7.refs_5_ = bf16[128,1024]{1,0:T(8,128)(2,1)S(1)} collective-permute-done((bf16[128,1024]{1,0:T(8,128)(2,1)S(1)}, bf16[128,1024]{1,0:T(8,128)(2,1)S(1)}, u32[]{:S(2)}, u32[]{:S(2)}) %collective-permute-start.7) | collective-permute-done | bytes 262176 | tf_op jit(solution)/shard_map/ppermute | solution.py:378
  81.8 0.0 copy-done.7
  81.8 17.4 %attend.2 = (bf16[32,16,3072]{2,1,0:T(8,128)(2,1)}, bf16[128,1536]{1,0:T(8,128)(2,1)}, f32[128,1536]{1,0:T(8,128)}, f32[128,1536]{1,0:T(8,128)}, f32[128,1536]{1,0:T(8,128)}, /*index=5*/f32[128,1536]{1,0:T(8,128)}) custom-call(s32[4]{0:T(128)S(1)} %pad_add_fusion.meta_ref, s32[1,128]{1,0:T(1,128)S(1)} %bitcast.18, ...), custom_call_target="tpu_custom_call" | custom-call | flops 6039797760 | bytes 18874368 | tf_op jit(solution)/shard_map/attend/pallas_call | solution.py:241
  99.2 1.2 collective-permute-start.8
  100.4 0.0 all-to-all-done.2.qd_ref
  100.4 1.0 copy-done.11
  101.4 8.5 %all-to-all-start.3 = ((bf16[32,16,3072]{2,1,0:T(8,128)(2,1)}), bf16[32,16,3072]{2,1,0:T(8,128)(2,1)}, u32[]{:S(2)}, u32[]{:S(2)}) async-start(bf16[32,16,3072]{2,1,0:T(8,128)(2,1)} %get-tuple-element.50), calls=%async_computation.3 | async-start | bytes 6291456 | tf_op jit(solution)/shard_map/all_to_all | solution.py:373
  109.9 0.0 collective-permute-done.8
  109.9 0.0 copy-done.14
  109.9 0.1 add_convert_fusion.2
  110.0 1.5 collective-permute-start.9
  111.5 7.2 %attend.3 = (bf16[32,16,1536]{2,1,0:T(8,128)(2,1)}, bf16[128,512]{1,0:T(8,128)(2,1)S(1)}, f32[128,512]{1,0:T(8,128)S(1)}, f32[128,512]{1,0:T(8,128)S(1)}, f32[12...) custom-call(s32[4]{0:T(128)S(1)} %pad_add_fusion.meta_ref, s32[1,128]{1,0:T(1,128)S(1)} %bitcast.19, ...), custom_call_target="tpu_custom_call" | custom-call | flops 6039797760 | bytes 6291456 | tf_op jit(solution)/shard_map/attend/pallas_call | solution.py:241
  118.7 0.2 collective-permute-start.12
  118.9 0.7 collective-permute-done.9
  119.7 0.1 add_convert_fusion.1
  119.7 1.8 collective-permute-start.10
  121.6 1.4 collective-permute-done.12
  123.0 2.5 %collective-permute-start.13 = (bf16[128,512]{1,0:T(8,128)(2,1)S(1)}, bf16[128,512]{1,0:T(8,128)(2,1)S(1)}, u32[]{:S(2)}, u32[]{:S(2)}) collective-permute-start(bf16[128,512]{1,0:T(8,128)(2,1)S(1)} %add_convert_fusion.5), channel_id=1, source_target_pairs={{0,7},{1,0},{2,1},{3,2},{4,3},{5,4},{6,5},{7,6},{8,15},{9,8},{10,9... | collective-permute-start | bytes 393224 | tf_op jit(solution)/shard_map/ppermute | solution.py:378
  125.5 7.3 %collective-permute-done.13 = bf16[128,512]{1,0:T(8,128)(2,1)S(1)} collective-permute-done((bf16[128,512]{1,0:T(8,128)(2,1)S(1)}, bf16[128,512]{1,0:T(8,128)(2,1)S(1)}, u32[]{:S(2)}, u32[]{:S(2)}) %collective-permute-start.13) | collective-permute-done | bytes 131104 | tf_op jit(solution)/shard_map/ppermute | solution.py:378
  132.8 2.2 %collective-permute-start.14 = (bf16[128,512]{1,0:T(8,128)(2,1)S(1)}, bf16[128,512]{1,0:T(8,128)(2,1)S(1)}, u32[]{:S(2)}, u32[]{:S(2)}) collective-permute-start(bf16[128,512]{1,0:T(8,128)(2,1)S(1)} %add_convert_fusion.4), channel_id=1, source_target_pairs={{0,7},{1,0},{2,1},{3,2},{4,3},{5,4},{6,5},{7,6},{8,15},{9,8},{10,9... | collective-permute-start | bytes 393224 | tf_op jit(solution)/shard_map/ppermute | solution.py:378
  135.1 0.0 collective-permute-done.10
  135.1 0.0 copy-done.12
  135.1 0.1 add_convert_fusion
  135.1 0.7 collective-permute-start.11
  135.8 1.4 collective-permute-done.14
  137.3 3.5 %collective-permute-start.15 = (bf16[128,512]{1,0:T(8,128)(2,1)S(1)}, bf16[128,512]{1,0:T(8,128)(2,1)S(1)}, u32[]{:S(2)}, u32[]{:S(2)}) collective-permute-start(bf16[128,512]{1,0:T(8,128)(2,1)S(1)} %add_convert_fusion.3), channel_id=1, source_target_pairs={{0,7},{1,0},{2,1},{3,2},{4,3},{5,4},{6,5},{7,6},{8,15},{9,8},{10,9... | collective-permute-start | bytes 393224 | tf_op jit(solution)/shard_map/ppermute | solution.py:378
  140.8 6.9 %collective-permute-done.15.refs_1_ = bf16[128,512]{1,0:T(8,128)(2,1)S(1)} collective-permute-done((bf16[128,512]{1,0:T(8,128)(2,1)S(1)}, bf16[128,512]{1,0:T(8,128)(2,1)S(1)}, u32[]{:S(2)}, u32[]{:S(2)}) %collective-permute-start.15) | collective-permute-done | bytes 131104 | tf_op jit(solution)/shard_map/ppermute | solution.py:378
  147.7 0.0 collective-permute-done.11.refs_0_
  147.8 1.3 return_kv.1
  149.1 0.0 all-to-all-done.3.in_ref
  149.1 10.3 %all-to-all-start.4 = ((bf16[32,16,1536]{2,1,0:T(8,128)(2,1)}), bf16[32,16,1536]{2,1,0:T(8,128)(2,1)S(1)}, u32[]{:S(2)}, u32[]{:S(2)}) async-start(bf16[32,16,1536]{2,1,0:T(8,128)(2,1)} %return_kv.1), calls=%async_computation.4 | async-start | bytes 3145728 | tf_op jit(solution)/shard_map/all_to_all | solution.py:373
  159.4 0.0 copy-start
  159.4 0.0 copy-start.4
  159.4 6.9 %finish.2 = (bf16[128,8192]{1,0:T(8,128)(2,1)}, bf16[128,8192]{1,0:T(8,128)(2,1)}) custom-call(s32[1,128]{1,0:T(1,128)S(1)} %bitcast.9, f32[1,128]{1,0:T(1,128)S(1)} %bitcast.13, bf16[128,8192]{1,0:T(8,128)(2,1)} %q_ref.7, bf16[32,16,3072]{2,1,0:T(8,128)(2,1)} %all-to-all-done.3.in_ref), custom_call_target="tpu_custom_call" | custom-call | flops 1610612736 | bytes 7864320 | tf_op jit(solution)/shard_map/finish/pallas_call | solution.py:358
  166.4 15.2 %all-to-all-done.4.in_ref = bf16[32,16,1536]{2,1,0:T(8,128)(2,1)S(1)} async-done(((bf16[32,16,1536]{2,1,0:T(8,128)(2,1)}), bf16[32,16,1536]{2,1,0:T(8,128)(2,1)S(1)}, u32[]{:S(2)}, u32[]{:S(2)}) %all-to-all-start.4) | async-done | bytes 1572896 | tf_op jit(solution)/shard_map/all_to_all | solution.py:373
  181.6 4.7 %finish.3 = (bf16[128,8192]{1,0:T(8,128)(2,1)}, bf16[128,8192]{1,0:T(8,128)(2,1)}, bf16[128,1024]{1,0:T(8,128)(2,1)}, bf16[128,1024]{1,0:T(8,128)(2,1)}) custom-call(s32[1,128]{1,0:T(1,128)S(1)} %bitcast.10, f32[1,128]{1,0:T(1,128)S(1)} %bitcast.14, bf16[128,8192]{1,0:T(8,128)(2,1)} %q_ref.7, ...), custom_call_target="tpu_custom_call", output_to_operand_aliasing={{0}: (6, {}), {1}: (7, {})} | custom-call | flops 536870912 | bytes 2621440 | tf_op jit(solution)/shard_map/finish/pallas_call | solution.py:358
  (30 shorter events, 0.1 us)
Async XLA Ops:
  3.1 20.1 %all-to-all-start = ((bf16[32,16,512]{2,1,0:T(8,128)(2,1)}), bf16[32,16,512]{2,1,0:T(8,128)(2,1)S(1)}, u32[]{:S(2)}, u32[]{:S(2)}) async-start(bf16[32,16,512]{2,1,0:T(8,128)(2,1)} %send_kv.1), calls=%async_computation | async-start | bytes 1048576 | tf_op jit(solution)/shard_map/all_to_all | solution.py:373
  22.3 7.5 %copy-start.5 = (s32[1,1,128]{2,1,0:T(1,128)S(1)}, s32[1,1,128]{2,1,0:T(1,128)}, u32[]{:S(2)}) copy-start(s32[1,1,128]{2,1,0:T(1,128)} %param.17) | copy-start | bytes 1540
  23.3 47.3 %all-to-all-start.1 = ((bf16[32,16,3072]{2,1,0:T(8,128)(2,1)}), bf16[32,16,3072]{2,1,0:T(8,128)(2,1)}, u32[]{:S(2)}, u32[]{:S(2)}) async-start(bf16[32,16,3072]{2,1,0:T(8,128)(2,1)} %send_rows.2), calls=%async_computation.1 | async-start | bytes 6291456 | tf_op jit(solution)/shard_map/all_to_all | solution.py:373
  29.8 49.1 %copy-start.17 = (s32[1,3]{1,0:T(1,128)S(1)}, s32[1,3]{1,0:T(1,128)}, u32[]{:S(2)}) copy-start(s32[1,3]{1,0:T(1,128)} %param.15) | copy-start | bytes 40
  30.3 51.5 %copy-start.7 = (bf16[128,1024]{1,0:T(8,128)(2,1)}, bf16[128,1024]{1,0:T(8,128)(2,1)S(1)}, u32[]{:S(2)}) copy-start(bf16[128,1024]{1,0:T(8,128)(2,1)S(1)} %get-tuple-element.32.refs_9_) | copy-start | bytes 786436
  30.3 68.9 %copy-start.6 = (bf16[128,1024]{1,0:T(8,128)(2,1)}, bf16[128,1024]{1,0:T(8,128)(2,1)S(1)}, u32[]{:S(2)}) copy-start(bf16[128,1024]{1,0:T(8,128)(2,1)S(1)} %get-tuple-element.42.refs_4_) | copy-start | bytes 786436
  30.3 12.2 %collective-permute-start = (bf16[128,1024]{1,0:T(8,128)(2,1)S(1)}, bf16[128,1024]{1,0:T(8,128)(2,1)S(1)}, u32[]{:S(2)}, u32[]{:S(2)}) collective-permute-start(bf16[128,1024]{1,0:T(8,128)(2,1)S(1)} %get-tuple-element.42.refs_4_), channel_id=1, source_target_pairs={{0,1},{1,2},{2,3},{3,4},{4,5},{5,6},{6,7},{7,0},{8,9},{9,10},{10,1... | collective-permute-start | bytes 786440 | tf_op jit(solution)/shard_map/ppermute | solution.py:378
  32.0 16.1 %collective-permute-start.2 = (bf16[128,1024]{1,0:T(8,128)(2,1)S(1)}, bf16[128,1024]{1,0:T(8,128)(2,1)S(1)}, u32[]{:S(2)}, u32[]{:S(2)}) collective-permute-start(bf16[128,1024]{1,0:T(8,128)(2,1)S(1)} %get-tuple-element.32.refs_9_), channel_id=1, source_target_pairs={{0,1},{1,2},{2,3},{3,4},{4,5},{5,6},{6,7},{7,0},{8,9},{9,10},{10,1... | collective-permute-start | bytes 786440 | tf_op jit(solution)/shard_map/ppermute | solution.py:378
  42.5 56.6 %copy-start.8 = (bf16[128,1024]{1,0:T(8,128)(2,1)}, bf16[128,1024]{1,0:T(8,128)(2,1)S(1)}, u32[]{:S(2)}) copy-start(bf16[128,1024]{1,0:T(8,128)(2,1)S(1)} %collective-permute-done.refs_3_) | copy-start | bytes 786436
  42.5 11.2 %collective-permute-start.1 = (bf16[128,1024]{1,0:T(8,128)(2,1)S(1)}, bf16[128,1024]{1,0:T(8,128)(2,1)S(1)}, u32[]{:S(2)}, u32[]{:S(2)}) collective-permute-start(bf16[128,1024]{1,0:T(8,128)(2,1)S(1)} %collective-permute-done.refs_3_), channel_id=1, source_target_pairs={{0,1},{1,2},{2,3},{3,4},{4,5},{5,6},{6,7},{7,0},{8,9},{9,10},{10,1... | collective-permute-start | bytes 786440 | tf_op jit(solution)/shard_map/ppermute | solution.py:378
  48.2 33.6 %copy-start.15 = (bf16[128,1024]{1,0:T(8,128)(2,1)}, bf16[128,1024]{1,0:T(8,128)(2,1)S(1)}, u32[]{:S(2)}) copy-start(bf16[128,1024]{1,0:T(8,128)(2,1)S(1)} %collective-permute-done.2.refs_8_) | copy-start | bytes 786436
  48.2 11.2 %collective-permute-start.4 = (bf16[128,1024]{1,0:T(8,128)(2,1)S(1)}, bf16[128,1024]{1,0:T(8,128)(2,1)S(1)}, u32[]{:S(2)}, u32[]{:S(2)}) collective-permute-start(bf16[128,1024]{1,0:T(8,128)(2,1)S(1)} %collective-permute-done.2.refs_8_), channel_id=1, source_target_pairs={{0,1},{1,2},{2,3},{3,4},{4,5},{5,6},{6,7},{7,0},{8,9},{9,10},{10,1... | collective-permute-start | bytes 786440 | tf_op jit(solution)/shard_map/ppermute | solution.py:378
  53.8 11.2 %collective-permute-start.3 = (bf16[128,1024]{1,0:T(8,128)(2,1)S(1)}, bf16[128,1024]{1,0:T(8,128)(2,1)S(1)}, u32[]{:S(2)}, u32[]{:S(2)}) collective-permute-start(bf16[128,1024]{1,0:T(8,128)(2,1)S(1)} %collective-permute-done.1.refs_2_), channel_id=1, source_target_pairs={{0,1},{1,2},{2,3},{3,4},{4,5},{5,6},{6,7},{7,0},{8,9},{9,10},{10,1... | collective-permute-start | bytes 786440 | tf_op jit(solution)/shard_map/ppermute | solution.py:378
  59.4 5.6 %copy-start.16 = (bf16[128,1024]{1,0:T(8,128)(2,1)}, bf16[128,1024]{1,0:T(8,128)(2,1)S(1)}, u32[]{:S(2)}) copy-start(bf16[128,1024]{1,0:T(8,128)(2,1)S(1)} %collective-permute-done.4.refs_7_) | copy-start | bytes 786436
  59.4 11.2 %collective-permute-start.6 = (bf16[128,1024]{1,0:T(8,128)(2,1)S(1)}, bf16[128,1024]{1,0:T(8,128)(2,1)S(1)}, u32[]{:S(2)}, u32[]{:S(2)}) collective-permute-start(bf16[128,1024]{1,0:T(8,128)(2,1)S(1)} %collective-permute-done.4.refs_7_), channel_id=1, source_target_pairs={{0,1},{1,2},{2,3},{3,4},{4,5},{5,6},{6,7},{7,0},{8,9},{9,10},{10,1... | collective-permute-start | bytes 786440 | tf_op jit(solution)/shard_map/ppermute | solution.py:378
  65.0 13.9 %collective-permute-start.5 = (bf16[128,1024]{1,0:T(8,128)(2,1)S(1)}, bf16[128,1024]{1,0:T(8,128)(2,1)S(1)}, u32[]{:S(2)}, u32[]{:S(2)}) collective-permute-start(bf16[128,1024]{1,0:T(8,128)(2,1)S(1)} %collective-permute-done.3.refs_1_), channel_id=1, source_target_pairs={{0,1},{1,2},{2,3},{3,4},{4,5},{5,6},{6,7},{7,0},{8,9},{9,10},{10,1... | collective-permute-start | bytes 786440 | tf_op jit(solution)/shard_map/ppermute | solution.py:378
  70.6 28.6 %copy-start.9 = (bf16[128,1024]{1,0:T(8,128)(2,1)}, bf16[128,1024]{1,0:T(8,128)(2,1)S(1)}, u32[]{:S(2)}) copy-start(bf16[128,1024]{1,0:T(8,128)(2,1)S(1)} %collective-permute-done.6.refs_6_) | copy-start | bytes 786436
  70.6 11.1 %collective-permute-start.7 = (bf16[128,1024]{1,0:T(8,128)(2,1)S(1)}, bf16[128,1024]{1,0:T(8,128)(2,1)S(1)}, u32[]{:S(2)}, u32[]{:S(2)}) collective-permute-start(bf16[128,1024]{1,0:T(8,128)(2,1)S(1)} %collective-permute-done.6.refs_6_), channel_id=1, source_target_pairs={{0,1},{1,2},{2,3},{3,4},{4,5},{5,6},{6,7},{7,0},{8,9},{9,10},{10,1... | collective-permute-start | bytes 786440 | tf_op jit(solution)/shard_map/ppermute | solution.py:378
  70.6 29.8 %all-to-all-start.2 = ((bf16[32,16,1024]{2,1,0:T(8,128)(2,1)}), bf16[32,16,1024]{2,1,0:T(8,128)(2,1)S(1)}, u32[]{:S(2)}, u32[]{:S(2)}) async-start(bf16[32,16,1024]{2,1,0:T(8,128)(2,1)} %send_rows.3), calls=%async_computation.2 | async-start | bytes 2097152 | tf_op jit(solution)/shard_map/all_to_all | solution.py:373
  81.8 17.4 %copy-start.10 = (bf16[128,1024]{1,0:T(8,128)(2,1)}, bf16[128,1024]{1,0:T(8,128)(2,1)S(1)}, u32[]{:S(2)}) copy-start(bf16[128,1024]{1,0:T(8,128)(2,1)S(1)} %collective-permute-done.7.refs_5_) | copy-start | bytes 786436
  99.2 10.7 %collective-permute-start.8 = (bf16[128,1536]{1,0:T(8,128)(2,1)}, bf16[128,1536]{1,0:T(8,128)(2,1)S(1)}, u32[]{:S(2)}, u32[]{:S(2)}) collective-permute-start(bf16[128,1536]{1,0:T(8,128)(2,1)} %get-tuple-element.35), channel_id=1, source_target_pairs={{0,7},{1,0},{2,1},{3,2},{4,3},{5,4},{6,5},{7,6},{8,15},{9,8},{10,9... | collective-permute-start | bytes 1179656 | tf_op jit(solution)/shard_map/ppermute | solution.py:378
  100.4 1.0 copy-start.11
  100.4 9.4 %copy-start.14 = (f32[128,1536]{1,0:T(8,128)S(1)}, f32[128,1536]{1,0:T(8,128)}, u32[]{:S(2)}) copy-start(f32[128,1536]{1,0:T(8,128)} %get-tuple-element.36) | copy-start | bytes 2359300
  101.4 47.7 %all-to-all-start.3 = ((bf16[32,16,3072]{2,1,0:T(8,128)(2,1)}), bf16[32,16,3072]{2,1,0:T(8,128)(2,1)}, u32[]{:S(2)}, u32[]{:S(2)}) async-start(bf16[32,16,3072]{2,1,0:T(8,128)(2,1)} %get-tuple-element.50), calls=%async_computation.3 | async-start | bytes 6291456 | tf_op jit(solution)/shard_map/all_to_all | solution.py:373
  110.0 9.7 %copy-start.13 = (f32[128,1536]{1,0:T(8,128)S(1)}, f32[128,1536]{1,0:T(8,128)}, u32[]{:S(2)}) copy-start(f32[128,1536]{1,0:T(8,128)} %get-tuple-element.37) | copy-start | bytes 2359300
  110.0 9.7 %collective-permute-start.9 = (bf16[128,1536]{1,0:T(8,128)(2,1)S(1)}, bf16[128,1536]{1,0:T(8,128)(2,1)S(1)}, u32[]{:S(2)}, u32[]{:S(2)}) collective-permute-start(bf16[128,1536]{1,0:T(8,128)(2,1)S(1)} %add_convert_fusion.2), channel_id=1, source_target_pairs={{0,7},{1,0},{2,1},{3,2},{4,3},{5,4},{6,5},{7,6},{8,15},{9,8},{10,9... | collective-permute-start | bytes 1179656 | tf_op jit(solution)/shard_map/ppermute | solution.py:378
  118.7 16.4 %copy-start.12 = (f32[128,1536]{1,0:T(8,128)S(1)}, f32[128,1536]{1,0:T(8,128)}, u32[]{:S(2)}) copy-start(f32[128,1536]{1,0:T(8,128)} %get-tuple-element.38) | copy-start | bytes 2359300
  118.7 4.3 %collective-permute-start.12 = (bf16[128,512]{1,0:T(8,128)(2,1)S(1)}, bf16[128,512]{1,0:T(8,128)(2,1)S(1)}, u32[]{:S(2)}, u32[]{:S(2)}) collective-permute-start(bf16[128,512]{1,0:T(8,128)(2,1)S(1)} %get-tuple-element.43), channel_id=1, source_target_pairs={{0,7},{1,0},{2,1},{3,2},{4,3},{5,4},{6,5},{7,6},{8,15},{9,8},{10,9... | collective-permute-start | bytes 393224 | tf_op jit(solution)/shard_map/ppermute | solution.py:378
  119.7 28.1 %copy-start.1 = (f32[128,1536]{1,0:T(8,128)S(1)}, f32[128,1536]{1,0:T(8,128)}, u32[]{:S(2)}) copy-start(f32[128,1536]{1,0:T(8,128)} %get-tuple-element.47.refs_2_) | copy-start | bytes 2359300
  119.7 15.3 %collective-permute-start.10 = (bf16[128,1536]{1,0:T(8,128)(2,1)S(1)}, bf16[128,1536]{1,0:T(8,128)(2,1)S(1)}, u32[]{:S(2)}, u32[]{:S(2)}) collective-permute-start(bf16[128,1536]{1,0:T(8,128)(2,1)S(1)} %add_convert_fusion.1), channel_id=1, source_target_pairs={{0,7},{1,0},{2,1},{3,2},{4,3},{5,4},{6,5},{7,6},{8,15},{9,8},{10,9... | collective-permute-start | bytes 1179656 | tf_op jit(solution)/shard_map/ppermute | solution.py:378
  123.0 9.8 %collective-permute-start.13 = (bf16[128,512]{1,0:T(8,128)(2,1)S(1)}, bf16[128,512]{1,0:T(8,128)(2,1)S(1)}, u32[]{:S(2)}, u32[]{:S(2)}) collective-permute-start(bf16[128,512]{1,0:T(8,128)(2,1)S(1)} %add_convert_fusion.5), channel_id=1, source_target_pairs={{0,7},{1,0},{2,1},{3,2},{4,3},{5,4},{6,5},{7,6},{8,15},{9,8},{10,9... | collective-permute-start | bytes 393224 | tf_op jit(solution)/shard_map/ppermute | solution.py:378
  132.8 4.4 %collective-permute-start.14 = (bf16[128,512]{1,0:T(8,128)(2,1)S(1)}, bf16[128,512]{1,0:T(8,128)(2,1)S(1)}, u32[]{:S(2)}, u32[]{:S(2)}) collective-permute-start(bf16[128,512]{1,0:T(8,128)(2,1)S(1)} %add_convert_fusion.4), channel_id=1, source_target_pairs={{0,7},{1,0},{2,1},{3,2},{4,3},{5,4},{6,5},{7,6},{8,15},{9,8},{10,9... | collective-permute-start | bytes 393224 | tf_op jit(solution)/shard_map/ppermute | solution.py:378
  135.1 12.6 %collective-permute-start.11 = (bf16[128,1536]{1,0:T(8,128)(2,1)S(1)}, bf16[128,1536]{1,0:T(8,128)(2,1)S(1)}, u32[]{:S(2)}, u32[]{:S(2)}) collective-permute-start(bf16[128,1536]{1,0:T(8,128)(2,1)S(1)} %add_convert_fusion), channel_id=1, source_target_pairs={{0,7},{1,0},{2,1},{3,2},{4,3},{5,4},{6,5},{7,6},{8,15},{9,8},{10,9... | collective-permute-start | bytes 1179656 | tf_op jit(solution)/shard_map/ppermute | solution.py:378
  137.3 10.4 %collective-permute-start.15 = (bf16[128,512]{1,0:T(8,128)(2,1)S(1)}, bf16[128,512]{1,0:T(8,128)(2,1)S(1)}, u32[]{:S(2)}, u32[]{:S(2)}) collective-permute-start(bf16[128,512]{1,0:T(8,128)(2,1)S(1)} %add_convert_fusion.3), channel_id=1, source_target_pairs={{0,7},{1,0},{2,1},{3,2},{4,3},{5,4},{6,5},{7,6},{8,15},{9,8},{10,9... | collective-permute-start | bytes 393224 | tf_op jit(solution)/shard_map/ppermute | solution.py:378
  149.1 10.3 %copy-start.2 = (s32[1,1,128]{2,1,0:T(1,128)S(1)}, s32[1,1,128]{2,1,0:T(1,128)}, u32[]{:S(2)}) copy-start(s32[1,1,128]{2,1,0:T(1,128)} %param.16) | copy-start | bytes 1540
  149.1 10.3 %copy-start.3 = (f32[128]{0:T(128)S(1)}, f32[128]{0:T(128)}, u32[]{:S(2)}) copy-start(f32[128]{0:T(128)} %param.13) | copy-start | bytes 1540
  149.1 32.5 %all-to-all-start.4 = ((bf16[32,16,1536]{2,1,0:T(8,128)(2,1)}), bf16[32,16,1536]{2,1,0:T(8,128)(2,1)S(1)}, u32[]{:S(2)}, u32[]{:S(2)}) async-start(bf16[32,16,1536]{2,1,0:T(8,128)(2,1)} %return_kv.1), calls=%async_computation.4 | async-start | bytes 3145728 | tf_op jit(solution)/shard_map/all_to_all | solution.py:373
  159.4 22.2 %copy-start = (bf16[128,1024]{1,0:T(8,128)(2,1)S(1)}, bf16[128,1024]{1,0:T(8,128)(2,1)}, u32[]{:S(2)}) copy-start(bf16[128,1024]{1,0:T(8,128)(2,1)} %refs_1_.1) | copy-start | bytes 786436
  159.4 22.2 %copy-start.4 = (f32[128]{0:T(128)S(1)}, f32[128]{0:T(128)}, u32[]{:S(2)}) copy-start(f32[128]{0:T(128)} %param.14) | copy-start | bytes 1540

commit v7 on v6

--- a/solution.py
+++ b/solution.py
@@ -23,9 +23,7 @@
 WINDOW = (BACK + 1) * ROWS
 SCALE = HEAD ** (-0.5)
 LOG2E = 1.4426950408889634
-FIRST = 6
-LAST = KV_HEADS - FIRST
-WEIGHTS = (12, 36)
+WEIGHT = 36
 VMEM_LIMIT = 52 * 1024 * 1024
 VMEM_WHOLE = 62 * 1024 * 1024
 F32 = jnp.float32
@@ -142,21 +140,18 @@
     out_ref[...] = sent.reshape(GROUPS, CHUNK, 2 * WIDE)
 
 
-def send_rows(order, gain, query, d_out, first, count):
+def send_rows(order, gain, query, d_out):
+    row = pl.BlockSpec((1, ROWS), lambda h: (0, 0))
+    block = pl.BlockSpec((ROWS, RATIO * HEAD), lambda h: (0, h))
     return pl.pallas_call(
         send_rows_kernel,
-        grid=(count,),
-        in_specs=[
-            pl.BlockSpec((1, ROWS), lambda h: (0, 0)),
-            pl.BlockSpec((1, HEAD), lambda h: (0, 0)),
-            pl.BlockSpec((ROWS, RATIO * HEAD), lambda h: (0, h + first)),
-            pl.BlockSpec((ROWS, RATIO * HEAD), lambda h: (0, h + first)),
-        ],
+        grid=(KV_HEADS,),
+        in_specs=[row, row, block, block],
         out_specs=pl.BlockSpec((GROUPS, CHUNK, 2 * WIDE), lambda h: (0, 0, h)),
-        out_shape=jax.ShapeDtypeStruct((GROUPS, CHUNK, count * 2 * WIDE), BF16),
+        out_shape=jax.ShapeDtypeStruct((GROUPS, CHUNK, KV_HEADS * 2 * WIDE), BF16),
         scratch_shapes=[pltpu.VMEM((TALL, TALL), BF16)],
         compiler_params=params(VMEM_WHOLE),
-        cost_estimate=cost(count * 2 * TALL * TALL * 2 * WIDE, count << 20),
+        cost_estimate=cost(KV_HEADS * 2 * TALL * TALL * 2 * WIDE, KV_HEADS << 20),
         name="send_rows",
     )(order, gain, query, d_out)
 
@@ -181,7 +176,8 @@
 
 def attend_kernel(meta_ref, order_ref, qd_ref, *refs):
     k_refs, v_refs = refs[: BACK + 1], refs[BACK + 1 : 2 * BACK + 2]
-    out_ref, *part_refs, bias_ref = refs[-(BACK + 3) :]
+    out_ref, *part_refs, bias_ref = refs[2 * BACK + 2 :]
+    dk_refs, dv_refs = part_refs[: BACK + 1], part_refs[BACK + 1 :]
 
     @pl.when(pl.program_id(0) == 0)
     def _():
@@ -228,75 +224,57 @@
             out_ref[:, :, low + e * HEAD : low + (e + 1) * HEAD] = value[
                 e * TALL : (e + 1) * TALL
             ].reshape(GROUPS, CHUNK, HEAD)
-    for n, ref in enumerate(part_refs):
-        ref[:, :HEAD] = dk[n * ROWS : (n + 1) * ROWS].astype(ref.dtype)
-        ref[:, HEAD:] = dv[n * ROWS : (n + 1) * ROWS].astype(ref.dtype)
-
-
-def attend(meta, order, received, keys, values, first, count, room, weight):
-    head_spec = pl.BlockSpec((ROWS, HEAD), lambda h: (0, h + first))
-    part_spec = pl.BlockSpec((ROWS, WIDE), lambda h: (0, h))
+    for whole, parts in ((dk, dk_refs), (dv, dv_refs)):
+        for n, ref in enumerate(parts):
+            ref[...] = whole[n * ROWS : (n + 1) * ROWS].astype(ref.dtype)
+
+
+def attend(meta, order, received, keys, values):
+    head_spec = pl.BlockSpec((ROWS, HEAD), lambda h: (0, h))
     rows_spec = pl.BlockSpec((GROUPS, CHUNK, 2 * WIDE), lambda h: (0, 0, h))
-    elements = count * RATIO * ROWS * WINDOW
-    return pl.pallas_call(
+    elements = Q_HEADS * ROWS * WINDOW
+    parts = [
+        jax.ShapeDtypeStruct((ROWS, KV_HEADS * HEAD), BF16 if n == 0 else F32)
+        for n in range(BACK + 1)
+    ]
+    out, *parts = pl.pallas_call(
         attend_kernel,
-        grid=(count,),
+        grid=(KV_HEADS,),
         in_specs=[
             pl.BlockSpec(memory_space=pltpu.SMEM),
             pl.BlockSpec((1, ROWS), lambda h: (0, 0)),
             rows_spec,
         ]
         + [head_spec] * (2 * BACK + 2),
-        out_specs=[rows_spec] + [part_spec] * (BACK + 1),
-        out_shape=[jax.ShapeDtypeStruct((GROUPS, CHUNK, (count + room) * 2 * WIDE), BF16)]
-        + [
-            jax.ShapeDtypeStruct((ROWS, count * WIDE), BF16 if n == 0 else F32)
-            for n in range(BACK + 1)
-        ],
+        out_specs=[rows_spec] + [head_spec] * (2 * BACK + 2),
+        out_shape=[jax.ShapeDtypeStruct(received.shape, BF16)] + parts * 2,
         scratch_shapes=[pltpu.VMEM((WINDOW, TALL), F32)],
         compiler_params=params(),
-        cost_estimate=cost(weight * elements * HEAD, count * (3 << 20), elements),
+        cost_estimate=cost(WEIGHT * elements * HEAD, 3 << 23, elements),
         name="attend",
     )(meta, order, received, *keys, *values)
-
-
-def return_kv_kernel(order_ref, *refs):
-    half = KV_HEADS * HEAD // 2
-    count, out_ref = (len(refs) - 2) // 2, refs[-1]
-    total = jnp.concatenate(
-        [
-            (got[...].astype(F32) + own[...]).astype(BF16)
-            for got, own in zip(refs[:count], refs[count : 2 * count])
-        ],
-        axis=1,
-    )
-
-    def columns(which, part):
-        heads = range(part * KV_HEADS // 2, (part + 1) * KV_HEADS // 2)
-        return jnp.concatenate([total[:, head_cols(2 * h + which)] for h in heads], axis=1)
-
-    stack = jnp.concatenate(
-        [columns(which, part) for which in range(2) for part in range(2)], axis=0
-    )
-    rows = dot(pack_matrix(order_ref), stack, MM).astype(BF16)
+    return out, parts[: BACK + 1], parts[BACK + 1 :]
+
+
+def return_kv_kernel(order_ref, dk_ref, dv_ref, own_dk_ref, own_dv_ref, out_ref):
+    half = KV_HEADS * HEAD // 2
+    stack = []
+    for got, own in ((dk_ref, own_dk_ref), (dv_ref, own_dv_ref)):
+        total = (got[...].astype(F32) + own[...]).astype(BF16)
+        stack += [total[:, :half], total[:, half:]]
+    rows = dot(pack_matrix(order_ref), jnp.concatenate(stack, axis=0), MM).astype(BF16)
     out_ref[...] = rows.reshape(GROUPS, CHUNK, half)
 
 
-def return_kv(order, got, own, result):
-    half = KV_HEADS * HEAD // 2
-    place = result.shape[2] // half - 1
-    small = [pl.BlockSpec(a.shape, lambda i: (0, 0)) for a in (order, *got, *own)]
+def return_kv(order, *sums):
+    half = KV_HEADS * HEAD // 2
     return pl.pallas_call(
         return_kv_kernel,
-        grid=(1,),
-        in_specs=small + [pl.BlockSpec(memory_space=pl.ANY)],
-        out_specs=pl.BlockSpec((GROUPS, CHUNK, half), lambda i: (0, 0, place)),
-        out_shape=jax.ShapeDtypeStruct(result.shape, BF16),
-        input_output_aliases={len(small): 0},
+        out_shape=jax.ShapeDtypeStruct((GROUPS, CHUNK, half), BF16),
         compiler_params=params(),
         cost_estimate=cost(2 * TALL**3, 3 << 20),
         name="return_kv",
-    )(order, *got, *own, result)
+    )(order, *sums)
 
 
 def finish_rows_step(rows, gain, q_ref, out_ref, dq_ref):
@@ -309,8 +287,39 @@
             dq_ref[:, at] = norm_back(q_ref[:, at].astype(F32), gain, dy).astype(BF16)
 
 
-def finish_kv_step(rows, gain, k_ref, dk_ref, dv_ref):
-    half = KV_HEADS * HEAD // 2
+def finish_rows_kernel(order_ref, gain_ref, q_ref, in_ref, *refs):
+    out_ref, dq_ref, home_ref = refs
+
+    @pl.when(pl.program_id(0) == 0)
+    def _():
+        home_ref[...] = home_matrix(order_ref)
+
+    rows = dot(home_ref[...], in_ref[...].reshape(TALL, 2 * WIDE), MM)
+    finish_rows_step(rows, gain_ref[...], q_ref, out_ref, dq_ref)
+
+
+def finish_rows(order, gain, query, received):
+    block = pl.BlockSpec((ROWS, RATIO * HEAD), lambda h: (0, h))
+    whole = jax.ShapeDtypeStruct((ROWS, Q_HEADS * HEAD), BF16)
+    row = pl.BlockSpec((1, ROWS), lambda h: (0, 0))
+    return pl.pallas_call(
+        finish_rows_kernel,
+        grid=(KV_HEADS,),
+        in_specs=[row, row, block]
+        + [pl.BlockSpec((GROUPS, CHUNK, 2 * WIDE), lambda h: (0, 0, h))],
+        out_specs=[block, block],
+        out_shape=[whole, whole],
+        scratch_shapes=[pltpu.VMEM((TALL, TALL), BF16)],
+        compiler_params=params(),
+        cost_estimate=cost(KV_HEADS * 2 * TALL * TALL * 2 * WIDE, KV_HEADS * (5 << 18)),
+        name="finish_rows",
+    )(order, gain, query, received)
+
+
+def finish_kv_kernel(order_ref, gain_ref, k_ref, in_ref, dk_ref, dv_ref):
+    half = KV_HEADS * HEAD // 2
+    gain = gain_ref[...]
+    rows = dot(home_matrix(order_ref), in_ref[...].reshape(TALL, half), MM)
     for h in range(KV_HEADS):
         part, cols = h // (KV_HEADS // 2), head_cols(h % (KV_HEADS // 2))
         dy = rows[part * ROWS : (part + 1) * ROWS, cols]
@@ -321,52 +330,15 @@
     dv_ref[:, half:] = rows[3 * ROWS :].astype(BF16)
 
 
-def finish_kernel(with_kv, order_ref, gain_ref, q_ref, in_ref, *refs):
-    home_ref = refs[-1]
-    step = pl.program_id(0)
-
-    @pl.when(step == 0)
-    def _():
-        home_ref[...] = home_matrix(order_ref)
-
-    rows = dot(home_ref[...], in_ref[...].reshape(TALL, 2 * WIDE), MM)
-    if with_kv:
-        k_gain_ref, k_ref, _, _, out_ref, dq_ref, dk_ref, dv_ref = refs[:-1]
-        last = pl.num_programs(0) - 1
-
-        @pl.when(step < last)
-        def _():
-            finish_rows_step(rows, gain_ref[...], q_ref, out_ref, dq_ref)
-
-        @pl.when(step == last)
-        def _():
-            finish_kv_step(rows, k_gain_ref[...], k_ref, dk_ref, dv_ref)
-    else:
-        out_ref, dq_ref = refs[:-1]
-        finish_rows_step(rows, gain_ref[...], q_ref, out_ref, dq_ref)
-
-
-def finish(order, gain, query, received, first, count, kv=(), earlier=()):
-    block = pl.BlockSpec((ROWS, RATIO * HEAD), lambda h: (0, jnp.minimum(h, count - 1) + first))
-    whole = jax.ShapeDtypeStruct((ROWS, Q_HEADS * HEAD), BF16)
-    row = pl.BlockSpec((1, ROWS), lambda h: (0, 0))
-    kv_block = pl.BlockSpec((ROWS, KV_HEADS * HEAD), lambda h: (0, 0))
-    kv_whole = jax.ShapeDtypeStruct((ROWS, KV_HEADS * HEAD), BF16)
-    in_specs = [row, row, block, pl.BlockSpec((GROUPS, CHUNK, 2 * WIDE), lambda h: (0, 0, h))]
-    if kv:
-        in_specs += [row, kv_block] + [pl.BlockSpec(memory_space=pl.ANY)] * 2
-    return pl.pallas_call(
-        functools.partial(finish_kernel, bool(kv)),
-        grid=(count + 1 if kv else count,),
-        in_specs=in_specs,
-        out_specs=[block, block] + ([kv_block] * 2 if kv else []),
-        out_shape=[whole, whole] + ([kv_whole] * 2 if kv else []),
-        scratch_shapes=[pltpu.VMEM((TALL, TALL), BF16)],
-        input_output_aliases={6: 0, 7: 1} if kv else {},
-        compiler_params=params(),
-        cost_estimate=cost(count * 2 * TALL * TALL * 2 * WIDE, count * (5 << 18)),
-        name="finish",
-    )(order, gain, query, received, *kv, *earlier)
+def finish_kv(order, gain, key_projection, received):
+    whole = jax.ShapeDtypeStruct((ROWS, KV_HEADS * HEAD), BF16)
+    return pl.pallas_call(
+        finish_kv_kernel,
+        out_shape=[whole, whole],
+        compiler_params=params(),
+        cost_estimate=cost(2 * TALL**3, 3 << 19),
+        name="finish_kv",
+    )(order, gain, key_projection, received)
 
 
 def exchange(array):
@@ -391,56 +363,28 @@
     k_gain = key_norm_gain.reshape(1, HEAD)
     place = lax.axis_index("seq").astype(jnp.int32)
     meta = jnp.concatenate([seq_lengths[0], place[None]])
-    counts = (FIRST, KV_HEADS - FIRST)
-    starts = (0, FIRST)
-
-    kv_sent = send_kv(leaving, k_gain, key_projection, value)
-    kv_received = exchange(kv_sent)
-    sent = [
-        send_rows(leaving, q_gain, query, d_out, first, count)
-        for first, count in zip(starts, counts)
-    ]
-    kv_received, *sent = lax.optimization_barrier((kv_received, *sent))
-    received_first = exchange(sent[0])
-
+
+    kv_received = exchange(send_kv(leaving, k_gain, key_projection, value))
+    sent = send_rows(leaving, q_gain, query, d_out)
     keys, values = ([block] for block in sort_kv(arriving, kv_received))
+    received = exchange(after(sent, keys[0]))
+
     for n in range(BACK):
         keys.append(along(after(keys[-1], values[n - 1] if n > 1 else None), 1))
         values.append(along(values[-1], 1))
-    received_last = exchange(after(after(sent[1], received_first), values[BACK - 1]))
-
-    def back_along(parts):
-        totals = parts[:1]
-        for part in parts[1:-1]:
-            totals.append((along(totals[-1], -1).astype(F32) + part).astype(BF16))
-        return totals + [along(totals[-1], -1)], parts[-1]
-
-    result, *parts = attend(
-        meta, arriving, received_first, keys[::-1], values[::-1], 0, FIRST, 0, WEIGHTS[0]
-    )
-    sums0, own0 = back_along(parts)
-    back_first = exchange(result)
-    keys[0] = after(keys[0], sums0[1])
-    result, *parts = attend(
-        meta, arriving, received_last, keys[::-1], values[::-1], FIRST, LAST, 1, WEIGHTS[1]
-    )
-    sums1, own1 = back_along(parts)
-    merged = return_kv(arriving, (sums0[-1], sums1[-1]), (own0, own1), result)
-    back_last = exchange(after(merged, back_first))
-
-    outs = finish(leaving, q_gain, query, back_first, starts[0], counts[0])
-    return tuple(
-        finish(
-            leaving,
-            q_gain,
-            query,
-            back_last,
-            starts[1],
-            counts[1],
-            kv=(k_gain, key_projection),
-            earlier=outs,
-        )
-    )
+
+    result, dk_parts, dv_parts = attend(meta, arriving, received, keys[::-1], values[::-1])
+    back = exchange(result)
+
+    dk, dv = dk_parts[0], dv_parts[0]
+    for n in range(1, BACK):
+        dk = (along(dk, -1).astype(F32) + dk_parts[n]).astype(BF16)
+        dv = (along(dv, -1).astype(F32) + dv_parts[n]).astype(BF16)
+    sums = along(dk, -1), along(dv, -1), dk_parts[-1], dv_parts[-1]
+    kv_back = exchange(after(return_kv(arriving, *sums), back))
+
+    outs = finish_rows(leaving, q_gain, query, back)
+    return *outs, *finish_kv(leaving, k_gain, key_projection, kv_back)
 
 
 def solution(mesh):

time: 188 us -> 186 us (0.989)
  waiting for transfers between devices: 73.8 us -> 88.2 us
  starting transfers between devices: 59.1 us -> 48.4 us
  Pallas kernels: 51.1 us -> 47 us
    ppermute x16, waiting for transfers between devices: 57.6 us -> 82.3 us  [along(): lax.ppermute(array, 'seq', [(i, (i + step) % count) for i in range(count)])]
    all_to_all x5 -> x4, starting transfers between devices: 42 us -> 29.8 us  [exchange(): return lax.all_to_all(array, 'dp', split_axis=0, concat_axis=0, tiled=True)]
    all_to_all x5 -> x4, waiting for transfers between devices: 16.2 us -> 5.94 us  [exchange(): return lax.all_to_all(array, 'dp', split_axis=0, concat_axis=0, tiled=True)]
    pallas_call x7 -> x5, Pallas kernels: 48.1 us -> 44 us  [the longest x1 22.4 us: attend(): pl.pallas_call(attend_kernel, grid=(KV_HEADS,), in_specs=[pl.BlockSpec(me...]
  transfers between devices with their start and end apart: 21 -> 20, of which waited for: 14 -> 19; matrix products, arithmetic and copies ran while one was open for 0% -> 0% of each run, Pallas kernels for 24% -> 11%
where the time goes in v7:
time: 186 us; the launch traced here: 185 us
  waiting for transfers between devices  88.2 us (47%)
  starting transfers between devices  48.4 us (26%)
  Pallas kernels  47 us (25%)
    ppermute x16, waiting for transfers between devices, along(): lax.ppermute(array, 'seq', [(i, (i + step) % count) for i in range(count)])  82.3 us
    all_to_all x4, starting transfers between devices, exchange(): return lax.all_to_all(array, 'dp', split_axis=0, concat_axis=0, tiled=True)  29.8 us
    pallas_call x1, Pallas kernels, attend(): pl.pallas_call(attend_kernel, grid=(KV_HEADS,), in_specs=[pl.BlockSpec(me...  22.4 us
    ppermute x16, starting transfers between devices, along(): lax.ppermute(array, 'seq', [(i, (i + step) % count) for i in range(count)])  18.5 us
    pallas_call x1, Pallas kernels, send_rows(): pl.pallas_call(send_rows_kernel, grid=(KV_HEADS,), in_specs=[row, row, bl...  9.09 us
    pallas_call x1, Pallas kernels, finish_rows(): pl.pallas_call(finish_rows_kernel, grid=(KV_HEADS,), in_specs=[row, row,...  8.76 us
    all_to_all x4, waiting for transfers between devices, exchange(): return lax.all_to_all(array, 'dp', split_axis=0, concat_axis=0, tiled=True)  5.94 us
  transfers between devices with their start and end apart: 20, of which 19 were waited for; matrix products, arithmetic and copies ran while one was open for 0% of the time, Pallas kernels for 11%

profile of v7, /device:TPU:1, one launch (start us, length us, event | category | flops | bytes accessed | tf_op | source)
XLA Modules:
  0.0 185.0 jit_solution(16265962298668065218)
XLA Ops:
  0.6 2.5 %send_kv.1 = bf16[32,16,512]{2,1,0:T(8,128)(2,1)} custom-call(s32[1,128]{1,0:T(1,128)} %bitcast.6, f32[1,128]{1,0:T(1,128)} %bitcast.10, bf16[128,1024]{1,0:T(8,128)(2,1)} %k_ref.3, bf16[128,1024]{1,0:T(8,128)(2,1)} %v_ref.1), custom_call_target="tpu_custom_call" | custom-call | flops 268435456 | bytes 1572864 | tf_op jit(solution)/shard_map/send_kv/pallas_call | solution.py:114
  3.1 8.6 %all-to-all-start = ((bf16[32,16,512]{2,1,0:T(8,128)(2,1)}), bf16[32,16,512]{2,1,0:T(8,128)(2,1)S(1)}, u32[]{:S(2)}, u32[]{:S(2)}) async-start(bf16[32,16,512]{2,1,0:T(8,128)(2,1)} %send_kv.1), calls=%async_computation | async-start | bytes 1048576 | tf_op jit(solution)/shard_map/all_to_all | solution.py:345
  11.7 0.0 copy-start.4
  11.8 9.1 %send_rows.1 = bf16[32,16,4096]{2,1,0:T(8,128)(2,1)} custom-call(s32[1,128]{1,0:T(1,128)} %bitcast.7, f32[1,128]{1,0:T(1,128)} %bitcast.15, bf16[128,8192]{1,0:T(8,128)(2,1)} %q_ref.3, bf16[128,8192]{1,0:T(8,128)(2,1)} %d_ref.1), custom_call_target="tpu_custom_call" | custom-call | flops 2147483648 | bytes 8388608 | tf_op jit(solution)/shard_map/send_rows/pallas_call | solution.py:146
  20.8 2.4 %all-to-all-done.in_ref = bf16[32,16,512]{2,1,0:T(8,128)(2,1)S(1)} async-done(((bf16[32,16,512]{2,1,0:T(8,128)(2,1)}), bf16[32,16,512]{2,1,0:T(8,128)(2,1)S(1)}, u32[]{:S(2)}, u32[]{:S(2)}) %all-to-all-start) | async-done | bytes 524320 | tf_op jit(solution)/shard_map/all_to_all | solution.py:345
  23.3 0.0 copy-done.4
  23.3 0.5 sort_kv.1
  23.8 0.0 copy-start.6
  23.8 0.0 copy-start.17
  23.8 5.1 %all-to-all-start.1 = ((bf16[32,16,4096]{2,1,0:T(8,128)(2,1)}), bf16[32,16,4096]{2,1,0:T(8,128)(2,1)}, u32[]{:S(2)}, u32[]{:S(2)}) async-start(bf16[32,16,4096]{2,1,0:T(8,128)(2,1)} %send_rows.1), calls=%async_computation.1 | async-start | bytes 8388608 | tf_op jit(solution)/shard_map/all_to_all | solution.py:345
  29.0 1.7 collective-permute-start
  30.7 1.6 collective-permute-start.2
  32.3 8.8 %collective-permute-done.refs_3_ = bf16[128,1024]{1,0:T(8,128)(2,1)S(1)} collective-permute-done((bf16[128,1024]{1,0:T(8,128)(2,1)S(1)}, bf16[128,1024]{1,0:T(8,128)(2,1)S(1)}, u32[]{:S(2)}, u32[]{:S(2)}) %collective-permute-start) | collective-permute-done | bytes 262176 | tf_op jit(solution)/shard_map/ppermute | solution.py:350
  41.2 0.0 collective-permute-start.1
  41.2 5.6 %collective-permute-done.2.refs_8_ = bf16[128,1024]{1,0:T(8,128)(2,1)S(1)} collective-permute-done((bf16[128,1024]{1,0:T(8,128)(2,1)S(1)}, bf16[128,1024]{1,0:T(8,128)(2,1)S(1)}, u32[]{:S(2)}, u32[]{:S(2)}) %collective-permute-start.2) | collective-permute-done | bytes 262176 | tf_op jit(solution)/shard_map/ppermute | solution.py:350
  46.8 0.0 collective-permute-start.4
  46.8 5.6 %collective-permute-done.1.refs_2_ = bf16[128,1024]{1,0:T(8,128)(2,1)S(1)} collective-permute-done((bf16[128,1024]{1,0:T(8,128)(2,1)S(1)}, bf16[128,1024]{1,0:T(8,128)(2,1)S(1)}, u32[]{:S(2)}, u32[]{:S(2)}) %collective-permute-start.1) | collective-permute-done | bytes 262176 | tf_op jit(solution)/shard_map/ppermute | solution.py:350
  52.4 0.0 collective-permute-start.3
  52.4 5.6 %collective-permute-done.4.refs_7_ = bf16[128,1024]{1,0:T(8,128)(2,1)S(1)} collective-permute-done((bf16[128,1024]{1,0:T(8,128)(2,1)S(1)}, bf16[128,1024]{1,0:T(8,128)(2,1)S(1)}, u32[]{:S(2)}, u32[]{:S(2)}) %collective-permute-start.4) | collective-permute-done | bytes 262176 | tf_op jit(solution)/shard_map/ppermute | solution.py:350
  58.0 0.0 collective-permute-start.6
  58.0 5.6 %collective-permute-done.3.refs_1_ = bf16[128,1024]{1,0:T(8,128)(2,1)S(1)} collective-permute-done((bf16[128,1024]{1,0:T(8,128)(2,1)S(1)}, bf16[128,1024]{1,0:T(8,128)(2,1)S(1)}, u32[]{:S(2)}, u32[]{:S(2)}) %collective-permute-start.3) | collective-permute-done | bytes 262176 | tf_op jit(solution)/shard_map/ppermute | solution.py:350
  63.6 5.6 %collective-permute-done.6.refs_6_ = bf16[128,1024]{1,0:T(8,128)(2,1)S(1)} collective-permute-done((bf16[128,1024]{1,0:T(8,128)(2,1)S(1)}, bf16[128,1024]{1,0:T(8,128)(2,1)S(1)}, u32[]{:S(2)}, u32[]{:S(2)}) %collective-permute-start.6) | collective-permute-done | bytes 262176 | tf_op jit(solution)/shard_map/ppermute | solution.py:350
  69.3 0.0 collective-permute-start.7
  69.3 0.0 collective-permute-start.5
  69.3 0.1 pad_add_fusion.meta_ref
  69.4 8.2 %collective-permute-done.7.refs_5_ = bf16[128,1024]{1,0:T(8,128)(2,1)S(1)} collective-permute-done((bf16[128,1024]{1,0:T(8,128)(2,1)S(1)}, bf16[128,1024]{1,0:T(8,128)(2,1)S(1)}, u32[]{:S(2)}, u32[]{:S(2)}) %collective-permute-start.7) | collective-permute-done | bytes 262176 | tf_op jit(solution)/shard_map/ppermute | solution.py:350
  77.6 5.6 %collective-permute-done.5.refs_0_ = bf16[128,1024]{1,0:T(8,128)(2,1)S(1)} collective-permute-done((bf16[128,1024]{1,0:T(8,128)(2,1)S(1)}, bf16[128,1024]{1,0:T(8,128)(2,1)S(1)}, u32[]{:S(2)}, u32[]{:S(2)}) %collective-permute-start.5) | collective-permute-done | bytes 262176 | tf_op jit(solution)/shard_map/ppermute | solution.py:350
  83.2 0.0 all-to-all-done.1.qd_ref
  83.3 22.4 %attend.1 = (bf16[32,16,4096]{2,1,0:T(8,128)(2,1)}, bf16[128,1024]{1,0:T(8,128)(2,1)S(1)}, f32[128,1024]{1,0:T(8,128)}, f32[128,1024]{1,0:T(8,128)}, f32[128,102...) custom-call(s32[4]{0:T(128)S(1)} %pad_add_fusion.meta_ref, ...), custom_call_target="tpu_custom_call" | custom-call | flops 24159191040 | bytes 25165824 | tf_op jit(solution)/shard_map/attend/pallas_call | solution.py:240
  105.7 0.0 copy-start.12
  105.7 0.0 copy-start.10
  105.7 0.0 copy-start.9
  105.7 8.7 %all-to-all-start.2 = ((bf16[32,16,4096]{2,1,0:T(8,128)(2,1)}), bf16[32,16,4096]{2,1,0:T(8,128)(2,1)}, u32[]{:S(2)}, u32[]{:S(2)}) async-start(bf16[32,16,4096]{2,1,0:T(8,128)(2,1)} %get-tuple-element.30), calls=%async_computation.2 | async-start | bytes 8388608 | tf_op jit(solution)/shard_map/all_to_all | solution.py:345
  114.5 1.3 collective-permute-start.8
  115.7 0.7 collective-permute-start.12
  116.5 5.9 %collective-permute-done.8 = bf16[128,1024]{1,0:T(8,128)(2,1)S(1)} collective-permute-done((bf16[128,1024]{1,0:T(8,128)(2,1)S(1)}, bf16[128,1024]{1,0:T(8,128)(2,1)S(1)}, u32[]{:S(2)}, u32[]{:S(2)}) %collective-permute-start.8) | collective-permute-done | bytes 262176 | tf_op jit(solution)/shard_map/ppermute | solution.py:350
  122.4 0.1 add_convert_fusion.5
  122.5 2.2 %collective-permute-start.9 = (bf16[128,1024]{1,0:T(8,128)(2,1)S(1)}, bf16[128,1024]{1,0:T(8,128)(2,1)S(1)}, u32[]{:S(2)}, u32[]{:S(2)}) collective-permute-start(bf16[128,1024]{1,0:T(8,128)(2,1)S(1)} %add_convert_fusion.5), channel_id=1, source_target_pairs={{0,7},{1,0},{2,1},{3,2},{4,3},{5,4},{6,5},{7,6},{8,15},{9,8},{10,9... | collective-permute-start | bytes 786440 | tf_op jit(solution)/shard_map/ppermute | solution.py:350
  124.7 3.3 %collective-permute-done.12 = bf16[128,1024]{1,0:T(8,128)(2,1)S(1)} collective-permute-done((bf16[128,1024]{1,0:T(8,128)(2,1)S(1)}, bf16[128,1024]{1,0:T(8,128)(2,1)S(1)}, u32[]{:S(2)}, u32[]{:S(2)}) %collective-permute-start.12) | collective-permute-done | bytes 262176 | tf_op jit(solution)/shard_map/ppermute | solution.py:350
  128.0 0.1 add_convert_fusion.2
  128.1 2.2 %collective-permute-start.13 = (bf16[128,1024]{1,0:T(8,128)(2,1)S(1)}, bf16[128,1024]{1,0:T(8,128)(2,1)S(1)}, u32[]{:S(2)}, u32[]{:S(2)}) collective-permute-start(bf16[128,1024]{1,0:T(8,128)(2,1)S(1)} %add_convert_fusion.2), channel_id=1, source_target_pairs={{0,7},{1,0},{2,1},{3,2},{4,3},{5,4},{6,5},{7,6},{8,15},{9,8},{10,9... | collective-permute-start | bytes 786440 | tf_op jit(solution)/shard_map/ppermute | solution.py:350
  130.3 3.3 %collective-permute-done.9 = bf16[128,1024]{1,0:T(8,128)(2,1)S(1)} collective-permute-done((bf16[128,1024]{1,0:T(8,128)(2,1)S(1)}, bf16[128,1024]{1,0:T(8,128)(2,1)S(1)}, u32[]{:S(2)}, u32[]{:S(2)}) %collective-permute-start.9) | collective-permute-done | bytes 262176 | tf_op jit(solution)/shard_map/ppermute | solution.py:350
  133.6 0.1 add_convert_fusion.4
  133.7 2.2 %collective-permute-start.10 = (bf16[128,1024]{1,0:T(8,128)(2,1)S(1)}, bf16[128,1024]{1,0:T(8,128)(2,1)S(1)}, u32[]{:S(2)}, u32[]{:S(2)}) collective-permute-start(bf16[128,1024]{1,0:T(8,128)(2,1)S(1)} %add_convert_fusion.4), channel_id=1, source_target_pairs={{0,7},{1,0},{2,1},{3,2},{4,3},{5,4},{6,5},{7,6},{8,15},{9,8},{10,9... | collective-permute-start | bytes 786440 | tf_op jit(solution)/shard_map/ppermute | solution.py:350
  135.9 3.3 %collective-permute-done.13 = bf16[128,1024]{1,0:T(8,128)(2,1)S(1)} collective-permute-done((bf16[128,1024]{1,0:T(8,128)(2,1)S(1)}, bf16[128,1024]{1,0:T(8,128)(2,1)S(1)}, u32[]{:S(2)}, u32[]{:S(2)}) %collective-permute-start.13) | collective-permute-done | bytes 262176 | tf_op jit(solution)/shard_map/ppermute | solution.py:350
  139.3 0.1 add_convert_fusion.1
  139.3 2.2 %collective-permute-start.14 = (bf16[128,1024]{1,0:T(8,128)(2,1)S(1)}, bf16[128,1024]{1,0:T(8,128)(2,1)S(1)}, u32[]{:S(2)}, u32[]{:S(2)}) collective-permute-start(bf16[128,1024]{1,0:T(8,128)(2,1)S(1)} %add_convert_fusion.1), channel_id=1, source_target_pairs={{0,7},{1,0},{2,1},{3,2},{4,3},{5,4},{6,5},{7,6},{8,15},{9,8},{10,9... | collective-permute-start | bytes 786440 | tf_op jit(solution)/shard_map/ppermute | solution.py:350
  141.5 3.3 %collective-permute-done.10 = bf16[128,1024]{1,0:T(8,128)(2,1)S(1)} collective-permute-done((bf16[128,1024]{1,0:T(8,128)(2,1)S(1)}, bf16[128,1024]{1,0:T(8,128)(2,1)S(1)}, u32[]{:S(2)}, u32[]{:S(2)}) %collective-permute-start.10) | collective-permute-done | bytes 262176 | tf_op jit(solution)/shard_map/ppermute | solution.py:350
  144.9 0.0 copy-done.8
  144.9 0.1 add_convert_fusion.3
  145.0 2.2 %collective-permute-start.11 = (bf16[128,1024]{1,0:T(8,128)(2,1)S(1)}, bf16[128,1024]{1,0:T(8,128)(2,1)S(1)}, u32[]{:S(2)}, u32[]{:S(2)}) collective-permute-start(bf16[128,1024]{1,0:T(8,128)(2,1)S(1)} %add_convert_fusion.3), channel_id=1, source_target_pairs={{0,7},{1,0},{2,1},{3,2},{4,3},{5,4},{6,5},{7,6},{8,15},{9,8},{10,9... | collective-permute-start | bytes 786440 | tf_op jit(solution)/shard_map/ppermute | solution.py:350
  147.1 3.3 %collective-permute-done.14 = bf16[128,1024]{1,0:T(8,128)(2,1)S(1)} collective-permute-done((bf16[128,1024]{1,0:T(8,128)(2,1)S(1)}, bf16[128,1024]{1,0:T(8,128)(2,1)S(1)}, u32[]{:S(2)}, u32[]{:S(2)}) %collective-permute-start.14) | collective-permute-done | bytes 262176 | tf_op jit(solution)/shard_map/ppermute | solution.py:350
  150.5 0.1 add_convert_fusion
  150.6 2.2 %collective-permute-start.15 = (bf16[128,1024]{1,0:T(8,128)(2,1)S(1)}, bf16[128,1024]{1,0:T(8,128)(2,1)S(1)}, u32[]{:S(2)}, u32[]{:S(2)}) collective-permute-start(bf16[128,1024]{1,0:T(8,128)(2,1)S(1)} %add_convert_fusion), channel_id=1, source_target_pairs={{0,7},{1,0},{2,1},{3,2},{4,3},{5,4},{6,5},{7,6},{8,15},{9,8},{10,9... | collective-permute-start | bytes 786440 | tf_op jit(solution)/shard_map/ppermute | solution.py:350
  152.8 3.3 %collective-permute-done.11.dk_ref = bf16[128,1024]{1,0:T(8,128)(2,1)S(1)} collective-permute-done((bf16[128,1024]{1,0:T(8,128)(2,1)S(1)}, bf16[128,1024]{1,0:T(8,128)(2,1)S(1)}, u32[]{:S(2)}, u32[]{:S(2)}) %collective-permute-start.11) | collective-permute-done | bytes 262176 | tf_op jit(solution)/shard_map/ppermute | solution.py:350
  156.1 5.5 %collective-permute-done.15.dv_ref = bf16[128,1024]{1,0:T(8,128)(2,1)S(1)} collective-permute-done((bf16[128,1024]{1,0:T(8,128)(2,1)S(1)}, bf16[128,1024]{1,0:T(8,128)(2,1)S(1)}, u32[]{:S(2)}, u32[]{:S(2)}) %collective-permute-start.15) | collective-permute-done | bytes 262176 | tf_op jit(solution)/shard_map/ppermute | solution.py:350
  161.6 2.3 %return_kv.1 = bf16[32,16,512]{2,1,0:T(8,128)(2,1)} custom-call(s32[1,128]{1,0:T(1,128)S(1)} %bitcast.14, bf16[128,1024]{1,0:T(8,128)(2,1)S(1)} %collective-permute-done.11.dk_ref, bf16[128,1024]{1,0:T(8,128)(2,1)S(1)} %collective-permute-done.15.dv_ref, f32[128,1024]{1,0:T(8,128)S(1)} %copy-done, f32[128,1024]{1,0:T(8,128)} %get-tuple-element.42.own_dv_ref), custom_call_target="tpu_custom_call" | custom-call | flops 268435456 | bytes 3145728 | tf_op jit(solution)/shard_map/return_kv/pallas_call | solution.py:271
  164.0 0.7 all-to-all-done.2.in_ref
  164.7 7.4 %all-to-all-start.3 = ((bf16[32,16,512]{2,1,0:T(8,128)(2,1)}), bf16[32,16,512]{2,1,0:T(8,128)(2,1)S(1)}, u32[]{:S(2)}, u32[]{:S(2)}) async-start(bf16[32,16,512]{2,1,0:T(8,128)(2,1)} %return_kv.1), calls=%async_computation.3 | async-start | bytes 1048576 | tf_op jit(solution)/shard_map/all_to_all | solution.py:345
  172.1 0.0 copy-start.1
  172.2 0.0 copy-start.3
  172.2 8.8 %finish_rows.1 = (bf16[128,8192]{1,0:T(8,128)(2,1)}, bf16[128,8192]{1,0:T(8,128)(2,1)}) custom-call(s32[1,128]{1,0:T(1,128)S(1)} %bitcast.8, f32[1,128]{1,0:T(1,128)S(1)} %bitcast.16, bf16[128,8192]{1,0:T(8,128)(2,1)} %q_ref.3, bf16[32,16,4096]{2,1,0:T(8,128)(2,1)} %all-to-all-done.2.in_ref), custom_call_target="tpu_custom_call" | custom-call | flops 2147483648 | bytes 10485760 | tf_op jit(solution)/shard_map/finish_rows/pallas_call | solution.py:305
  180.9 2.7 %all-to-all-done.3.in_ref = bf16[32,16,512]{2,1,0:T(8,128)(2,1)S(1)} async-done(((bf16[32,16,512]{2,1,0:T(8,128)(2,1)}), bf16[32,16,512]{2,1,0:T(8,128)(2,1)S(1)}, u32[]{:S(2)}, u32[]{:S(2)}) %all-to-all-start.3) | async-done | bytes 524320 | tf_op jit(solution)/shard_map/all_to_all | solution.py:345
  183.7 1.4 finish_kv.1
  (26 shorter events, 0.1 us)
Async XLA Ops:
  3.1 20.1 %all-to-all-start = ((bf16[32,16,512]{2,1,0:T(8,128)(2,1)}), bf16[32,16,512]{2,1,0:T(8,128)(2,1)S(1)}, u32[]{:S(2)}, u32[]{:S(2)}) async-start(bf16[32,16,512]{2,1,0:T(8,128)(2,1)} %send_kv.1), calls=%async_computation | async-start | bytes 1048576 | tf_op jit(solution)/shard_map/all_to_all | solution.py:345
  11.7 11.6 %copy-start.4 = (s32[1,1,128]{2,1,0:T(1,128)S(1)}, s32[1,1,128]{2,1,0:T(1,128)}, u32[]{:S(2)}) copy-start(s32[1,1,128]{2,1,0:T(1,128)} %param.17) | copy-start | bytes 1540
  23.8 6.9 %copy-start.6 = (bf16[128,1024]{1,0:T(8,128)(2,1)}, bf16[128,1024]{1,0:T(8,128)(2,1)S(1)}, u32[]{:S(2)}) copy-start(bf16[128,1024]{1,0:T(8,128)(2,1)S(1)} %get-tuple-element.27.refs_9_) | copy-start | bytes 786436
  23.8 45.5 %copy-start.17 = (s32[1,3]{1,0:T(1,128)S(1)}, s32[1,3]{1,0:T(1,128)}, u32[]{:S(2)}) copy-start(s32[1,3]{1,0:T(1,128)} %param.15) | copy-start | bytes 40
  23.8 59.4 %all-to-all-start.1 = ((bf16[32,16,4096]{2,1,0:T(8,128)(2,1)}), bf16[32,16,4096]{2,1,0:T(8,128)(2,1)}, u32[]{:S(2)}, u32[]{:S(2)}) async-start(bf16[32,16,4096]{2,1,0:T(8,128)(2,1)} %send_rows.1), calls=%async_computation.1 | async-start | bytes 8388608 | tf_op jit(solution)/shard_map/all_to_all | solution.py:345
  29.0 12.2 %collective-permute-start = (bf16[128,1024]{1,0:T(8,128)(2,1)S(1)}, bf16[128,1024]{1,0:T(8,128)(2,1)S(1)}, u32[]{:S(2)}, u32[]{:S(2)}) collective-permute-start(bf16[128,1024]{1,0:T(8,128)(2,1)S(1)} %get-tuple-element.25.refs_4_), channel_id=1, source_target_pairs={{0,1},{1,2},{2,3},{3,4},{4,5},{5,6},{6,7},{7,0},{8,9},{9,10},{10,1... | collective-permute-start | bytes 786440 | tf_op jit(solution)/shard_map/ppermute | solution.py:350
  30.7 16.1 %collective-permute-start.2 = (bf16[128,1024]{1,0:T(8,128)(2,1)S(1)}, bf16[128,1024]{1,0:T(8,128)(2,1)S(1)}, u32[]{:S(2)}, u32[]{:S(2)}) collective-permute-start(bf16[128,1024]{1,0:T(8,128)(2,1)S(1)} %get-tuple-element.27.refs_9_), channel_id=1, source_target_pairs={{0,1},{1,2},{2,3},{3,4},{4,5},{5,6},{6,7},{7,0},{8,9},{9,10},{10,1... | collective-permute-start | bytes 786440 | tf_op jit(solution)/shard_map/ppermute | solution.py:350
  41.2 11.2 %collective-permute-start.1 = (bf16[128,1024]{1,0:T(8,128)(2,1)S(1)}, bf16[128,1024]{1,0:T(8,128)(2,1)S(1)}, u32[]{:S(2)}, u32[]{:S(2)}) collective-permute-start(bf16[128,1024]{1,0:T(8,128)(2,1)S(1)} %collective-permute-done.refs_3_), channel_id=1, source_target_pairs={{0,1},{1,2},{2,3},{3,4},{4,5},{5,6},{6,7},{7,0},{8,9},{9,10},{10,1... | collective-permute-start | bytes 786440 | tf_op jit(solution)/shard_map/ppermute | solution.py:350
  46.8 36.4 %copy-start.13 = (bf16[128,1024]{1,0:T(8,128)(2,1)}, bf16[128,1024]{1,0:T(8,128)(2,1)S(1)}, u32[]{:S(2)}) copy-start(bf16[128,1024]{1,0:T(8,128)(2,1)S(1)} %collective-permute-done.2.refs_8_) | copy-start | bytes 786436
  46.8 11.2 %collective-permute-start.4 = (bf16[128,1024]{1,0:T(8,128)(2,1)S(1)}, bf16[128,1024]{1,0:T(8,128)(2,1)S(1)}, u32[]{:S(2)}, u32[]{:S(2)}) collective-permute-start(bf16[128,1024]{1,0:T(8,128)(2,1)S(1)} %collective-permute-done.2.refs_8_), channel_id=1, source_target_pairs={{0,1},{1,2},{2,3},{3,4},{4,5},{5,6},{6,7},{7,0},{8,9},{9,10},{10,1... | collective-permute-start | bytes 786440 | tf_op jit(solution)/shard_map/ppermute | solution.py:350
  52.4 11.2 %collective-permute-start.3 = (bf16[128,1024]{1,0:T(8,128)(2,1)S(1)}, bf16[128,1024]{1,0:T(8,128)(2,1)S(1)}, u32[]{:S(2)}, u32[]{:S(2)}) collective-permute-start(bf16[128,1024]{1,0:T(8,128)(2,1)S(1)} %collective-permute-done.1.refs_2_), channel_id=1, source_target_pairs={{0,1},{1,2},{2,3},{3,4},{4,5},{5,6},{6,7},{7,0},{8,9},{9,10},{10,1... | collective-permute-start | bytes 786440 | tf_op jit(solution)/shard_map/ppermute | solution.py:350
  58.0 25.2 %copy-start.14 = (bf16[128,1024]{1,0:T(8,128)(2,1)}, bf16[128,1024]{1,0:T(8,128)(2,1)S(1)}, u32[]{:S(2)}) copy-start(bf16[128,1024]{1,0:T(8,128)(2,1)S(1)} %collective-permute-done.4.refs_7_) | copy-start | bytes 786436
  58.0 11.2 %collective-permute-start.6 = (bf16[128,1024]{1,0:T(8,128)(2,1)S(1)}, bf16[128,1024]{1,0:T(8,128)(2,1)S(1)}, u32[]{:S(2)}, u32[]{:S(2)}) collective-permute-start(bf16[128,1024]{1,0:T(8,128)(2,1)S(1)} %collective-permute-done.4.refs_7_), channel_id=1, source_target_pairs={{0,1},{1,2},{2,3},{3,4},{4,5},{5,6},{6,7},{7,0},{8,9},{9,10},{10,1... | collective-permute-start | bytes 786440 | tf_op jit(solution)/shard_map/ppermute | solution.py:350
  69.3 14.0 %copy-start.15 = (bf16[128,1024]{1,0:T(8,128)(2,1)}, bf16[128,1024]{1,0:T(8,128)(2,1)S(1)}, u32[]{:S(2)}) copy-start(bf16[128,1024]{1,0:T(8,128)(2,1)S(1)} %collective-permute-done.6.refs_6_) | copy-start | bytes 786436
  69.3 8.3 %collective-permute-start.7 = (bf16[128,1024]{1,0:T(8,128)(2,1)S(1)}, bf16[128,1024]{1,0:T(8,128)(2,1)S(1)}, u32[]{:S(2)}, u32[]{:S(2)}) collective-permute-start(bf16[128,1024]{1,0:T(8,128)(2,1)S(1)} %collective-permute-done.6.refs_6_), channel_id=1, source_target_pairs={{0,1},{1,2},{2,3},{3,4},{4,5},{5,6},{6,7},{7,0},{8,9},{9,10},{10,1... | collective-permute-start | bytes 786440 | tf_op jit(solution)/shard_map/ppermute | solution.py:350
  69.3 13.9 %collective-permute-start.5 = (bf16[128,1024]{1,0:T(8,128)(2,1)S(1)}, bf16[128,1024]{1,0:T(8,128)(2,1)S(1)}, u32[]{:S(2)}, u32[]{:S(2)}) collective-permute-start(bf16[128,1024]{1,0:T(8,128)(2,1)S(1)} %collective-permute-done.3.refs_1_), channel_id=1, source_target_pairs={{0,1},{1,2},{2,3},{3,4},{4,5},{5,6},{6,7},{7,0},{8,9},{9,10},{10,1... | collective-permute-start | bytes 786440 | tf_op jit(solution)/shard_map/ppermute | solution.py:350
  77.6 5.6 %copy-start.16 = (bf16[128,1024]{1,0:T(8,128)(2,1)}, bf16[128,1024]{1,0:T(8,128)(2,1)S(1)}, u32[]{:S(2)}) copy-start(bf16[128,1024]{1,0:T(8,128)(2,1)S(1)} %collective-permute-done.7.refs_5_) | copy-start | bytes 786436
  105.7 16.7 %copy-start.12 = (f32[128,1024]{1,0:T(8,128)S(1)}, f32[128,1024]{1,0:T(8,128)}, u32[]{:S(2)}) copy-start(f32[128,1024]{1,0:T(8,128)} %get-tuple-element.34) | copy-start | bytes 1572868
  105.7 22.3 %copy-start.11 = (f32[128,1024]{1,0:T(8,128)S(1)}, f32[128,1024]{1,0:T(8,128)}, u32[]{:S(2)}) copy-start(f32[128,1024]{1,0:T(8,128)} %get-tuple-element.38) | copy-start | bytes 1572868
  105.7 27.9 %copy-start.10 = (f32[128,1024]{1,0:T(8,128)S(1)}, f32[128,1024]{1,0:T(8,128)}, u32[]{:S(2)}) copy-start(f32[128,1024]{1,0:T(8,128)} %get-tuple-element.35) | copy-start | bytes 1572868
  105.7 33.5 %copy-start.9 = (f32[128,1024]{1,0:T(8,128)S(1)}, f32[128,1024]{1,0:T(8,128)}, u32[]{:S(2)}) copy-start(f32[128,1024]{1,0:T(8,128)} %get-tuple-element.39) | copy-start | bytes 1572868
  105.7 58.9 %all-to-all-start.2 = ((bf16[32,16,4096]{2,1,0:T(8,128)(2,1)}), bf16[32,16,4096]{2,1,0:T(8,128)(2,1)}, u32[]{:S(2)}, u32[]{:S(2)}) async-start(bf16[32,16,4096]{2,1,0:T(8,128)(2,1)} %get-tuple-element.30), calls=%async_computation.2 | async-start | bytes 8388608 | tf_op jit(solution)/shard_map/all_to_all | solution.py:345
  114.4 30.5 %copy-start.8 = (f32[128,1024]{1,0:T(8,128)S(1)}, f32[128,1024]{1,0:T(8,128)}, u32[]{:S(2)}) copy-start(f32[128,1024]{1,0:T(8,128)} %get-tuple-element.36) | copy-start | bytes 1572868
  114.4 36.1 %copy-start.7 = (f32[128,1024]{1,0:T(8,128)S(1)}, f32[128,1024]{1,0:T(8,128)}, u32[]{:S(2)}) copy-start(f32[128,1024]{1,0:T(8,128)} %get-tuple-element.40) | copy-start | bytes 1572868
  114.4 47.2 %copy-start = (f32[128,1024]{1,0:T(8,128)S(1)}, f32[128,1024]{1,0:T(8,128)}, u32[]{:S(2)}) copy-start(f32[128,1024]{1,0:T(8,128)} %get-tuple-element.41.own_dk_ref) | copy-start | bytes 1572868
  114.5 7.9 %collective-permute-start.8 = (bf16[128,1024]{1,0:T(8,128)(2,1)S(1)}, bf16[128,1024]{1,0:T(8,128)(2,1)S(1)}, u32[]{:S(2)}, u32[]{:S(2)}) collective-permute-start(bf16[128,1024]{1,0:T(8,128)(2,1)S(1)} %get-tuple-element.33), channel_id=1, source_target_pairs={{0,7},{1,0},{2,1},{3,2},{4,3},{5,4},{6,5},{7,6},{8,15},{9,8},{10,9... | collective-permute-start | bytes 786440 | tf_op jit(solution)/shard_map/ppermute | solution.py:350
  115.7 12.3 %collective-permute-start.12 = (bf16[128,1024]{1,0:T(8,128)(2,1)S(1)}, bf16[128,1024]{1,0:T(8,128)(2,1)S(1)}, u32[]{:S(2)}, u32[]{:S(2)}) collective-permute-start(bf16[128,1024]{1,0:T(8,128)(2,1)S(1)} %get-tuple-element.37), channel_id=1, source_target_pairs={{0,7},{1,0},{2,1},{3,2},{4,3},{5,4},{6,5},{7,6},{8,15},{9,8},{10,9... | collective-permute-start | bytes 786440 | tf_op jit(solution)/shard_map/ppermute | solution.py:350
  122.5 11.2 %collective-permute-start.9 = (bf16[128,1024]{1,0:T(8,128)(2,1)S(1)}, bf16[128,1024]{1,0:T(8,128)(2,1)S(1)}, u32[]{:S(2)}, u32[]{:S(2)}) collective-permute-start(bf16[128,1024]{1,0:T(8,128)(2,1)S(1)} %add_convert_fusion.5), channel_id=1, source_target_pairs={{0,7},{1,0},{2,1},{3,2},{4,3},{5,4},{6,5},{7,6},{8,15},{9,8},{10,9... | collective-permute-start | bytes 786440 | tf_op jit(solution)/shard_map/ppermute | solution.py:350
  128.0 44.1 %copy-start.2 = (s32[1,1,128]{2,1,0:T(1,128)S(1)}, s32[1,1,128]{2,1,0:T(1,128)}, u32[]{:S(2)}) copy-start(s32[1,1,128]{2,1,0:T(1,128)} %param.16) | copy-start | bytes 1540
  128.0 44.1 %copy-start.5 = (f32[128]{0:T(128)S(1)}, f32[128]{0:T(128)}, u32[]{:S(2)}) copy-start(f32[128]{0:T(128)} %param.13) | copy-start | bytes 1540
  128.1 11.2 %collective-permute-start.13 = (bf16[128,1024]{1,0:T(8,128)(2,1)S(1)}, bf16[128,1024]{1,0:T(8,128)(2,1)S(1)}, u32[]{:S(2)}, u32[]{:S(2)}) collective-permute-start(bf16[128,1024]{1,0:T(8,128)(2,1)S(1)} %add_convert_fusion.2), channel_id=1, source_target_pairs={{0,7},{1,0},{2,1},{3,2},{4,3},{5,4},{6,5},{7,6},{8,15},{9,8},{10,9... | collective-permute-start | bytes 786440 | tf_op jit(solution)/shard_map/ppermute | solution.py:350
  133.7 11.2 %collective-permute-start.10 = (bf16[128,1024]{1,0:T(8,128)(2,1)S(1)}, bf16[128,1024]{1,0:T(8,128)(2,1)S(1)}, u32[]{:S(2)}, u32[]{:S(2)}) collective-permute-start(bf16[128,1024]{1,0:T(8,128)(2,1)S(1)} %add_convert_fusion.4), channel_id=1, source_target_pairs={{0,7},{1,0},{2,1},{3,2},{4,3},{5,4},{6,5},{7,6},{8,15},{9,8},{10,9... | collective-permute-start | bytes 786440 | tf_op jit(solution)/shard_map/ppermute | solution.py:350
  139.3 11.2 %collective-permute-start.14 = (bf16[128,1024]{1,0:T(8,128)(2,1)S(1)}, bf16[128,1024]{1,0:T(8,128)(2,1)S(1)}, u32[]{:S(2)}, u32[]{:S(2)}) collective-permute-start(bf16[128,1024]{1,0:T(8,128)(2,1)S(1)} %add_convert_fusion.1), channel_id=1, source_target_pairs={{0,7},{1,0},{2,1},{3,2},{4,3},{5,4},{6,5},{7,6},{8,15},{9,8},{10,9... | collective-permute-start | bytes 786440 | tf_op jit(solution)/shard_map/ppermute | solution.py:350
  145.0 11.2 %collective-permute-start.11 = (bf16[128,1024]{1,0:T(8,128)(2,1)S(1)}, bf16[128,1024]{1,0:T(8,128)(2,1)S(1)}, u32[]{:S(2)}, u32[]{:S(2)}) collective-permute-start(bf16[128,1024]{1,0:T(8,128)(2,1)S(1)} %add_convert_fusion.3), channel_id=1, source_target_pairs={{0,7},{1,0},{2,1},{3,2},{4,3},{5,4},{6,5},{7,6},{8,15},{9,8},{10,9... | collective-permute-start | bytes 786440 | tf_op jit(solution)/shard_map/ppermute | solution.py:350
  150.6 11.1 %collective-permute-start.15 = (bf16[128,1024]{1,0:T(8,128)(2,1)S(1)}, bf16[128,1024]{1,0:T(8,128)(2,1)S(1)}, u32[]{:S(2)}, u32[]{:S(2)}) collective-permute-start(bf16[128,1024]{1,0:T(8,128)(2,1)S(1)} %add_convert_fusion), channel_id=1, source_target_pairs={{0,7},{1,0},{2,1},{3,2},{4,3},{5,4},{6,5},{7,6},{8,15},{9,8},{10,9... | collective-permute-start | bytes 786440 | tf_op jit(solution)/shard_map/ppermute | solution.py:350
  164.7 19.0 %all-to-all-start.3 = ((bf16[32,16,512]{2,1,0:T(8,128)(2,1)}), bf16[32,16,512]{2,1,0:T(8,128)(2,1)S(1)}, u32[]{:S(2)}, u32[]{:S(2)}) async-start(bf16[32,16,512]{2,1,0:T(8,128)(2,1)} %return_kv.1), calls=%async_computation.3 | async-start | bytes 1048576 | tf_op jit(solution)/shard_map/all_to_all | solution.py:345
  172.1 11.5 %copy-start.1 = (bf16[128,1024]{1,0:T(8,128)(2,1)S(1)}, bf16[128,1024]{1,0:T(8,128)(2,1)}, u32[]{:S(2)}) copy-start(bf16[128,1024]{1,0:T(8,128)(2,1)} %k_ref.3) | copy-start | bytes 786436
  172.2 11.5 %copy-start.3 = (f32[128]{0:T(128)S(1)}, f32[128]{0:T(128)}, u32[]{:S(2)}) copy-start(f32[128]{0:T(128)} %param.14) | copy-start | bytes 1540

commit v8 on v6

--- a/solution.py
+++ b/solution.py
@@ -391,23 +391,17 @@
     k_gain = key_norm_gain.reshape(1, HEAD)
     place = lax.axis_index("seq").astype(jnp.int32)
     meta = jnp.concatenate([seq_lengths[0], place[None]])
-    counts = (FIRST, KV_HEADS - FIRST)
-    starts = (0, FIRST)
-
     kv_sent = send_kv(leaving, k_gain, key_projection, value)
     kv_received = exchange(kv_sent)
-    sent = [
-        send_rows(leaving, q_gain, query, d_out, first, count)
-        for first, count in zip(starts, counts)
-    ]
-    kv_received, *sent = lax.optimization_barrier((kv_received, *sent))
-    received_first = exchange(sent[0])
+    sent_first = send_rows(leaving, q_gain, query, d_out, 0, FIRST)
 
     keys, values = ([block] for block in sort_kv(arriving, kv_received))
+    received_first = exchange(after(sent_first, keys[0]))
+    sent_last = send_rows(after(leaving, keys[0]), q_gain, query, d_out, FIRST, LAST)
     for n in range(BACK):
         keys.append(along(after(keys[-1], values[n - 1] if n > 1 else None), 1))
         values.append(along(values[-1], 1))
-    received_last = exchange(after(after(sent[1], received_first), values[BACK - 1]))
+    received_last = exchange(after(after(sent_last, received_first), values[BACK - 1]))
 
     def back_along(parts):
         totals = parts[:1]
@@ -428,15 +422,15 @@
     merged = return_kv(arriving, (sums0[-1], sums1[-1]), (own0, own1), result)
     back_last = exchange(after(merged, back_first))
 
-    outs = finish(leaving, q_gain, query, back_first, starts[0], counts[0])
+    outs = finish(leaving, q_gain, query, back_first, 0, FIRST)
     return tuple(
         finish(
             leaving,
             q_gain,
             query,
             back_last,
-            starts[1],
-            counts[1],
+            FIRST,
+            LAST,
             kv=(k_gain, key_projection),
             earlier=outs,
         )

time: 188 us -> 191 us (1.016)
    all_to_all x5, waiting for transfers between devices: 16.2 us -> 19.5 us  [exchange(): return lax.all_to_all(array, 'dp', split_axis=0, concat_axis=0, tiled=True)]
    ppermute x16, starting transfers between devices: 17.1 us -> 20 us  [along(): lax.ppermute(array, 'seq', [(i, (i + step) % count) for i in range(count)])]
    ppermute x16, waiting for transfers between devices: 57.6 us -> 55 us  [along(): lax.ppermute(array, 'seq', [(i, (i + step) % count) for i in range(count)])]
  transfers between devices with their start and end apart: 21 -> 21, of which waited for: 14 -> 12; matrix products, arithmetic and copies ran while one was open for 0% -> 1% of each run, Pallas kernels for 24% -> 23%
where the time goes in v8:
time: 191 us; the launch traced here: 189 us
  waiting for transfers between devices  74.5 us (39%)
  starting transfers between devices  60.2 us (32%)
  Pallas kernels  51.3 us (27%)
    ppermute x16, waiting for transfers between devices, along(): lax.ppermute(array, 'seq', [(i, (i + step) % count) for i in range(count)])  55 us
    all_to_all x5, starting transfers between devices, exchange(): return lax.all_to_all(array, 'dp', split_axis=0, concat_axis=0, tiled=True)  40.1 us
    pallas_call x2, Pallas kernels, attend(): pl.pallas_call(attend_kernel, grid=(count,), in_specs=[pl.BlockSpec(memor...  24.6 us
    ppermute x16, starting transfers between devices, along(): lax.ppermute(array, 'seq', [(i, (i + step) % count) for i in range(count)])  20 us
    all_to_all x5, waiting for transfers between devices, exchange(): return lax.all_to_all(array, 'dp', split_axis=0, concat_axis=0, tiled=True)  19.5 us
    pallas_call x2, Pallas kernels, finish(): pl.pallas_call(functools.partial(finish_kernel, bool(kv)), grid=(count +...  11.6 us
    pallas_call x2, Pallas kernels, send_rows(): pl.pallas_call(send_rows_kernel, grid=(count,), in_specs=[pl.BlockSpec((1...  10.7 us
  transfers between devices with their start and end apart: 21, of which 12 were waited for; matrix products, arithmetic and copies ran while one was open for 1% of the time, Pallas kernels for 23%

profile of v8, /device:TPU:1, one launch (start us, length us, event | category | flops | bytes accessed | tf_op | source)
XLA Modules:
  0.0 189.4 jit_solution(13264953425514843443)
XLA Ops:
  0.6 2.5 %send_kv.1 = bf16[32,16,512]{2,1,0:T(8,128)(2,1)} custom-call(s32[1,128]{1,0:T(1,128)} %bitcast.6, f32[1,128]{1,0:T(1,128)} %bitcast.15, bf16[128,1024]{1,0:T(8,128)(2,1)} %refs_1_.1, bf16[128,1024]{1,0:T(8,128)(2,1)} %v_ref.1), custom_call_target="tpu_custom_call" | custom-call | flops 268435456 | bytes 1572864 | tf_op jit(solution)/shard_map/send_kv/pallas_call | solution.py:116
  3.1 8.6 %all-to-all-start = ((bf16[32,16,512]{2,1,0:T(8,128)(2,1)}), bf16[32,16,512]{2,1,0:T(8,128)(2,1)S(1)}, u32[]{:S(2)}, u32[]{:S(2)}) async-start(bf16[32,16,512]{2,1,0:T(8,128)(2,1)} %send_kv.1), calls=%async_computation | async-start | bytes 1048576 | tf_op jit(solution)/shard_map/all_to_all | solution.py:373
  11.7 0.0 copy-start.5
  11.8 7.3 %send_rows.2 = bf16[32,16,3072]{2,1,0:T(8,128)(2,1)} custom-call(s32[1,128]{1,0:T(1,128)} %bitcast.7, f32[1,128]{1,0:T(1,128)} %bitcast.11, bf16[128,8192]{1,0:T(8,128)(2,1)} %q_ref.7, bf16[128,8192]{1,0:T(8,128)(2,1)} %d_ref.3), custom_call_target="tpu_custom_call" | custom-call | flops 1610612736 | bytes 6291456 | tf_op jit(solution)/shard_map/send_rows/pallas_call | solution.py:146
  19.0 4.3 %all-to-all-done.in_ref = bf16[32,16,512]{2,1,0:T(8,128)(2,1)S(1)} async-done(((bf16[32,16,512]{2,1,0:T(8,128)(2,1)}), bf16[32,16,512]{2,1,0:T(8,128)(2,1)S(1)}, u32[]{:S(2)}, u32[]{:S(2)}) %all-to-all-start) | async-done | bytes 524320 | tf_op jit(solution)/shard_map/all_to_all | solution.py:373
  23.3 0.0 copy-done.5
  23.3 0.5 sort_kv.1
  23.8 4.9 %all-to-all-start.1 = ((bf16[32,16,3072]{2,1,0:T(8,128)(2,1)}), bf16[32,16,3072]{2,1,0:T(8,128)(2,1)}, u32[]{:S(2)}, u32[]{:S(2)}) async-start(bf16[32,16,3072]{2,1,0:T(8,128)(2,1)} %send_rows.2), calls=%async_computation.1 | async-start | bytes 6291456 | tf_op jit(solution)/shard_map/all_to_all | solution.py:373
  28.7 1.7 collective-permute-start
  30.4 1.6 collective-permute-start.2
  32.1 8.7 %collective-permute-done.refs_3_ = bf16[128,1024]{1,0:T(8,128)(2,1)S(1)} collective-permute-done((bf16[128,1024]{1,0:T(8,128)(2,1)S(1)}, bf16[128,1024]{1,0:T(8,128)(2,1)S(1)}, u32[]{:S(2)}, u32[]{:S(2)}) %collective-permute-start) | collective-permute-done | bytes 262176 | tf_op jit(solution)/shard_map/ppermute | solution.py:378
  40.8 0.0 collective-permute-start.1
  40.8 5.6 %collective-permute-done.2.refs_8_ = bf16[128,1024]{1,0:T(8,128)(2,1)S(1)} collective-permute-done((bf16[128,1024]{1,0:T(8,128)(2,1)S(1)}, bf16[128,1024]{1,0:T(8,128)(2,1)S(1)}, u32[]{:S(2)}, u32[]{:S(2)}) %collective-permute-start.2) | collective-permute-done | bytes 262176 | tf_op jit(solution)/shard_map/ppermute | solution.py:378
  46.4 0.0 collective-permute-start.4
  46.4 5.6 %collective-permute-done.1.refs_2_ = bf16[128,1024]{1,0:T(8,128)(2,1)S(1)} collective-permute-done((bf16[128,1024]{1,0:T(8,128)(2,1)S(1)}, bf16[128,1024]{1,0:T(8,128)(2,1)S(1)}, u32[]{:S(2)}, u32[]{:S(2)}) %collective-permute-start.1) | collective-permute-done | bytes 262176 | tf_op jit(solution)/shard_map/ppermute | solution.py:378
  52.0 0.0 collective-permute-start.3
  52.0 5.6 %collective-permute-done.4.refs_7_ = bf16[128,1024]{1,0:T(8,128)(2,1)S(1)} collective-permute-done((bf16[128,1024]{1,0:T(8,128)(2,1)S(1)}, bf16[128,1024]{1,0:T(8,128)(2,1)S(1)}, u32[]{:S(2)}, u32[]{:S(2)}) %collective-permute-start.4) | collective-permute-done | bytes 262176 | tf_op jit(solution)/shard_map/ppermute | solution.py:378
  57.6 0.0 collective-permute-start.6
  57.6 5.6 %collective-permute-done.3.refs_1_ = bf16[128,1024]{1,0:T(8,128)(2,1)S(1)} collective-permute-done((bf16[128,1024]{1,0:T(8,128)(2,1)S(1)}, bf16[128,1024]{1,0:T(8,128)(2,1)S(1)}, u32[]{:S(2)}, u32[]{:S(2)}) %collective-permute-start.3) | collective-permute-done | bytes 262176 | tf_op jit(solution)/shard_map/ppermute | solution.py:378
  63.3 0.0 collective-permute-start.5
  63.3 5.6 %collective-permute-done.6.refs_6_ = bf16[128,1024]{1,0:T(8,128)(2,1)S(1)} collective-permute-done((bf16[128,1024]{1,0:T(8,128)(2,1)S(1)}, bf16[128,1024]{1,0:T(8,128)(2,1)S(1)}, u32[]{:S(2)}, u32[]{:S(2)}) %collective-permute-start.6) | collective-permute-done | bytes 262176 | tf_op jit(solution)/shard_map/ppermute | solution.py:378
  68.9 0.0 collective-permute-start.7
  68.9 3.4 %send_rows.3 = bf16[32,16,1024]{2,1,0:T(8,128)(2,1)} custom-call(s32[1,128]{1,0:T(1,128)} %bitcast.8, f32[1,128]{1,0:T(1,128)} %bitcast.12, bf16[128,8192]{1,0:T(8,128)(2,1)} %q_ref.7, bf16[128,8192]{1,0:T(8,128)(2,1)} %d_ref.3), custom_call_target="tpu_custom_call" | custom-call | flops 536870912 | bytes 2097152 | tf_op jit(solution)/shard_map/send_rows/pallas_call | solution.py:146
  72.3 0.0 all-to-all-done.1.qd_ref
  72.4 8.5 %all-to-all-start.2 = ((bf16[32,16,1024]{2,1,0:T(8,128)(2,1)}), bf16[32,16,1024]{2,1,0:T(8,128)(2,1)S(1)}, u32[]{:S(2)}, u32[]{:S(2)}) async-start(bf16[32,16,1024]{2,1,0:T(8,128)(2,1)} %send_rows.3), calls=%async_computation.2 | async-start | bytes 2097152 | tf_op jit(solution)/shard_map/all_to_all | solution.py:373
  80.8 0.1 pad_add_fusion.meta_ref
  80.9 0.0 collective-permute-done.5.refs_0_
  80.9 0.0 collective-permute-done.7.refs_5_
  80.9 17.4 %attend.2 = (bf16[32,16,3072]{2,1,0:T(8,128)(2,1)}, bf16[128,1536]{1,0:T(8,128)(2,1)}, f32[128,1536]{1,0:T(8,128)}, f32[128,1536]{1,0:T(8,128)}, f32[128,1536]{1,0:T(8,128)}, /*index=5*/f32[128,1536]{1,0:T(8,128)}) custom-call(s32[4]{0:T(128)S(1)} %pad_add_fusion.meta_ref, s32[1,128]{1,0:T(1,128)S(1)} %bitcast.18, ...), custom_call_target="tpu_custom_call" | custom-call | flops 6039797760 | bytes 18874368 | tf_op jit(solution)/shard_map/attend/pallas_call | solution.py:241
  98.4 2.9 %collective-permute-start.8 = (bf16[128,1536]{1,0:T(8,128)(2,1)}, bf16[128,1536]{1,0:T(8,128)(2,1)S(1)}, u32[]{:S(2)}, u32[]{:S(2)}) collective-permute-start(bf16[128,1536]{1,0:T(8,128)(2,1)} %get-tuple-element.33), channel_id=1, source_target_pairs={{0,7},{1,0},{2,1},{3,2},{4,3},{5,4},{6,5},{7,6},{8,15},{9,8},{10,9... | collective-permute-start | bytes 1179656 | tf_op jit(solution)/shard_map/ppermute | solution.py:378
  101.3 0.0 all-to-all-done.2.qd_ref
  101.3 1.0 copy-done.11
  102.3 7.7 %all-to-all-start.3 = ((bf16[32,16,3072]{2,1,0:T(8,128)(2,1)}), bf16[32,16,3072]{2,1,0:T(8,128)(2,1)}, u32[]{:S(2)}, u32[]{:S(2)}) async-start(bf16[32,16,3072]{2,1,0:T(8,128)(2,1)} %get-tuple-element.48), calls=%async_computation.3 | async-start | bytes 6291456 | tf_op jit(solution)/shard_map/all_to_all | solution.py:373
  110.0 0.0 collective-permute-done.8
  110.0 1.2 add_convert_fusion.2
  111.2 3.1 %collective-permute-start.9 = (bf16[128,1536]{1,0:T(8,128)(2,1)S(1)}, bf16[128,1536]{1,0:T(8,128)(2,1)S(1)}, u32[]{:S(2)}, u32[]{:S(2)}) collective-permute-start(bf16[128,1536]{1,0:T(8,128)(2,1)S(1)} %add_convert_fusion.2), channel_id=1, source_target_pairs={{0,7},{1,0},{2,1},{3,2},{4,3},{5,4},{6,5},{7,6},{8,15},{9,8},{10,9... | collective-permute-start | bytes 1179656 | tf_op jit(solution)/shard_map/ppermute | solution.py:378
  114.3 7.2 %attend.3 = (bf16[32,16,1536]{2,1,0:T(8,128)(2,1)}, bf16[128,512]{1,0:T(8,128)(2,1)S(1)}, f32[128,512]{1,0:T(8,128)S(1)}, f32[128,512]{1,0:T(8,128)S(1)}, f32[12...) custom-call(s32[4]{0:T(128)S(1)} %pad_add_fusion.meta_ref, s32[1,128]{1,0:T(1,128)S(1)} %bitcast.19, ...), custom_call_target="tpu_custom_call" | custom-call | flops 6039797760 | bytes 6291456 | tf_op jit(solution)/shard_map/attend/pallas_call | solution.py:241
  121.5 0.2 collective-permute-start.12
  121.7 0.0 collective-permute-done.9
  121.7 0.0 copy-done.13
  121.7 0.1 add_convert_fusion.1
  121.8 3.4 %collective-permute-start.10 = (bf16[128,1536]{1,0:T(8,128)(2,1)S(1)}, bf16[128,1536]{1,0:T(8,128)(2,1)S(1)}, u32[]{:S(2)}, u32[]{:S(2)}) collective-permute-start(bf16[128,1536]{1,0:T(8,128)(2,1)S(1)} %add_convert_fusion.1), channel_id=1, source_target_pairs={{0,7},{1,0},{2,1},{3,2},{4,3},{5,4},{6,5},{7,6},{8,15},{9,8},{10,9... | collective-permute-start | bytes 1179656 | tf_op jit(solution)/shard_map/ppermute | solution.py:378
  125.2 0.7 collective-permute-done.12
  125.9 2.9 %collective-permute-start.13 = (bf16[128,512]{1,0:T(8,128)(2,1)S(1)}, bf16[128,512]{1,0:T(8,128)(2,1)S(1)}, u32[]{:S(2)}, u32[]{:S(2)}) collective-permute-start(bf16[128,512]{1,0:T(8,128)(2,1)S(1)} %add_convert_fusion.5), channel_id=1, source_target_pairs={{0,7},{1,0},{2,1},{3,2},{4,3},{5,4},{6,5},{7,6},{8,15},{9,8},{10,9... | collective-permute-start | bytes 393224 | tf_op jit(solution)/shard_map/ppermute | solution.py:378
  128.7 7.7 %collective-permute-done.13 = bf16[128,512]{1,0:T(8,128)(2,1)S(1)} collective-permute-done((bf16[128,512]{1,0:T(8,128)(2,1)S(1)}, bf16[128,512]{1,0:T(8,128)(2,1)S(1)}, u32[]{:S(2)}, u32[]{:S(2)}) %collective-permute-start.13) | collective-permute-done | bytes 131104 | tf_op jit(solution)/shard_map/ppermute | solution.py:378
  136.5 1.3 collective-permute-start.14
  137.8 0.0 collective-permute-done.10
  137.8 0.1 add_convert_fusion
  137.9 0.1 collective-permute-start.11
  138.0 2.8 %collective-permute-done.14 = bf16[128,512]{1,0:T(8,128)(2,1)S(1)} collective-permute-done((bf16[128,512]{1,0:T(8,128)(2,1)S(1)}, bf16[128,512]{1,0:T(8,128)(2,1)S(1)}, u32[]{:S(2)}, u32[]{:S(2)}) %collective-permute-start.14) | collective-permute-done | bytes 131104 | tf_op jit(solution)/shard_map/ppermute | solution.py:378
  140.8 2.8 %collective-permute-start.15 = (bf16[128,512]{1,0:T(8,128)(2,1)S(1)}, bf16[128,512]{1,0:T(8,128)(2,1)S(1)}, u32[]{:S(2)}, u32[]{:S(2)}) collective-permute-start(bf16[128,512]{1,0:T(8,128)(2,1)S(1)} %add_convert_fusion.3), channel_id=1, source_target_pairs={{0,7},{1,0},{2,1},{3,2},{4,3},{5,4},{6,5},{7,6},{8,15},{9,8},{10,9... | collective-permute-start | bytes 393224 | tf_op jit(solution)/shard_map/ppermute | solution.py:378
  143.5 7.0 %collective-permute-done.15.refs_1_ = bf16[128,512]{1,0:T(8,128)(2,1)S(1)} collective-permute-done((bf16[128,512]{1,0:T(8,128)(2,1)S(1)}, bf16[128,512]{1,0:T(8,128)(2,1)S(1)}, u32[]{:S(2)}, u32[]{:S(2)}) %collective-permute-start.15) | collective-permute-done | bytes 131104 | tf_op jit(solution)/shard_map/ppermute | solution.py:378
  150.6 0.0 collective-permute-done.11.refs_0_
  150.6 0.0 copy-done.1
  150.6 1.4 return_kv.1
  152.0 0.0 all-to-all-done.3.in_ref
  152.0 10.5 %all-to-all-start.4 = ((bf16[32,16,1536]{2,1,0:T(8,128)(2,1)}), bf16[32,16,1536]{2,1,0:T(8,128)(2,1)S(1)}, u32[]{:S(2)}, u32[]{:S(2)}) async-start(bf16[32,16,1536]{2,1,0:T(8,128)(2,1)} %return_kv.1), calls=%async_computation.4 | async-start | bytes 3145728 | tf_op jit(solution)/shard_map/all_to_all | solution.py:373
  162.5 0.0 copy-done.2
  162.5 0.0 copy-done.3
  162.5 0.0 copy-start
  162.5 0.0 copy-start.4
  162.5 6.9 %finish.2 = (bf16[128,8192]{1,0:T(8,128)(2,1)}, bf16[128,8192]{1,0:T(8,128)(2,1)}) custom-call(s32[1,128]{1,0:T(1,128)S(1)} %bitcast.9, f32[1,128]{1,0:T(1,128)S(1)} %bitcast.13, bf16[128,8192]{1,0:T(8,128)(2,1)} %q_ref.7, bf16[32,16,3072]{2,1,0:T(8,128)(2,1)} %all-to-all-done.3.in_ref), custom_call_target="tpu_custom_call" | custom-call | flops 1610612736 | bytes 7864320 | tf_op jit(solution)/shard_map/finish/pallas_call | solution.py:358
  169.5 15.2 %all-to-all-done.4.in_ref = bf16[32,16,1536]{2,1,0:T(8,128)(2,1)S(1)} async-done(((bf16[32,16,1536]{2,1,0:T(8,128)(2,1)}), bf16[32,16,1536]{2,1,0:T(8,128)(2,1)S(1)}, u32[]{:S(2)}, u32[]{:S(2)}) %all-to-all-start.4) | async-done | bytes 1572896 | tf_op jit(solution)/shard_map/all_to_all | solution.py:373
  184.7 4.7 %finish.3 = (bf16[128,8192]{1,0:T(8,128)(2,1)}, bf16[128,8192]{1,0:T(8,128)(2,1)}, bf16[128,1024]{1,0:T(8,128)(2,1)}, bf16[128,1024]{1,0:T(8,128)(2,1)}) custom-call(s32[1,128]{1,0:T(1,128)S(1)} %bitcast.10, f32[1,128]{1,0:T(1,128)S(1)} %bitcast.14, bf16[128,8192]{1,0:T(8,128)(2,1)} %q_ref.7, ...), custom_call_target="tpu_custom_call", output_to_operand_aliasing={{0}: (6, {}), {1}: (7, {})} | custom-call | flops 536870912 | bytes 2621440 | tf_op jit(solution)/shard_map/finish/pallas_call | solution.py:358
  (28 shorter events, 0.1 us)
Async XLA Ops:
  3.1 20.1 %all-to-all-start = ((bf16[32,16,512]{2,1,0:T(8,128)(2,1)}), bf16[32,16,512]{2,1,0:T(8,128)(2,1)S(1)}, u32[]{:S(2)}, u32[]{:S(2)}) async-start(bf16[32,16,512]{2,1,0:T(8,128)(2,1)} %send_kv.1), calls=%async_computation | async-start | bytes 1048576 | tf_op jit(solution)/shard_map/all_to_all | solution.py:373
  11.7 11.6 %copy-start.5 = (s32[1,1,128]{2,1,0:T(1,128)S(1)}, s32[1,1,128]{2,1,0:T(1,128)}, u32[]{:S(2)}) copy-start(s32[1,1,128]{2,1,0:T(1,128)} %param.17) | copy-start | bytes 1540
  23.8 6.6 %copy-start.7 = (bf16[128,1024]{1,0:T(8,128)(2,1)}, bf16[128,1024]{1,0:T(8,128)(2,1)S(1)}, u32[]{:S(2)}) copy-start(bf16[128,1024]{1,0:T(8,128)(2,1)S(1)} %get-tuple-element.30.refs_9_) | copy-start | bytes 786436
  23.8 57.1 %copy-start.6 = (bf16[128,1024]{1,0:T(8,128)(2,1)}, bf16[128,1024]{1,0:T(8,128)(2,1)S(1)}, u32[]{:S(2)}) copy-start(bf16[128,1024]{1,0:T(8,128)(2,1)S(1)} %get-tuple-element.40.refs_4_) | copy-start | bytes 786436
  23.8 48.5 %all-to-all-start.1 = ((bf16[32,16,3072]{2,1,0:T(8,128)(2,1)}), bf16[32,16,3072]{2,1,0:T(8,128)(2,1)}, u32[]{:S(2)}, u32[]{:S(2)}) async-start(bf16[32,16,3072]{2,1,0:T(8,128)(2,1)} %send_rows.2), calls=%async_computation.1 | async-start | bytes 6291456 | tf_op jit(solution)/shard_map/all_to_all | solution.py:373
  28.7 12.1 %collective-permute-start = (bf16[128,1024]{1,0:T(8,128)(2,1)S(1)}, bf16[128,1024]{1,0:T(8,128)(2,1)S(1)}, u32[]{:S(2)}, u32[]{:S(2)}) collective-permute-start(bf16[128,1024]{1,0:T(8,128)(2,1)S(1)} %get-tuple-element.40.refs_4_), channel_id=1, source_target_pairs={{0,1},{1,2},{2,3},{3,4},{4,5},{5,6},{6,7},{7,0},{8,9},{9,10},{10,1... | collective-permute-start | bytes 786440 | tf_op jit(solution)/shard_map/ppermute | solution.py:378
  30.4 16.0 %collective-permute-start.2 = (bf16[128,1024]{1,0:T(8,128)(2,1)S(1)}, bf16[128,1024]{1,0:T(8,128)(2,1)S(1)}, u32[]{:S(2)}, u32[]{:S(2)}) collective-permute-start(bf16[128,1024]{1,0:T(8,128)(2,1)S(1)} %get-tuple-element.30.refs_9_), channel_id=1, source_target_pairs={{0,1},{1,2},{2,3},{3,4},{4,5},{5,6},{6,7},{7,0},{8,9},{9,10},{10,1... | collective-permute-start | bytes 786440 | tf_op jit(solution)/shard_map/ppermute | solution.py:378
  40.8 40.1 %copy-start.8 = (bf16[128,1024]{1,0:T(8,128)(2,1)}, bf16[128,1024]{1,0:T(8,128)(2,1)S(1)}, u32[]{:S(2)}) copy-start(bf16[128,1024]{1,0:T(8,128)(2,1)S(1)} %collective-permute-done.refs_3_) | copy-start | bytes 786436
  40.8 11.2 %collective-permute-start.1 = (bf16[128,1024]{1,0:T(8,128)(2,1)S(1)}, bf16[128,1024]{1,0:T(8,128)(2,1)S(1)}, u32[]{:S(2)}, u32[]{:S(2)}) collective-permute-start(bf16[128,1024]{1,0:T(8,128)(2,1)S(1)} %collective-permute-done.refs_3_), channel_id=1, source_target_pairs={{0,1},{1,2},{2,3},{3,4},{4,5},{5,6},{6,7},{7,0},{8,9},{9,10},{10,1... | collective-permute-start | bytes 786440 | tf_op jit(solution)/shard_map/ppermute | solution.py:378
  46.4 22.5 %copy-start.14 = (bf16[128,1024]{1,0:T(8,128)(2,1)}, bf16[128,1024]{1,0:T(8,128)(2,1)S(1)}, u32[]{:S(2)}) copy-start(bf16[128,1024]{1,0:T(8,128)(2,1)S(1)} %collective-permute-done.2.refs_8_) | copy-start | bytes 786436
  46.4 11.2 %collective-permute-start.4 = (bf16[128,1024]{1,0:T(8,128)(2,1)S(1)}, bf16[128,1024]{1,0:T(8,128)(2,1)S(1)}, u32[]{:S(2)}, u32[]{:S(2)}) collective-permute-start(bf16[128,1024]{1,0:T(8,128)(2,1)S(1)} %collective-permute-done.2.refs_8_), channel_id=1, source_target_pairs={{0,1},{1,2},{2,3},{3,4},{4,5},{5,6},{6,7},{7,0},{8,9},{9,10},{10,1... | collective-permute-start | bytes 786440 | tf_op jit(solution)/shard_map/ppermute | solution.py:378
  52.0 11.2 %collective-permute-start.3 = (bf16[128,1024]{1,0:T(8,128)(2,1)S(1)}, bf16[128,1024]{1,0:T(8,128)(2,1)S(1)}, u32[]{:S(2)}, u32[]{:S(2)}) collective-permute-start(bf16[128,1024]{1,0:T(8,128)(2,1)S(1)} %collective-permute-done.1.refs_2_), channel_id=1, source_target_pairs={{0,1},{1,2},{2,3},{3,4},{4,5},{5,6},{6,7},{7,0},{8,9},{9,10},{10,1... | collective-permute-start | bytes 786440 | tf_op jit(solution)/shard_map/ppermute | solution.py:378
  57.6 11.2 %copy-start.15 = (bf16[128,1024]{1,0:T(8,128)(2,1)}, bf16[128,1024]{1,0:T(8,128)(2,1)S(1)}, u32[]{:S(2)}) copy-start(bf16[128,1024]{1,0:T(8,128)(2,1)S(1)} %collective-permute-done.4.refs_7_) | copy-start | bytes 786436
  57.6 11.2 %collective-permute-start.6 = (bf16[128,1024]{1,0:T(8,128)(2,1)S(1)}, bf16[128,1024]{1,0:T(8,128)(2,1)S(1)}, u32[]{:S(2)}, u32[]{:S(2)}) collective-permute-start(bf16[128,1024]{1,0:T(8,128)(2,1)S(1)} %collective-permute-done.4.refs_7_), channel_id=1, source_target_pairs={{0,1},{1,2},{2,3},{3,4},{4,5},{5,6},{6,7},{7,0},{8,9},{9,10},{10,1... | collective-permute-start | bytes 786440 | tf_op jit(solution)/shard_map/ppermute | solution.py:378
  63.3 17.6 %collective-permute-start.5 = (bf16[128,1024]{1,0:T(8,128)(2,1)S(1)}, bf16[128,1024]{1,0:T(8,128)(2,1)S(1)}, u32[]{:S(2)}, u32[]{:S(2)}) collective-permute-start(bf16[128,1024]{1,0:T(8,128)(2,1)S(1)} %collective-permute-done.3.refs_1_), channel_id=1, source_target_pairs={{0,1},{1,2},{2,3},{3,4},{4,5},{5,6},{6,7},{7,0},{8,9},{9,10},{10,1... | collective-permute-start | bytes 786440 | tf_op jit(solution)/shard_map/ppermute | solution.py:378
  68.9 12.0 %copy-start.9 = (bf16[128,1024]{1,0:T(8,128)(2,1)}, bf16[128,1024]{1,0:T(8,128)(2,1)S(1)}, u32[]{:S(2)}) copy-start(bf16[128,1024]{1,0:T(8,128)(2,1)S(1)} %collective-permute-done.6.refs_6_) | copy-start | bytes 786436
  68.9 12.0 %collective-permute-start.7 = (bf16[128,1024]{1,0:T(8,128)(2,1)S(1)}, bf16[128,1024]{1,0:T(8,128)(2,1)S(1)}, u32[]{:S(2)}, u32[]{:S(2)}) collective-permute-start(bf16[128,1024]{1,0:T(8,128)(2,1)S(1)} %collective-permute-done.6.refs_6_), channel_id=1, source_target_pairs={{0,1},{1,2},{2,3},{3,4},{4,5},{5,6},{6,7},{7,0},{8,9},{9,10},{10,1... | collective-permute-start | bytes 786440 | tf_op jit(solution)/shard_map/ppermute | solution.py:378
  72.3 8.5 %copy-start.16 = (s32[1,3]{1,0:T(1,128)S(1)}, s32[1,3]{1,0:T(1,128)}, u32[]{:S(2)}) copy-start(s32[1,3]{1,0:T(1,128)} %param.15) | copy-start | bytes 40
  72.4 29.0 %all-to-all-start.2 = ((bf16[32,16,1024]{2,1,0:T(8,128)(2,1)}), bf16[32,16,1024]{2,1,0:T(8,128)(2,1)S(1)}, u32[]{:S(2)}, u32[]{:S(2)}) async-start(bf16[32,16,1024]{2,1,0:T(8,128)(2,1)} %send_rows.3), calls=%async_computation.2 | async-start | bytes 2097152 | tf_op jit(solution)/shard_map/all_to_all | solution.py:373
  80.9 17.4 %copy-start.10 = (bf16[128,1024]{1,0:T(8,128)(2,1)}, bf16[128,1024]{1,0:T(8,128)(2,1)S(1)}, u32[]{:S(2)}) copy-start(bf16[128,1024]{1,0:T(8,128)(2,1)S(1)} %collective-permute-done.7.refs_5_) | copy-start | bytes 786436
  98.4 11.6 %collective-permute-start.8 = (bf16[128,1536]{1,0:T(8,128)(2,1)}, bf16[128,1536]{1,0:T(8,128)(2,1)S(1)}, u32[]{:S(2)}, u32[]{:S(2)}) collective-permute-start(bf16[128,1536]{1,0:T(8,128)(2,1)} %get-tuple-element.33), channel_id=1, source_target_pairs={{0,7},{1,0},{2,1},{3,2},{4,3},{5,4},{6,5},{7,6},{8,15},{9,8},{10,9... | collective-permute-start | bytes 1179656 | tf_op jit(solution)/shard_map/ppermute | solution.py:378
  101.3 1.0 copy-start.11
  102.3 49.7 %all-to-all-start.3 = ((bf16[32,16,3072]{2,1,0:T(8,128)(2,1)}), bf16[32,16,3072]{2,1,0:T(8,128)(2,1)}, u32[]{:S(2)}, u32[]{:S(2)}) async-start(bf16[32,16,3072]{2,1,0:T(8,128)(2,1)} %get-tuple-element.48), calls=%async_computation.3 | async-start | bytes 6291456 | tf_op jit(solution)/shard_map/all_to_all | solution.py:373
  111.2 10.5 %copy-start.13 = (f32[128,1536]{1,0:T(8,128)S(1)}, f32[128,1536]{1,0:T(8,128)}, u32[]{:S(2)}) copy-start(f32[128,1536]{1,0:T(8,128)} %get-tuple-element.35) | copy-start | bytes 2359300
  111.2 10.5 %collective-permute-start.9 = (bf16[128,1536]{1,0:T(8,128)(2,1)S(1)}, bf16[128,1536]{1,0:T(8,128)(2,1)S(1)}, u32[]{:S(2)}, u32[]{:S(2)}) collective-permute-start(bf16[128,1536]{1,0:T(8,128)(2,1)S(1)} %add_convert_fusion.2), channel_id=1, source_target_pairs={{0,7},{1,0},{2,1},{3,2},{4,3},{5,4},{6,5},{7,6},{8,15},{9,8},{10,9... | collective-permute-start | bytes 1179656 | tf_op jit(solution)/shard_map/ppermute | solution.py:378
  121.5 16.3 %copy-start.12 = (f32[128,1536]{1,0:T(8,128)S(1)}, f32[128,1536]{1,0:T(8,128)}, u32[]{:S(2)}) copy-start(f32[128,1536]{1,0:T(8,128)} %get-tuple-element.36) | copy-start | bytes 2359300
  121.5 4.3 %collective-permute-start.12 = (bf16[128,512]{1,0:T(8,128)(2,1)S(1)}, bf16[128,512]{1,0:T(8,128)(2,1)S(1)}, u32[]{:S(2)}, u32[]{:S(2)}) collective-permute-start(bf16[128,512]{1,0:T(8,128)(2,1)S(1)} %get-tuple-element.41), channel_id=1, source_target_pairs={{0,7},{1,0},{2,1},{3,2},{4,3},{5,4},{6,5},{7,6},{8,15},{9,8},{10,9... | collective-permute-start | bytes 393224 | tf_op jit(solution)/shard_map/ppermute | solution.py:378
  121.7 28.9 %copy-start.1 = (f32[128,1536]{1,0:T(8,128)S(1)}, f32[128,1536]{1,0:T(8,128)}, u32[]{:S(2)}) copy-start(f32[128,1536]{1,0:T(8,128)} %get-tuple-element.45.refs_2_) | copy-start | bytes 2359300
  121.8 16.0 %collective-permute-start.10 = (bf16[128,1536]{1,0:T(8,128)(2,1)S(1)}, bf16[128,1536]{1,0:T(8,128)(2,1)S(1)}, u32[]{:S(2)}, u32[]{:S(2)}) collective-permute-start(bf16[128,1536]{1,0:T(8,128)(2,1)S(1)} %add_convert_fusion.1), channel_id=1, source_target_pairs={{0,7},{1,0},{2,1},{3,2},{4,3},{5,4},{6,5},{7,6},{8,15},{9,8},{10,9... | collective-permute-start | bytes 1179656 | tf_op jit(solution)/shard_map/ppermute | solution.py:378
  125.9 10.6 %collective-permute-start.13 = (bf16[128,512]{1,0:T(8,128)(2,1)S(1)}, bf16[128,512]{1,0:T(8,128)(2,1)S(1)}, u32[]{:S(2)}, u32[]{:S(2)}) collective-permute-start(bf16[128,512]{1,0:T(8,128)(2,1)S(1)} %add_convert_fusion.5), channel_id=1, source_target_pairs={{0,7},{1,0},{2,1},{3,2},{4,3},{5,4},{6,5},{7,6},{8,15},{9,8},{10,9... | collective-permute-start | bytes 393224 | tf_op jit(solution)/shard_map/ppermute | solution.py:378
  136.5 4.3 %collective-permute-start.14 = (bf16[128,512]{1,0:T(8,128)(2,1)S(1)}, bf16[128,512]{1,0:T(8,128)(2,1)S(1)}, u32[]{:S(2)}, u32[]{:S(2)}) collective-permute-start(bf16[128,512]{1,0:T(8,128)(2,1)S(1)} %add_convert_fusion.4), channel_id=1, source_target_pairs={{0,7},{1,0},{2,1},{3,2},{4,3},{5,4},{6,5},{7,6},{8,15},{9,8},{10,9... | collective-permute-start | bytes 393224 | tf_op jit(solution)/shard_map/ppermute | solution.py:378
  137.9 12.7 %collective-permute-start.11 = (bf16[128,1536]{1,0:T(8,128)(2,1)S(1)}, bf16[128,1536]{1,0:T(8,128)(2,1)S(1)}, u32[]{:S(2)}, u32[]{:S(2)}) collective-permute-start(bf16[128,1536]{1,0:T(8,128)(2,1)S(1)} %add_convert_fusion), channel_id=1, source_target_pairs={{0,7},{1,0},{2,1},{3,2},{4,3},{5,4},{6,5},{7,6},{8,15},{9,8},{10,9... | collective-permute-start | bytes 1179656 | tf_op jit(solution)/shard_map/ppermute | solution.py:378
  140.8 9.8 %collective-permute-start.15 = (bf16[128,512]{1,0:T(8,128)(2,1)S(1)}, bf16[128,512]{1,0:T(8,128)(2,1)S(1)}, u32[]{:S(2)}, u32[]{:S(2)}) collective-permute-start(bf16[128,512]{1,0:T(8,128)(2,1)S(1)} %add_convert_fusion.3), channel_id=1, source_target_pairs={{0,7},{1,0},{2,1},{3,2},{4,3},{5,4},{6,5},{7,6},{8,15},{9,8},{10,9... | collective-permute-start | bytes 393224 | tf_op jit(solution)/shard_map/ppermute | solution.py:378
  152.0 10.5 %copy-start.2 = (s32[1,1,128]{2,1,0:T(1,128)S(1)}, s32[1,1,128]{2,1,0:T(1,128)}, u32[]{:S(2)}) copy-start(s32[1,1,128]{2,1,0:T(1,128)} %param.16) | copy-start | bytes 1540
  152.0 10.6 %copy-start.3 = (f32[128]{0:T(128)S(1)}, f32[128]{0:T(128)}, u32[]{:S(2)}) copy-start(f32[128]{0:T(128)} %param.13) | copy-start | bytes 1540
  152.0 32.7 %all-to-all-start.4 = ((bf16[32,16,1536]{2,1,0:T(8,128)(2,1)}), bf16[32,16,1536]{2,1,0:T(8,128)(2,1)S(1)}, u32[]{:S(2)}, u32[]{:S(2)}) async-start(bf16[32,16,1536]{2,1,0:T(8,128)(2,1)} %return_kv.1), calls=%async_computation.4 | async-start | bytes 3145728 | tf_op jit(solution)/shard_map/all_to_all | solution.py:373
  162.5 22.2 %copy-start = (bf16[128,1024]{1,0:T(8,128)(2,1)S(1)}, bf16[128,1024]{1,0:T(8,128)(2,1)}, u32[]{:S(2)}) copy-start(bf16[128,1024]{1,0:T(8,128)(2,1)} %refs_1_.1) | copy-start | bytes 786436
  162.5 22.2 %copy-start.4 = (f32[128]{0:T(128)S(1)}, f32[128]{0:T(128)}, u32[]{:S(2)}) copy-start(f32[128]{0:T(128)} %param.14) | copy-start | bytes 1540
